TPU v7x, 32 devices: a whole 2x2x4 slice. The times are simulated.
32 devices in a mesh: paths: 2 (over x), qa: 8 (over z, y), qb: 2 (over core).
Axes of the slice: x: 2, y: 2, z: 4, core: 2. Of those that a mesh axis runs over, the one named last changes fastest.
Arguments:
- state: float32 [2, 4194304], P(None, ('paths', 'qa', 'qb')), parts along dimension 1, may hold values from -6 to 6
- gate_terms: float32 [18, 2, 2, 128, 128], replicated, may hold values from -0.375 to 0.375
- path_bits: int32 [36], P('paths'), parts along dimension 0, may hold values from 0 to 1
Outputs:
- final_state: float32 [2, 4194304], P(None, ('paths', 'qa', 'qb')), parts along dimension 1
There are 2 independent parts, one for each index of `paths`. A program takes and returns all parts, laid end to end along the dimension named above; an argument that names none is the same for every part. Nothing has to cross between parts.
All inputs are finite; a program needn't handle non-finite values.
Results may differ from a plain program's by a relative error of at most 0.00013.
Values sent between devices are 32-bit elements; how exact they have to be, the bound alone decides.
No kernel may reach another device: no remote copies, remote signals or barrier semaphores. Data moves between devices by JAX's collectives and lax.ppermute only.
A program may use at most 64 MiB of HBM per device.

v0:
```python
import functools

import jax
import jax.numpy as jnp
from jax import lax
from jax.experimental import pallas as pl
from jax.experimental.pallas import tpu as pltpu
from jax.sharding import PartitionSpec as P

F32 = jnp.float32
BF16 = jnp.bfloat16
VMEM_LIMIT = 48 * 1024 * 1024


def window_offsets(span, gate_bits):
    return [0, span, gate_bits, span - 1, gate_bits + 1, span - 2]


def plan_gates(local_bits, gate_bits):
    outer = window_offsets(local_bits - gate_bits, gate_bits)
    inner = window_offsets(local_bits - gate_bits - 1, gate_bits)
    low, sections = [], []
    for number, offsets in enumerate((outer, inner, outer)):
        section = []
        for index, offset in enumerate(offsets):
            gate = 6 * number + index
            if offset == 0:
                low.append(gate)
            elif section and section[-1][0] == offset:
                section[-1][1].append(gate)
            else:
                section.append((offset, [gate]))
        sections.append(section)
    return low, sections


def exact_dot(a, b):
    return lax.dot_general(
        a, b, (((1,), (0,)), ((), ())), precision=lax.Precision.HIGHEST, preferred_element_type=F32
    )


def split(x):
    high = x.astype(BF16)
    return high, (x - high.astype(F32)).astype(BF16)


def bf_dot(a, b):
    return jnp.dot(a, b, preferred_element_type=F32)


def prepare_kernel(low, products, bits_ref, gates_ref, low_ref, rows_ref, held, sems):
    count = held.shape[0]
    copies = []
    for gate in range(count):
        copy = pltpu.make_async_copy(gates_ref.at[gate, bits_ref[gate]], held.at[gate], sems.at[gate])
        copy.start()
        copies.append(copy)
    for copy in copies:
        copy.wait()

    def block(real, imag):
        return jnp.concatenate(
            [jnp.concatenate([real, -imag], axis=1), jnp.concatenate([imag, real], axis=1)], axis=0
        )

    def product(gates):
        real, imag = held[gates[0], 0], held[gates[0], 1]
        for gate in gates[1:]:
            column = exact_dot(block(held[gate, 0], held[gate, 1]), jnp.concatenate([real, imag], axis=0))
            half = column.shape[0] // 2
            real, imag = column[:half], column[half:]
        return real, imag

    real, imag = product(low)
    real, imag = real.T, imag.T
    high, rest = split(block(real, -imag))
    low_ref[0], low_ref[1] = high, rest
    for slot, gates in enumerate(products):
        high, rest = split(block(*product(gates)))
        rows_ref[slot, 0], rows_ref[slot, 1] = high, rest


def three_dots(high_w, rest_w, x):
    high, rest = split(x)
    return bf_dot(high_w, rest) + bf_dot(rest_w, high) + bf_dot(high_w, high)


def apply_rows(weights_ref, slot, offset, lane_bits, rows, load, store):
    dim = weights_ref.shape[-1] // 2
    stride = 2 ** (offset - lane_bits)
    starts = [h * dim * stride + l for h in range(rows // (dim * stride)) for l in range(stride)]
    high_w, rest_w = weights_ref[slot, 0], weights_ref[slot, 1]
    for pair in range(0, len(starts), 2):
        group = starts[pair : pair + 2]
        x = jnp.concatenate(
            [jnp.concatenate([load(part, start, stride) for start in group], axis=1) for part in range(2)],
            axis=0,
        )
        y = three_dots(high_w, rest_w, x)
        lanes = y.shape[1] // len(group)
        for part in range(2):
            for place, start in enumerate(group):
                store(part, start, stride, y[part * dim : (part + 1) * dim, place * lanes : (place + 1) * lanes])


def run_gates(section, first_slot, weights_ref, lane_bits, buffers, last_store):
    dim = weights_ref.shape[-1] // 2
    rows = buffers[0].shape[1]

    def loader(ref):
        return lambda part, start, stride: ref[part, pl.ds(start, dim, stride=stride), :]

    def storer(ref):
        def store(part, start, stride, value):
            ref[part, pl.ds(start, dim, stride=stride), :] = value

        return store

    now = 0
    for index, (offset, _) in enumerate(section):
        last = index == len(section) - 1
        store = last_store if last and last_store is not None else storer(buffers[1 - now])
        apply_rows(weights_ref, first_slot + index, offset, lane_bits, rows, loader(buffers[now]), store)
        now = 1 - now
    return now


def first_kernel(section, lane_bits, x_ref, low_ref, rows_ref, out_ref, one, two):
    rows = one.shape[1]
    lanes = one.shape[2]
    step = 256
    for start in range(0, rows, step):
        real = x_ref[pl.ds(2 * start, step, stride=2), :]
        imag = x_ref[pl.ds(2 * start + 1, step, stride=2), :]
        high, rest = split(jnp.concatenate([real, imag], axis=1))
        y = bf_dot(rest, low_ref[0]) + bf_dot(high, low_ref[1]) + bf_dot(high, low_ref[0])
        one[0, pl.ds(start, step), :] = y[:, :lanes]
        one[1, pl.ds(start, step), :] = y[:, lanes:]
    buffers = (one, two)
    now = run_gates(section, 0, rows_ref, lane_bits, buffers, None)
    done = buffers[now]
    dests, tops, mids, _, inner, _ = out_ref.shape
    for top in range(tops):
        for mid in range(mids):
            for dest in range(dests):
                start = ((top * mids + mid) * dests + dest) * inner
                for part in range(2):
                    out_ref[dest, top, mid, part] = done[part, pl.ds(start, inner), :]


def second_kernel(section, lane_bits, x_ref, rows_ref, out_ref, one, two):
    dim = rows_ref.shape[-1] // 2
    dests, tops, mids, _, inner, _ = x_ref.shape
    for top in range(tops):
        for mid in range(mids):
            for dest in range(dests):
                start = ((top * mids + mid) * dests + dest) * inner
                for part in range(2):
                    one[part, pl.ds(start, inner), :] = x_ref[dest, top, mid, part]

    def last_store(part, start, stride, value):
        out_ref[pl.ds(2 * start + part, dim, stride=2 * stride), :] = value

    run_gates(section, 0, rows_ref, lane_bits, (one, two), last_store)


def in_vmem(count):
    return [pl.BlockSpec(memory_space=pltpu.VMEM)] * count


def matmul_cost(matmuls, order, columns, moved):
    return pl.CostEstimate(flops=matmuls * 3 * 2 * order * order * columns, bytes_accessed=moved, transcendentals=0)


def per_device(state, gate_terms, path_bits):
    amps_local = state.shape[1]
    local_bits = amps_local.bit_length() - 1
    dim = gate_terms.shape[-1]
    gate_bits = dim.bit_length() - 1
    lanes = dim
    lane_bits = gate_bits
    rows = amps_local // lanes
    qa = lax.axis_size("qa")
    qb = lax.axis_size("qb")
    low, sections = plan_gates(local_bits, gate_bits)
    head = sections[0]
    tail = sections[1] + sections[2]
    products = [gates for _, gates in head + tail]
    order = 2 * dim

    params = pltpu.CompilerParams(vmem_limit_bytes=VMEM_LIMIT)
    low_w, rows_w = pl.pallas_call(
        functools.partial(prepare_kernel, low, products),
        out_shape=(
            jax.ShapeDtypeStruct((2, order, order), BF16),
            jax.ShapeDtypeStruct((len(products), 2, order, order), BF16),
        ),
        in_specs=[pl.BlockSpec(memory_space=pltpu.SMEM), pl.BlockSpec(memory_space=pl.ANY)],
        out_specs=tuple(in_vmem(2)),
        scratch_shapes=[
            pltpu.VMEM((gate_terms.shape[0], 2, dim, dim), F32),
            pltpu.SemaphoreType.DMA((gate_terms.shape[0],)),
        ],
        compiler_params=params,
        cost_estimate=matmul_cost(10, order, order, 6 * 2**20),
        name="prepare_gates",
    )(path_bits, gate_terms)

    amplitudes = state.reshape(2, rows, lanes).swapaxes(0, 1).reshape(qa, 2 * rows // qa, lanes)
    amplitudes = lax.all_to_all(amplitudes, "qa", split_axis=0, concat_axis=0, tiled=True)

    inner = rows // (qa * qa)
    view = (qa, qb, qa // qb, 2, inner, lanes)
    buffers = [pltpu.VMEM((2, rows, lanes), F32)] * 2
    amplitudes = pl.pallas_call(
        functools.partial(first_kernel, head, lane_bits),
        out_shape=jax.ShapeDtypeStruct(view, F32),
        in_specs=in_vmem(3),
        out_specs=in_vmem(1)[0],
        scratch_shapes=buffers,
        compiler_params=params,
        cost_estimate=matmul_cost(len(head) + 1, order, rows, 4 * 2**20),
        name="first_section",
    )(amplitudes.reshape(2 * rows, lanes), low_w, rows_w[: len(head)])

    amplitudes = amplitudes.reshape(qa * qb, 2 * rows // (qa * qb), lanes)
    amplitudes = lax.all_to_all(amplitudes, ("qa", "qb"), split_axis=0, concat_axis=0, tiled=True)

    amplitudes = pl.pallas_call(
        functools.partial(second_kernel, tail, lane_bits),
        out_shape=jax.ShapeDtypeStruct((2 * rows, lanes), F32),
        in_specs=in_vmem(2),
        out_specs=in_vmem(1)[0],
        scratch_shapes=buffers,
        compiler_params=params,
        cost_estimate=matmul_cost(len(tail), order, rows, 4 * 2**20),
        name="later_sections",
    )(amplitudes.reshape(view), rows_w[len(head) :])
    return amplitudes.reshape(rows, 2, lanes).swapaxes(0, 1).reshape(2, amps_local)


def solution(mesh):
    return jax.shard_map(
        per_device,
        mesh=mesh,
        in_specs=(P(None, ("paths", "qa", "qb")), P(), P("paths")),
        out_specs=P(None, ("paths", "qa", "qb")),
        check_vma=False,
    )
```

profile of v0, /device:TPU:0, one launch (start us, length us, event | category | flops | bytes accessed | tf_op | source)
XLA Modules:
  0.0 77.6 jit_solution(17903104072575114287)
XLA Ops:
  0.0 0.0 copy-start.3
  0.0 1.3 %copy.8 = f32[1,2,1024,128]{3,2,1,0:T(8,128)S(1)} copy(f32[1,2,1024,128]{3,1,2,0:T(2,128)} %bitcast.18) | data formatting | bytes 2097152
  1.3 1.8 %copy.4 = f32[1024,2,128]{2,1,0:T(2,128)} copy(f32[1024,2,128]{2,0,1:T(8,128)S(1)} %bitcast.17) | data formatting | bytes 2097152 | tf_op jit(solution)/shard_map/transpose | solution.py:210
  3.1 7.3 %all-to-all-start = ((f32[8,256,128]{2,1,0:T(8,128)}), f32[8,256,128]{2,1,0:T(8,128)}, u32[]{:S(2)}, u32[]{:S(2)}) async-start(f32[8,256,128]{2,1,0:T(8,128)} %bitcast.1), calls=%async_computation | async-start | bytes 2097152 | tf_op jit(solution)/shard_map/all_to_all | solution.py:211
  10.4 0.0 copy-done.3
  10.4 4.1 %prepare_gates.1 = (bf16[2,256,256]{2,1,0:T(8,128)(2,1)S(1)}, bf16[12,2,256,256]{3,2,1,0:T(8,128)(2,1)S(1)}) custom-call(s32[18]{0:T(128)S(1)} %copy-done.3, f32[18,2,2,128,128]{4,3,2,1,0:T(8,128)} %gates_ref.1), custom_call_target="tpu_custom_call" | custom-call | flops 1006632960 | bytes 6291456 | tf_op jit(solution)/shard_map/prepare_gates/pallas_call | solution.py:193
  14.5 1.1 %slice.6.rows_ref = bf16[4,2,256,256]{3,2,1,0:T(8,128)(2,1)} slice(bf16[12,2,256,256]{3,2,1,0:T(8,128)(2,1)S(1)} %get-tuple-element.8), slice={[0:4], [0:2], [0:256], [0:256]} | slice | bytes 2097152 | tf_op jit(solution)/shard_map/slice | solution.py:225
  15.6 20.7 %all-to-all-done = f32[8,256,128]{2,1,0:T(8,128)} async-done(((f32[8,256,128]{2,1,0:T(8,128)}), f32[8,256,128]{2,1,0:T(8,128)}, u32[]{:S(2)}, u32[]{:S(2)}) %all-to-all-start) | async-done | bytes 1048608 | tf_op jit(solution)/shard_map/all_to_all | solution.py:211
  36.2 0.0 copy-start.2
  36.2 1.2 %copy-done.2 = bf16[4,2,256,256]{3,2,1,0:T(8,128)(2,1)S(1)} copy-done((bf16[4,2,256,256]{3,2,1,0:T(8,128)(2,1)S(1)}, bf16[4,2,256,256]{3,2,1,0:T(8,128)(2,1)}, u32[]{:S(2)}) %copy-start.2) | copy-done | bytes 1048600
  37.5 4.0 %first_section.1 = f32[8,2,4,2,16,128]{5,4,3,2,1,0:T(8,128)S(1)} custom-call(f32[2048,128]{1,0:T(8,128)} %bitcast.2.x_ref, bf16[2,256,256]{2,1,0:T(8,128)(2,1)S(1)} %get-tuple-element.7.low_ref, bf16[4,2,256,256]{3,2,1,0:T(8,128)(2,1)S(1)} %copy-done.2), custom_call_target="tpu_custom_call" | custom-call | flops 2013265920 | bytes 4194304 | tf_op jit(solution)/shard_map/first_section/pallas_call | solution.py:216
  41.5 0.0 copy-start.1
  41.5 1.0 %copy-done.1 = f32[8,2,4,2,16,128]{5,4,3,2,1,0:T(8,128)} copy-done((f32[8,2,4,2,16,128]{5,4,3,2,1,0:T(8,128)}, f32[8,2,4,2,16,128]{5,4,3,2,1,0:T(8,128)S(1)}, u32[]{:S(2)}) %copy-start.1) | copy-done | bytes 1048600
  42.5 4.3 %all-to-all-start.1 = ((f32[16,128,128]{2,1,0:T(8,128)}), f32[16,128,128]{2,1,0:T(8,128)}, u32[]{:S(2)}, u32[]{:S(2)}) async-start(f32[16,128,128]{2,1,0:T(8,128)} %bitcast.16), calls=%async_computation.1 | async-start | bytes 2097152 | tf_op jit(solution)/shard_map/all_to_all | solution.py:228
  46.8 1.5 %slice.7.rows_ref = bf16[8,2,256,256]{3,2,1,0:T(8,128)(2,1)} slice(bf16[12,2,256,256]{3,2,1,0:T(8,128)(2,1)S(1)} %get-tuple-element.8), slice={[4:12], [0:2], [0:256], [0:256]} | slice | bytes 4194304 | tf_op jit(solution)/shard_map/slice | solution.py:239
  48.3 21.4 %all-to-all-done.1 = f32[16,128,128]{2,1,0:T(8,128)} async-done(((f32[16,128,128]{2,1,0:T(8,128)}), f32[16,128,128]{2,1,0:T(8,128)}, u32[]{:S(2)}, u32[]{:S(2)}) %all-to-all-start.1) | async-done | bytes 1048608 | tf_op jit(solution)/shard_map/all_to_all | solution.py:228
  69.8 0.0 copy-start
  69.8 1.6 %copy-done = bf16[8,2,256,256]{3,2,1,0:T(8,128)(2,1)S(1)} copy-done((bf16[8,2,256,256]{3,2,1,0:T(8,128)(2,1)S(1)}, bf16[8,2,256,256]{3,2,1,0:T(8,128)(2,1)}, u32[]{:S(2)}) %copy-start) | copy-done | bytes 2097176
  71.3 6.3 %later_sections.1 = f32[2048,128]{1,0:T(8,128)} custom-call(f32[8,2,4,2,16,128]{5,4,3,2,1,0:T(8,128)} %bitcast.4.x_ref, bf16[8,2,256,256]{3,2,1,0:T(8,128)(2,1)S(1)} %copy-done), custom_call_target="tpu_custom_call" | custom-call | flops 3221225472 | bytes 4194304 | tf_op jit(solution)/shard_map/later_sections/pallas_call | solution.py:230
Async XLA Ops:
  0.0 10.4 %copy-start.3 = (s32[18]{0:T(128)S(1)}, s32[18]{0:T(128)}, u32[]{:S(2)}) copy-start(s32[18]{0:T(128)} %bits_ref.1) | copy-start | bytes 220
  3.1 33.2 %all-to-all-start = ((f32[8,256,128]{2,1,0:T(8,128)}), f32[8,256,128]{2,1,0:T(8,128)}, u32[]{:S(2)}, u32[]{:S(2)}) async-start(f32[8,256,128]{2,1,0:T(8,128)} %bitcast.1), calls=%async_computation | async-start | bytes 2097152 | tf_op jit(solution)/shard_map/all_to_all | solution.py:211
  36.2 1.2 %copy-start.2 = (bf16[4,2,256,256]{3,2,1,0:T(8,128)(2,1)S(1)}, bf16[4,2,256,256]{3,2,1,0:T(8,128)(2,1)}, u32[]{:S(2)}) copy-start(bf16[4,2,256,256]{3,2,1,0:T(8,128)(2,1)} %slice.6.rows_ref) | copy-start | bytes 3145732
  41.5 1.0 %copy-start.1 = (f32[8,2,4,2,16,128]{5,4,3,2,1,0:T(8,128)}, f32[8,2,4,2,16,128]{5,4,3,2,1,0:T(8,128)S(1)}, u32[]{:S(2)}) copy-start(f32[8,2,4,2,16,128]{5,4,3,2,1,0:T(8,128)S(1)} %first_section.1) | copy-start | bytes 3145732
  42.5 27.3 %all-to-all-start.1 = ((f32[16,128,128]{2,1,0:T(8,128)}), f32[16,128,128]{2,1,0:T(8,128)}, u32[]{:S(2)}, u32[]{:S(2)}) async-start(f32[16,128,128]{2,1,0:T(8,128)} %bitcast.16), calls=%async_computation.1 | async-start | bytes 2097152 | tf_op jit(solution)/shard_map/all_to_all | solution.py:228
  69.8 1.6 %copy-start = (bf16[8,2,256,256]{3,2,1,0:T(8,128)(2,1)S(1)}, bf16[8,2,256,256]{3,2,1,0:T(8,128)(2,1)}, u32[]{:S(2)}) copy-start(bf16[8,2,256,256]{3,2,1,0:T(8,128)(2,1)} %slice.7.rows_ref) | copy-start | bytes 6291460
where the time goes:
time: 79.2 us; the launch traced here: 77.6 us
  waiting for transfers between devices  42.1 us (53%)
  Pallas kernels  14.4 us (18%)
  starting transfers between devices  11.6 us (15%)
  local copies, waits for them, and re-layouts  9.46 us (12%)
    all_to_all x1, waiting for transfers between devices, per_device(): lax.all_to_all(amplitudes, ('qa', 'qb'), split_axis=0, concat_axis=0, til...  21.4 us
    all_to_all x1, waiting for transfers between devices, per_device(): lax.all_to_all(amplitudes, 'qa', split_axis=0, concat_axis=0, tiled=True)  20.7 us
    all_to_all x1, starting transfers between devices, per_device(): lax.all_to_all(amplitudes, 'qa', split_axis=0, concat_axis=0, tiled=True)  7.28 us
    pallas_call x1, Pallas kernels, per_device(): pl.pallas_call(functools.partial(second_kernel, tail, lane_bits), out_sha...  6.28 us
    unnamed x9, local copies, waits for them, and re-layouts  5.09 us
    all_to_all x1, starting transfers between devices, per_device(): lax.all_to_all(amplitudes, ('qa', 'qb'), split_axis=0, concat_axis=0, til...  4.34 us
    pallas_call x1, Pallas kernels, per_device(): pl.pallas_call(functools.partial(prepare_kernel, low, products), out_shap...  4.07 us
    pallas_call x1, Pallas kernels, per_device(): pl.pallas_call(functools.partial(first_kernel, head, lane_bits), out_shap...  4.01 us
  transfers between devices with their start and end apart: 2, of which 2 were waited for; matrix products, arithmetic and copies ran while one was open for 3% of the time, Pallas kernels for 5%

commit v1 on v0

--- a/solution.py
+++ b/solution.py
@@ -4,6 +4,7 @@
 import jax.numpy as jnp
 from jax import lax
 from jax.experimental import pallas as pl
+from jax.experimental.layout import Layout, with_layout_constraint
 from jax.experimental.pallas import tpu as pltpu
 from jax.sharding import PartitionSpec as P
 
@@ -49,7 +50,7 @@
     return jnp.dot(a, b, preferred_element_type=F32)
 
 
-def prepare_kernel(low, products, bits_ref, gates_ref, low_ref, rows_ref, held, sems):
+def prepare_kernel(low, heads, tails, bits_ref, gates_ref, low_ref, heads_ref, tails_ref, held, sems):
     count = held.shape[0]
     copies = []
     for gate in range(count):
@@ -76,9 +77,10 @@
     real, imag = real.T, imag.T
     high, rest = split(block(real, -imag))
     low_ref[0], low_ref[1] = high, rest
-    for slot, gates in enumerate(products):
-        high, rest = split(block(*product(gates)))
-        rows_ref[slot, 0], rows_ref[slot, 1] = high, rest
+    for target, products in ((heads_ref, heads), (tails_ref, tails)):
+        for slot, gates in enumerate(products):
+            high, rest = split(block(*product(gates)))
+            target[slot, 0], target[slot, 1] = high, rest
 
 
 def three_dots(high_w, rest_w, x):
@@ -126,7 +128,7 @@
     return now
 
 
-def first_kernel(section, lane_bits, x_ref, low_ref, rows_ref, out_ref, one, two):
+def first_kernel(section, lane_bits, x_ref, low_ref, rows_ref, out_hbm, one, two, out_ref, sem):
     rows = one.shape[1]
     lanes = one.shape[2]
     step = 256
@@ -147,6 +149,9 @@
                 start = ((top * mids + mid) * dests + dest) * inner
                 for part in range(2):
                     out_ref[dest, top, mid, part] = done[part, pl.ds(start, inner), :]
+    copy = pltpu.make_async_copy(out_ref, out_hbm, sem)
+    copy.start()
+    copy.wait()
 
 
 def second_kernel(section, lane_bits, x_ref, rows_ref, out_ref, one, two):
@@ -186,18 +191,18 @@
     low, sections = plan_gates(local_bits, gate_bits)
     head = sections[0]
     tail = sections[1] + sections[2]
-    products = [gates for _, gates in head + tail]
     order = 2 * dim
 
     params = pltpu.CompilerParams(vmem_limit_bytes=VMEM_LIMIT)
-    low_w, rows_w = pl.pallas_call(
-        functools.partial(prepare_kernel, low, products),
+    low_w, head_w, tail_w = pl.pallas_call(
+        functools.partial(prepare_kernel, low, [gates for _, gates in head], [gates for _, gates in tail]),
         out_shape=(
             jax.ShapeDtypeStruct((2, order, order), BF16),
-            jax.ShapeDtypeStruct((len(products), 2, order, order), BF16),
+            jax.ShapeDtypeStruct((len(head), 2, order, order), BF16),
+            jax.ShapeDtypeStruct((len(tail), 2, order, order), BF16),
         ),
         in_specs=[pl.BlockSpec(memory_space=pltpu.SMEM), pl.BlockSpec(memory_space=pl.ANY)],
-        out_specs=tuple(in_vmem(2)),
+        out_specs=tuple(in_vmem(3)),
         scratch_shapes=[
             pltpu.VMEM((gate_terms.shape[0], 2, dim, dim), F32),
             pltpu.SemaphoreType.DMA((gate_terms.shape[0],)),
@@ -207,7 +212,8 @@
         name="prepare_gates",
     )(path_bits, gate_terms)
 
-    amplitudes = state.reshape(2, rows, lanes).swapaxes(0, 1).reshape(qa, 2 * rows // qa, lanes)
+    amplitudes = with_layout_constraint(state.reshape(2, rows, lanes), Layout(major_to_minor=(1, 0, 2)))
+    amplitudes = amplitudes.swapaxes(0, 1).reshape(qa, 2 * rows // qa, lanes)
     amplitudes = lax.all_to_all(amplitudes, "qa", split_axis=0, concat_axis=0, tiled=True)
 
     inner = rows // (qa * qa)
@@ -215,14 +221,14 @@
     buffers = [pltpu.VMEM((2, rows, lanes), F32)] * 2
     amplitudes = pl.pallas_call(
         functools.partial(first_kernel, head, lane_bits),
-        out_shape=jax.ShapeDtypeStruct(view, F32),
+        out_shape=pltpu.HBM(view, F32),
         in_specs=in_vmem(3),
-        out_specs=in_vmem(1)[0],
-        scratch_shapes=buffers,
+        out_specs=pl.BlockSpec(memory_space=pltpu.HBM),
+        scratch_shapes=buffers + [pltpu.VMEM(view, F32), pltpu.SemaphoreType.DMA],
         compiler_params=params,
         cost_estimate=matmul_cost(len(head) + 1, order, rows, 4 * 2**20),
         name="first_section",
-    )(amplitudes.reshape(2 * rows, lanes), low_w, rows_w[: len(head)])
+    )(amplitudes.reshape(2 * rows, lanes), low_w, head_w)
 
     amplitudes = amplitudes.reshape(qa * qb, 2 * rows // (qa * qb), lanes)
     amplitudes = lax.all_to_all(amplitudes, ("qa", "qb"), split_axis=0, concat_axis=0, tiled=True)
@@ -236,7 +242,7 @@
         compiler_params=params,
         cost_estimate=matmul_cost(len(tail), order, rows, 4 * 2**20),
         name="later_sections",
-    )(amplitudes.reshape(view), rows_w[len(head) :])
+    )(amplitudes.reshape(view), tail_w)
     return amplitudes.reshape(rows, 2, lanes).swapaxes(0, 1).reshape(2, amps_local)
 
 

time: 79.2 us -> 72.3 us (0.913); the launches traced: 77.6 us -> 71.6 us
  blocking collectives: 0 us -> 28.6 us
  waiting for transfers between devices: 42.1 us -> 20.1 us
  local copies, waits for them, and re-layouts: 9.46 us -> 2.84 us
  starting transfers between devices: 11.6 us -> 7.28 us
  Pallas kernels: 14.4 us -> 12.9 us
    all_to_all x0 -> x1, blocking collectives: none -> 28.6 us  [per_device(): lax.all_to_all(amplitudes, ('qa', 'qb'), split_axis=0, concat_axis=0, til...]
    all_to_all x1 -> x0, waiting for transfers between devices: 21.4 us -> none  [per_device(): lax.all_to_all(amplitudes, ('qa', 'qb'), split_axis=0, concat_axis=0, til...]
    all_to_all x1 -> x0, starting transfers between devices: 4.34 us -> none  [per_device(): lax.all_to_all(amplitudes, ('qa', 'qb'), split_axis=0, concat_axis=0, til...]
    slice x2 -> x0, local copies, waits for them, and re-layouts: 2.59 us -> none  [the longest x1 1.49 us: per_device(): rows_w[len(head):]]
    unnamed x9 -> x6, local copies, waits for them, and re-layouts: 5.09 us -> 2.84 us
    transpose x1 -> x0, local copies, waits for them, and re-layouts: 1.78 us -> none  [per_device(): state.reshape(2, rows, lanes).swapaxes(0, 1)]
    pallas_call x1, Pallas kernels: 6.28 us -> 5.05 us  [per_device(): pl.pallas_call(functools.partial(second_kernel, tail, lane_bits), out_sha...]
  transfers between devices with their start and end apart: 2 -> 1, of which waited for: 2 -> 1; matrix products, arithmetic and copies ran while one was open for 3% -> 0% of each run, Pallas kernels for 5% -> 6%
where the time goes in v1:
time: 72.3 us; the launch traced here: 71.6 us
  blocking collectives  28.6 us (40%)
  waiting for transfers between devices  20.1 us (28%)
  Pallas kernels  12.9 us (18%)
  starting transfers between devices  7.28 us (10%)
  local copies, waits for them, and re-layouts  2.84 us (4%)
    all_to_all x1, blocking collectives, per_device(): lax.all_to_all(amplitudes, ('qa', 'qb'), split_axis=0, concat_axis=0, til...  28.6 us
    all_to_all x1, waiting for transfers between devices, per_device(): lax.all_to_all(amplitudes, 'qa', split_axis=0, concat_axis=0, tiled=True)  20.1 us
    all_to_all x1, starting transfers between devices, per_device(): lax.all_to_all(amplitudes, 'qa', split_axis=0, concat_axis=0, tiled=True)  7.28 us
    pallas_call x1, Pallas kernels, per_device(): pl.pallas_call(functools.partial(second_kernel, tail, lane_bits), out_sha...  5.05 us
    pallas_call x1, Pallas kernels, per_device(): pl.pallas_call(functools.partial(prepare_kernel, low, [gates for _, gates...  4.08 us
    pallas_call x1, Pallas kernels, per_device(): pl.pallas_call(functools.partial(first_kernel, head, lane_bits), out_shap...  3.75 us
    unnamed x6, local copies, waits for them, and re-layouts  2.84 us
  transfers between devices with their start and end apart: 1, of which 1 were waited for; matrix products, arithmetic and copies ran while one was open for 0% of the time, Pallas kernels for 6%

profile of v1, /device:TPU:0, one launch (start us, length us, event | category | flops | bytes accessed | tf_op | source)
XLA Modules:
  0.0 71.6 jit_solution(473672985048479446)
XLA Ops:
  0.0 7.3 %all-to-all-start = ((f32[8,256,128]{2,1,0:T(8,128)}), f32[8,256,128]{2,1,0:T(8,128)S(1)}, u32[]{:S(2)}, u32[]{:S(2)}) async-start(f32[8,256,128]{2,1,0:T(8,128)} %bitcast.15), calls=%async_computation | async-start | bytes 2097152 | tf_op jit(solution)/shard_map/all_to_all | solution.py:217
  7.3 0.0 copy-start
  7.3 0.7 copy-done
  7.9 4.1 %prepare_gates.1 = (bf16[2,256,256]{2,1,0:T(8,128)(2,1)S(1)}, bf16[4,2,256,256]{3,2,1,0:T(8,128)(2,1)S(1)}, bf16[8,2,256,256]{3,2,1,0:T(8,128)(2,1)S(1)}) custom-call(s32[18]{0:T(128)S(1)} %copy-done, f32[18,2,2,128,128]{4,3,2,1,0:T(8,128)} %gates_ref.1), custom_call_target="tpu_custom_call" | custom-call | flops 1006632960 | bytes 6291456 | tf_op jit(solution)/shard_map/prepare_gates/pallas_call | solution.py:197
  12.0 0.0 copy-start.1
  12.0 1.0 %copy-done.1 = bf16[4,2,256,256]{3,2,1,0:T(8,128)(2,1)} copy-done((bf16[4,2,256,256]{3,2,1,0:T(8,128)(2,1)}, bf16[4,2,256,256]{3,2,1,0:T(8,128)(2,1)S(1)}, u32[]{:S(2)}) %copy-start.1) | copy-done | bytes 1048600
  13.0 20.1 %all-to-all-done = f32[8,256,128]{2,1,0:T(8,128)S(1)} async-done(((f32[8,256,128]{2,1,0:T(8,128)}), f32[8,256,128]{2,1,0:T(8,128)S(1)}, u32[]{:S(2)}, u32[]{:S(2)}) %all-to-all-start) | async-done | bytes 1048608 | tf_op jit(solution)/shard_map/all_to_all | solution.py:217
  33.0 0.0 copy-start.2
  33.1 1.2 %copy-done.2 = bf16[4,2,256,256]{3,2,1,0:T(8,128)(2,1)S(1)} copy-done((bf16[4,2,256,256]{3,2,1,0:T(8,128)(2,1)S(1)}, bf16[4,2,256,256]{3,2,1,0:T(8,128)(2,1)}, u32[]{:S(2)}) %copy-start.2) | copy-done | bytes 1048600
  34.3 3.7 %first_section.1 = f32[8,2,4,2,16,128]{5,4,3,2,1,0:T(8,128)} custom-call(f32[2048,128]{1,0:T(8,128)S(1)} %bitcast.13, bf16[2,256,256]{2,1,0:T(8,128)(2,1)S(1)} %get-tuple-element.8.low_ref, bf16[4,2,256,256]{3,2,1,0:T(8,128)(2,1)S(1)} %copy-done.2), custom_call_target="tpu_custom_call" | custom-call | flops 2013265920 | bytes 4194304 | tf_op jit(solution)/shard_map/first_section/pallas_call | solution.py:222
  38.0 28.6 %all_to_all.10 = f32[16,128,128]{2,1,0:T(8,128)S(1)} all-to-all(f32[16,128,128]{2,1,0:T(8,128)} %bitcast.16), channel_id=1, replica_groups=mesh['paths'=2,'qa'=8,'qb'=2] {'qa','qb'}, dimensions={0} | all-to-all | bytes 2097152 | tf_op jit(solution)/shard_map/all_to_all | solution.py:234
  66.6 5.1 %later_sections.1 = f32[2048,128]{1,0:T(8,128)} custom-call(f32[8,2,4,2,16,128]{5,4,3,2,1,0:T(8,128)S(1)} %bitcast.14, bf16[8,2,256,256]{3,2,1,0:T(8,128)(2,1)S(1)} %get-tuple-element.10.rows_ref), custom_call_target="tpu_custom_call" | custom-call | flops 3221225472 | bytes 4194304 | tf_op jit(solution)/shard_map/later_sections/pallas_call | solution.py:236
Async XLA Ops:
  0.0 33.0 %all-to-all-start = ((f32[8,256,128]{2,1,0:T(8,128)}), f32[8,256,128]{2,1,0:T(8,128)S(1)}, u32[]{:S(2)}, u32[]{:S(2)}) async-start(f32[8,256,128]{2,1,0:T(8,128)} %bitcast.15), calls=%async_computation | async-start | bytes 2097152 | tf_op jit(solution)/shard_map/all_to_all | solution.py:217
  7.3 0.7 copy-start
  12.0 1.0 %copy-start.1 = (bf16[4,2,256,256]{3,2,1,0:T(8,128)(2,1)}, bf16[4,2,256,256]{3,2,1,0:T(8,128)(2,1)S(1)}, u32[]{:S(2)}) copy-start(bf16[4,2,256,256]{3,2,1,0:T(8,128)(2,1)S(1)} %get-tuple-element.9.rows_ref) | copy-start | bytes 3145732
  33.0 1.2 %copy-start.2 = (bf16[4,2,256,256]{3,2,1,0:T(8,128)(2,1)S(1)}, bf16[4,2,256,256]{3,2,1,0:T(8,128)(2,1)}, u32[]{:S(2)}) copy-start(bf16[4,2,256,256]{3,2,1,0:T(8,128)(2,1)} %copy-done.1) | copy-start | bytes 3145732

commit v2 on v0

v2 whole, which is shorter than its diff:
```python
import functools

import jax
import jax.numpy as jnp
from jax import lax
from jax.experimental import pallas as pl
from jax.experimental.layout import Layout, with_layout_constraint
from jax.experimental.pallas import tpu as pltpu
from jax.sharding import PartitionSpec as P

F32 = jnp.float32
BF16 = jnp.bfloat16
VMEM_LIMIT = 14 * 1024 * 1024
WHOLE_VMEM = 60 * 1024 * 1024


def window_offsets(span, gate_bits):
    return [0, span, gate_bits, span - 1, gate_bits + 1, span - 2]


def plan_gates(local_bits, gate_bits):
    outer = window_offsets(local_bits - gate_bits, gate_bits)
    inner = window_offsets(local_bits - gate_bits - 1, gate_bits)
    low, sections = [], []
    for number, offsets in enumerate((outer, inner, outer)):
        section = []
        for index, offset in enumerate(offsets):
            gate = 6 * number + index
            if offset == 0:
                low.append(gate)
            elif section and section[-1][0] == offset:
                section[-1][1].append(gate)
            else:
                section.append((offset, [gate]))
        sections.append(section)
    return low, sections


def exact_dot(a, b):
    return lax.dot_general(
        a, b, (((1,), (0,)), ((), ())), precision=lax.Precision.HIGHEST, preferred_element_type=F32
    )


def split(x):
    high = x.astype(BF16)
    return high, (x - high.astype(F32)).astype(BF16)


def bf_dot(a, b):
    return jnp.dot(a, b, preferred_element_type=F32)


def block(real, imag):
    return jnp.concatenate(
        [jnp.concatenate([real, -imag], axis=1), jnp.concatenate([imag, real], axis=1)], axis=0
    )


def prepare_kernel(low, sections, bits_ref, gates_ref, low_ref, *refs):
    *targets, held, sems = refs
    copies = []
    for gate in range(held.shape[0]):
        copy = pltpu.make_async_copy(gates_ref.at[gate, bits_ref[gate]], held.at[gate], sems.at[gate])
        copy.start()
        copies.append(copy)
    for copy in copies:
        copy.wait()

    def product(gates):
        real, imag = held[gates[0], 0], held[gates[0], 1]
        for gate in gates[1:]:
            column = exact_dot(block(held[gate, 0], held[gate, 1]), jnp.concatenate([real, imag], axis=0))
            half = column.shape[0] // 2
            real, imag = column[:half], column[half:]
        return real, imag

    real, imag = product(low)
    low_ref[0], low_ref[1] = split(block(real.T, -imag.T))
    for target, section in zip(targets, sections):
        for slot, (_, gates) in enumerate(section):
            target[slot, 0], target[slot, 1] = split(block(*product(gates)))


def distances_of(count):
    half = count // 2
    return [0, half - 1, *range(count - 1, half - 1, -1), *range(half - 2, 0, -1)]


def partner(distance):
    return jnp.bitwise_xor(lax.axis_index("qa"), distance)


def split_kernel(x_ref, *refs):
    *outs, sems = refs
    copies = []
    for place, distance in enumerate(distances_of(len(outs))):
        copy = pltpu.make_async_copy(x_ref.at[partner(distance)], outs[place], sems.at[place])
        copy.start()
        copies.append(copy)
    for copy in copies:
        copy.wait()


def apply_rows(weights_ref, slot, offset, lane_bits, rows, load, store):
    dim = weights_ref.shape[-1] // 2
    stride = 2 ** (offset - lane_bits)
    starts = [h * dim * stride + l for h in range(rows // (dim * stride)) for l in range(stride)]
    high_w, rest_w = weights_ref[slot, 0], weights_ref[slot, 1]
    for pair in range(0, len(starts), 2):
        group = starts[pair : pair + 2]
        x = jnp.concatenate(
            [jnp.concatenate([load(part, start, stride) for start in group], axis=1) for part in range(2)],
            axis=0,
        )
        high, rest = split(x)
        y = bf_dot(high_w, rest) + bf_dot(rest_w, high) + bf_dot(high_w, high)
        lanes = y.shape[1] // len(group)
        for part in range(2):
            for place, start in enumerate(group):
                store(part, start, stride, y[part * dim : (part + 1) * dim, place * lanes : (place + 1) * lanes])


def run_gates(section, weights_ref, lane_bits, buffers, last_store=None):
    dim = weights_ref.shape[-1] // 2
    rows = buffers[0].shape[1]

    def loader(ref):
        return lambda part, start, stride: ref[part, pl.ds(start, dim, stride=stride), :]

    def storer(ref):
        def store(part, start, stride, value):
            ref[part, pl.ds(start, dim, stride=stride), :] = value

        return store

    now = 0
    for index, (offset, _) in enumerate(section):
        last = index == len(section) - 1
        store = last_store if last and last_store is not None else storer(buffers[1 - now])
        apply_rows(weights_ref, index, offset, lane_bits, rows, loader(buffers[now]), store)
        now = 1 - now
    return now


def first_kernel(section, lane_bits, count, *refs):
    blocks, (low_ref, rows_ref), outs, (one, two) = (
        refs[:count],
        refs[count : count + 2],
        refs[count + 2 : -2],
        refs[-2:],
    )
    lanes = one.shape[2]
    for distance, block_ref in zip(distances_of(count), blocks):
        size = block_ref.shape[0] // 2
        start = pl.multiple_of(partner(distance) * size, size)
        real = block_ref[pl.ds(0, size, stride=2), :]
        imag = block_ref[pl.ds(1, size, stride=2), :]
        high, rest = split(jnp.concatenate([real, imag], axis=1))
        y = bf_dot(rest, low_ref[0]) + bf_dot(high, low_ref[1]) + bf_dot(high, low_ref[0])
        one[0, pl.ds(start, size), :] = y[:, :lanes]
        one[1, pl.ds(start, size), :] = y[:, lanes:]
    buffers = (one, two)
    done = buffers[run_gates(section, rows_ref, lane_bits, buffers)]
    for distance, out_ref in zip(distances_of(count), outs):
        dest = partner(distance)
        tops, mids, _, inner, _ = out_ref.shape
        for top in range(tops):
            for mid in range(mids):
                start = pl.multiple_of(((top * mids + mid) * count + dest) * inner, inner)
                for part in range(2):
                    out_ref[top, mid, part] = done[part, pl.ds(start, inner), :]


def second_kernel(section, lane_bits, count, stays, *refs):
    blocks, (rows_ref, out_ref, one, two) = refs[:count], refs[count:]
    core = lax.axis_index("qb")
    top = core if stays else 1 - core
    for distance, block_ref in zip(distances_of(count), blocks):
        source = partner(distance)
        _, mids, _, inner, _ = block_ref.shape
        for mid in range(mids):
            start = pl.multiple_of((mid * count + source) * inner, inner)
            for part in range(2):
                one[part, pl.ds(start, inner), :] = block_ref[top, mid, part]
    dim = rows_ref.shape[-1] // 2

    def last_store(part, start, stride, value):
        out_ref[part, pl.ds(start, dim, stride=stride), :] = value

    run_gates(section, rows_ref, lane_bits, (one, two), last_store)


def third_kernel(section, lane_bits, kept_ref, came_ref, rows_ref, out_ref, one, two):
    dim = rows_ref.shape[-1] // 2
    half = kept_ref.shape[1]
    core = lax.axis_index("qb")
    one[:, pl.ds(pl.multiple_of(core * half, half), half), :] = kept_ref[...]
    one[:, pl.ds(pl.multiple_of((1 - core) * half, half), half), :] = came_ref[...]

    def last_store(part, start, stride, value):
        out_ref[pl.ds(2 * start + part, dim, stride=2 * stride), :] = value

    run_gates(section, rows_ref, lane_bits, (one, two), last_store)


def call(kernel, name, out_shapes, in_specs, scratch, matmuls, *operands, limit=VMEM_LIMIT):
    many = isinstance(out_shapes, tuple)
    vmem = pl.BlockSpec(memory_space=pltpu.VMEM)
    return pl.pallas_call(
        kernel,
        out_shape=out_shapes,
        in_specs=in_specs,
        out_specs=(vmem,) * len(out_shapes) if many else vmem,
        scratch_shapes=scratch,
        compiler_params=pltpu.CompilerParams(vmem_limit_bytes=limit),
        cost_estimate=pl.CostEstimate(
            flops=int(matmuls * 3 * 2 * 256 * 256 * 1024), bytes_accessed=4 * 2**20, transcendentals=0
        ),
        name=name,
    )(*operands)


def per_device(state, gate_terms, path_bits):
    amps_local = state.shape[1]
    local_bits = amps_local.bit_length() - 1
    dim = gate_terms.shape[-1]
    gate_bits = dim.bit_length() - 1
    lanes, lane_bits = dim, gate_bits
    rows = amps_local // lanes
    qa = lax.axis_size("qa")
    qb = lax.axis_size("qb")
    low, sections = plan_gates(local_bits, gate_bits)
    order = 2 * dim
    vmem = pl.BlockSpec(memory_space=pltpu.VMEM)
    hbm = pl.BlockSpec(memory_space=pltpu.HBM)
    shape = jax.ShapeDtypeStruct

    state = with_layout_constraint(state.reshape(2, rows, lanes), Layout(major_to_minor=(1, 0, 2)))
    state = state.swapaxes(0, 1).reshape(qa, 2 * rows // qa, lanes)
    blocks = call(
        split_kernel,
        "split_state",
        (shape((2 * rows // qa, lanes), F32),) * qa,
        [hbm],
        [pltpu.SemaphoreType.DMA((qa,))],
        0,
        state,
        limit=WHOLE_VMEM,
    )

    def exchange(blocks):
        came = [blocks[0]]
        for distance, piece in zip(distances_of(qa)[1:], blocks[1:]):
            came.append(lax.ppermute(piece, "qa", [(i, i ^ distance) for i in range(qa)]))
        return came

    blocks = exchange(blocks)
    low_w, *weights = call(
        functools.partial(prepare_kernel, low, sections),
        "prepare_gates",
        (shape((2, order, order), BF16),) + tuple(shape((len(s), 2, order, order), BF16) for s in sections),
        [pl.BlockSpec(memory_space=pltpu.SMEM), hbm],
        [pltpu.VMEM((gate_terms.shape[0], 2, dim, dim), F32), pltpu.SemaphoreType.DMA((gate_terms.shape[0],))],
        4,
        path_bits,
        gate_terms,
    )
    inner = rows // (qa * qa)
    blocks = call(
        functools.partial(first_kernel, sections[0], lane_bits, qa),
        "first_section",
        (shape((qb, qa // qb, 2, inner, lanes), F32),) * qa,
        [vmem] * (qa + 2),
        [pltpu.VMEM((2, rows, lanes), F32)] * 2,
        len(sections[0]) + 1,
        *blocks,
        low_w,
        weights[0],
    )
    blocks = exchange(blocks)
    halves = []
    for stays in (False, True):
        halves.append(
            call(
                functools.partial(second_kernel, sections[1], lane_bits, qa, stays),
                "second_section_kept" if stays else "second_section_sent",
                shape((2, rows // qb, lanes), F32),
                [vmem] * (qa + 1),
                [pltpu.VMEM((2, rows // qb, lanes), F32)] * 2,
                len(sections[1]) / 2,
                *blocks,
                weights[1],
            )
        )
        if not stays:
            came = lax.ppermute(halves[0], "qb", [(i, 1 - i) for i in range(qb)])
    final = call(
        functools.partial(third_kernel, sections[2], lane_bits),
        "third_section",
        shape((2 * rows, lanes), F32),
        [vmem] * 3,
        [pltpu.VMEM((2, rows, lanes), F32)] * 2,
        len(sections[2]),
        halves[1],
        came,
        weights[2],
    )
    return final.reshape(rows, 2, lanes).swapaxes(0, 1).reshape(2, amps_local)


def solution(mesh):
    return jax.shard_map(
        per_device,
        mesh=mesh,
        in_specs=(P(None, ("paths", "qa", "qb")), P(), P("paths")),
        out_specs=P(None, ("paths", "qa", "qb")),
        check_vma=False,
    )
```

time: 79.2 us -> 68.4 us (0.86); the launches traced: 77.6 us -> 68.2 us
  waiting for transfers between devices: 42.1 us -> 20.7 us
  starting transfers between devices: 11.6 us -> 27.4 us
  local copies, waits for them, and re-layouts: 9.46 us -> 2.99 us
  Pallas kernels: 14.4 us -> 17 us
    all_to_all x2 -> x0, waiting for transfers between devices: 42.1 us -> none  [the longest x1 21.4 us: per_device(): lax.all_to_all(amplitudes, ('qa', 'qb'), split_axis=0, concat_axis=0, til...]
    ppermute x0 -> x15, starting transfers between devices: none -> 27.4 us  [the longest x14 27.4 us: exchange(): lax.ppermute(piece, 'qa', [(i, i ^ distance) for i in range(qa)])]
    ppermute x0 -> x15, waiting for transfers between devices: none -> 20.7 us  [the longest x14 20.3 us: exchange(): lax.ppermute(piece, 'qa', [(i, i ^ distance) for i in range(qa)])]
    all_to_all x2 -> x0, starting transfers between devices: 11.6 us -> none  [the longest x1 7.28 us: per_device(): lax.all_to_all(amplitudes, 'qa', split_axis=0, concat_axis=0, tiled=True)]
    pallas_call x3 -> x6, Pallas kernels: 14.4 us -> 17 us  [call(): pl.pallas_call(kernel, out_shape=out_shapes, in_specs=in_specs, out_specs...]
    slice x2 -> x0, local copies, waits for them, and re-layouts: 2.59 us -> none  [the longest x1 1.49 us: per_device(): rows_w[len(head):]]
    unnamed x9 -> x6, local copies, waits for them, and re-layouts: 5.09 us -> 2.99 us
    transpose x1 -> x0, local copies, waits for them, and re-layouts: 1.78 us -> none  [per_device(): state.reshape(2, rows, lanes).swapaxes(0, 1)]
  transfers between devices with their start and end apart: 2 -> 15, of which waited for: 2 -> 8; matrix products, arithmetic and copies ran while one was open for 3% -> 0% of each run, Pallas kernels for 5% -> 10%
where the time goes in v2:
time: 68.4 us; the launch traced here: 68.2 us
  starting transfers between devices  27.4 us (40%)
  waiting for transfers between devices  20.7 us (30%)
  Pallas kernels  17 us (25%)
  local copies, waits for them, and re-layouts  2.99 us (4%)
    ppermute x14, starting transfers between devices, exchange(): lax.ppermute(piece, 'qa', [(i, i ^ distance) for i in range(qa)])  27.4 us
    ppermute x14, waiting for transfers between devices, exchange(): lax.ppermute(piece, 'qa', [(i, i ^ distance) for i in range(qa)])  20.3 us
    pallas_call x6, Pallas kernels, call(): pl.pallas_call(kernel, out_shape=out_shapes, in_specs=in_specs, out_specs...  17 us
    unnamed x6, local copies, waits for them, and re-layouts  2.99 us
  transfers between devices with their start and end apart: 15, of which 8 were waited for; matrix products, arithmetic and copies ran while one was open for 0% of the time, Pallas kernels for 10%

profile of v2, /device:TPU:0, one launch (start us, length us, event | category | flops | bytes accessed | tf_op | source)
XLA Modules:
  0.0 68.2 jit_solution(3261061952649460545)
XLA Ops:
  0.0 2.3 %split_state.1 = (f32[256,128]{1,0:T(8,128)}, f32[256,128]{1,0:T(8,128)}, f32[256,128]{1,0:T(8,128)}, f32[256,128]{1,0:T(8,128)}, f32[256,128]{1,0:T(8,128)}, /*...) custom-call(f32[8,256,128]{2,1,0:T(8,128)} %bitcast.10), custom_call_target="tpu_custom_call" | custom-call | bytes 4194304 | tf_op jit(solution)/shard_map/split_state/pallas_call | solution.py:210
  2.3 4.0 %collective-permute-start = (f32[256,128]{1,0:T(8,128)}, f32[256,128]{1,0:T(8,128)S(1)}, u32[]{:S(2)}, u32[]{:S(2)}) collective-permute-start(f32[256,128]{1,0:T(8,128)} %get-tuple-element.26), channel_id=1, source_target_pairs={{0,6},{2,4},{4,2},{6,0},{8,14},{10,12},{12,10},{14,8},{1,7},{3,5},... | collective-permute-start | bytes 393224 | tf_op jit(solution)/shard_map/ppermute | solution.py:255
  6.4 2.4 %collective-permute-start.1 = (f32[256,128]{1,0:T(8,128)}, f32[256,128]{1,0:T(8,128)S(1)}, u32[]{:S(2)}, u32[]{:S(2)}) collective-permute-start(f32[256,128]{1,0:T(8,128)} %get-tuple-element.27), channel_id=1, source_target_pairs={{0,14},{2,12},{4,10},{6,8},{8,6},{10,4},{12,2},{14,0},{1,15},{3,13... | collective-permute-start | bytes 393224 | tf_op jit(solution)/shard_map/ppermute | solution.py:255
  8.8 1.3 %collective-permute-start.2 = (f32[256,128]{1,0:T(8,128)}, f32[256,128]{1,0:T(8,128)S(1)}, u32[]{:S(2)}, u32[]{:S(2)}) collective-permute-start(f32[256,128]{1,0:T(8,128)} %get-tuple-element.28), channel_id=1, source_target_pairs={{0,12},{2,14},{4,8},{6,10},{8,4},{10,6},{12,0},{14,2},{1,13},{3,15... | collective-permute-start | bytes 393224 | tf_op jit(solution)/shard_map/ppermute | solution.py:255
  10.1 1.7 %collective-permute-start.3 = (f32[256,128]{1,0:T(8,128)}, f32[256,128]{1,0:T(8,128)S(1)}, u32[]{:S(2)}, u32[]{:S(2)}) collective-permute-start(f32[256,128]{1,0:T(8,128)} %get-tuple-element.29), channel_id=1, source_target_pairs={{0,10},{2,8},{4,14},{6,12},{8,2},{10,0},{12,6},{14,4},{1,11},{3,9}... | collective-permute-start | bytes 393224 | tf_op jit(solution)/shard_map/ppermute | solution.py:255
  11.9 2.1 %collective-permute-start.4 = (f32[256,128]{1,0:T(8,128)}, f32[256,128]{1,0:T(8,128)S(1)}, u32[]{:S(2)}, u32[]{:S(2)}) collective-permute-start(f32[256,128]{1,0:T(8,128)} %get-tuple-element.30), channel_id=1, source_target_pairs={{0,8},{2,10},{4,12},{6,14},{8,0},{10,2},{12,4},{14,6},{1,9},{3,11}... | collective-permute-start | bytes 393224 | tf_op jit(solution)/shard_map/ppermute | solution.py:255
  14.0 0.0 collective-permute-done.refs_1_
  14.0 0.1 collective-permute-start.5
  14.1 1.7 %collective-permute-done.1.refs_2_ = f32[256,128]{1,0:T(8,128)S(1)} collective-permute-done((f32[256,128]{1,0:T(8,128)}, f32[256,128]{1,0:T(8,128)S(1)}, u32[]{:S(2)}, u32[]{:S(2)}) %collective-permute-start.1) | collective-permute-done | bytes 131104 | tf_op jit(solution)/shard_map/ppermute | solution.py:255
  15.9 2.0 %collective-permute-start.6 = (f32[256,128]{1,0:T(8,128)}, f32[256,128]{1,0:T(8,128)S(1)}, u32[]{:S(2)}, u32[]{:S(2)}) collective-permute-start(f32[256,128]{1,0:T(8,128)} %get-tuple-element.32), channel_id=1, source_target_pairs={{0,2},{2,0},{4,6},{6,4},{8,10},{10,8},{12,14},{14,12},{1,3},{3,1},... | collective-permute-start | bytes 393224 | tf_op jit(solution)/shard_map/ppermute | solution.py:255
  17.9 2.3 %copy-done = f32[18,2,2,128,128]{4,3,2,1,0:T(8,128)S(1)} copy-done((f32[18,2,2,128,128]{4,3,2,1,0:T(8,128)S(1)}, f32[18,2,2,128,128]{4,3,2,1,0:T(8,128)}, u32[]{:S(2)}) %copy-start) | copy-done | bytes 4718616
  20.2 0.7 copy-done.2
  20.9 5.5 %prepare_gates.1 = (bf16[2,256,256]{2,1,0:T(8,128)(2,1)S(1)}, bf16[4,2,256,256]{3,2,1,0:T(8,128)(2,1)S(1)}, bf16[4,2,256,256]{3,2,1,0:T(8,128)(2,1)S(1)}, bf16[4,2,256,256]{3,2,1,0:T(8,128)(2,1)S(1)}) custom-call(s32[18]{0:T(128)S(1)} %copy-done.2, f32[18,2,2,128,128]{4,3,2,1,0:T(8,128)S(1)} %copy-done), custom_call_target="tpu_custom_call" | custom-call | flops 1610612736 | bytes 4194304 | tf_op jit(solution)/shard_map/prepare_gates/pallas_call | solution.py:210
  26.4 0.0 collective-permute-done.2.refs_3_
  26.4 4.3 %collective-permute-done.3.refs_4_ = f32[256,128]{1,0:T(8,128)S(1)} collective-permute-done((f32[256,128]{1,0:T(8,128)}, f32[256,128]{1,0:T(8,128)S(1)}, u32[]{:S(2)}, u32[]{:S(2)}) %collective-permute-start.3) | collective-permute-done | bytes 131104 | tf_op jit(solution)/shard_map/ppermute | solution.py:255
  30.7 1.6 %collective-permute-done.4.refs_5_ = f32[256,128]{1,0:T(8,128)S(1)} collective-permute-done((f32[256,128]{1,0:T(8,128)}, f32[256,128]{1,0:T(8,128)S(1)}, u32[]{:S(2)}, u32[]{:S(2)}) %collective-permute-start.4) | collective-permute-done | bytes 131104 | tf_op jit(solution)/shard_map/ppermute | solution.py:255
  32.3 2.8 %first_section.1 = (f32[2,4,2,16,128]{4,3,2,1,0:T(8,128)S(1)}, f32[2,4,2,16,128]{4,3,2,1,0:T(8,128)S(1)}, f32[2,4,2,16,128]{4,3,2,1,0:T(8,128)S(1)}, f32[2,4,2,1...) custom-call(f32[256,128]{1,0:T(8,128)S(1)} %copy-done.1, ...), custom_call_target="tpu_custom_call" | custom-call | flops 2013265920 | bytes 4194304 | tf_op jit(solution)/shard_map/first_section/pallas_call | solution.py:210
  35.1 3.5 %collective-permute-start.7 = (f32[2,4,2,16,128]{4,3,2,1,0:T(8,128)S(1)}, f32[2,4,2,16,128]{4,3,2,1,0:T(8,128)S(1)}, u32[]{:S(2)}, u32[]{:S(2)}) collective-permute-start(f32[2,4,2,16,128]{4,3,2,1,0:T(8,128)S(1)} %get-tuple-element.36), channel_id=1, source_target_pairs={{0,6},{2,4},{4,2},{6,0},{8,14},{10,12},{12,10},{14,8},{1,7},{3,5},... | collective-permute-start | bytes 393224 | tf_op jit(solution)/shard_map/ppermute | solution.py:255
  38.6 3.1 %collective-permute-start.8 = (f32[2,4,2,16,128]{4,3,2,1,0:T(8,128)S(1)}, f32[2,4,2,16,128]{4,3,2,1,0:T(8,128)S(1)}, u32[]{:S(2)}, u32[]{:S(2)}) collective-permute-start(f32[2,4,2,16,128]{4,3,2,1,0:T(8,128)S(1)} %get-tuple-element.37), channel_id=1, source_target_pairs={{0,14},{2,12},{4,10},{6,8},{8,6},{10,4},{12,2},{14,0},{1,15},{3,13... | collective-permute-start | bytes 393224 | tf_op jit(solution)/shard_map/ppermute | solution.py:255
  41.7 1.5 %collective-permute-start.9 = (f32[2,4,2,16,128]{4,3,2,1,0:T(8,128)S(1)}, f32[2,4,2,16,128]{4,3,2,1,0:T(8,128)S(1)}, u32[]{:S(2)}, u32[]{:S(2)}) collective-permute-start(f32[2,4,2,16,128]{4,3,2,1,0:T(8,128)S(1)} %get-tuple-element.38), channel_id=1, source_target_pairs={{0,12},{2,14},{4,8},{6,10},{8,4},{10,6},{12,0},{14,2},{1,13},{3,15... | collective-permute-start | bytes 393224 | tf_op jit(solution)/shard_map/ppermute | solution.py:255
  43.2 3.0 %collective-permute-start.11 = (f32[2,4,2,16,128]{4,3,2,1,0:T(8,128)S(1)}, f32[2,4,2,16,128]{4,3,2,1,0:T(8,128)S(1)}, u32[]{:S(2)}, u32[]{:S(2)}) collective-permute-start(f32[2,4,2,16,128]{4,3,2,1,0:T(8,128)S(1)} %get-tuple-element.40), channel_id=1, source_target_pairs={{0,8},{2,10},{4,12},{6,14},{8,0},{10,2},{12,4},{14,6},{1,9},{3,11}... | collective-permute-start | bytes 393224 | tf_op jit(solution)/shard_map/ppermute | solution.py:255
  46.2 0.9 %collective-permute-start.12 = (f32[2,4,2,16,128]{4,3,2,1,0:T(8,128)S(1)}, f32[2,4,2,16,128]{4,3,2,1,0:T(8,128)S(1)}, u32[]{:S(2)}, u32[]{:S(2)}) collective-permute-start(f32[2,4,2,16,128]{4,3,2,1,0:T(8,128)S(1)} %get-tuple-element.41), channel_id=1, source_target_pairs={{0,4},{2,6},{4,0},{6,2},{8,12},{10,14},{12,8},{14,10},{1,5},{3,7},... | collective-permute-start | bytes 393224 | tf_op jit(solution)/shard_map/ppermute | solution.py:255
  47.1 1.7 %collective-permute-done.8.refs_2_ = f32[2,4,2,16,128]{4,3,2,1,0:T(8,128)S(1)} collective-permute-done((f32[2,4,2,16,128]{4,3,2,1,0:T(8,128)S(1)}, f32[2,4,2,16,128]{4,3,2,1,0:T(8,128)S(1)}, u32[]{:S(2)}, u32[]{:S(2)}) %collective-permute-start.8) | collective-permute-done | bytes 131104 | tf_op jit(solution)/shard_map/ppermute | solution.py:255
  48.8 1.6 %collective-permute-start.13 = (f32[2,4,2,16,128]{4,3,2,1,0:T(8,128)S(1)}, f32[2,4,2,16,128]{4,3,2,1,0:T(8,128)S(1)}, u32[]{:S(2)}, u32[]{:S(2)}) collective-permute-start(f32[2,4,2,16,128]{4,3,2,1,0:T(8,128)S(1)} %get-tuple-element.42), channel_id=1, source_target_pairs={{0,2},{2,0},{4,6},{6,4},{8,10},{10,8},{12,14},{14,12},{1,3},{3,1},... | collective-permute-start | bytes 393224 | tf_op jit(solution)/shard_map/ppermute | solution.py:255
  50.4 1.3 %collective-permute-done.9.refs_3_ = f32[2,4,2,16,128]{4,3,2,1,0:T(8,128)S(1)} collective-permute-done((f32[2,4,2,16,128]{4,3,2,1,0:T(8,128)S(1)}, f32[2,4,2,16,128]{4,3,2,1,0:T(8,128)S(1)}, u32[]{:S(2)}, u32[]{:S(2)}) %collective-permute-start.9) | collective-permute-done | bytes 131104 | tf_op jit(solution)/shard_map/ppermute | solution.py:255
  51.7 8.5 %collective-permute-done.10.refs_4_ = f32[2,4,2,16,128]{4,3,2,1,0:T(8,128)S(1)} collective-permute-done((f32[2,4,2,16,128]{4,3,2,1,0:T(8,128)S(1)}, f32[2,4,2,16,128]{4,3,2,1,0:T(8,128)S(1)}, u32[]{:S(2)}, u32[]{:S(2)}) %collective-permute-start.10) | collective-permute-done | bytes 131104 | tf_op jit(solution)/shard_map/ppermute | solution.py:255
  60.2 1.1 %collective-permute-done.11.refs_5_ = f32[2,4,2,16,128]{4,3,2,1,0:T(8,128)S(1)} collective-permute-done((f32[2,4,2,16,128]{4,3,2,1,0:T(8,128)S(1)}, f32[2,4,2,16,128]{4,3,2,1,0:T(8,128)S(1)}, u32[]{:S(2)}, u32[]{:S(2)}) %collective-permute-start.11) | collective-permute-done | bytes 131104 | tf_op jit(solution)/shard_map/ppermute | solution.py:255
  61.3 1.5 %second_section_sent.1 = f32[2,512,128]{2,1,0:T(8,128)S(1)} custom-call(f32[2,4,2,16,128]{4,3,2,1,0:T(8,128)S(1)} %get-tuple-element.35.refs_0_, f32[2,4,2,16,128]{4,3,2,1,0:T(8,128)S(1)} %collective-permute-done.7.refs_1_, f32[2,4,2,16,128]{4,3,2,1,0:T(8,128)S(1)} %collective-permute-done.8.refs_2_, ...), custom_call_target="tpu_custom_call" | custom-call | flops 805306368 | bytes 4194304 | tf_op jit(solution)/shard_map/second_section_sent/pallas_call | solution.py:210
  62.9 0.1 collective-permute-start.14
  63.0 1.5 %second_section_kept.1.kept_ref = f32[2,512,128]{2,1,0:T(8,128)S(1)} custom-call(f32[2,4,2,16,128]{4,3,2,1,0:T(8,128)S(1)} %get-tuple-element.35.refs_0_, f32[2,4,2,16,128]{4,3,2,1,0:T(8,128)S(1)} %collective-permute-done.7.refs_1_, f32[2,4,2,16,128]{4,3,2,1,0:T(8,128)S(1)} %collective-permute-done.8.refs_2_, ...), custom_call_target="tpu_custom_call" | custom-call | flops 805306368 | bytes 4194304 | tf_op jit(solution)/shard_map/second_section_kept/pallas_call | solution.py:210
  64.5 0.4 collective-permute-done.14.came_ref
  64.8 3.3 %third_section.1 = f32[2048,128]{1,0:T(8,128)} custom-call(f32[2,512,128]{2,1,0:T(8,128)S(1)} %second_section_kept.1.kept_ref, f32[2,512,128]{2,1,0:T(8,128)S(1)} %collective-permute-done.14.came_ref, bf16[4,2,256,256]{3,2,1,0:T(8,128)(2,1)S(1)} %get-tuple-element.44.rows_ref), custom_call_target="tpu_custom_call" | custom-call | flops 1610612736 | bytes 4194304 | tf_op jit(solution)/shard_map/third_section/pallas_call | solution.py:210
  (10 shorter events, 0.0 us)
Async XLA Ops:
  2.3 11.7 %collective-permute-start = (f32[256,128]{1,0:T(8,128)}, f32[256,128]{1,0:T(8,128)S(1)}, u32[]{:S(2)}, u32[]{:S(2)}) collective-permute-start(f32[256,128]{1,0:T(8,128)} %get-tuple-element.26), channel_id=1, source_target_pairs={{0,6},{2,4},{4,2},{6,0},{8,14},{10,12},{12,10},{14,8},{1,7},{3,5},... | collective-permute-start | bytes 393224 | tf_op jit(solution)/shard_map/ppermute | solution.py:255
  6.4 9.5 %collective-permute-start.1 = (f32[256,128]{1,0:T(8,128)}, f32[256,128]{1,0:T(8,128)S(1)}, u32[]{:S(2)}, u32[]{:S(2)}) collective-permute-start(f32[256,128]{1,0:T(8,128)} %get-tuple-element.27), channel_id=1, source_target_pairs={{0,14},{2,12},{4,10},{6,8},{8,6},{10,4},{12,2},{14,0},{1,15},{3,13... | collective-permute-start | bytes 393224 | tf_op jit(solution)/shard_map/ppermute | solution.py:255
  8.8 17.6 %collective-permute-start.2 = (f32[256,128]{1,0:T(8,128)}, f32[256,128]{1,0:T(8,128)S(1)}, u32[]{:S(2)}, u32[]{:S(2)}) collective-permute-start(f32[256,128]{1,0:T(8,128)} %get-tuple-element.28), channel_id=1, source_target_pairs={{0,12},{2,14},{4,8},{6,10},{8,4},{10,6},{12,0},{14,2},{1,13},{3,15... | collective-permute-start | bytes 393224 | tf_op jit(solution)/shard_map/ppermute | solution.py:255
  10.1 20.6 %collective-permute-start.3 = (f32[256,128]{1,0:T(8,128)}, f32[256,128]{1,0:T(8,128)S(1)}, u32[]{:S(2)}, u32[]{:S(2)}) collective-permute-start(f32[256,128]{1,0:T(8,128)} %get-tuple-element.29), channel_id=1, source_target_pairs={{0,10},{2,8},{4,14},{6,12},{8,2},{10,0},{12,6},{14,4},{1,11},{3,9}... | collective-permute-start | bytes 393224 | tf_op jit(solution)/shard_map/ppermute | solution.py:255
  11.9 20.4 %collective-permute-start.4 = (f32[256,128]{1,0:T(8,128)}, f32[256,128]{1,0:T(8,128)S(1)}, u32[]{:S(2)}, u32[]{:S(2)}) collective-permute-start(f32[256,128]{1,0:T(8,128)} %get-tuple-element.30), channel_id=1, source_target_pairs={{0,8},{2,10},{4,12},{6,14},{8,0},{10,2},{12,4},{14,6},{1,9},{3,11}... | collective-permute-start | bytes 393224 | tf_op jit(solution)/shard_map/ppermute | solution.py:255
  14.0 18.3 %collective-permute-start.5 = (f32[256,128]{1,0:T(8,128)}, f32[256,128]{1,0:T(8,128)S(1)}, u32[]{:S(2)}, u32[]{:S(2)}) collective-permute-start(f32[256,128]{1,0:T(8,128)} %get-tuple-element.31), channel_id=1, source_target_pairs={{0,4},{2,6},{4,0},{6,2},{8,12},{10,14},{12,8},{14,10},{1,5},{3,7},... | collective-permute-start | bytes 393224 | tf_op jit(solution)/shard_map/ppermute | solution.py:255
  15.9 16.4 %collective-permute-start.6 = (f32[256,128]{1,0:T(8,128)}, f32[256,128]{1,0:T(8,128)S(1)}, u32[]{:S(2)}, u32[]{:S(2)}) collective-permute-start(f32[256,128]{1,0:T(8,128)} %get-tuple-element.32), channel_id=1, source_target_pairs={{0,2},{2,0},{4,6},{6,4},{8,10},{10,8},{12,14},{14,12},{1,3},{3,1},... | collective-permute-start | bytes 393224 | tf_op jit(solution)/shard_map/ppermute | solution.py:255
  17.9 2.3 %copy-start = (f32[18,2,2,128,128]{4,3,2,1,0:T(8,128)S(1)}, f32[18,2,2,128,128]{4,3,2,1,0:T(8,128)}, u32[]{:S(2)}) copy-start(f32[18,2,2,128,128]{4,3,2,1,0:T(8,128)} %gates_ref.1) | copy-start | bytes 14155780
  20.2 0.7 copy-start.2
  20.9 11.4 %copy-start.1 = (f32[256,128]{1,0:T(8,128)S(1)}, f32[256,128]{1,0:T(8,128)}, u32[]{:S(2)}) copy-start(f32[256,128]{1,0:T(8,128)} %get-tuple-element.25.refs_0_) | copy-start | bytes 393220
  35.1 11.1 %collective-permute-start.7 = (f32[2,4,2,16,128]{4,3,2,1,0:T(8,128)S(1)}, f32[2,4,2,16,128]{4,3,2,1,0:T(8,128)S(1)}, u32[]{:S(2)}, u32[]{:S(2)}) collective-permute-start(f32[2,4,2,16,128]{4,3,2,1,0:T(8,128)S(1)} %get-tuple-element.36), channel_id=1, source_target_pairs={{0,6},{2,4},{4,2},{6,0},{8,14},{10,12},{12,10},{14,8},{1,7},{3,5},... | collective-permute-start | bytes 393224 | tf_op jit(solution)/shard_map/ppermute | solution.py:255
  38.6 10.3 %collective-permute-start.8 = (f32[2,4,2,16,128]{4,3,2,1,0:T(8,128)S(1)}, f32[2,4,2,16,128]{4,3,2,1,0:T(8,128)S(1)}, u32[]{:S(2)}, u32[]{:S(2)}) collective-permute-start(f32[2,4,2,16,128]{4,3,2,1,0:T(8,128)S(1)} %get-tuple-element.37), channel_id=1, source_target_pairs={{0,14},{2,12},{4,10},{6,8},{8,6},{10,4},{12,2},{14,0},{1,15},{3,13... | collective-permute-start | bytes 393224 | tf_op jit(solution)/shard_map/ppermute | solution.py:255
  41.7 10.0 %collective-permute-start.9 = (f32[2,4,2,16,128]{4,3,2,1,0:T(8,128)S(1)}, f32[2,4,2,16,128]{4,3,2,1,0:T(8,128)S(1)}, u32[]{:S(2)}, u32[]{:S(2)}) collective-permute-start(f32[2,4,2,16,128]{4,3,2,1,0:T(8,128)S(1)} %get-tuple-element.38), channel_id=1, source_target_pairs={{0,12},{2,14},{4,8},{6,10},{8,4},{10,6},{12,0},{14,2},{1,13},{3,15... | collective-permute-start | bytes 393224 | tf_op jit(solution)/shard_map/ppermute | solution.py:255
  43.2 17.1 %collective-permute-start.10 = (f32[2,4,2,16,128]{4,3,2,1,0:T(8,128)S(1)}, f32[2,4,2,16,128]{4,3,2,1,0:T(8,128)S(1)}, u32[]{:S(2)}, u32[]{:S(2)}) collective-permute-start(f32[2,4,2,16,128]{4,3,2,1,0:T(8,128)S(1)} %get-tuple-element.39), channel_id=1, source_target_pairs={{0,10},{2,8},{4,14},{6,12},{8,2},{10,0},{12,6},{14,4},{1,11},{3,9}... | collective-permute-start | bytes 393224 | tf_op jit(solution)/shard_map/ppermute | solution.py:255
  43.2 18.2 %collective-permute-start.11 = (f32[2,4,2,16,128]{4,3,2,1,0:T(8,128)S(1)}, f32[2,4,2,16,128]{4,3,2,1,0:T(8,128)S(1)}, u32[]{:S(2)}, u32[]{:S(2)}) collective-permute-start(f32[2,4,2,16,128]{4,3,2,1,0:T(8,128)S(1)} %get-tuple-element.40), channel_id=1, source_target_pairs={{0,8},{2,10},{4,12},{6,14},{8,0},{10,2},{12,4},{14,6},{1,9},{3,11}... | collective-permute-start | bytes 393224 | tf_op jit(solution)/shard_map/ppermute | solution.py:255
  46.2 15.1 %collective-permute-start.12 = (f32[2,4,2,16,128]{4,3,2,1,0:T(8,128)S(1)}, f32[2,4,2,16,128]{4,3,2,1,0:T(8,128)S(1)}, u32[]{:S(2)}, u32[]{:S(2)}) collective-permute-start(f32[2,4,2,16,128]{4,3,2,1,0:T(8,128)S(1)} %get-tuple-element.41), channel_id=1, source_target_pairs={{0,4},{2,6},{4,0},{6,2},{8,12},{10,14},{12,8},{14,10},{1,5},{3,7},... | collective-permute-start | bytes 393224 | tf_op jit(solution)/shard_map/ppermute | solution.py:255
  48.8 12.5 %collective-permute-start.13 = (f32[2,4,2,16,128]{4,3,2,1,0:T(8,128)S(1)}, f32[2,4,2,16,128]{4,3,2,1,0:T(8,128)S(1)}, u32[]{:S(2)}, u32[]{:S(2)}) collective-permute-start(f32[2,4,2,16,128]{4,3,2,1,0:T(8,128)S(1)} %get-tuple-element.42), channel_id=1, source_target_pairs={{0,2},{2,0},{4,6},{6,4},{8,10},{10,8},{12,14},{14,12},{1,3},{3,1},... | collective-permute-start | bytes 393224 | tf_op jit(solution)/shard_map/ppermute | solution.py:255
  62.9 2.0 %collective-permute-start.14 = (f32[2,512,128]{2,1,0:T(8,128)S(1)}, f32[2,512,128]{2,1,0:T(8,128)S(1)}, u32[]{:S(2)}, u32[]{:S(2)}) collective-permute-start(f32[2,512,128]{2,1,0:T(8,128)S(1)} %second_section_sent.1), channel_id=1, source_target_pairs={{0,1},{1,0},{2,3},{3,2},{4,5},{5,4},{6,7},{7,6},{8,9},{9,8},{10,11... | collective-permute-start | bytes 1572872 | tf_op jit(solution)/shard_map/ppermute | solution.py:297

commit v3 on v2

--- a/solution.py
+++ b/solution.py
@@ -11,7 +11,7 @@
 F32 = jnp.float32
 BF16 = jnp.bfloat16
 VMEM_LIMIT = 14 * 1024 * 1024
-WHOLE_VMEM = 60 * 1024 * 1024
+LARGE_VMEM = 48 * 1024 * 1024
 
 
 def window_offsets(span, gate_bits):
@@ -83,23 +83,16 @@
 
 
 def distances_of(count):
-    half = count // 2
-    return [0, half - 1, *range(count - 1, half - 1, -1), *range(half - 2, 0, -1)]
+    return [0, *range(count - 1, 0, -1)]
 
 
 def partner(distance):
     return jnp.bitwise_xor(lax.axis_index("qa"), distance)
 
 
-def split_kernel(x_ref, *refs):
-    *outs, sems = refs
-    copies = []
-    for place, distance in enumerate(distances_of(len(outs))):
-        copy = pltpu.make_async_copy(x_ref.at[partner(distance)], outs[place], sems.at[place])
-        copy.start()
-        copies.append(copy)
-    for copy in copies:
-        copy.wait()
+def split_kernel(x_ref, *outs):
+    for distance, out_ref in zip(distances_of(len(outs)), outs):
+        out_ref[...] = x_ref[partner(distance)]
 
 
 def apply_rows(weights_ref, slot, offset, lane_bits, rows, load, store):
@@ -242,11 +235,10 @@
         split_kernel,
         "split_state",
         (shape((2 * rows // qa, lanes), F32),) * qa,
-        [hbm],
-        [pltpu.SemaphoreType.DMA((qa,))],
+        [vmem],
+        [],
         0,
         state,
-        limit=WHOLE_VMEM,
     )
 
     def exchange(blocks):
@@ -265,6 +257,7 @@
         4,
         path_bits,
         gate_terms,
+        limit=LARGE_VMEM,
     )
     inner = rows // (qa * qa)
     blocks = call(

time: 68.4 us -> 65.5 us (0.958)
  starting transfers between devices: 27.4 us -> 40.4 us
  waiting for transfers between devices: 20.7 us -> 9.59 us
  Pallas kernels: 17 us -> 13.3 us
  local copies, waits for them, and re-layouts: 2.99 us -> 1.88 us
    ppermute x14, starting transfers between devices: 27.4 us -> 40.4 us  [exchange(): lax.ppermute(piece, 'qa', [(i, i ^ distance) for i in range(qa)])]
    ppermute x14, waiting for transfers between devices: 20.3 us -> 9.23 us  [exchange(): lax.ppermute(piece, 'qa', [(i, i ^ distance) for i in range(qa)])]
    pallas_call x6, Pallas kernels: 17 us -> 13.3 us  [call(): pl.pallas_call(kernel, out_shape=out_shapes, in_specs=in_specs, out_specs...]
    unnamed x6 -> x4, local copies, waits for them, and re-layouts: 2.99 us -> 1.88 us
  transfers between devices with their start and end apart: 15 -> 15, of which waited for: 8 -> 7; matrix products, arithmetic and copies ran while one was open for 0% -> 0% of each run, Pallas kernels for 10% -> 9%
where the time goes in v3:
time: 65.5 us; the launch traced here: 65.3 us
  starting transfers between devices  40.4 us (62%)
  Pallas kernels  13.3 us (20%)
  waiting for transfers between devices  9.59 us (15%)
  local copies, waits for them, and re-layouts  1.88 us (3%)
    ppermute x14, starting transfers between devices, exchange(): lax.ppermute(piece, 'qa', [(i, i ^ distance) for i in range(qa)])  40.4 us
    pallas_call x6, Pallas kernels, call(): pl.pallas_call(kernel, out_shape=out_shapes, in_specs=in_specs, out_specs...  13.3 us
    ppermute x14, waiting for transfers between devices, exchange(): lax.ppermute(piece, 'qa', [(i, i ^ distance) for i in range(qa)])  9.23 us
    unnamed x4, local copies, waits for them, and re-layouts  1.88 us
  transfers between devices with their start and end apart: 15, of which 7 were waited for; matrix products, arithmetic and copies ran while one was open for 0% of the time, Pallas kernels for 9%

profile of v3, /device:TPU:0, one launch (start us, length us, event | category | flops | bytes accessed | tf_op | source)
XLA Modules:
  0.0 65.3 jit_solution(7856701328378561890)
XLA Ops:
  0.0 1.2 %copy-done = f32[2,131072]{1,0:T(2,128)S(1)} copy-done((f32[2,131072]{1,0:T(2,128)S(1)}, f32[2,131072]{1,0:T(2,128)}, u32[]{:S(2)}) %copy-start) | copy-done | bytes 1048600
  1.2 0.1 split_state.1
  1.3 6.1 %collective-permute-start = (f32[256,128]{1,0:T(8,128)S(1)}, f32[256,128]{1,0:T(8,128)S(1)}, u32[]{:S(2)}, u32[]{:S(2)}) collective-permute-start(f32[256,128]{1,0:T(8,128)S(1)} %get-tuple-element.26), channel_id=1, source_target_pairs={{0,14},{2,12},{4,10},{6,8},{8,6},{10,4},{12,2},{14,0},{1,15},{3,13... | collective-permute-start | bytes 393224 | tf_op jit(solution)/shard_map/ppermute | solution.py:247
  7.4 0.2 collective-permute-start.1
  7.6 0.7 %collective-permute-start.2 = (f32[256,128]{1,0:T(8,128)S(1)}, f32[256,128]{1,0:T(8,128)S(1)}, u32[]{:S(2)}, u32[]{:S(2)}) collective-permute-start(f32[256,128]{1,0:T(8,128)S(1)} %get-tuple-element.28), channel_id=1, source_target_pairs={{0,10},{2,8},{4,14},{6,12},{8,2},{10,0},{12,6},{14,4},{1,11},{3,9}... | collective-permute-start | bytes 393224 | tf_op jit(solution)/shard_map/ppermute | solution.py:247
  8.3 2.0 %collective-permute-start.3 = (f32[256,128]{1,0:T(8,128)S(1)}, f32[256,128]{1,0:T(8,128)S(1)}, u32[]{:S(2)}, u32[]{:S(2)}) collective-permute-start(f32[256,128]{1,0:T(8,128)S(1)} %get-tuple-element.29), channel_id=1, source_target_pairs={{0,8},{2,10},{4,12},{6,14},{8,0},{10,2},{12,4},{14,6},{1,9},{3,11}... | collective-permute-start | bytes 393224 | tf_op jit(solution)/shard_map/ppermute | solution.py:247
  10.4 2.3 %collective-permute-start.4 = (f32[256,128]{1,0:T(8,128)S(1)}, f32[256,128]{1,0:T(8,128)S(1)}, u32[]{:S(2)}, u32[]{:S(2)}) collective-permute-start(f32[256,128]{1,0:T(8,128)S(1)} %get-tuple-element.30), channel_id=1, source_target_pairs={{0,6},{2,4},{4,2},{6,0},{8,14},{10,12},{12,10},{14,8},{1,7},{3,5},... | collective-permute-start | bytes 393224 | tf_op jit(solution)/shard_map/ppermute | solution.py:247
  12.7 10.4 %collective-permute-start.5 = (f32[256,128]{1,0:T(8,128)S(1)}, f32[256,128]{1,0:T(8,128)S(1)}, u32[]{:S(2)}, u32[]{:S(2)}) collective-permute-start(f32[256,128]{1,0:T(8,128)S(1)} %get-tuple-element.31), channel_id=1, source_target_pairs={{0,4},{2,6},{4,0},{6,2},{8,12},{10,14},{12,8},{14,10},{1,5},{3,7},... | collective-permute-start | bytes 393224 | tf_op jit(solution)/shard_map/ppermute | solution.py:247
  23.1 0.0 collective-permute-done.1.refs_2_
  23.1 1.3 %collective-permute-start.6 = (f32[256,128]{1,0:T(8,128)S(1)}, f32[256,128]{1,0:T(8,128)S(1)}, u32[]{:S(2)}, u32[]{:S(2)}) collective-permute-start(f32[256,128]{1,0:T(8,128)S(1)} %get-tuple-element.32), channel_id=1, source_target_pairs={{0,2},{2,0},{4,6},{6,4},{8,10},{10,8},{12,14},{14,12},{1,3},{3,1},... | collective-permute-start | bytes 393224 | tf_op jit(solution)/shard_map/ppermute | solution.py:247
  24.5 0.7 %copy-done.1 = s32[18]{0:T(128)S(1)} copy-done((s32[18]{0:T(128)S(1)}, s32[18]{0:T(128)}, u32[]{:S(2)}) %copy-start.1) | copy-done | bytes 96
  25.1 4.1 %prepare_gates.1 = (bf16[2,256,256]{2,1,0:T(8,128)(2,1)S(1)}, bf16[4,2,256,256]{3,2,1,0:T(8,128)(2,1)S(1)}, bf16[4,2,256,256]{3,2,1,0:T(8,128)(2,1)S(1)}, bf16[4,2,256,256]{3,2,1,0:T(8,128)(2,1)S(1)}) custom-call(s32[18]{0:T(128)S(1)} %copy-done.1, f32[18,2,2,128,128]{4,3,2,1,0:T(8,128)} %gates_ref.1), custom_call_target="tpu_custom_call" | custom-call | flops 1610612736 | bytes 4194304 | tf_op jit(solution)/shard_map/prepare_gates/pallas_call | solution.py:203
  29.2 0.0 collective-permute-done.2.refs_3_
  29.2 0.6 collective-permute-done.3.refs_4_
  29.8 1.1 %collective-permute-done.5.refs_6_ = f32[256,128]{1,0:T(8,128)S(1)} collective-permute-done((f32[256,128]{1,0:T(8,128)S(1)}, f32[256,128]{1,0:T(8,128)S(1)}, u32[]{:S(2)}, u32[]{:S(2)}) %collective-permute-start.5) | collective-permute-done | bytes 131104 | tf_op jit(solution)/shard_map/ppermute | solution.py:247
  30.9 2.8 %first_section.1 = (f32[2,4,2,16,128]{4,3,2,1,0:T(8,128)S(1)}, f32[2,4,2,16,128]{4,3,2,1,0:T(8,128)S(1)}, f32[2,4,2,16,128]{4,3,2,1,0:T(8,128)S(1)}, f32[2,4,2,1...) custom-call(f32[256,128]{1,0:T(8,128)S(1)} %get-tuple-element.25.ref, ...), custom_call_target="tpu_custom_call" | custom-call | flops 2013265920 | bytes 4194304 | tf_op jit(solution)/shard_map/first_section/pallas_call | solution.py:203
  33.7 2.7 %collective-permute-start.7 = (f32[2,4,2,16,128]{4,3,2,1,0:T(8,128)S(1)}, f32[2,4,2,16,128]{4,3,2,1,0:T(8,128)S(1)}, u32[]{:S(2)}, u32[]{:S(2)}) collective-permute-start(f32[2,4,2,16,128]{4,3,2,1,0:T(8,128)S(1)} %get-tuple-element.36), channel_id=1, source_target_pairs={{0,14},{2,12},{4,10},{6,8},{8,6},{10,4},{12,2},{14,0},{1,15},{3,13... | collective-permute-start | bytes 393224 | tf_op jit(solution)/shard_map/ppermute | solution.py:247
  36.4 1.3 %collective-permute-start.8 = (f32[2,4,2,16,128]{4,3,2,1,0:T(8,128)S(1)}, f32[2,4,2,16,128]{4,3,2,1,0:T(8,128)S(1)}, u32[]{:S(2)}, u32[]{:S(2)}) collective-permute-start(f32[2,4,2,16,128]{4,3,2,1,0:T(8,128)S(1)} %get-tuple-element.37), channel_id=1, source_target_pairs={{0,12},{2,14},{4,8},{6,10},{8,4},{10,6},{12,0},{14,2},{1,13},{3,15... | collective-permute-start | bytes 393224 | tf_op jit(solution)/shard_map/ppermute | solution.py:247
  37.7 0.2 collective-permute-start.9
  37.9 3.6 %collective-permute-start.10 = (f32[2,4,2,16,128]{4,3,2,1,0:T(8,128)S(1)}, f32[2,4,2,16,128]{4,3,2,1,0:T(8,128)S(1)}, u32[]{:S(2)}, u32[]{:S(2)}) collective-permute-start(f32[2,4,2,16,128]{4,3,2,1,0:T(8,128)S(1)} %get-tuple-element.39), channel_id=1, source_target_pairs={{0,8},{2,10},{4,12},{6,14},{8,0},{10,2},{12,4},{14,6},{1,9},{3,11}... | collective-permute-start | bytes 393224 | tf_op jit(solution)/shard_map/ppermute | solution.py:247
  41.4 0.2 collective-permute-start.11
  41.7 1.2 %collective-permute-done.7.refs_1_ = f32[2,4,2,16,128]{4,3,2,1,0:T(8,128)S(1)} collective-permute-done((f32[2,4,2,16,128]{4,3,2,1,0:T(8,128)S(1)}, f32[2,4,2,16,128]{4,3,2,1,0:T(8,128)S(1)}, u32[]{:S(2)}, u32[]{:S(2)}) %collective-permute-start.7) | collective-permute-done | bytes 131104 | tf_op jit(solution)/shard_map/ppermute | solution.py:247
  42.9 8.5 %collective-permute-start.12 = (f32[2,4,2,16,128]{4,3,2,1,0:T(8,128)S(1)}, f32[2,4,2,16,128]{4,3,2,1,0:T(8,128)S(1)}, u32[]{:S(2)}, u32[]{:S(2)}) collective-permute-start(f32[2,4,2,16,128]{4,3,2,1,0:T(8,128)S(1)} %get-tuple-element.41), channel_id=1, source_target_pairs={{0,4},{2,6},{4,0},{6,2},{8,12},{10,14},{12,8},{14,10},{1,5},{3,7},... | collective-permute-start | bytes 393224 | tf_op jit(solution)/shard_map/ppermute | solution.py:247
  51.4 0.8 %collective-permute-start.13 = (f32[2,4,2,16,128]{4,3,2,1,0:T(8,128)S(1)}, f32[2,4,2,16,128]{4,3,2,1,0:T(8,128)S(1)}, u32[]{:S(2)}, u32[]{:S(2)}) collective-permute-start(f32[2,4,2,16,128]{4,3,2,1,0:T(8,128)S(1)} %get-tuple-element.42), channel_id=1, source_target_pairs={{0,2},{2,0},{4,6},{6,4},{8,10},{10,8},{12,14},{14,12},{1,3},{3,1},... | collective-permute-start | bytes 393224 | tf_op jit(solution)/shard_map/ppermute | solution.py:247
  52.2 3.6 %collective-permute-done.9.refs_3_ = f32[2,4,2,16,128]{4,3,2,1,0:T(8,128)S(1)} collective-permute-done((f32[2,4,2,16,128]{4,3,2,1,0:T(8,128)S(1)}, f32[2,4,2,16,128]{4,3,2,1,0:T(8,128)S(1)}, u32[]{:S(2)}, u32[]{:S(2)}) %collective-permute-start.9) | collective-permute-done | bytes 131104 | tf_op jit(solution)/shard_map/ppermute | solution.py:247
  55.8 1.5 %collective-permute-done.10.refs_4_ = f32[2,4,2,16,128]{4,3,2,1,0:T(8,128)S(1)} collective-permute-done((f32[2,4,2,16,128]{4,3,2,1,0:T(8,128)S(1)}, f32[2,4,2,16,128]{4,3,2,1,0:T(8,128)S(1)}, u32[]{:S(2)}, u32[]{:S(2)}) %collective-permute-start.10) | collective-permute-done | bytes 131104 | tf_op jit(solution)/shard_map/ppermute | solution.py:247
  57.3 1.2 %collective-permute-done.12.refs_6_ = f32[2,4,2,16,128]{4,3,2,1,0:T(8,128)S(1)} collective-permute-done((f32[2,4,2,16,128]{4,3,2,1,0:T(8,128)S(1)}, f32[2,4,2,16,128]{4,3,2,1,0:T(8,128)S(1)}, u32[]{:S(2)}, u32[]{:S(2)}) %collective-permute-start.12) | collective-permute-done | bytes 131104 | tf_op jit(solution)/shard_map/ppermute | solution.py:247
  58.5 1.5 %second_section_sent.1 = f32[2,512,128]{2,1,0:T(8,128)S(1)} custom-call(f32[2,4,2,16,128]{4,3,2,1,0:T(8,128)S(1)} %get-tuple-element.35.refs_0_, f32[2,4,2,16,128]{4,3,2,1,0:T(8,128)S(1)} %collective-permute-done.7.refs_1_, f32[2,4,2,16,128]{4,3,2,1,0:T(8,128)S(1)} %collective-permute-done.8.refs_2_, ...), custom_call_target="tpu_custom_call" | custom-call | flops 805306368 | bytes 4194304 | tf_op jit(solution)/shard_map/second_section_sent/pallas_call | solution.py:203
  60.0 0.1 collective-permute-start.14
  60.1 1.5 %second_section_kept.1.kept_ref = f32[2,512,128]{2,1,0:T(8,128)S(1)} custom-call(f32[2,4,2,16,128]{4,3,2,1,0:T(8,128)S(1)} %get-tuple-element.35.refs_0_, f32[2,4,2,16,128]{4,3,2,1,0:T(8,128)S(1)} %collective-permute-done.7.refs_1_, f32[2,4,2,16,128]{4,3,2,1,0:T(8,128)S(1)} %collective-permute-done.8.refs_2_, ...), custom_call_target="tpu_custom_call" | custom-call | flops 805306368 | bytes 4194304 | tf_op jit(solution)/shard_map/second_section_kept/pallas_call | solution.py:203
  61.6 0.4 collective-permute-done.14.came_ref
  62.0 3.4 %third_section.1 = f32[2048,128]{1,0:T(8,128)} custom-call(f32[2,512,128]{2,1,0:T(8,128)S(1)} %second_section_kept.1.kept_ref, f32[2,512,128]{2,1,0:T(8,128)S(1)} %collective-permute-done.14.came_ref, bf16[4,2,256,256]{3,2,1,0:T(8,128)(2,1)S(1)} %get-tuple-element.44.rows_ref), custom_call_target="tpu_custom_call" | custom-call | flops 1610612736 | bytes 4194304 | tf_op jit(solution)/shard_map/third_section/pallas_call | solution.py:203
  (8 shorter events, 0.0 us)
Async XLA Ops:
  0.0 1.2 %copy-start = (f32[2,131072]{1,0:T(2,128)S(1)}, f32[2,131072]{1,0:T(2,128)}, u32[]{:S(2)}) copy-start(f32[2,131072]{1,0:T(2,128)} %param.3) | copy-start | bytes 3145732
  1.3 11.4 %collective-permute-start = (f32[256,128]{1,0:T(8,128)S(1)}, f32[256,128]{1,0:T(8,128)S(1)}, u32[]{:S(2)}, u32[]{:S(2)}) collective-permute-start(f32[256,128]{1,0:T(8,128)S(1)} %get-tuple-element.26), channel_id=1, source_target_pairs={{0,14},{2,12},{4,10},{6,8},{8,6},{10,4},{12,2},{14,0},{1,15},{3,13... | collective-permute-start | bytes 393224 | tf_op jit(solution)/shard_map/ppermute | solution.py:247
  7.4 15.7 %collective-permute-start.1 = (f32[256,128]{1,0:T(8,128)S(1)}, f32[256,128]{1,0:T(8,128)S(1)}, u32[]{:S(2)}, u32[]{:S(2)}) collective-permute-start(f32[256,128]{1,0:T(8,128)S(1)} %get-tuple-element.27), channel_id=1, source_target_pairs={{0,12},{2,14},{4,8},{6,10},{8,4},{10,6},{12,0},{14,2},{1,13},{3,15... | collective-permute-start | bytes 393224 | tf_op jit(solution)/shard_map/ppermute | solution.py:247
  7.6 21.6 %collective-permute-start.2 = (f32[256,128]{1,0:T(8,128)S(1)}, f32[256,128]{1,0:T(8,128)S(1)}, u32[]{:S(2)}, u32[]{:S(2)}) collective-permute-start(f32[256,128]{1,0:T(8,128)S(1)} %get-tuple-element.28), channel_id=1, source_target_pairs={{0,10},{2,8},{4,14},{6,12},{8,2},{10,0},{12,6},{14,4},{1,11},{3,9}... | collective-permute-start | bytes 393224 | tf_op jit(solution)/shard_map/ppermute | solution.py:247
  8.3 21.5 %collective-permute-start.3 = (f32[256,128]{1,0:T(8,128)S(1)}, f32[256,128]{1,0:T(8,128)S(1)}, u32[]{:S(2)}, u32[]{:S(2)}) collective-permute-start(f32[256,128]{1,0:T(8,128)S(1)} %get-tuple-element.29), channel_id=1, source_target_pairs={{0,8},{2,10},{4,12},{6,14},{8,0},{10,2},{12,4},{14,6},{1,9},{3,11}... | collective-permute-start | bytes 393224 | tf_op jit(solution)/shard_map/ppermute | solution.py:247
  10.4 19.4 %collective-permute-start.4 = (f32[256,128]{1,0:T(8,128)S(1)}, f32[256,128]{1,0:T(8,128)S(1)}, u32[]{:S(2)}, u32[]{:S(2)}) collective-permute-start(f32[256,128]{1,0:T(8,128)S(1)} %get-tuple-element.30), channel_id=1, source_target_pairs={{0,6},{2,4},{4,2},{6,0},{8,14},{10,12},{12,10},{14,8},{1,7},{3,5},... | collective-permute-start | bytes 393224 | tf_op jit(solution)/shard_map/ppermute | solution.py:247
  12.7 18.3 %collective-permute-start.5 = (f32[256,128]{1,0:T(8,128)S(1)}, f32[256,128]{1,0:T(8,128)S(1)}, u32[]{:S(2)}, u32[]{:S(2)}) collective-permute-start(f32[256,128]{1,0:T(8,128)S(1)} %get-tuple-element.31), channel_id=1, source_target_pairs={{0,4},{2,6},{4,0},{6,2},{8,12},{10,14},{12,8},{14,10},{1,5},{3,7},... | collective-permute-start | bytes 393224 | tf_op jit(solution)/shard_map/ppermute | solution.py:247
  23.1 7.8 %collective-permute-start.6 = (f32[256,128]{1,0:T(8,128)S(1)}, f32[256,128]{1,0:T(8,128)S(1)}, u32[]{:S(2)}, u32[]{:S(2)}) collective-permute-start(f32[256,128]{1,0:T(8,128)S(1)} %get-tuple-element.32), channel_id=1, source_target_pairs={{0,2},{2,0},{4,6},{6,4},{8,10},{10,8},{12,14},{14,12},{1,3},{3,1},... | collective-permute-start | bytes 393224 | tf_op jit(solution)/shard_map/ppermute | solution.py:247
  24.4 0.7 %copy-start.1 = (s32[18]{0:T(128)S(1)}, s32[18]{0:T(128)}, u32[]{:S(2)}) copy-start(s32[18]{0:T(128)} %bits_ref.1) | copy-start | bytes 220
  33.7 9.2 %collective-permute-start.7 = (f32[2,4,2,16,128]{4,3,2,1,0:T(8,128)S(1)}, f32[2,4,2,16,128]{4,3,2,1,0:T(8,128)S(1)}, u32[]{:S(2)}, u32[]{:S(2)}) collective-permute-start(f32[2,4,2,16,128]{4,3,2,1,0:T(8,128)S(1)} %get-tuple-element.36), channel_id=1, source_target_pairs={{0,14},{2,12},{4,10},{6,8},{8,6},{10,4},{12,2},{14,0},{1,15},{3,13... | collective-permute-start | bytes 393224 | tf_op jit(solution)/shard_map/ppermute | solution.py:247
  36.4 15.0 %collective-permute-start.8 = (f32[2,4,2,16,128]{4,3,2,1,0:T(8,128)S(1)}, f32[2,4,2,16,128]{4,3,2,1,0:T(8,128)S(1)}, u32[]{:S(2)}, u32[]{:S(2)}) collective-permute-start(f32[2,4,2,16,128]{4,3,2,1,0:T(8,128)S(1)} %get-tuple-element.37), channel_id=1, source_target_pairs={{0,12},{2,14},{4,8},{6,10},{8,4},{10,6},{12,0},{14,2},{1,13},{3,15... | collective-permute-start | bytes 393224 | tf_op jit(solution)/shard_map/ppermute | solution.py:247
  37.7 18.1 %collective-permute-start.9 = (f32[2,4,2,16,128]{4,3,2,1,0:T(8,128)S(1)}, f32[2,4,2,16,128]{4,3,2,1,0:T(8,128)S(1)}, u32[]{:S(2)}, u32[]{:S(2)}) collective-permute-start(f32[2,4,2,16,128]{4,3,2,1,0:T(8,128)S(1)} %get-tuple-element.38), channel_id=1, source_target_pairs={{0,10},{2,8},{4,14},{6,12},{8,2},{10,0},{12,6},{14,4},{1,11},{3,9}... | collective-permute-start | bytes 393224 | tf_op jit(solution)/shard_map/ppermute | solution.py:247
  37.9 19.4 %collective-permute-start.10 = (f32[2,4,2,16,128]{4,3,2,1,0:T(8,128)S(1)}, f32[2,4,2,16,128]{4,3,2,1,0:T(8,128)S(1)}, u32[]{:S(2)}, u32[]{:S(2)}) collective-permute-start(f32[2,4,2,16,128]{4,3,2,1,0:T(8,128)S(1)} %get-tuple-element.39), channel_id=1, source_target_pairs={{0,8},{2,10},{4,12},{6,14},{8,0},{10,2},{12,4},{14,6},{1,9},{3,11}... | collective-permute-start | bytes 393224 | tf_op jit(solution)/shard_map/ppermute | solution.py:247
  41.4 15.8 %collective-permute-start.11 = (f32[2,4,2,16,128]{4,3,2,1,0:T(8,128)S(1)}, f32[2,4,2,16,128]{4,3,2,1,0:T(8,128)S(1)}, u32[]{:S(2)}, u32[]{:S(2)}) collective-permute-start(f32[2,4,2,16,128]{4,3,2,1,0:T(8,128)S(1)} %get-tuple-element.40), channel_id=1, source_target_pairs={{0,6},{2,4},{4,2},{6,0},{8,14},{10,12},{12,10},{14,8},{1,7},{3,5},... | collective-permute-start | bytes 393224 | tf_op jit(solution)/shard_map/ppermute | solution.py:247
  42.9 15.5 %collective-permute-start.12 = (f32[2,4,2,16,128]{4,3,2,1,0:T(8,128)S(1)}, f32[2,4,2,16,128]{4,3,2,1,0:T(8,128)S(1)}, u32[]{:S(2)}, u32[]{:S(2)}) collective-permute-start(f32[2,4,2,16,128]{4,3,2,1,0:T(8,128)S(1)} %get-tuple-element.41), channel_id=1, source_target_pairs={{0,4},{2,6},{4,0},{6,2},{8,12},{10,14},{12,8},{14,10},{1,5},{3,7},... | collective-permute-start | bytes 393224 | tf_op jit(solution)/shard_map/ppermute | solution.py:247
  51.4 7.1 %collective-permute-start.13 = (f32[2,4,2,16,128]{4,3,2,1,0:T(8,128)S(1)}, f32[2,4,2,16,128]{4,3,2,1,0:T(8,128)S(1)}, u32[]{:S(2)}, u32[]{:S(2)}) collective-permute-start(f32[2,4,2,16,128]{4,3,2,1,0:T(8,128)S(1)} %get-tuple-element.42), channel_id=1, source_target_pairs={{0,2},{2,0},{4,6},{6,4},{8,10},{10,8},{12,14},{14,12},{1,3},{3,1},... | collective-permute-start | bytes 393224 | tf_op jit(solution)/shard_map/ppermute | solution.py:247
  60.0 2.0 %collective-permute-start.14 = (f32[2,512,128]{2,1,0:T(8,128)S(1)}, f32[2,512,128]{2,1,0:T(8,128)S(1)}, u32[]{:S(2)}, u32[]{:S(2)}) collective-permute-start(f32[2,512,128]{2,1,0:T(8,128)S(1)} %second_section_sent.1), channel_id=1, source_target_pairs={{0,1},{1,0},{2,3},{3,2},{4,5},{5,4},{6,7},{7,6},{8,9},{9,8},{10,11... | collective-permute-start | bytes 1572872 | tf_op jit(solution)/shard_map/ppermute | solution.py:290

commit v4 on v3

--- a/solution.py
+++ b/solution.py
@@ -83,7 +83,13 @@
 
 
 def distances_of(count):
-    return [0, *range(count - 1, 0, -1)]
+    half = count // 2
+    far, near = list(range(count - 1, half - 1, -1)), list(range(half - 1, 0, -1))
+    order = [0]
+    while far or near:
+        order += far[:2] + near[:2]
+        far, near = far[2:], near[2:]
+    return order
 
 
 def partner(distance):

time: 65.5 us -> 62.7 us (0.957)
  starting transfers between devices: 40.4 us -> 29.7 us
  waiting for transfers between devices: 9.59 us -> 17.5 us
    ppermute x14, starting transfers between devices: 40.4 us -> 29.6 us  [exchange(): lax.ppermute(piece, 'qa', [(i, i ^ distance) for i in range(qa)])]
    ppermute x14, waiting for transfers between devices: 9.23 us -> 17.1 us  [exchange(): lax.ppermute(piece, 'qa', [(i, i ^ distance) for i in range(qa)])]
  transfers between devices with their start and end apart: 15 -> 15, of which waited for: 7 -> 9; matrix products, arithmetic and copies ran while one was open for 0% -> 0% of each run, Pallas kernels for 9% -> 9%
where the time goes in v4:
time: 62.7 us; the launch traced here: 62.5 us
  starting transfers between devices  29.7 us (47%)
  waiting for transfers between devices  17.5 us (28%)
  Pallas kernels  13.3 us (21%)
  local copies, waits for them, and re-layouts  1.88 us (3%)
    ppermute x14, starting transfers between devices, exchange(): lax.ppermute(piece, 'qa', [(i, i ^ distance) for i in range(qa)])  29.6 us
    ppermute x14, waiting for transfers between devices, exchange(): lax.ppermute(piece, 'qa', [(i, i ^ distance) for i in range(qa)])  17.1 us
    pallas_call x6, Pallas kernels, call(): pl.pallas_call(kernel, out_shape=out_shapes, in_specs=in_specs, out_specs...  13.3 us
    unnamed x4, local copies, waits for them, and re-layouts  1.88 us
  transfers between devices with their start and end apart: 15, of which 9 were waited for; matrix products, arithmetic and copies ran while one was open for 0% of the time, Pallas kernels for 9%

profile of v4, /device:TPU:0, one launch (start us, length us, event | category | flops | bytes accessed | tf_op | source)
XLA Modules:
  0.0 62.5 jit_solution(792522218252841785)
XLA Ops:
  0.0 1.2 %copy-done = f32[2,131072]{1,0:T(2,128)S(1)} copy-done((f32[2,131072]{1,0:T(2,128)S(1)}, f32[2,131072]{1,0:T(2,128)}, u32[]{:S(2)}) %copy-start) | copy-done | bytes 1048600
  1.2 0.1 split_state.1
  1.3 6.1 %collective-permute-start = (f32[256,128]{1,0:T(8,128)S(1)}, f32[256,128]{1,0:T(8,128)S(1)}, u32[]{:S(2)}, u32[]{:S(2)}) collective-permute-start(f32[256,128]{1,0:T(8,128)S(1)} %get-tuple-element.26), channel_id=1, source_target_pairs={{0,14},{2,12},{4,10},{6,8},{8,6},{10,4},{12,2},{14,0},{1,15},{3,13... | collective-permute-start | bytes 393224 | tf_op jit(solution)/shard_map/ppermute | solution.py:253
  7.4 0.2 collective-permute-start.1
  7.6 0.0 collective-permute-start.2
  7.6 1.9 %collective-permute-start.3 = (f32[256,128]{1,0:T(8,128)S(1)}, f32[256,128]{1,0:T(8,128)S(1)}, u32[]{:S(2)}, u32[]{:S(2)}) collective-permute-start(f32[256,128]{1,0:T(8,128)S(1)} %get-tuple-element.29), channel_id=1, source_target_pairs={{0,4},{2,6},{4,0},{6,2},{8,12},{10,14},{12,8},{14,10},{1,5},{3,7},... | collective-permute-start | bytes 393224 | tf_op jit(solution)/shard_map/ppermute | solution.py:253
  9.5 3.2 %collective-permute-start.4 = (f32[256,128]{1,0:T(8,128)S(1)}, f32[256,128]{1,0:T(8,128)S(1)}, u32[]{:S(2)}, u32[]{:S(2)}) collective-permute-start(f32[256,128]{1,0:T(8,128)S(1)} %get-tuple-element.30), channel_id=1, source_target_pairs={{0,10},{2,8},{4,14},{6,12},{8,2},{10,0},{12,6},{14,4},{1,11},{3,9}... | collective-permute-start | bytes 393224 | tf_op jit(solution)/shard_map/ppermute | solution.py:253
  12.7 0.0 collective-permute-done.refs_1_
  12.7 5.6 %collective-permute-start.5 = (f32[256,128]{1,0:T(8,128)S(1)}, f32[256,128]{1,0:T(8,128)S(1)}, u32[]{:S(2)}, u32[]{:S(2)}) collective-permute-start(f32[256,128]{1,0:T(8,128)S(1)} %get-tuple-element.31), channel_id=1, source_target_pairs={{0,8},{2,10},{4,12},{6,14},{8,0},{10,2},{12,4},{14,6},{1,9},{3,11}... | collective-permute-start | bytes 393224 | tf_op jit(solution)/shard_map/ppermute | solution.py:253
  18.3 1.5 %collective-permute-start.6 = (f32[256,128]{1,0:T(8,128)S(1)}, f32[256,128]{1,0:T(8,128)S(1)}, u32[]{:S(2)}, u32[]{:S(2)}) collective-permute-start(f32[256,128]{1,0:T(8,128)S(1)} %get-tuple-element.32), channel_id=1, source_target_pairs={{0,2},{2,0},{4,6},{6,4},{8,10},{10,8},{12,14},{14,12},{1,3},{3,1},... | collective-permute-start | bytes 393224 | tf_op jit(solution)/shard_map/ppermute | solution.py:253
  19.8 0.7 %copy-done.1 = s32[18]{0:T(128)S(1)} copy-done((s32[18]{0:T(128)S(1)}, s32[18]{0:T(128)}, u32[]{:S(2)}) %copy-start.1) | copy-done | bytes 96
  20.5 4.1 %prepare_gates.1 = (bf16[2,256,256]{2,1,0:T(8,128)(2,1)S(1)}, bf16[4,2,256,256]{3,2,1,0:T(8,128)(2,1)S(1)}, bf16[4,2,256,256]{3,2,1,0:T(8,128)(2,1)S(1)}, bf16[4,2,256,256]{3,2,1,0:T(8,128)(2,1)S(1)}) custom-call(s32[18]{0:T(128)S(1)} %copy-done.1, f32[18,2,2,128,128]{4,3,2,1,0:T(8,128)} %gates_ref.1), custom_call_target="tpu_custom_call" | custom-call | flops 1610612736 | bytes 4194304 | tf_op jit(solution)/shard_map/prepare_gates/pallas_call | solution.py:209
  24.6 3.2 %collective-permute-done.4.refs_5_ = f32[256,128]{1,0:T(8,128)S(1)} collective-permute-done((f32[256,128]{1,0:T(8,128)S(1)}, f32[256,128]{1,0:T(8,128)S(1)}, u32[]{:S(2)}, u32[]{:S(2)}) %collective-permute-start.4) | collective-permute-done | bytes 131104 | tf_op jit(solution)/shard_map/ppermute | solution.py:253
  27.8 1.8 %collective-permute-done.5.refs_6_ = f32[256,128]{1,0:T(8,128)S(1)} collective-permute-done((f32[256,128]{1,0:T(8,128)S(1)}, f32[256,128]{1,0:T(8,128)S(1)}, u32[]{:S(2)}, u32[]{:S(2)}) %collective-permute-start.5) | collective-permute-done | bytes 131104 | tf_op jit(solution)/shard_map/ppermute | solution.py:253
  29.7 2.8 %first_section.1 = (f32[2,4,2,16,128]{4,3,2,1,0:T(8,128)S(1)}, f32[2,4,2,16,128]{4,3,2,1,0:T(8,128)S(1)}, f32[2,4,2,16,128]{4,3,2,1,0:T(8,128)S(1)}, f32[2,4,2,1...) custom-call(f32[256,128]{1,0:T(8,128)S(1)} %get-tuple-element.25.ref, ...), custom_call_target="tpu_custom_call" | custom-call | flops 2013265920 | bytes 4194304 | tf_op jit(solution)/shard_map/first_section/pallas_call | solution.py:209
  32.5 2.5 %collective-permute-start.7 = (f32[2,4,2,16,128]{4,3,2,1,0:T(8,128)S(1)}, f32[2,4,2,16,128]{4,3,2,1,0:T(8,128)S(1)}, u32[]{:S(2)}, u32[]{:S(2)}) collective-permute-start(f32[2,4,2,16,128]{4,3,2,1,0:T(8,128)S(1)} %get-tuple-element.36), channel_id=1, source_target_pairs={{0,14},{2,12},{4,10},{6,8},{8,6},{10,4},{12,2},{14,0},{1,15},{3,13... | collective-permute-start | bytes 393224 | tf_op jit(solution)/shard_map/ppermute | solution.py:253
  35.0 1.4 %collective-permute-start.8 = (f32[2,4,2,16,128]{4,3,2,1,0:T(8,128)S(1)}, f32[2,4,2,16,128]{4,3,2,1,0:T(8,128)S(1)}, u32[]{:S(2)}, u32[]{:S(2)}) collective-permute-start(f32[2,4,2,16,128]{4,3,2,1,0:T(8,128)S(1)} %get-tuple-element.37), channel_id=1, source_target_pairs={{0,12},{2,14},{4,8},{6,10},{8,4},{10,6},{12,0},{14,2},{1,13},{3,15... | collective-permute-start | bytes 393224 | tf_op jit(solution)/shard_map/ppermute | solution.py:253
  36.3 3.0 %collective-permute-start.10 = (f32[2,4,2,16,128]{4,3,2,1,0:T(8,128)S(1)}, f32[2,4,2,16,128]{4,3,2,1,0:T(8,128)S(1)}, u32[]{:S(2)}, u32[]{:S(2)}) collective-permute-start(f32[2,4,2,16,128]{4,3,2,1,0:T(8,128)S(1)} %get-tuple-element.39), channel_id=1, source_target_pairs={{0,4},{2,6},{4,0},{6,2},{8,12},{10,14},{12,8},{14,10},{1,5},{3,7},... | collective-permute-start | bytes 393224 | tf_op jit(solution)/shard_map/ppermute | solution.py:253
  39.3 1.0 %collective-permute-start.11 = (f32[2,4,2,16,128]{4,3,2,1,0:T(8,128)S(1)}, f32[2,4,2,16,128]{4,3,2,1,0:T(8,128)S(1)}, u32[]{:S(2)}, u32[]{:S(2)}) collective-permute-start(f32[2,4,2,16,128]{4,3,2,1,0:T(8,128)S(1)} %get-tuple-element.40), channel_id=1, source_target_pairs={{0,10},{2,8},{4,14},{6,12},{8,2},{10,0},{12,6},{14,4},{1,11},{3,9}... | collective-permute-start | bytes 393224 | tf_op jit(solution)/shard_map/ppermute | solution.py:253
  40.3 1.1 %collective-permute-done.7.refs_1_ = f32[2,4,2,16,128]{4,3,2,1,0:T(8,128)S(1)} collective-permute-done((f32[2,4,2,16,128]{4,3,2,1,0:T(8,128)S(1)}, f32[2,4,2,16,128]{4,3,2,1,0:T(8,128)S(1)}, u32[]{:S(2)}, u32[]{:S(2)}) %collective-permute-start.7) | collective-permute-done | bytes 131104 | tf_op jit(solution)/shard_map/ppermute | solution.py:253
  41.4 1.7 %collective-permute-start.12 = (f32[2,4,2,16,128]{4,3,2,1,0:T(8,128)S(1)}, f32[2,4,2,16,128]{4,3,2,1,0:T(8,128)S(1)}, u32[]{:S(2)}, u32[]{:S(2)}) collective-permute-start(f32[2,4,2,16,128]{4,3,2,1,0:T(8,128)S(1)} %get-tuple-element.41), channel_id=1, source_target_pairs={{0,8},{2,10},{4,12},{6,14},{8,0},{10,2},{12,4},{14,6},{1,9},{3,11}... | collective-permute-start | bytes 393224 | tf_op jit(solution)/shard_map/ppermute | solution.py:253
  43.2 0.1 collective-permute-done.8.refs_2_
  43.3 1.5 %collective-permute-start.13 = (f32[2,4,2,16,128]{4,3,2,1,0:T(8,128)S(1)}, f32[2,4,2,16,128]{4,3,2,1,0:T(8,128)S(1)}, u32[]{:S(2)}, u32[]{:S(2)}) collective-permute-start(f32[2,4,2,16,128]{4,3,2,1,0:T(8,128)S(1)} %get-tuple-element.42), channel_id=1, source_target_pairs={{0,2},{2,0},{4,6},{6,4},{8,10},{10,8},{12,14},{14,12},{1,3},{3,1},... | collective-permute-start | bytes 393224 | tf_op jit(solution)/shard_map/ppermute | solution.py:253
  44.8 3.7 %collective-permute-done.9.refs_3_ = f32[2,4,2,16,128]{4,3,2,1,0:T(8,128)S(1)} collective-permute-done((f32[2,4,2,16,128]{4,3,2,1,0:T(8,128)S(1)}, f32[2,4,2,16,128]{4,3,2,1,0:T(8,128)S(1)}, u32[]{:S(2)}, u32[]{:S(2)}) %collective-permute-start.9) | collective-permute-done | bytes 131104 | tf_op jit(solution)/shard_map/ppermute | solution.py:253
  48.5 2.6 %collective-permute-done.10.refs_4_ = f32[2,4,2,16,128]{4,3,2,1,0:T(8,128)S(1)} collective-permute-done((f32[2,4,2,16,128]{4,3,2,1,0:T(8,128)S(1)}, f32[2,4,2,16,128]{4,3,2,1,0:T(8,128)S(1)}, u32[]{:S(2)}, u32[]{:S(2)}) %collective-permute-start.10) | collective-permute-done | bytes 131104 | tf_op jit(solution)/shard_map/ppermute | solution.py:253
  51.1 4.1 %collective-permute-done.11.refs_5_ = f32[2,4,2,16,128]{4,3,2,1,0:T(8,128)S(1)} collective-permute-done((f32[2,4,2,16,128]{4,3,2,1,0:T(8,128)S(1)}, f32[2,4,2,16,128]{4,3,2,1,0:T(8,128)S(1)}, u32[]{:S(2)}, u32[]{:S(2)}) %collective-permute-start.11) | collective-permute-done | bytes 131104 | tf_op jit(solution)/shard_map/ppermute | solution.py:253
  55.1 0.5 collective-permute-done.12.refs_6_
  55.6 1.5 %second_section_sent.1 = f32[2,512,128]{2,1,0:T(8,128)S(1)} custom-call(f32[2,4,2,16,128]{4,3,2,1,0:T(8,128)S(1)} %get-tuple-element.35.refs_0_, f32[2,4,2,16,128]{4,3,2,1,0:T(8,128)S(1)} %collective-permute-done.7.refs_1_, f32[2,4,2,16,128]{4,3,2,1,0:T(8,128)S(1)} %collective-permute-done.8.refs_2_, ...), custom_call_target="tpu_custom_call" | custom-call | flops 805306368 | bytes 4194304 | tf_op jit(solution)/shard_map/second_section_sent/pallas_call | solution.py:209
  57.1 0.1 collective-permute-start.14
  57.2 1.5 %second_section_kept.1.kept_ref = f32[2,512,128]{2,1,0:T(8,128)S(1)} custom-call(f32[2,4,2,16,128]{4,3,2,1,0:T(8,128)S(1)} %get-tuple-element.35.refs_0_, f32[2,4,2,16,128]{4,3,2,1,0:T(8,128)S(1)} %collective-permute-done.7.refs_1_, f32[2,4,2,16,128]{4,3,2,1,0:T(8,128)S(1)} %collective-permute-done.8.refs_2_, ...), custom_call_target="tpu_custom_call" | custom-call | flops 805306368 | bytes 4194304 | tf_op jit(solution)/shard_map/second_section_kept/pallas_call | solution.py:209
  58.8 0.4 collective-permute-done.14.came_ref
  59.1 3.3 %third_section.1 = f32[2048,128]{1,0:T(8,128)} custom-call(f32[2,512,128]{2,1,0:T(8,128)S(1)} %second_section_kept.1.kept_ref, f32[2,512,128]{2,1,0:T(8,128)S(1)} %collective-permute-done.14.came_ref, bf16[4,2,256,256]{3,2,1,0:T(8,128)(2,1)S(1)} %get-tuple-element.44.rows_ref), custom_call_target="tpu_custom_call" | custom-call | flops 1610612736 | bytes 4194304 | tf_op jit(solution)/shard_map/third_section/pallas_call | solution.py:209
  (8 shorter events, 0.0 us)
Async XLA Ops:
  0.0 1.2 %copy-start = (f32[2,131072]{1,0:T(2,128)S(1)}, f32[2,131072]{1,0:T(2,128)}, u32[]{:S(2)}) copy-start(f32[2,131072]{1,0:T(2,128)} %param.3) | copy-start | bytes 3145732
  1.3 11.4 %collective-permute-start = (f32[256,128]{1,0:T(8,128)S(1)}, f32[256,128]{1,0:T(8,128)S(1)}, u32[]{:S(2)}, u32[]{:S(2)}) collective-permute-start(f32[256,128]{1,0:T(8,128)S(1)} %get-tuple-element.26), channel_id=1, source_target_pairs={{0,14},{2,12},{4,10},{6,8},{8,6},{10,4},{12,2},{14,0},{1,15},{3,13... | collective-permute-start | bytes 393224 | tf_op jit(solution)/shard_map/ppermute | solution.py:253
  7.4 10.9 %collective-permute-start.1 = (f32[256,128]{1,0:T(8,128)S(1)}, f32[256,128]{1,0:T(8,128)S(1)}, u32[]{:S(2)}, u32[]{:S(2)}) collective-permute-start(f32[256,128]{1,0:T(8,128)S(1)} %get-tuple-element.27), channel_id=1, source_target_pairs={{0,12},{2,14},{4,8},{6,10},{8,4},{10,6},{12,0},{14,2},{1,13},{3,15... | collective-permute-start | bytes 393224 | tf_op jit(solution)/shard_map/ppermute | solution.py:253
  7.6 17.0 %collective-permute-start.2 = (f32[256,128]{1,0:T(8,128)S(1)}, f32[256,128]{1,0:T(8,128)S(1)}, u32[]{:S(2)}, u32[]{:S(2)}) collective-permute-start(f32[256,128]{1,0:T(8,128)S(1)} %get-tuple-element.28), channel_id=1, source_target_pairs={{0,6},{2,4},{4,2},{6,0},{8,14},{10,12},{12,10},{14,8},{1,7},{3,5},... | collective-permute-start | bytes 393224 | tf_op jit(solution)/shard_map/ppermute | solution.py:253
  7.6 17.0 %collective-permute-start.3 = (f32[256,128]{1,0:T(8,128)S(1)}, f32[256,128]{1,0:T(8,128)S(1)}, u32[]{:S(2)}, u32[]{:S(2)}) collective-permute-start(f32[256,128]{1,0:T(8,128)S(1)} %get-tuple-element.29), channel_id=1, source_target_pairs={{0,4},{2,6},{4,0},{6,2},{8,12},{10,14},{12,8},{14,10},{1,5},{3,7},... | collective-permute-start | bytes 393224 | tf_op jit(solution)/shard_map/ppermute | solution.py:253
  9.5 18.4 %collective-permute-start.4 = (f32[256,128]{1,0:T(8,128)S(1)}, f32[256,128]{1,0:T(8,128)S(1)}, u32[]{:S(2)}, u32[]{:S(2)}) collective-permute-start(f32[256,128]{1,0:T(8,128)S(1)} %get-tuple-element.30), channel_id=1, source_target_pairs={{0,10},{2,8},{4,14},{6,12},{8,2},{10,0},{12,6},{14,4},{1,11},{3,9}... | collective-permute-start | bytes 393224 | tf_op jit(solution)/shard_map/ppermute | solution.py:253
  12.7 17.0 %collective-permute-start.5 = (f32[256,128]{1,0:T(8,128)S(1)}, f32[256,128]{1,0:T(8,128)S(1)}, u32[]{:S(2)}, u32[]{:S(2)}) collective-permute-start(f32[256,128]{1,0:T(8,128)S(1)} %get-tuple-element.31), channel_id=1, source_target_pairs={{0,8},{2,10},{4,12},{6,14},{8,0},{10,2},{12,4},{14,6},{1,9},{3,11}... | collective-permute-start | bytes 393224 | tf_op jit(solution)/shard_map/ppermute | solution.py:253
  18.3 11.4 %collective-permute-start.6 = (f32[256,128]{1,0:T(8,128)S(1)}, f32[256,128]{1,0:T(8,128)S(1)}, u32[]{:S(2)}, u32[]{:S(2)}) collective-permute-start(f32[256,128]{1,0:T(8,128)S(1)} %get-tuple-element.32), channel_id=1, source_target_pairs={{0,2},{2,0},{4,6},{6,4},{8,10},{10,8},{12,14},{14,12},{1,3},{3,1},... | collective-permute-start | bytes 393224 | tf_op jit(solution)/shard_map/ppermute | solution.py:253
  19.8 0.7 %copy-start.1 = (s32[18]{0:T(128)S(1)}, s32[18]{0:T(128)}, u32[]{:S(2)}) copy-start(s32[18]{0:T(128)} %bits_ref.1) | copy-start | bytes 220
  32.5 9.0 %collective-permute-start.7 = (f32[2,4,2,16,128]{4,3,2,1,0:T(8,128)S(1)}, f32[2,4,2,16,128]{4,3,2,1,0:T(8,128)S(1)}, u32[]{:S(2)}, u32[]{:S(2)}) collective-permute-start(f32[2,4,2,16,128]{4,3,2,1,0:T(8,128)S(1)} %get-tuple-element.36), channel_id=1, source_target_pairs={{0,14},{2,12},{4,10},{6,8},{8,6},{10,4},{12,2},{14,0},{1,15},{3,13... | collective-permute-start | bytes 393224 | tf_op jit(solution)/shard_map/ppermute | solution.py:253
  35.0 8.3 %collective-permute-start.8 = (f32[2,4,2,16,128]{4,3,2,1,0:T(8,128)S(1)}, f32[2,4,2,16,128]{4,3,2,1,0:T(8,128)S(1)}, u32[]{:S(2)}, u32[]{:S(2)}) collective-permute-start(f32[2,4,2,16,128]{4,3,2,1,0:T(8,128)S(1)} %get-tuple-element.37), channel_id=1, source_target_pairs={{0,12},{2,14},{4,8},{6,10},{8,4},{10,6},{12,0},{14,2},{1,13},{3,15... | collective-permute-start | bytes 393224 | tf_op jit(solution)/shard_map/ppermute | solution.py:253
  36.3 12.2 %collective-permute-start.9 = (f32[2,4,2,16,128]{4,3,2,1,0:T(8,128)S(1)}, f32[2,4,2,16,128]{4,3,2,1,0:T(8,128)S(1)}, u32[]{:S(2)}, u32[]{:S(2)}) collective-permute-start(f32[2,4,2,16,128]{4,3,2,1,0:T(8,128)S(1)} %get-tuple-element.38), channel_id=1, source_target_pairs={{0,6},{2,4},{4,2},{6,0},{8,14},{10,12},{12,10},{14,8},{1,7},{3,5},... | collective-permute-start | bytes 393224 | tf_op jit(solution)/shard_map/ppermute | solution.py:253
  36.3 14.8 %collective-permute-start.10 = (f32[2,4,2,16,128]{4,3,2,1,0:T(8,128)S(1)}, f32[2,4,2,16,128]{4,3,2,1,0:T(8,128)S(1)}, u32[]{:S(2)}, u32[]{:S(2)}) collective-permute-start(f32[2,4,2,16,128]{4,3,2,1,0:T(8,128)S(1)} %get-tuple-element.39), channel_id=1, source_target_pairs={{0,4},{2,6},{4,0},{6,2},{8,12},{10,14},{12,8},{14,10},{1,5},{3,7},... | collective-permute-start | bytes 393224 | tf_op jit(solution)/shard_map/ppermute | solution.py:253
  39.3 15.9 %collective-permute-start.11 = (f32[2,4,2,16,128]{4,3,2,1,0:T(8,128)S(1)}, f32[2,4,2,16,128]{4,3,2,1,0:T(8,128)S(1)}, u32[]{:S(2)}, u32[]{:S(2)}) collective-permute-start(f32[2,4,2,16,128]{4,3,2,1,0:T(8,128)S(1)} %get-tuple-element.40), channel_id=1, source_target_pairs={{0,10},{2,8},{4,14},{6,12},{8,2},{10,0},{12,6},{14,4},{1,11},{3,9}... | collective-permute-start | bytes 393224 | tf_op jit(solution)/shard_map/ppermute | solution.py:253
  41.4 14.2 %collective-permute-start.12 = (f32[2,4,2,16,128]{4,3,2,1,0:T(8,128)S(1)}, f32[2,4,2,16,128]{4,3,2,1,0:T(8,128)S(1)}, u32[]{:S(2)}, u32[]{:S(2)}) collective-permute-start(f32[2,4,2,16,128]{4,3,2,1,0:T(8,128)S(1)} %get-tuple-element.41), channel_id=1, source_target_pairs={{0,8},{2,10},{4,12},{6,14},{8,0},{10,2},{12,4},{14,6},{1,9},{3,11}... | collective-permute-start | bytes 393224 | tf_op jit(solution)/shard_map/ppermute | solution.py:253
  43.3 12.3 %collective-permute-start.13 = (f32[2,4,2,16,128]{4,3,2,1,0:T(8,128)S(1)}, f32[2,4,2,16,128]{4,3,2,1,0:T(8,128)S(1)}, u32[]{:S(2)}, u32[]{:S(2)}) collective-permute-start(f32[2,4,2,16,128]{4,3,2,1,0:T(8,128)S(1)} %get-tuple-element.42), channel_id=1, source_target_pairs={{0,2},{2,0},{4,6},{6,4},{8,10},{10,8},{12,14},{14,12},{1,3},{3,1},... | collective-permute-start | bytes 393224 | tf_op jit(solution)/shard_map/ppermute | solution.py:253
  57.1 2.0 %collective-permute-start.14 = (f32[2,512,128]{2,1,0:T(8,128)S(1)}, f32[2,512,128]{2,1,0:T(8,128)S(1)}, u32[]{:S(2)}, u32[]{:S(2)}) collective-permute-start(f32[2,512,128]{2,1,0:T(8,128)S(1)} %second_section_sent.1), channel_id=1, source_target_pairs={{0,1},{1,0},{2,3},{3,2},{4,5},{5,4},{6,7},{7,6},{8,9},{9,8},{10,11... | collective-permute-start | bytes 1572872 | tf_op jit(solution)/shard_map/ppermute | solution.py:296

commit v5 on v4

v5 whole, which is shorter than its diff:
```python
import functools

import jax
import jax.numpy as jnp
from jax import lax
from jax.experimental import pallas as pl
from jax.experimental.layout import Layout, with_layout_constraint
from jax.experimental.pallas import tpu as pltpu
from jax.sharding import PartitionSpec as P

F32 = jnp.float32
BF16 = jnp.bfloat16
VMEM_LIMIT = 14 * 1024 * 1024
LARGE_VMEM = 48 * 1024 * 1024


def window_offsets(span, gate_bits):
    return [0, span, gate_bits, span - 1, gate_bits + 1, span - 2]


def plan_gates(local_bits, gate_bits):
    outer = window_offsets(local_bits - gate_bits, gate_bits)
    inner = window_offsets(local_bits - gate_bits - 1, gate_bits)
    low, sections = [], []
    for number, offsets in enumerate((outer, inner, outer)):
        section = []
        for index, offset in enumerate(offsets):
            gate = 6 * number + index
            if offset == 0:
                low.append(gate)
            elif section and section[-1][0] == offset:
                section[-1][1].append(gate)
            else:
                section.append((offset, [gate]))
        sections.append(section)
    return low, sections


def join_windows(section, gate_bits):
    stages = []
    for offset, gates in section:
        if stages:
            offsets = [o for o, _ in stages[-1]] + [offset]
            if max(offsets) - min(offsets) <= 1:
                stages[-1].append((offset, gates))
                continue
        stages.append([(offset, gates)])
    return [
        (min(o for o, _ in parts), gate_bits + (len(parts) > 1), parts)
        for parts in stages
    ]


def interleaved(stage):
    base, _, parts = stage
    return parts[0][0] != base


def exact_dot(a, b):
    return lax.dot_general(
        a, b, (((1,), (0,)), ((), ())), precision=lax.Precision.HIGHEST, preferred_element_type=F32
    )


def split(x):
    high = x.astype(BF16)
    return high, (x - high.astype(F32)).astype(BF16)


def bf_dot(a, b):
    return jnp.dot(a, b, preferred_element_type=F32)


def block(real, imag):
    return jnp.concatenate(
        [jnp.concatenate([real, -imag], axis=1), jnp.concatenate([imag, real], axis=1)], axis=0
    )


def prepare_kernel(low, sections, bits_ref, gates_ref, low_ref, *refs):
    *targets, held, wide, sems = refs
    copies = []
    for gate in range(held.shape[0]):
        copy = pltpu.make_async_copy(gates_ref.at[gate, bits_ref[gate]], held.at[gate], sems.at[gate])
        copy.start()
        copies.append(copy)
    for copy in copies:
        copy.wait()
    dim = held.shape[-1]

    def product(gates):
        real, imag = held[gates[0], 0], held[gates[0], 1]
        for gate in gates[1:]:
            column = exact_dot(block(held[gate, 0], held[gate, 1]), jnp.concatenate([real, imag], axis=0))
            real, imag = column[:dim], column[dim:]
        return real, imag

    def joined(base, parts):
        wide[...] = jnp.zeros_like(wide)
        for index, (offset, gates) in enumerate(parts):
            real, imag = product(gates)
            for t in range(2):
                at = pl.ds(t * dim, dim) if offset == base else pl.ds(t, dim, stride=2)
                if index == 0:
                    wide[0, t, at, :] = real
                    wide[1, t, at, :] = imag
                else:
                    x = jnp.concatenate(
                        [jnp.concatenate([wide[p, c, at, :] for c in range(2)], axis=1) for p in range(2)], axis=0
                    )
                    y = exact_dot(block(real, imag), x)
                    for p in range(2):
                        for c in range(2):
                            wide[p, c, at, :] = y[p * dim : (p + 1) * dim, c * dim : (c + 1) * dim]
        return [jnp.concatenate([wide[p, 0], wide[p, 1]], axis=1) for p in range(2)]

    targets = iter(targets)
    for section in sections:
        for base, _, parts in section:
            target = next(targets)
            target[0], target[1] = split(block(*(joined(base, parts) if len(parts) > 1 else product(parts[0][1]))))
    real, imag = product(low)
    low_ref[0], low_ref[1] = split(block(real.T, -imag.T))


def distances_of(count):
    half = count // 2
    far, near = list(range(count - 1, half - 1, -1)), list(range(half - 1, 0, -1))
    order = [0]
    while far or near:
        order += far[:2] + near[:2]
        far, near = far[2:], near[2:]
    return order


def partner(distance):
    return jnp.bitwise_xor(lax.axis_index("qa"), distance)


def split_kernel(x_ref, *outs):
    for distance, out_ref in zip(distances_of(len(outs)), outs):
        out_ref[...] = x_ref[partner(distance)]


def apply_stage(weights_ref, starts, load, store):
    dim = weights_ref.shape[-1] // 2
    high_w, rest_w = weights_ref[0], weights_ref[1]
    for pair in range(0, len(starts), 2):
        group = starts[pair : pair + 2]
        x = jnp.concatenate(
            [jnp.concatenate([load(part, start) for start in group], axis=1) for part in range(2)], axis=0
        )
        high, rest = split(x)
        y = bf_dot(high_w, rest) + bf_dot(rest_w, high) + bf_dot(high_w, high)
        lanes = y.shape[1] // len(group)
        for part in range(2):
            for place, start in enumerate(group):
                store(part, start, y[part * dim : (part + 1) * dim, place * lanes : (place + 1) * lanes])


def stage_starts(stage, lane_bits, rows):
    base, bits, _ = stage
    dim, stride = 2**bits, 2 ** (base - lane_bits)
    return dim, stride, [h * dim * stride + l for h in range(rows // (dim * stride)) for l in range(stride)]


def run_stage(stage, weights_ref, lane_bits, source, target=None, store=None):
    dim, stride, starts = stage_starts(stage, lane_bits, source.shape[1])

    def load(part, start):
        if not interleaved(stage):
            return source[part, pl.ds(start, dim, stride=stride), :]
        half = dim // 2
        return jnp.concatenate(
            [source[part, pl.ds(start + t * stride, half, stride=2 * stride), :] for t in range(2)], axis=0
        )

    def plain(part, start, value):
        target[part, pl.ds(start, dim, stride=stride), :] = value

    apply_stage(weights_ref, starts, load, store or plain)


def run_top_stage(stage, weights_ref, lane_bits, source, halves):
    dim, stride, starts = stage_starts(stage, lane_bits, source.shape[1])

    def store(part, start, value):
        for t in range(2):
            halves[t][part, pl.ds(start, dim // 2, stride=stride), :] = value[t * dim // 2 : (t + 1) * dim // 2]

    apply_stage(weights_ref, starts, lambda part, start: source[part, pl.ds(start, dim, stride=stride), :], store)


def run_halves(stages, weights, lane_bits, halves, spares, last_store=None):
    for index, (stage, weights_ref) in enumerate(zip(stages, weights)):
        for t in range(2):
            store = None
            if last_store is not None and index == len(stages) - 1:
                store = functools.partial(last_store, t)
            run_stage(stage, weights_ref, lane_bits, halves[t], spares[t], store)
        halves, spares = spares, halves
    return halves


def first_kernel(stages, lane_bits, count, *refs):
    blocks, refs = refs[:count], refs[count:]
    low_ref, weights, refs = refs[0], refs[1 : 1 + len(stages)], refs[1 + len(stages) :]
    outs, (whole, *halves) = refs[:count], refs[count:]
    lanes = whole.shape[2]
    for distance, block_ref in zip(distances_of(count), blocks):
        size = block_ref.shape[0] // 2
        start = pl.multiple_of(partner(distance) * size, size)
        real = block_ref[pl.ds(0, size, stride=2), :]
        imag = block_ref[pl.ds(1, size, stride=2), :]
        high, rest = split(jnp.concatenate([real, imag], axis=1))
        y = bf_dot(rest, low_ref[0]) + bf_dot(high, low_ref[1]) + bf_dot(high, low_ref[0])
        whole[0, pl.ds(start, size), :] = y[:, :lanes]
        whole[1, pl.ds(start, size), :] = y[:, lanes:]
    run_top_stage(stages[0], weights[0], lane_bits, whole, halves[:2])
    done = run_halves(stages[1:], weights[1:], lane_bits, halves[:2], halves[2:])
    tops, mids, _, inner, _ = outs[0].shape
    for top in range(tops):
        for distance, out_ref in zip(distances_of(count), outs):
            dest = partner(distance)
            for mid in range(mids):
                start = pl.multiple_of((mid * count + dest) * inner, inner)
                for part in range(2):
                    out_ref[top, mid, part] = done[top][part, pl.ds(start, inner), :]


def second_kernel(stages, lane_bits, count, stays, *refs):
    blocks, weights, refs = refs[:count], refs[count : count + len(stages)], refs[count + len(stages) :]
    out_ref, one, two = refs
    core = lax.axis_index("qb")
    top = core if stays else 1 - core
    for distance, block_ref in zip(distances_of(count), blocks):
        source = partner(distance)
        _, mids, _, inner, _ = block_ref.shape
        for mid in range(mids):
            start = pl.multiple_of((mid * count + source) * inner, inner)
            for part in range(2):
                one[part, pl.ds(start, inner), :] = block_ref[top, mid, part]
    for index, (stage, weights_ref) in enumerate(zip(stages, weights)):
        run_stage(stage, weights_ref, lane_bits, one, out_ref if index == len(stages) - 1 else two)
        one, two = two, one


def third_kernel(stages, lane_bits, kept_ref, came_ref, *refs):
    weights, (out_ref, whole, *halves, sems) = refs[: len(stages)], refs[len(stages) :]
    results = halves[4:]
    half = kept_ref.shape[1]
    core = lax.axis_index("qb")
    whole[:, pl.ds(pl.multiple_of(core * half, half), half), :] = kept_ref[...]
    whole[:, pl.ds(pl.multiple_of((1 - core) * half, half), half), :] = came_ref[...]
    run_top_stage(stages[0], weights[0], lane_bits, whole, halves[:2])
    done = run_halves(stages[1:-1], weights[1:-1], lane_bits, halves[:2], halves[2:4])
    copies = []
    for t in range(2):
        dim, stride, _ = stage_starts(stages[-1], lane_bits, half)

        def store(part, start, value, t=t):
            results[t][pl.ds(2 * start + part, dim, stride=2 * stride), :] = value

        run_stage(stages[-1], weights[-1], lane_bits, done[t], store=store)
        copies.append(pltpu.make_async_copy(results[t], out_ref.at[pl.ds(t * 2 * half, 2 * half)], sems.at[t]))
        copies[-1].start()
    for copy in copies:
        copy.wait()


def call(kernel, name, out_shapes, in_specs, scratch, matmuls, *operands, limit=VMEM_LIMIT, out_spec=None):
    many = isinstance(out_shapes, tuple)
    vmem = out_spec or pl.BlockSpec(memory_space=pltpu.VMEM)
    return pl.pallas_call(
        kernel,
        out_shape=out_shapes,
        in_specs=in_specs,
        out_specs=(vmem,) * len(out_shapes) if many else vmem,
        scratch_shapes=scratch,
        compiler_params=pltpu.CompilerParams(vmem_limit_bytes=limit),
        cost_estimate=pl.CostEstimate(
            flops=int(matmuls * 3 * 2 * 256 * 256 * 1024), bytes_accessed=4 * 2**20, transcendentals=0
        ),
        name=name,
    )(*operands)


def per_device(state, gate_terms, path_bits):
    amps_local = state.shape[1]
    local_bits = amps_local.bit_length() - 1
    dim = gate_terms.shape[-1]
    gate_bits = dim.bit_length() - 1
    lanes, lane_bits = dim, gate_bits
    rows = amps_local // lanes
    qa = lax.axis_size("qa")
    qb = lax.axis_size("qb")
    low, sections = plan_gates(local_bits, gate_bits)
    sections = [join_windows(section, gate_bits) for section in sections]
    order = 2 * dim
    vmem = pl.BlockSpec(memory_space=pltpu.VMEM)
    hbm = pl.BlockSpec(memory_space=pltpu.HBM)
    shape = jax.ShapeDtypeStruct

    state = with_layout_constraint(state.reshape(2, rows, lanes), Layout(major_to_minor=(1, 0, 2)))
    state = state.swapaxes(0, 1).reshape(qa, 2 * rows // qa, lanes)
    blocks = call(
        split_kernel,
        "split_state",
        (shape((2 * rows // qa, lanes), F32),) * qa,
        [vmem],
        [],
        0,
        state,
    )

    def exchange(blocks):
        came = [blocks[0]]
        for distance, piece in zip(distances_of(qa)[1:], blocks[1:]):
            came.append(lax.ppermute(piece, "qa", [(i, i ^ distance) for i in range(qa)]))
        return came

    blocks = exchange(blocks)
    low_w, *weights = call(
        functools.partial(prepare_kernel, low, sections),
        "prepare_gates",
        (shape((2, order, order), BF16),)
        + tuple(shape((2, 2 * 2**bits, 2 * 2**bits), BF16) for section in sections for _, bits, _ in section),
        [pl.BlockSpec(memory_space=pltpu.SMEM), hbm],
        [
            pltpu.VMEM((gate_terms.shape[0], 2, dim, dim), F32),
            pltpu.VMEM((2, 2, 2 * dim, dim), F32),
            pltpu.SemaphoreType.DMA((gate_terms.shape[0],)),
        ],
        8,
        path_bits,
        gate_terms,
        limit=LARGE_VMEM,
    )
    counts = [len(section) for section in sections]
    weights = [weights[: counts[0]], weights[counts[0] : counts[0] + counts[1]], weights[counts[0] + counts[1] :]]
    inner = rows // (qa * qa)
    whole = pltpu.VMEM((2, rows, lanes), F32)
    half = pltpu.VMEM((2, rows // 2, lanes), F32)
    blocks = call(
        functools.partial(first_kernel, sections[0], lane_bits, qa),
        "first_section",
        (shape((qb, qa // qb, 2, inner, lanes), F32),) * qa,
        [vmem] * (qa + 1 + counts[0]),
        [whole] + [half] * 4,
        5,
        *blocks,
        low_w,
        *weights[0],
    )
    blocks = exchange(blocks)
    halves = []
    for stays in (False, True):
        halves.append(
            call(
                functools.partial(second_kernel, sections[1], lane_bits, qa, stays),
                "second_section_kept" if stays else "second_section_sent",
                shape((2, rows // qb, lanes), F32),
                [vmem] * (qa + counts[1]),
                [half] * 2,
                1.5,
                *blocks,
                *weights[1],
            )
        )
        if not stays:
            came = lax.ppermute(halves[0], "qb", [(i, 1 - i) for i in range(qb)])
    final = call(
        functools.partial(third_kernel, sections[2], lane_bits),
        "third_section",
        shape((2 * rows, lanes), F32),
        [vmem] * (2 + counts[2]),
        [whole] + [half] * 4 + [pltpu.VMEM((rows, lanes), F32)] * 2 + [pltpu.SemaphoreType.DMA((2,))],
        4,
        halves[1],
        came,
        *weights[2],
        out_spec=hbm,
    )
    return final.reshape(rows, 2, lanes).swapaxes(0, 1).reshape(2, amps_local)


def solution(mesh):
    return jax.shard_map(
        per_device,
        mesh=mesh,
        in_specs=(P(None, ("paths", "qa", "qb")), P(), P("paths")),
        out_specs=P(None, ("paths", "qa", "qb")),
        check_vma=False,
    )
```

time: 62.7 us -> 62.2 us (level)
  waiting for transfers between devices: 17.5 us -> 13.9 us
  Pallas kernels: 13.3 us -> 15.4 us
  starting transfers between devices: 29.7 us -> 30.8 us
    ppermute x14, waiting for transfers between devices: 17.1 us -> 13 us  [exchange(): lax.ppermute(piece, 'qa', [(i, i ^ distance) for i in range(qa)])]
    pallas_call x6, Pallas kernels: 13.3 us -> 15.4 us  [call(): pl.pallas_call(kernel, out_shape=out_shapes, in_specs=in_specs, out_specs...]
    ppermute x14, starting transfers between devices: 29.6 us -> 30.7 us  [exchange(): lax.ppermute(piece, 'qa', [(i, i ^ distance) for i in range(qa)])]
  transfers between devices with their start and end apart: 15 -> 15, of which waited for: 9 -> 9; matrix products, arithmetic and copies ran while one was open for 0% -> 0% of each run, Pallas kernels for 9% -> 13%
where the time goes in v5:
time: 62.2 us; the launch traced here: 62 us
  starting transfers between devices  30.8 us (50%)
  Pallas kernels  15.4 us (25%)
  waiting for transfers between devices  13.9 us (22%)
  local copies, waits for them, and re-layouts  1.88 us (3%)
    ppermute x14, starting transfers between devices, exchange(): lax.ppermute(piece, 'qa', [(i, i ^ distance) for i in range(qa)])  30.7 us
    pallas_call x6, Pallas kernels, call(): pl.pallas_call(kernel, out_shape=out_shapes, in_specs=in_specs, out_specs...  15.4 us
    ppermute x14, waiting for transfers between devices, exchange(): lax.ppermute(piece, 'qa', [(i, i ^ distance) for i in range(qa)])  13 us
    unnamed x4, local copies, waits for them, and re-layouts  1.88 us
  transfers between devices with their start and end apart: 15, of which 9 were waited for; matrix products, arithmetic and copies ran while one was open for 0% of the time, Pallas kernels for 13%

profile of v5, /device:TPU:0, one launch (start us, length us, event | category | flops | bytes accessed | tf_op | source)
XLA Modules:
  0.0 62.0 jit_solution(948246678612869598)
XLA Ops:
  0.0 1.2 %copy-done = f32[2,131072]{1,0:T(2,128)S(1)} copy-done((f32[2,131072]{1,0:T(2,128)S(1)}, f32[2,131072]{1,0:T(2,128)}, u32[]{:S(2)}) %copy-start) | copy-done | bytes 1048600
  1.2 0.1 split_state.1
  1.3 6.1 %collective-permute-start = (f32[256,128]{1,0:T(8,128)S(1)}, f32[256,128]{1,0:T(8,128)S(1)}, u32[]{:S(2)}, u32[]{:S(2)}) collective-permute-start(f32[256,128]{1,0:T(8,128)S(1)} %get-tuple-element.31), channel_id=1, source_target_pairs={{0,14},{2,12},{4,10},{6,8},{8,6},{10,4},{12,2},{14,0},{1,15},{3,13... | collective-permute-start | bytes 393224 | tf_op jit(solution)/shard_map/ppermute | solution.py:319
  7.4 0.2 collective-permute-start.1
  7.6 0.0 collective-permute-start.2
  7.6 1.9 %collective-permute-start.3 = (f32[256,128]{1,0:T(8,128)S(1)}, f32[256,128]{1,0:T(8,128)S(1)}, u32[]{:S(2)}, u32[]{:S(2)}) collective-permute-start(f32[256,128]{1,0:T(8,128)S(1)} %get-tuple-element.34), channel_id=1, source_target_pairs={{0,4},{2,6},{4,0},{6,2},{8,12},{10,14},{12,8},{14,10},{1,5},{3,7},... | collective-permute-start | bytes 393224 | tf_op jit(solution)/shard_map/ppermute | solution.py:319
  9.5 3.2 %collective-permute-start.4 = (f32[256,128]{1,0:T(8,128)S(1)}, f32[256,128]{1,0:T(8,128)S(1)}, u32[]{:S(2)}, u32[]{:S(2)}) collective-permute-start(f32[256,128]{1,0:T(8,128)S(1)} %get-tuple-element.35), channel_id=1, source_target_pairs={{0,10},{2,8},{4,14},{6,12},{8,2},{10,0},{12,6},{14,4},{1,11},{3,9}... | collective-permute-start | bytes 393224 | tf_op jit(solution)/shard_map/ppermute | solution.py:319
  12.7 0.0 collective-permute-done.refs_1_
  12.7 5.6 %collective-permute-start.5 = (f32[256,128]{1,0:T(8,128)S(1)}, f32[256,128]{1,0:T(8,128)S(1)}, u32[]{:S(2)}, u32[]{:S(2)}) collective-permute-start(f32[256,128]{1,0:T(8,128)S(1)} %get-tuple-element.36), channel_id=1, source_target_pairs={{0,8},{2,10},{4,12},{6,14},{8,0},{10,2},{12,4},{14,6},{1,9},{3,11}... | collective-permute-start | bytes 393224 | tf_op jit(solution)/shard_map/ppermute | solution.py:319
  18.3 1.5 %collective-permute-start.6 = (f32[256,128]{1,0:T(8,128)S(1)}, f32[256,128]{1,0:T(8,128)S(1)}, u32[]{:S(2)}, u32[]{:S(2)}) collective-permute-start(f32[256,128]{1,0:T(8,128)S(1)} %get-tuple-element.37), channel_id=1, source_target_pairs={{0,2},{2,0},{4,6},{6,4},{8,10},{10,8},{12,14},{14,12},{1,3},{3,1},... | collective-permute-start | bytes 393224 | tf_op jit(solution)/shard_map/ppermute | solution.py:319
  19.8 0.7 %copy-done.1 = s32[18]{0:T(128)S(1)} copy-done((s32[18]{0:T(128)S(1)}, s32[18]{0:T(128)}, u32[]{:S(2)}) %copy-start.1) | copy-done | bytes 96
  20.5 7.1 %prepare_gates.1 = (bf16[2,256,256]{2,1,0:T(8,128)(2,1)S(1)}, bf16[2,256,256]{2,1,0:T(8,128)(2,1)S(1)}, bf16[2,256,256]{2,1,0:T(8,128)(2,1)S(1)}, bf16[2,512,512...) custom-call(s32[18]{0:T(128)S(1)} %copy-done.1, ...), custom_call_target="tpu_custom_call" | custom-call | flops 3221225472 | bytes 4194304 | tf_op jit(solution)/shard_map/prepare_gates/pallas_call | solution.py:274
  27.7 0.2 collective-permute-done.4.refs_5_
  27.8 1.8 %collective-permute-done.5.refs_6_ = f32[256,128]{1,0:T(8,128)S(1)} collective-permute-done((f32[256,128]{1,0:T(8,128)S(1)}, f32[256,128]{1,0:T(8,128)S(1)}, u32[]{:S(2)}, u32[]{:S(2)}) %collective-permute-start.5) | collective-permute-done | bytes 131104 | tf_op jit(solution)/shard_map/ppermute | solution.py:319
  29.7 2.8 %first_section.1 = (f32[2,4,2,16,128]{4,3,2,1,0:T(8,128)S(1)}, f32[2,4,2,16,128]{4,3,2,1,0:T(8,128)S(1)}, f32[2,4,2,16,128]{4,3,2,1,0:T(8,128)S(1)}, f32[2,4,2,1...) custom-call(f32[256,128]{1,0:T(8,128)S(1)} %get-tuple-element.30.ref, ...), custom_call_target="tpu_custom_call" | custom-call | flops 2013265920 | bytes 4194304 | tf_op jit(solution)/shard_map/first_section/pallas_call | solution.py:274
  32.5 2.5 %collective-permute-start.7 = (f32[2,4,2,16,128]{4,3,2,1,0:T(8,128)S(1)}, f32[2,4,2,16,128]{4,3,2,1,0:T(8,128)S(1)}, u32[]{:S(2)}, u32[]{:S(2)}) collective-permute-start(f32[2,4,2,16,128]{4,3,2,1,0:T(8,128)S(1)} %get-tuple-element.43), channel_id=1, source_target_pairs={{0,14},{2,12},{4,10},{6,8},{8,6},{10,4},{12,2},{14,0},{1,15},{3,13... | collective-permute-start | bytes 393224 | tf_op jit(solution)/shard_map/ppermute | solution.py:319
  35.0 1.4 %collective-permute-start.8 = (f32[2,4,2,16,128]{4,3,2,1,0:T(8,128)S(1)}, f32[2,4,2,16,128]{4,3,2,1,0:T(8,128)S(1)}, u32[]{:S(2)}, u32[]{:S(2)}) collective-permute-start(f32[2,4,2,16,128]{4,3,2,1,0:T(8,128)S(1)} %get-tuple-element.44), channel_id=1, source_target_pairs={{0,12},{2,14},{4,8},{6,10},{8,4},{10,6},{12,0},{14,2},{1,13},{3,15... | collective-permute-start | bytes 393224 | tf_op jit(solution)/shard_map/ppermute | solution.py:319
  36.4 3.0 %collective-permute-start.10 = (f32[2,4,2,16,128]{4,3,2,1,0:T(8,128)S(1)}, f32[2,4,2,16,128]{4,3,2,1,0:T(8,128)S(1)}, u32[]{:S(2)}, u32[]{:S(2)}) collective-permute-start(f32[2,4,2,16,128]{4,3,2,1,0:T(8,128)S(1)} %get-tuple-element.46), channel_id=1, source_target_pairs={{0,4},{2,6},{4,0},{6,2},{8,12},{10,14},{12,8},{14,10},{1,5},{3,7},... | collective-permute-start | bytes 393224 | tf_op jit(solution)/shard_map/ppermute | solution.py:319
  39.4 1.0 %collective-permute-start.11 = (f32[2,4,2,16,128]{4,3,2,1,0:T(8,128)S(1)}, f32[2,4,2,16,128]{4,3,2,1,0:T(8,128)S(1)}, u32[]{:S(2)}, u32[]{:S(2)}) collective-permute-start(f32[2,4,2,16,128]{4,3,2,1,0:T(8,128)S(1)} %get-tuple-element.47), channel_id=1, source_target_pairs={{0,10},{2,8},{4,14},{6,12},{8,2},{10,0},{12,6},{14,4},{1,11},{3,9}... | collective-permute-start | bytes 393224 | tf_op jit(solution)/shard_map/ppermute | solution.py:319
  40.4 1.1 %collective-permute-done.7.refs_1_ = f32[2,4,2,16,128]{4,3,2,1,0:T(8,128)S(1)} collective-permute-done((f32[2,4,2,16,128]{4,3,2,1,0:T(8,128)S(1)}, f32[2,4,2,16,128]{4,3,2,1,0:T(8,128)S(1)}, u32[]{:S(2)}, u32[]{:S(2)}) %collective-permute-start.7) | collective-permute-done | bytes 131104 | tf_op jit(solution)/shard_map/ppermute | solution.py:319
  41.5 1.8 %collective-permute-start.12 = (f32[2,4,2,16,128]{4,3,2,1,0:T(8,128)S(1)}, f32[2,4,2,16,128]{4,3,2,1,0:T(8,128)S(1)}, u32[]{:S(2)}, u32[]{:S(2)}) collective-permute-start(f32[2,4,2,16,128]{4,3,2,1,0:T(8,128)S(1)} %get-tuple-element.48), channel_id=1, source_target_pairs={{0,8},{2,10},{4,12},{6,14},{8,0},{10,2},{12,4},{14,6},{1,9},{3,11}... | collective-permute-start | bytes 393224 | tf_op jit(solution)/shard_map/ppermute | solution.py:319
  43.3 0.1 collective-permute-done.8.refs_2_
  43.4 2.5 %collective-permute-start.13 = (f32[2,4,2,16,128]{4,3,2,1,0:T(8,128)S(1)}, f32[2,4,2,16,128]{4,3,2,1,0:T(8,128)S(1)}, u32[]{:S(2)}, u32[]{:S(2)}) collective-permute-start(f32[2,4,2,16,128]{4,3,2,1,0:T(8,128)S(1)} %get-tuple-element.49), channel_id=1, source_target_pairs={{0,2},{2,0},{4,6},{6,4},{8,10},{10,8},{12,14},{14,12},{1,3},{3,1},... | collective-permute-start | bytes 393224 | tf_op jit(solution)/shard_map/ppermute | solution.py:319
  45.9 2.7 %collective-permute-done.9.refs_3_ = f32[2,4,2,16,128]{4,3,2,1,0:T(8,128)S(1)} collective-permute-done((f32[2,4,2,16,128]{4,3,2,1,0:T(8,128)S(1)}, f32[2,4,2,16,128]{4,3,2,1,0:T(8,128)S(1)}, u32[]{:S(2)}, u32[]{:S(2)}) %collective-permute-start.9) | collective-permute-done | bytes 131104 | tf_op jit(solution)/shard_map/ppermute | solution.py:319
  48.6 2.6 %collective-permute-done.10.refs_4_ = f32[2,4,2,16,128]{4,3,2,1,0:T(8,128)S(1)} collective-permute-done((f32[2,4,2,16,128]{4,3,2,1,0:T(8,128)S(1)}, f32[2,4,2,16,128]{4,3,2,1,0:T(8,128)S(1)}, u32[]{:S(2)}, u32[]{:S(2)}) %collective-permute-start.10) | collective-permute-done | bytes 131104 | tf_op jit(solution)/shard_map/ppermute | solution.py:319
  51.2 4.1 %collective-permute-done.11.refs_5_ = f32[2,4,2,16,128]{4,3,2,1,0:T(8,128)S(1)} collective-permute-done((f32[2,4,2,16,128]{4,3,2,1,0:T(8,128)S(1)}, f32[2,4,2,16,128]{4,3,2,1,0:T(8,128)S(1)}, u32[]{:S(2)}, u32[]{:S(2)}) %collective-permute-start.11) | collective-permute-done | bytes 131104 | tf_op jit(solution)/shard_map/ppermute | solution.py:319
  55.2 0.5 collective-permute-done.12.refs_6_
  55.7 1.0 %second_section_sent.1 = f32[2,512,128]{2,1,0:T(8,128)S(1)} custom-call(f32[2,4,2,16,128]{4,3,2,1,0:T(8,128)S(1)} %get-tuple-element.42.refs_0_, f32[2,4,2,16,128]{4,3,2,1,0:T(8,128)S(1)} %collective-permute-done.7.refs_1_, f32[2,4,2,16,128]{4,3,2,1,0:T(8,128)S(1)} %collective-permute-done.8.refs_2_, ...), custom_call_target="tpu_custom_call" | custom-call | flops 603979776 | bytes 4194304 | tf_op jit(solution)/shard_map/second_section_sent/pallas_call | solution.py:274
  56.7 0.1 collective-permute-start.14
  56.8 1.0 %second_section_kept.1.kept_ref = f32[2,512,128]{2,1,0:T(8,128)S(1)} custom-call(f32[2,4,2,16,128]{4,3,2,1,0:T(8,128)S(1)} %get-tuple-element.42.refs_0_, f32[2,4,2,16,128]{4,3,2,1,0:T(8,128)S(1)} %collective-permute-done.7.refs_1_, f32[2,4,2,16,128]{4,3,2,1,0:T(8,128)S(1)} %collective-permute-done.8.refs_2_, ...), custom_call_target="tpu_custom_call" | custom-call | flops 603979776 | bytes 4194304 | tf_op jit(solution)/shard_map/second_section_kept/pallas_call | solution.py:274
  57.8 0.9 %collective-permute-done.14.came_ref = f32[2,512,128]{2,1,0:T(8,128)S(1)} collective-permute-done((f32[2,512,128]{2,1,0:T(8,128)S(1)}, f32[2,512,128]{2,1,0:T(8,128)S(1)}, u32[]{:S(2)}, u32[]{:S(2)}) %collective-permute-start.14) | collective-permute-done | bytes 524320 | tf_op jit(solution)/shard_map/ppermute | solution.py:371
  58.7 3.3 %third_section.1 = f32[2048,128]{1,0:T(8,128)} custom-call(f32[2,512,128]{2,1,0:T(8,128)S(1)} %second_section_kept.1.kept_ref, f32[2,512,128]{2,1,0:T(8,128)S(1)} %collective-permute-done.14.came_ref, bf16[2,256,256]{2,1,0:T(8,128)(2,1)S(1)} %get-tuple-element.52.refs_0_, bf16[2,256,256]{2,1,0:T(8,128)(2,1)S(1)} %get-tuple-element.53.refs_1_, ...), custom_call_target="tpu_custom_call" | custom-call | flops 1610612736 | bytes 4194304 | tf_op jit(solution)/shard_map/third_section/pallas_call | solution.py:274
  (8 shorter events, 0.0 us)
Async XLA Ops:
  0.0 1.2 %copy-start = (f32[2,131072]{1,0:T(2,128)S(1)}, f32[2,131072]{1,0:T(2,128)}, u32[]{:S(2)}) copy-start(f32[2,131072]{1,0:T(2,128)} %param.3) | copy-start | bytes 3145732
  1.3 11.4 %collective-permute-start = (f32[256,128]{1,0:T(8,128)S(1)}, f32[256,128]{1,0:T(8,128)S(1)}, u32[]{:S(2)}, u32[]{:S(2)}) collective-permute-start(f32[256,128]{1,0:T(8,128)S(1)} %get-tuple-element.31), channel_id=1, source_target_pairs={{0,14},{2,12},{4,10},{6,8},{8,6},{10,4},{12,2},{14,0},{1,15},{3,13... | collective-permute-start | bytes 393224 | tf_op jit(solution)/shard_map/ppermute | solution.py:319
  7.4 10.9 %collective-permute-start.1 = (f32[256,128]{1,0:T(8,128)S(1)}, f32[256,128]{1,0:T(8,128)S(1)}, u32[]{:S(2)}, u32[]{:S(2)}) collective-permute-start(f32[256,128]{1,0:T(8,128)S(1)} %get-tuple-element.32), channel_id=1, source_target_pairs={{0,12},{2,14},{4,8},{6,10},{8,4},{10,6},{12,0},{14,2},{1,13},{3,15... | collective-permute-start | bytes 393224 | tf_op jit(solution)/shard_map/ppermute | solution.py:319
  7.6 20.0 %collective-permute-start.2 = (f32[256,128]{1,0:T(8,128)S(1)}, f32[256,128]{1,0:T(8,128)S(1)}, u32[]{:S(2)}, u32[]{:S(2)}) collective-permute-start(f32[256,128]{1,0:T(8,128)S(1)} %get-tuple-element.33), channel_id=1, source_target_pairs={{0,6},{2,4},{4,2},{6,0},{8,14},{10,12},{12,10},{14,8},{1,7},{3,5},... | collective-permute-start | bytes 393224 | tf_op jit(solution)/shard_map/ppermute | solution.py:319
  7.6 20.1 %collective-permute-start.3 = (f32[256,128]{1,0:T(8,128)S(1)}, f32[256,128]{1,0:T(8,128)S(1)}, u32[]{:S(2)}, u32[]{:S(2)}) collective-permute-start(f32[256,128]{1,0:T(8,128)S(1)} %get-tuple-element.34), channel_id=1, source_target_pairs={{0,4},{2,6},{4,0},{6,2},{8,12},{10,14},{12,8},{14,10},{1,5},{3,7},... | collective-permute-start | bytes 393224 | tf_op jit(solution)/shard_map/ppermute | solution.py:319
  9.5 18.4 %collective-permute-start.4 = (f32[256,128]{1,0:T(8,128)S(1)}, f32[256,128]{1,0:T(8,128)S(1)}, u32[]{:S(2)}, u32[]{:S(2)}) collective-permute-start(f32[256,128]{1,0:T(8,128)S(1)} %get-tuple-element.35), channel_id=1, source_target_pairs={{0,10},{2,8},{4,14},{6,12},{8,2},{10,0},{12,6},{14,4},{1,11},{3,9}... | collective-permute-start | bytes 393224 | tf_op jit(solution)/shard_map/ppermute | solution.py:319
  12.7 17.0 %collective-permute-start.5 = (f32[256,128]{1,0:T(8,128)S(1)}, f32[256,128]{1,0:T(8,128)S(1)}, u32[]{:S(2)}, u32[]{:S(2)}) collective-permute-start(f32[256,128]{1,0:T(8,128)S(1)} %get-tuple-element.36), channel_id=1, source_target_pairs={{0,8},{2,10},{4,12},{6,14},{8,0},{10,2},{12,4},{14,6},{1,9},{3,11}... | collective-permute-start | bytes 393224 | tf_op jit(solution)/shard_map/ppermute | solution.py:319
  18.3 11.4 %collective-permute-start.6 = (f32[256,128]{1,0:T(8,128)S(1)}, f32[256,128]{1,0:T(8,128)S(1)}, u32[]{:S(2)}, u32[]{:S(2)}) collective-permute-start(f32[256,128]{1,0:T(8,128)S(1)} %get-tuple-element.37), channel_id=1, source_target_pairs={{0,2},{2,0},{4,6},{6,4},{8,10},{10,8},{12,14},{14,12},{1,3},{3,1},... | collective-permute-start | bytes 393224 | tf_op jit(solution)/shard_map/ppermute | solution.py:319
  19.8 0.7 %copy-start.1 = (s32[18]{0:T(128)S(1)}, s32[18]{0:T(128)}, u32[]{:S(2)}) copy-start(s32[18]{0:T(128)} %bits_ref.1) | copy-start | bytes 220
  32.5 8.9 %collective-permute-start.7 = (f32[2,4,2,16,128]{4,3,2,1,0:T(8,128)S(1)}, f32[2,4,2,16,128]{4,3,2,1,0:T(8,128)S(1)}, u32[]{:S(2)}, u32[]{:S(2)}) collective-permute-start(f32[2,4,2,16,128]{4,3,2,1,0:T(8,128)S(1)} %get-tuple-element.43), channel_id=1, source_target_pairs={{0,14},{2,12},{4,10},{6,8},{8,6},{10,4},{12,2},{14,0},{1,15},{3,13... | collective-permute-start | bytes 393224 | tf_op jit(solution)/shard_map/ppermute | solution.py:319
  35.0 8.4 %collective-permute-start.8 = (f32[2,4,2,16,128]{4,3,2,1,0:T(8,128)S(1)}, f32[2,4,2,16,128]{4,3,2,1,0:T(8,128)S(1)}, u32[]{:S(2)}, u32[]{:S(2)}) collective-permute-start(f32[2,4,2,16,128]{4,3,2,1,0:T(8,128)S(1)} %get-tuple-element.44), channel_id=1, source_target_pairs={{0,12},{2,14},{4,8},{6,10},{8,4},{10,6},{12,0},{14,2},{1,13},{3,15... | collective-permute-start | bytes 393224 | tf_op jit(solution)/shard_map/ppermute | solution.py:319
  36.4 12.2 %collective-permute-start.9 = (f32[2,4,2,16,128]{4,3,2,1,0:T(8,128)S(1)}, f32[2,4,2,16,128]{4,3,2,1,0:T(8,128)S(1)}, u32[]{:S(2)}, u32[]{:S(2)}) collective-permute-start(f32[2,4,2,16,128]{4,3,2,1,0:T(8,128)S(1)} %get-tuple-element.45), channel_id=1, source_target_pairs={{0,6},{2,4},{4,2},{6,0},{8,14},{10,12},{12,10},{14,8},{1,7},{3,5},... | collective-permute-start | bytes 393224 | tf_op jit(solution)/shard_map/ppermute | solution.py:319
  36.4 14.8 %collective-permute-start.10 = (f32[2,4,2,16,128]{4,3,2,1,0:T(8,128)S(1)}, f32[2,4,2,16,128]{4,3,2,1,0:T(8,128)S(1)}, u32[]{:S(2)}, u32[]{:S(2)}) collective-permute-start(f32[2,4,2,16,128]{4,3,2,1,0:T(8,128)S(1)} %get-tuple-element.46), channel_id=1, source_target_pairs={{0,4},{2,6},{4,0},{6,2},{8,12},{10,14},{12,8},{14,10},{1,5},{3,7},... | collective-permute-start | bytes 393224 | tf_op jit(solution)/shard_map/ppermute | solution.py:319
  39.4 15.9 %collective-permute-start.11 = (f32[2,4,2,16,128]{4,3,2,1,0:T(8,128)S(1)}, f32[2,4,2,16,128]{4,3,2,1,0:T(8,128)S(1)}, u32[]{:S(2)}, u32[]{:S(2)}) collective-permute-start(f32[2,4,2,16,128]{4,3,2,1,0:T(8,128)S(1)} %get-tuple-element.47), channel_id=1, source_target_pairs={{0,10},{2,8},{4,14},{6,12},{8,2},{10,0},{12,6},{14,4},{1,11},{3,9}... | collective-permute-start | bytes 393224 | tf_op jit(solution)/shard_map/ppermute | solution.py:319
  41.5 14.2 %collective-permute-start.12 = (f32[2,4,2,16,128]{4,3,2,1,0:T(8,128)S(1)}, f32[2,4,2,16,128]{4,3,2,1,0:T(8,128)S(1)}, u32[]{:S(2)}, u32[]{:S(2)}) collective-permute-start(f32[2,4,2,16,128]{4,3,2,1,0:T(8,128)S(1)} %get-tuple-element.48), channel_id=1, source_target_pairs={{0,8},{2,10},{4,12},{6,14},{8,0},{10,2},{12,4},{14,6},{1,9},{3,11}... | collective-permute-start | bytes 393224 | tf_op jit(solution)/shard_map/ppermute | solution.py:319
  43.4 12.3 %collective-permute-start.13 = (f32[2,4,2,16,128]{4,3,2,1,0:T(8,128)S(1)}, f32[2,4,2,16,128]{4,3,2,1,0:T(8,128)S(1)}, u32[]{:S(2)}, u32[]{:S(2)}) collective-permute-start(f32[2,4,2,16,128]{4,3,2,1,0:T(8,128)S(1)} %get-tuple-element.49), channel_id=1, source_target_pairs={{0,2},{2,0},{4,6},{6,4},{8,10},{10,8},{12,14},{14,12},{1,3},{3,1},... | collective-permute-start | bytes 393224 | tf_op jit(solution)/shard_map/ppermute | solution.py:319
  56.7 2.0 %collective-permute-start.14 = (f32[2,512,128]{2,1,0:T(8,128)S(1)}, f32[2,512,128]{2,1,0:T(8,128)S(1)}, u32[]{:S(2)}, u32[]{:S(2)}) collective-permute-start(f32[2,512,128]{2,1,0:T(8,128)S(1)} %second_section_sent.1), channel_id=1, source_target_pairs={{0,1},{1,0},{2,3},{3,2},{4,5},{5,4},{6,7},{7,6},{8,9},{9,8},{10,11... | collective-permute-start | bytes 1572872 | tf_op jit(solution)/shard_map/ppermute | solution.py:371

commit v6 on v5

--- a/solution.py
+++ b/solution.py
@@ -12,6 +12,9 @@
 BF16 = jnp.bfloat16
 VMEM_LIMIT = 14 * 1024 * 1024
 LARGE_VMEM = 48 * 1024 * 1024
+SPLIT_VMEM = 62 * 1024 * 1024
+PIECES = 4
+FIRST = 2
 
 
 def window_offsets(span, gate_bits):
@@ -137,21 +140,34 @@
     return jnp.bitwise_xor(lax.axis_index("qa"), distance)
 
 
-def split_kernel(x_ref, *outs):
-    for distance, out_ref in zip(distances_of(len(outs)), outs):
+def far_kernel(distances, x_ref, *refs):
+    *outs, sems = refs
+    copies = []
+    for place, distance in enumerate(distances):
+        copy = pltpu.make_async_copy(x_ref.at[partner(distance)], outs[place], sems.at[place])
+        copy.start()
+        copies.append(copy)
+    for copy in copies:
+        copy.wait()
+
+
+def rest_kernel(distances, x_ref, *outs):
+    for distance, out_ref in zip(distances, outs):
         out_ref[...] = x_ref[partner(distance)]
 
 
 def apply_stage(weights_ref, starts, load, store):
     dim = weights_ref.shape[-1] // 2
-    high_w, rest_w = weights_ref[0], weights_ref[1]
+    both_w = weights_ref[...].reshape(4 * dim, 2 * dim)
+    high_w = weights_ref[0]
     for pair in range(0, len(starts), 2):
         group = starts[pair : pair + 2]
         x = jnp.concatenate(
             [jnp.concatenate([load(part, start) for start in group], axis=1) for part in range(2)], axis=0
         )
         high, rest = split(x)
-        y = bf_dot(high_w, rest) + bf_dot(rest_w, high) + bf_dot(high_w, high)
+        both = bf_dot(both_w, high)
+        y = bf_dot(high_w, rest) + both[2 * dim :] + both[: 2 * dim]
         lanes = y.shape[1] // len(group)
         for part in range(2):
             for place, start in enumerate(group):
@@ -262,8 +278,13 @@
             results[t][pl.ds(2 * start + part, dim, stride=2 * stride), :] = value
 
         run_stage(stages[-1], weights[-1], lane_bits, done[t], store=store)
-        copies.append(pltpu.make_async_copy(results[t], out_ref.at[pl.ds(t * 2 * half, 2 * half)], sems.at[t]))
-        copies[-1].start()
+        size = 2 * half // PIECES
+        for piece in range(PIECES):
+            to = out_ref.at[pl.ds(t * 2 * half + piece * size, size)]
+            copies.append(
+                pltpu.make_async_copy(results[t].at[pl.ds(piece * size, size)], to, sems.at[t * PIECES + piece])
+            )
+            copies[-1].start()
     for copy in copies:
         copy.wait()
 
@@ -303,15 +324,23 @@
 
     state = with_layout_constraint(state.reshape(2, rows, lanes), Layout(major_to_minor=(1, 0, 2)))
     state = state.swapaxes(0, 1).reshape(qa, 2 * rows // qa, lanes)
-    blocks = call(
-        split_kernel,
-        "split_state",
-        (shape((2 * rows // qa, lanes), F32),) * qa,
-        [vmem],
-        [],
+    order_of = distances_of(qa)
+    first, rest = order_of[1 : 1 + FIRST], [0, *order_of[1 + FIRST :]]
+    one_block = shape((2 * rows // qa, lanes), F32)
+    early = call(
+        functools.partial(far_kernel, first),
+        "split_first",
+        (one_block,) * len(first),
+        [hbm],
+        [pltpu.SemaphoreType.DMA((len(first),))],
         0,
         state,
-    )
+        limit=SPLIT_VMEM,
+    )
+    late = call(
+        functools.partial(rest_kernel, rest), "split_rest", (one_block,) * len(rest), [vmem], [], 0, state
+    )
+    blocks = [late[0], *early, *late[1:]]
 
     def exchange(blocks):
         came = [blocks[0]]
@@ -374,7 +403,7 @@
         "third_section",
         shape((2 * rows, lanes), F32),
         [vmem] * (2 + counts[2]),
-        [whole] + [half] * 4 + [pltpu.VMEM((rows, lanes), F32)] * 2 + [pltpu.SemaphoreType.DMA((2,))],
+        [whole] + [half] * 4 + [pltpu.VMEM((rows, lanes), F32)] * 2 + [pltpu.SemaphoreType.DMA((2 * PIECES,))],
         4,
         halves[1],
         came,

time: 62.2 us -> 62.9 us (1.011)
  Pallas kernels: 15.4 us -> 17.4 us
  starting transfers between devices: 30.8 us -> 29.9 us
    pallas_call x6 -> x7, Pallas kernels: 15.4 us -> 17.4 us  [call(): pl.pallas_call(kernel, out_shape=out_shapes, in_specs=in_specs, out_specs...]
    ppermute x14, starting transfers between devices: 30.7 us -> 29.8 us  [exchange(): lax.ppermute(piece, 'qa', [(i, i ^ distance) for i in range(qa)])]
  transfers between devices with their start and end apart: 15 -> 15, of which waited for: 9 -> 8; matrix products, arithmetic and copies ran while one was open for 0% -> 0% of each run, Pallas kernels for 13% -> 14%
where the time goes in v6:
time: 62.9 us; the launch traced here: 62.7 us
  starting transfers between devices  29.9 us (48%)
  Pallas kernels  17.4 us (28%)
  waiting for transfers between devices  13.4 us (21%)
  local copies, waits for them, and re-layouts  1.88 us (3%)
    ppermute x14, starting transfers between devices, exchange(): lax.ppermute(piece, 'qa', [(i, i ^ distance) for i in range(qa)])  29.8 us
    pallas_call x7, Pallas kernels, call(): pl.pallas_call(kernel, out_shape=out_shapes, in_specs=in_specs, out_specs...  17.4 us
    ppermute x14, waiting for transfers between devices, exchange(): lax.ppermute(piece, 'qa', [(i, i ^ distance) for i in range(qa)])  12.8 us
    unnamed x4, local copies, waits for them, and re-layouts  1.88 us
  transfers between devices with their start and end apart: 15, of which 8 were waited for; matrix products, arithmetic and copies ran while one was open for 0% of the time, Pallas kernels for 14%

profile of v6, /device:TPU:0, one launch (start us, length us, event | category | flops | bytes accessed | tf_op | source)
XLA Modules:
  0.0 62.7 jit_solution(9044391107158852660)
XLA Ops:
  0.0 1.7 %split_first.1 = (f32[256,128]{1,0:T(8,128)}, f32[256,128]{1,0:T(8,128)}) custom-call(f32[8,256,128]{2,1,0:T(8,128)} %bitcast.10), custom_call_target="tpu_custom_call" | custom-call | bytes 4194304 | tf_op jit(solution)/shard_map/split_first/pallas_call | solution.py:295
  1.7 6.1 %collective-permute-start = (f32[256,128]{1,0:T(8,128)}, f32[256,128]{1,0:T(8,128)S(1)}, u32[]{:S(2)}, u32[]{:S(2)}) collective-permute-start(f32[256,128]{1,0:T(8,128)} %get-tuple-element.31), channel_id=1, source_target_pairs={{0,14},{2,12},{4,10},{6,8},{8,6},{10,4},{12,2},{14,0},{1,15},{3,13... | collective-permute-start | bytes 393224 | tf_op jit(solution)/shard_map/ppermute | solution.py:348
  7.8 0.2 collective-permute-start.1
  8.0 1.2 %copy-done = f32[2,131072]{1,0:T(2,128)S(1)} copy-done((f32[2,131072]{1,0:T(2,128)S(1)}, f32[2,131072]{1,0:T(2,128)}, u32[]{:S(2)}) %copy-start) | copy-done | bytes 1048600
  9.2 0.1 split_rest.1
  9.3 0.1 collective-permute-start.2
  9.3 1.9 %collective-permute-start.3 = (f32[256,128]{1,0:T(8,128)S(1)}, f32[256,128]{1,0:T(8,128)S(1)}, u32[]{:S(2)}, u32[]{:S(2)}) collective-permute-start(f32[256,128]{1,0:T(8,128)S(1)} %get-tuple-element.34), channel_id=1, source_target_pairs={{0,4},{2,6},{4,0},{6,2},{8,12},{10,14},{12,8},{14,10},{1,5},{3,7},... | collective-permute-start | bytes 393224 | tf_op jit(solution)/shard_map/ppermute | solution.py:348
  11.2 3.2 %collective-permute-start.4 = (f32[256,128]{1,0:T(8,128)S(1)}, f32[256,128]{1,0:T(8,128)S(1)}, u32[]{:S(2)}, u32[]{:S(2)}) collective-permute-start(f32[256,128]{1,0:T(8,128)S(1)} %get-tuple-element.35), channel_id=1, source_target_pairs={{0,10},{2,8},{4,14},{6,12},{8,2},{10,0},{12,6},{14,4},{1,11},{3,9}... | collective-permute-start | bytes 393224 | tf_op jit(solution)/shard_map/ppermute | solution.py:348
  14.4 4.5 %collective-permute-start.5 = (f32[256,128]{1,0:T(8,128)S(1)}, f32[256,128]{1,0:T(8,128)S(1)}, u32[]{:S(2)}, u32[]{:S(2)}) collective-permute-start(f32[256,128]{1,0:T(8,128)S(1)} %get-tuple-element.36), channel_id=1, source_target_pairs={{0,8},{2,10},{4,12},{6,14},{8,0},{10,2},{12,4},{14,6},{1,9},{3,11}... | collective-permute-start | bytes 393224 | tf_op jit(solution)/shard_map/ppermute | solution.py:348
  18.9 1.5 %collective-permute-start.6 = (f32[256,128]{1,0:T(8,128)S(1)}, f32[256,128]{1,0:T(8,128)S(1)}, u32[]{:S(2)}, u32[]{:S(2)}) collective-permute-start(f32[256,128]{1,0:T(8,128)S(1)} %get-tuple-element.37), channel_id=1, source_target_pairs={{0,2},{2,0},{4,6},{6,4},{8,10},{10,8},{12,14},{14,12},{1,3},{3,1},... | collective-permute-start | bytes 393224 | tf_op jit(solution)/shard_map/ppermute | solution.py:348
  20.4 0.7 %copy-done.1 = s32[18]{0:T(128)S(1)} copy-done((s32[18]{0:T(128)S(1)}, s32[18]{0:T(128)}, u32[]{:S(2)}) %copy-start.1) | copy-done | bytes 96
  21.1 7.1 %prepare_gates.1 = (bf16[2,256,256]{2,1,0:T(8,128)(2,1)S(1)}, bf16[2,256,256]{2,1,0:T(8,128)(2,1)S(1)}, bf16[2,256,256]{2,1,0:T(8,128)(2,1)S(1)}, bf16[2,512,512...) custom-call(s32[18]{0:T(128)S(1)} %copy-done.1, ...), custom_call_target="tpu_custom_call" | custom-call | flops 3221225472 | bytes 4194304 | tf_op jit(solution)/shard_map/prepare_gates/pallas_call | solution.py:295
  28.3 0.2 collective-permute-done.4.refs_5_
  28.4 1.8 %collective-permute-done.5.refs_6_ = f32[256,128]{1,0:T(8,128)S(1)} collective-permute-done((f32[256,128]{1,0:T(8,128)S(1)}, f32[256,128]{1,0:T(8,128)S(1)}, u32[]{:S(2)}, u32[]{:S(2)}) %collective-permute-start.5) | collective-permute-done | bytes 131104 | tf_op jit(solution)/shard_map/ppermute | solution.py:348
  30.3 2.8 %first_section.1 = (f32[2,4,2,16,128]{4,3,2,1,0:T(8,128)S(1)}, f32[2,4,2,16,128]{4,3,2,1,0:T(8,128)S(1)}, f32[2,4,2,16,128]{4,3,2,1,0:T(8,128)S(1)}, f32[2,4,2,1...) custom-call(f32[256,128]{1,0:T(8,128)S(1)} %get-tuple-element.30.ref, ...), custom_call_target="tpu_custom_call" | custom-call | flops 2013265920 | bytes 4194304 | tf_op jit(solution)/shard_map/first_section/pallas_call | solution.py:295
  33.1 2.5 %collective-permute-start.7 = (f32[2,4,2,16,128]{4,3,2,1,0:T(8,128)S(1)}, f32[2,4,2,16,128]{4,3,2,1,0:T(8,128)S(1)}, u32[]{:S(2)}, u32[]{:S(2)}) collective-permute-start(f32[2,4,2,16,128]{4,3,2,1,0:T(8,128)S(1)} %get-tuple-element.43), channel_id=1, source_target_pairs={{0,14},{2,12},{4,10},{6,8},{8,6},{10,4},{12,2},{14,0},{1,15},{3,13... | collective-permute-start | bytes 393224 | tf_op jit(solution)/shard_map/ppermute | solution.py:348
  35.6 1.3 %collective-permute-start.8 = (f32[2,4,2,16,128]{4,3,2,1,0:T(8,128)S(1)}, f32[2,4,2,16,128]{4,3,2,1,0:T(8,128)S(1)}, u32[]{:S(2)}, u32[]{:S(2)}) collective-permute-start(f32[2,4,2,16,128]{4,3,2,1,0:T(8,128)S(1)} %get-tuple-element.44), channel_id=1, source_target_pairs={{0,12},{2,14},{4,8},{6,10},{8,4},{10,6},{12,0},{14,2},{1,13},{3,15... | collective-permute-start | bytes 393224 | tf_op jit(solution)/shard_map/ppermute | solution.py:348
  36.9 3.0 %collective-permute-start.10 = (f32[2,4,2,16,128]{4,3,2,1,0:T(8,128)S(1)}, f32[2,4,2,16,128]{4,3,2,1,0:T(8,128)S(1)}, u32[]{:S(2)}, u32[]{:S(2)}) collective-permute-start(f32[2,4,2,16,128]{4,3,2,1,0:T(8,128)S(1)} %get-tuple-element.46), channel_id=1, source_target_pairs={{0,4},{2,6},{4,0},{6,2},{8,12},{10,14},{12,8},{14,10},{1,5},{3,7},... | collective-permute-start | bytes 393224 | tf_op jit(solution)/shard_map/ppermute | solution.py:348
  39.9 1.0 %collective-permute-start.11 = (f32[2,4,2,16,128]{4,3,2,1,0:T(8,128)S(1)}, f32[2,4,2,16,128]{4,3,2,1,0:T(8,128)S(1)}, u32[]{:S(2)}, u32[]{:S(2)}) collective-permute-start(f32[2,4,2,16,128]{4,3,2,1,0:T(8,128)S(1)} %get-tuple-element.47), channel_id=1, source_target_pairs={{0,10},{2,8},{4,14},{6,12},{8,2},{10,0},{12,6},{14,4},{1,11},{3,9}... | collective-permute-start | bytes 393224 | tf_op jit(solution)/shard_map/ppermute | solution.py:348
  40.9 1.1 %collective-permute-done.7.refs_1_ = f32[2,4,2,16,128]{4,3,2,1,0:T(8,128)S(1)} collective-permute-done((f32[2,4,2,16,128]{4,3,2,1,0:T(8,128)S(1)}, f32[2,4,2,16,128]{4,3,2,1,0:T(8,128)S(1)}, u32[]{:S(2)}, u32[]{:S(2)}) %collective-permute-start.7) | collective-permute-done | bytes 131104 | tf_op jit(solution)/shard_map/ppermute | solution.py:348
  42.0 1.8 %collective-permute-start.12 = (f32[2,4,2,16,128]{4,3,2,1,0:T(8,128)S(1)}, f32[2,4,2,16,128]{4,3,2,1,0:T(8,128)S(1)}, u32[]{:S(2)}, u32[]{:S(2)}) collective-permute-start(f32[2,4,2,16,128]{4,3,2,1,0:T(8,128)S(1)} %get-tuple-element.48), channel_id=1, source_target_pairs={{0,8},{2,10},{4,12},{6,14},{8,0},{10,2},{12,4},{14,6},{1,9},{3,11}... | collective-permute-start | bytes 393224 | tf_op jit(solution)/shard_map/ppermute | solution.py:348
  43.8 0.0 collective-permute-done.8.refs_2_
  43.9 2.8 %collective-permute-start.13 = (f32[2,4,2,16,128]{4,3,2,1,0:T(8,128)S(1)}, f32[2,4,2,16,128]{4,3,2,1,0:T(8,128)S(1)}, u32[]{:S(2)}, u32[]{:S(2)}) collective-permute-start(f32[2,4,2,16,128]{4,3,2,1,0:T(8,128)S(1)} %get-tuple-element.49), channel_id=1, source_target_pairs={{0,2},{2,0},{4,6},{6,4},{8,10},{10,8},{12,14},{14,12},{1,3},{3,1},... | collective-permute-start | bytes 393224 | tf_op jit(solution)/shard_map/ppermute | solution.py:348
  46.6 2.4 %collective-permute-done.9.refs_3_ = f32[2,4,2,16,128]{4,3,2,1,0:T(8,128)S(1)} collective-permute-done((f32[2,4,2,16,128]{4,3,2,1,0:T(8,128)S(1)}, f32[2,4,2,16,128]{4,3,2,1,0:T(8,128)S(1)}, u32[]{:S(2)}, u32[]{:S(2)}) %collective-permute-start.9) | collective-permute-done | bytes 131104 | tf_op jit(solution)/shard_map/ppermute | solution.py:348
  49.1 2.6 %collective-permute-done.10.refs_4_ = f32[2,4,2,16,128]{4,3,2,1,0:T(8,128)S(1)} collective-permute-done((f32[2,4,2,16,128]{4,3,2,1,0:T(8,128)S(1)}, f32[2,4,2,16,128]{4,3,2,1,0:T(8,128)S(1)}, u32[]{:S(2)}, u32[]{:S(2)}) %collective-permute-start.10) | collective-permute-done | bytes 131104 | tf_op jit(solution)/shard_map/ppermute | solution.py:348
  51.7 4.1 %collective-permute-done.11.refs_5_ = f32[2,4,2,16,128]{4,3,2,1,0:T(8,128)S(1)} collective-permute-done((f32[2,4,2,16,128]{4,3,2,1,0:T(8,128)S(1)}, f32[2,4,2,16,128]{4,3,2,1,0:T(8,128)S(1)}, u32[]{:S(2)}, u32[]{:S(2)}) %collective-permute-start.11) | collective-permute-done | bytes 131104 | tf_op jit(solution)/shard_map/ppermute | solution.py:348
  55.8 0.5 collective-permute-done.12.refs_6_
  56.3 1.3 %second_section_sent.1 = f32[2,512,128]{2,1,0:T(8,128)S(1)} custom-call(f32[2,4,2,16,128]{4,3,2,1,0:T(8,128)S(1)} %get-tuple-element.42.refs_0_, f32[2,4,2,16,128]{4,3,2,1,0:T(8,128)S(1)} %collective-permute-done.7.refs_1_, f32[2,4,2,16,128]{4,3,2,1,0:T(8,128)S(1)} %collective-permute-done.8.refs_2_, ...), custom_call_target="tpu_custom_call" | custom-call | flops 603979776 | bytes 4194304 | tf_op jit(solution)/shard_map/second_section_sent/pallas_call | solution.py:295
  57.5 0.1 collective-permute-start.14
  57.6 1.3 %second_section_kept.1.kept_ref = f32[2,512,128]{2,1,0:T(8,128)S(1)} custom-call(f32[2,4,2,16,128]{4,3,2,1,0:T(8,128)S(1)} %get-tuple-element.42.refs_0_, f32[2,4,2,16,128]{4,3,2,1,0:T(8,128)S(1)} %collective-permute-done.7.refs_1_, f32[2,4,2,16,128]{4,3,2,1,0:T(8,128)S(1)} %collective-permute-done.8.refs_2_, ...), custom_call_target="tpu_custom_call" | custom-call | flops 603979776 | bytes 4194304 | tf_op jit(solution)/shard_map/second_section_kept/pallas_call | solution.py:295
  58.9 0.6 collective-permute-done.14.came_ref
  59.5 3.2 %third_section.1 = f32[2048,128]{1,0:T(8,128)} custom-call(f32[2,512,128]{2,1,0:T(8,128)S(1)} %second_section_kept.1.kept_ref, f32[2,512,128]{2,1,0:T(8,128)S(1)} %collective-permute-done.14.came_ref, bf16[2,256,256]{2,1,0:T(8,128)(2,1)S(1)} %get-tuple-element.52.refs_0_, bf16[2,256,256]{2,1,0:T(8,128)(2,1)S(1)} %get-tuple-element.53.refs_1_, ...), custom_call_target="tpu_custom_call" | custom-call | flops 1610612736 | bytes 4194304 | tf_op jit(solution)/shard_map/third_section/pallas_call | solution.py:295
  (9 shorter events, 0.0 us)
Async XLA Ops:
  1.7 12.7 %collective-permute-start = (f32[256,128]{1,0:T(8,128)}, f32[256,128]{1,0:T(8,128)S(1)}, u32[]{:S(2)}, u32[]{:S(2)}) collective-permute-start(f32[256,128]{1,0:T(8,128)} %get-tuple-element.31), channel_id=1, source_target_pairs={{0,14},{2,12},{4,10},{6,8},{8,6},{10,4},{12,2},{14,0},{1,15},{3,13... | collective-permute-start | bytes 393224 | tf_op jit(solution)/shard_map/ppermute | solution.py:348
  7.8 11.1 %collective-permute-start.1 = (f32[256,128]{1,0:T(8,128)}, f32[256,128]{1,0:T(8,128)S(1)}, u32[]{:S(2)}, u32[]{:S(2)}) collective-permute-start(f32[256,128]{1,0:T(8,128)} %get-tuple-element.32), channel_id=1, source_target_pairs={{0,12},{2,14},{4,8},{6,10},{8,4},{10,6},{12,0},{14,2},{1,13},{3,15... | collective-permute-start | bytes 393224 | tf_op jit(solution)/shard_map/ppermute | solution.py:348
  8.0 1.2 %copy-start = (f32[2,131072]{1,0:T(2,128)S(1)}, f32[2,131072]{1,0:T(2,128)}, u32[]{:S(2)}) copy-start(f32[2,131072]{1,0:T(2,128)} %param.3) | copy-start | bytes 3145732
  9.3 19.0 %collective-permute-start.2 = (f32[256,128]{1,0:T(8,128)S(1)}, f32[256,128]{1,0:T(8,128)S(1)}, u32[]{:S(2)}, u32[]{:S(2)}) collective-permute-start(f32[256,128]{1,0:T(8,128)S(1)} %get-tuple-element.33), channel_id=1, source_target_pairs={{0,6},{2,4},{4,2},{6,0},{8,14},{10,12},{12,10},{14,8},{1,7},{3,5},... | collective-permute-start | bytes 393224 | tf_op jit(solution)/shard_map/ppermute | solution.py:348
  9.3 18.9 %collective-permute-start.3 = (f32[256,128]{1,0:T(8,128)S(1)}, f32[256,128]{1,0:T(8,128)S(1)}, u32[]{:S(2)}, u32[]{:S(2)}) collective-permute-start(f32[256,128]{1,0:T(8,128)S(1)} %get-tuple-element.34), channel_id=1, source_target_pairs={{0,4},{2,6},{4,0},{6,2},{8,12},{10,14},{12,8},{14,10},{1,5},{3,7},... | collective-permute-start | bytes 393224 | tf_op jit(solution)/shard_map/ppermute | solution.py:348
  11.2 17.2 %collective-permute-start.4 = (f32[256,128]{1,0:T(8,128)S(1)}, f32[256,128]{1,0:T(8,128)S(1)}, u32[]{:S(2)}, u32[]{:S(2)}) collective-permute-start(f32[256,128]{1,0:T(8,128)S(1)} %get-tuple-element.35), channel_id=1, source_target_pairs={{0,10},{2,8},{4,14},{6,12},{8,2},{10,0},{12,6},{14,4},{1,11},{3,9}... | collective-permute-start | bytes 393224 | tf_op jit(solution)/shard_map/ppermute | solution.py:348
  14.4 15.9 %collective-permute-start.5 = (f32[256,128]{1,0:T(8,128)S(1)}, f32[256,128]{1,0:T(8,128)S(1)}, u32[]{:S(2)}, u32[]{:S(2)}) collective-permute-start(f32[256,128]{1,0:T(8,128)S(1)} %get-tuple-element.36), channel_id=1, source_target_pairs={{0,8},{2,10},{4,12},{6,14},{8,0},{10,2},{12,4},{14,6},{1,9},{3,11}... | collective-permute-start | bytes 393224 | tf_op jit(solution)/shard_map/ppermute | solution.py:348
  18.9 11.4 %collective-permute-start.6 = (f32[256,128]{1,0:T(8,128)S(1)}, f32[256,128]{1,0:T(8,128)S(1)}, u32[]{:S(2)}, u32[]{:S(2)}) collective-permute-start(f32[256,128]{1,0:T(8,128)S(1)} %get-tuple-element.37), channel_id=1, source_target_pairs={{0,2},{2,0},{4,6},{6,4},{8,10},{10,8},{12,14},{14,12},{1,3},{3,1},... | collective-permute-start | bytes 393224 | tf_op jit(solution)/shard_map/ppermute | solution.py:348
  20.4 0.7 %copy-start.1 = (s32[18]{0:T(128)S(1)}, s32[18]{0:T(128)}, u32[]{:S(2)}) copy-start(s32[18]{0:T(128)} %bits_ref.1) | copy-start | bytes 220
  33.1 8.9 %collective-permute-start.7 = (f32[2,4,2,16,128]{4,3,2,1,0:T(8,128)S(1)}, f32[2,4,2,16,128]{4,3,2,1,0:T(8,128)S(1)}, u32[]{:S(2)}, u32[]{:S(2)}) collective-permute-start(f32[2,4,2,16,128]{4,3,2,1,0:T(8,128)S(1)} %get-tuple-element.43), channel_id=1, source_target_pairs={{0,14},{2,12},{4,10},{6,8},{8,6},{10,4},{12,2},{14,0},{1,15},{3,13... | collective-permute-start | bytes 393224 | tf_op jit(solution)/shard_map/ppermute | solution.py:348
  35.6 8.3 %collective-permute-start.8 = (f32[2,4,2,16,128]{4,3,2,1,0:T(8,128)S(1)}, f32[2,4,2,16,128]{4,3,2,1,0:T(8,128)S(1)}, u32[]{:S(2)}, u32[]{:S(2)}) collective-permute-start(f32[2,4,2,16,128]{4,3,2,1,0:T(8,128)S(1)} %get-tuple-element.44), channel_id=1, source_target_pairs={{0,12},{2,14},{4,8},{6,10},{8,4},{10,6},{12,0},{14,2},{1,13},{3,15... | collective-permute-start | bytes 393224 | tf_op jit(solution)/shard_map/ppermute | solution.py:348
  36.9 12.1 %collective-permute-start.9 = (f32[2,4,2,16,128]{4,3,2,1,0:T(8,128)S(1)}, f32[2,4,2,16,128]{4,3,2,1,0:T(8,128)S(1)}, u32[]{:S(2)}, u32[]{:S(2)}) collective-permute-start(f32[2,4,2,16,128]{4,3,2,1,0:T(8,128)S(1)} %get-tuple-element.45), channel_id=1, source_target_pairs={{0,6},{2,4},{4,2},{6,0},{8,14},{10,12},{12,10},{14,8},{1,7},{3,5},... | collective-permute-start | bytes 393224 | tf_op jit(solution)/shard_map/ppermute | solution.py:348
  36.9 14.7 %collective-permute-start.10 = (f32[2,4,2,16,128]{4,3,2,1,0:T(8,128)S(1)}, f32[2,4,2,16,128]{4,3,2,1,0:T(8,128)S(1)}, u32[]{:S(2)}, u32[]{:S(2)}) collective-permute-start(f32[2,4,2,16,128]{4,3,2,1,0:T(8,128)S(1)} %get-tuple-element.46), channel_id=1, source_target_pairs={{0,4},{2,6},{4,0},{6,2},{8,12},{10,14},{12,8},{14,10},{1,5},{3,7},... | collective-permute-start | bytes 393224 | tf_op jit(solution)/shard_map/ppermute | solution.py:348
  39.9 15.9 %collective-permute-start.11 = (f32[2,4,2,16,128]{4,3,2,1,0:T(8,128)S(1)}, f32[2,4,2,16,128]{4,3,2,1,0:T(8,128)S(1)}, u32[]{:S(2)}, u32[]{:S(2)}) collective-permute-start(f32[2,4,2,16,128]{4,3,2,1,0:T(8,128)S(1)} %get-tuple-element.47), channel_id=1, source_target_pairs={{0,10},{2,8},{4,14},{6,12},{8,2},{10,0},{12,6},{14,4},{1,11},{3,9}... | collective-permute-start | bytes 393224 | tf_op jit(solution)/shard_map/ppermute | solution.py:348
  42.0 14.2 %collective-permute-start.12 = (f32[2,4,2,16,128]{4,3,2,1,0:T(8,128)S(1)}, f32[2,4,2,16,128]{4,3,2,1,0:T(8,128)S(1)}, u32[]{:S(2)}, u32[]{:S(2)}) collective-permute-start(f32[2,4,2,16,128]{4,3,2,1,0:T(8,128)S(1)} %get-tuple-element.48), channel_id=1, source_target_pairs={{0,8},{2,10},{4,12},{6,14},{8,0},{10,2},{12,4},{14,6},{1,9},{3,11}... | collective-permute-start | bytes 393224 | tf_op jit(solution)/shard_map/ppermute | solution.py:348
  43.9 12.4 %collective-permute-start.13 = (f32[2,4,2,16,128]{4,3,2,1,0:T(8,128)S(1)}, f32[2,4,2,16,128]{4,3,2,1,0:T(8,128)S(1)}, u32[]{:S(2)}, u32[]{:S(2)}) collective-permute-start(f32[2,4,2,16,128]{4,3,2,1,0:T(8,128)S(1)} %get-tuple-element.49), channel_id=1, source_target_pairs={{0,2},{2,0},{4,6},{6,4},{8,10},{10,8},{12,14},{14,12},{1,3},{3,1},... | collective-permute-start | bytes 393224 | tf_op jit(solution)/shard_map/ppermute | solution.py:348
  57.5 2.0 %collective-permute-start.14 = (f32[2,512,128]{2,1,0:T(8,128)S(1)}, f32[2,512,128]{2,1,0:T(8,128)S(1)}, u32[]{:S(2)}, u32[]{:S(2)}) collective-permute-start(f32[2,512,128]{2,1,0:T(8,128)S(1)} %second_section_sent.1), channel_id=1, source_target_pairs={{0,1},{1,0},{2,3},{3,2},{4,5},{5,4},{6,7},{7,6},{8,9},{9,8},{10,11... | collective-permute-start | bytes 1572872 | tf_op jit(solution)/shard_map/ppermute | solution.py:400

commit v7 on v5

--- a/solution.py
+++ b/solution.py
@@ -12,6 +12,7 @@
 BF16 = jnp.bfloat16
 VMEM_LIMIT = 14 * 1024 * 1024
 LARGE_VMEM = 48 * 1024 * 1024
+PIECES = 4
 
 
 def window_offsets(span, gate_bits):
@@ -118,9 +119,11 @@
     for section in sections:
         for base, _, parts in section:
             target = next(targets)
-            target[0], target[1] = split(block(*(joined(base, parts) if len(parts) > 1 else product(parts[0][1]))))
+            high, rest = split(block(*(joined(base, parts) if len(parts) > 1 else product(parts[0][1]))))
+            target[...] = jnp.concatenate([high, rest, high], axis=1)
     real, imag = product(low)
-    low_ref[0], low_ref[1] = split(block(real.T, -imag.T))
+    high, rest = split(block(real.T, -imag.T))
+    low_ref[...] = jnp.concatenate([high, rest, high], axis=0)
 
 
 def distances_of(count):
@@ -143,15 +146,14 @@
 
 
 def apply_stage(weights_ref, starts, load, store):
-    dim = weights_ref.shape[-1] // 2
-    high_w, rest_w = weights_ref[0], weights_ref[1]
+    dim = weights_ref.shape[0] // 2
     for pair in range(0, len(starts), 2):
         group = starts[pair : pair + 2]
         x = jnp.concatenate(
             [jnp.concatenate([load(part, start) for start in group], axis=1) for part in range(2)], axis=0
         )
         high, rest = split(x)
-        y = bf_dot(high_w, rest) + bf_dot(rest_w, high) + bf_dot(high_w, high)
+        y = bf_dot(weights_ref[...], jnp.concatenate([rest, high, high], axis=0))
         lanes = y.shape[1] // len(group)
         for part in range(2):
             for place, start in enumerate(group):
@@ -213,7 +215,7 @@
         real = block_ref[pl.ds(0, size, stride=2), :]
         imag = block_ref[pl.ds(1, size, stride=2), :]
         high, rest = split(jnp.concatenate([real, imag], axis=1))
-        y = bf_dot(rest, low_ref[0]) + bf_dot(high, low_ref[1]) + bf_dot(high, low_ref[0])
+        y = bf_dot(jnp.concatenate([rest, high, high], axis=1), low_ref[...])
         whole[0, pl.ds(start, size), :] = y[:, :lanes]
         whole[1, pl.ds(start, size), :] = y[:, lanes:]
     run_top_stage(stages[0], weights[0], lane_bits, whole, halves[:2])
@@ -262,8 +264,13 @@
             results[t][pl.ds(2 * start + part, dim, stride=2 * stride), :] = value
 
         run_stage(stages[-1], weights[-1], lane_bits, done[t], store=store)
-        copies.append(pltpu.make_async_copy(results[t], out_ref.at[pl.ds(t * 2 * half, 2 * half)], sems.at[t]))
-        copies[-1].start()
+        size = 2 * half // PIECES
+        for piece in range(PIECES):
+            to = out_ref.at[pl.ds(t * 2 * half + piece * size, size)]
+            copies.append(
+                pltpu.make_async_copy(results[t].at[pl.ds(piece * size, size)], to, sems.at[t * PIECES + piece])
+            )
+            copies[-1].start()
     for copy in copies:
         copy.wait()
 
@@ -323,8 +330,8 @@
     low_w, *weights = call(
         functools.partial(prepare_kernel, low, sections),
         "prepare_gates",
-        (shape((2, order, order), BF16),)
-        + tuple(shape((2, 2 * 2**bits, 2 * 2**bits), BF16) for section in sections for _, bits, _ in section),
+        (shape((3 * order, order), BF16),)
+        + tuple(shape((2 * 2**bits, 6 * 2**bits), BF16) for section in sections for _, bits, _ in section),
         [pl.BlockSpec(memory_space=pltpu.SMEM), hbm],
         [
             pltpu.VMEM((gate_terms.shape[0], 2, dim, dim), F32),
@@ -374,7 +381,7 @@
         "third_section",
         shape((2 * rows, lanes), F32),
         [vmem] * (2 + counts[2]),
-        [whole] + [half] * 4 + [pltpu.VMEM((rows, lanes), F32)] * 2 + [pltpu.SemaphoreType.DMA((2,))],
+        [whole] + [half] * 4 + [pltpu.VMEM((rows, lanes), F32)] * 2 + [pltpu.SemaphoreType.DMA((2 * PIECES,))],
         4,
         halves[1],
         came,

time: 62.2 us -> 62 us (level)
  waiting for transfers between devices: 13.9 us -> 12.8 us
  starting transfers between devices: 30.8 us -> 31.6 us
    ppermute x14, waiting for transfers between devices: 13 us -> 11.9 us  [exchange(): lax.ppermute(piece, 'qa', [(i, i ^ distance) for i in range(qa)])]
    ppermute x14, starting transfers between devices: 30.7 us -> 31.5 us  [exchange(): lax.ppermute(piece, 'qa', [(i, i ^ distance) for i in range(qa)])]
    unnamed x4 -> x6, local copies, waits for them, and re-layouts: 1.88 us -> 1.88 us
  transfers between devices with their start and end apart: 15 -> 15, of which waited for: 9 -> 8; matrix products, arithmetic and copies ran while one was open for 0% -> 0% of each run, Pallas kernels for 13% -> 14%
where the time goes in v7:
time: 62 us; the launch traced here: 61.8 us
  starting transfers between devices  31.6 us (51%)
  Pallas kernels  15.4 us (25%)
  waiting for transfers between devices  12.8 us (21%)
  local copies, waits for them, and re-layouts  1.88 us (3%)
    ppermute x14, starting transfers between devices, exchange(): lax.ppermute(piece, 'qa', [(i, i ^ distance) for i in range(qa)])  31.5 us
    pallas_call x6, Pallas kernels, call(): pl.pallas_call(kernel, out_shape=out_shapes, in_specs=in_specs, out_specs...  15.4 us
    ppermute x14, waiting for transfers between devices, exchange(): lax.ppermute(piece, 'qa', [(i, i ^ distance) for i in range(qa)])  11.9 us
    unnamed x6, local copies, waits for them, and re-layouts  1.88 us
  transfers between devices with their start and end apart: 15, of which 8 were waited for; matrix products, arithmetic and copies ran while one was open for 0% of the time, Pallas kernels for 14%

profile of v7, /device:TPU:0, one launch (start us, length us, event | category | flops | bytes accessed | tf_op | source)
XLA Modules:
  0.0 61.8 jit_solution(5636478952171700186)
XLA Ops:
  0.0 1.2 %copy-done = f32[2,131072]{1,0:T(2,128)S(1)} copy-done((f32[2,131072]{1,0:T(2,128)S(1)}, f32[2,131072]{1,0:T(2,128)}, u32[]{:S(2)}) %copy-start) | copy-done | bytes 1048600
  1.2 0.1 split_state.1
  1.3 6.1 %collective-permute-start = (f32[256,128]{1,0:T(8,128)S(1)}, f32[256,128]{1,0:T(8,128)S(1)}, u32[]{:S(2)}, u32[]{:S(2)}) collective-permute-start(f32[256,128]{1,0:T(8,128)S(1)} %get-tuple-element.31), channel_id=1, source_target_pairs={{0,14},{2,12},{4,10},{6,8},{8,6},{10,4},{12,2},{14,0},{1,15},{3,13... | collective-permute-start | bytes 393224 | tf_op jit(solution)/shard_map/ppermute | solution.py:326
  7.4 0.2 collective-permute-start.1
  7.6 0.0 collective-permute-start.2
  7.6 1.9 %collective-permute-start.3 = (f32[256,128]{1,0:T(8,128)S(1)}, f32[256,128]{1,0:T(8,128)S(1)}, u32[]{:S(2)}, u32[]{:S(2)}) collective-permute-start(f32[256,128]{1,0:T(8,128)S(1)} %get-tuple-element.34), channel_id=1, source_target_pairs={{0,4},{2,6},{4,0},{6,2},{8,12},{10,14},{12,8},{14,10},{1,5},{3,7},... | collective-permute-start | bytes 393224 | tf_op jit(solution)/shard_map/ppermute | solution.py:326
  9.5 3.2 %collective-permute-start.4 = (f32[256,128]{1,0:T(8,128)S(1)}, f32[256,128]{1,0:T(8,128)S(1)}, u32[]{:S(2)}, u32[]{:S(2)}) collective-permute-start(f32[256,128]{1,0:T(8,128)S(1)} %get-tuple-element.35), channel_id=1, source_target_pairs={{0,10},{2,8},{4,14},{6,12},{8,2},{10,0},{12,6},{14,4},{1,11},{3,9}... | collective-permute-start | bytes 393224 | tf_op jit(solution)/shard_map/ppermute | solution.py:326
  12.7 0.0 collective-permute-done.refs_1_
  12.7 5.6 %collective-permute-start.5 = (f32[256,128]{1,0:T(8,128)S(1)}, f32[256,128]{1,0:T(8,128)S(1)}, u32[]{:S(2)}, u32[]{:S(2)}) collective-permute-start(f32[256,128]{1,0:T(8,128)S(1)} %get-tuple-element.36), channel_id=1, source_target_pairs={{0,8},{2,10},{4,12},{6,14},{8,0},{10,2},{12,4},{14,6},{1,9},{3,11}... | collective-permute-start | bytes 393224 | tf_op jit(solution)/shard_map/ppermute | solution.py:326
  18.3 0.0 collective-permute-done.1.refs_2_
  18.3 1.5 %collective-permute-start.6 = (f32[256,128]{1,0:T(8,128)S(1)}, f32[256,128]{1,0:T(8,128)S(1)}, u32[]{:S(2)}, u32[]{:S(2)}) collective-permute-start(f32[256,128]{1,0:T(8,128)S(1)} %get-tuple-element.37), channel_id=1, source_target_pairs={{0,2},{2,0},{4,6},{6,4},{8,10},{10,8},{12,14},{14,12},{1,3},{3,1},... | collective-permute-start | bytes 393224 | tf_op jit(solution)/shard_map/ppermute | solution.py:326
  19.8 0.7 %copy-done.1 = s32[18]{0:T(128)S(1)} copy-done((s32[18]{0:T(128)S(1)}, s32[18]{0:T(128)}, u32[]{:S(2)}) %copy-start.1) | copy-done | bytes 96
  20.5 7.4 %prepare_gates.1 = (bf16[768,256]{1,0:T(8,128)(2,1)S(1)}, bf16[256,768]{1,0:T(8,128)(2,1)S(1)}, bf16[256,768]{1,0:T(8,128)(2,1)S(1)}, bf16[512,1536]{1,0:T(8,128...) custom-call(s32[18]{0:T(128)S(1)} %copy-done.1, ...), custom_call_target="tpu_custom_call" | custom-call | flops 3221225472 | bytes 4194304 | tf_op jit(solution)/shard_map/prepare_gates/pallas_call | solution.py:281
  27.9 1.7 %collective-permute-done.5.refs_6_ = f32[256,128]{1,0:T(8,128)S(1)} collective-permute-done((f32[256,128]{1,0:T(8,128)S(1)}, f32[256,128]{1,0:T(8,128)S(1)}, u32[]{:S(2)}, u32[]{:S(2)}) %collective-permute-start.5) | collective-permute-done | bytes 131104 | tf_op jit(solution)/shard_map/ppermute | solution.py:326
  29.7 2.8 %first_section.1 = (f32[2,4,2,16,128]{4,3,2,1,0:T(8,128)S(1)}, f32[2,4,2,16,128]{4,3,2,1,0:T(8,128)S(1)}, f32[2,4,2,16,128]{4,3,2,1,0:T(8,128)S(1)}, f32[2,4,2,1...) custom-call(f32[256,128]{1,0:T(8,128)S(1)} %get-tuple-element.30.ref, ...), custom_call_target="tpu_custom_call" | custom-call | flops 2013265920 | bytes 4194304 | tf_op jit(solution)/shard_map/first_section/pallas_call | solution.py:281
  32.5 2.5 %collective-permute-start.7 = (f32[2,4,2,16,128]{4,3,2,1,0:T(8,128)S(1)}, f32[2,4,2,16,128]{4,3,2,1,0:T(8,128)S(1)}, u32[]{:S(2)}, u32[]{:S(2)}) collective-permute-start(f32[2,4,2,16,128]{4,3,2,1,0:T(8,128)S(1)} %get-tuple-element.43), channel_id=1, source_target_pairs={{0,14},{2,12},{4,10},{6,8},{8,6},{10,4},{12,2},{14,0},{1,15},{3,13... | collective-permute-start | bytes 393224 | tf_op jit(solution)/shard_map/ppermute | solution.py:326
  35.0 1.3 %collective-permute-start.8 = (f32[2,4,2,16,128]{4,3,2,1,0:T(8,128)S(1)}, f32[2,4,2,16,128]{4,3,2,1,0:T(8,128)S(1)}, u32[]{:S(2)}, u32[]{:S(2)}) collective-permute-start(f32[2,4,2,16,128]{4,3,2,1,0:T(8,128)S(1)} %get-tuple-element.44), channel_id=1, source_target_pairs={{0,12},{2,14},{4,8},{6,10},{8,4},{10,6},{12,0},{14,2},{1,13},{3,15... | collective-permute-start | bytes 393224 | tf_op jit(solution)/shard_map/ppermute | solution.py:326
  36.3 3.0 %collective-permute-start.10 = (f32[2,4,2,16,128]{4,3,2,1,0:T(8,128)S(1)}, f32[2,4,2,16,128]{4,3,2,1,0:T(8,128)S(1)}, u32[]{:S(2)}, u32[]{:S(2)}) collective-permute-start(f32[2,4,2,16,128]{4,3,2,1,0:T(8,128)S(1)} %get-tuple-element.46), channel_id=1, source_target_pairs={{0,4},{2,6},{4,0},{6,2},{8,12},{10,14},{12,8},{14,10},{1,5},{3,7},... | collective-permute-start | bytes 393224 | tf_op jit(solution)/shard_map/ppermute | solution.py:326
  39.3 1.0 %collective-permute-start.11 = (f32[2,4,2,16,128]{4,3,2,1,0:T(8,128)S(1)}, f32[2,4,2,16,128]{4,3,2,1,0:T(8,128)S(1)}, u32[]{:S(2)}, u32[]{:S(2)}) collective-permute-start(f32[2,4,2,16,128]{4,3,2,1,0:T(8,128)S(1)} %get-tuple-element.47), channel_id=1, source_target_pairs={{0,10},{2,8},{4,14},{6,12},{8,2},{10,0},{12,6},{14,4},{1,11},{3,9}... | collective-permute-start | bytes 393224 | tf_op jit(solution)/shard_map/ppermute | solution.py:326
  40.3 1.1 %collective-permute-done.7.refs_1_ = f32[2,4,2,16,128]{4,3,2,1,0:T(8,128)S(1)} collective-permute-done((f32[2,4,2,16,128]{4,3,2,1,0:T(8,128)S(1)}, f32[2,4,2,16,128]{4,3,2,1,0:T(8,128)S(1)}, u32[]{:S(2)}, u32[]{:S(2)}) %collective-permute-start.7) | collective-permute-done | bytes 131104 | tf_op jit(solution)/shard_map/ppermute | solution.py:326
  41.4 1.8 %collective-permute-start.12 = (f32[2,4,2,16,128]{4,3,2,1,0:T(8,128)S(1)}, f32[2,4,2,16,128]{4,3,2,1,0:T(8,128)S(1)}, u32[]{:S(2)}, u32[]{:S(2)}) collective-permute-start(f32[2,4,2,16,128]{4,3,2,1,0:T(8,128)S(1)} %get-tuple-element.48), channel_id=1, source_target_pairs={{0,8},{2,10},{4,12},{6,14},{8,0},{10,2},{12,4},{14,6},{1,9},{3,11}... | collective-permute-start | bytes 393224 | tf_op jit(solution)/shard_map/ppermute | solution.py:326
  43.2 0.1 collective-permute-done.8.refs_2_
  43.3 3.4 %collective-permute-start.13 = (f32[2,4,2,16,128]{4,3,2,1,0:T(8,128)S(1)}, f32[2,4,2,16,128]{4,3,2,1,0:T(8,128)S(1)}, u32[]{:S(2)}, u32[]{:S(2)}) collective-permute-start(f32[2,4,2,16,128]{4,3,2,1,0:T(8,128)S(1)} %get-tuple-element.49), channel_id=1, source_target_pairs={{0,2},{2,0},{4,6},{6,4},{8,10},{10,8},{12,14},{14,12},{1,3},{3,1},... | collective-permute-start | bytes 393224 | tf_op jit(solution)/shard_map/ppermute | solution.py:326
  46.7 1.8 %collective-permute-done.9.refs_3_ = f32[2,4,2,16,128]{4,3,2,1,0:T(8,128)S(1)} collective-permute-done((f32[2,4,2,16,128]{4,3,2,1,0:T(8,128)S(1)}, f32[2,4,2,16,128]{4,3,2,1,0:T(8,128)S(1)}, u32[]{:S(2)}, u32[]{:S(2)}) %collective-permute-start.9) | collective-permute-done | bytes 131104 | tf_op jit(solution)/shard_map/ppermute | solution.py:326
  48.5 2.6 %collective-permute-done.10.refs_4_ = f32[2,4,2,16,128]{4,3,2,1,0:T(8,128)S(1)} collective-permute-done((f32[2,4,2,16,128]{4,3,2,1,0:T(8,128)S(1)}, f32[2,4,2,16,128]{4,3,2,1,0:T(8,128)S(1)}, u32[]{:S(2)}, u32[]{:S(2)}) %collective-permute-start.10) | collective-permute-done | bytes 131104 | tf_op jit(solution)/shard_map/ppermute | solution.py:326
  51.1 4.1 %collective-permute-done.11.refs_5_ = f32[2,4,2,16,128]{4,3,2,1,0:T(8,128)S(1)} collective-permute-done((f32[2,4,2,16,128]{4,3,2,1,0:T(8,128)S(1)}, f32[2,4,2,16,128]{4,3,2,1,0:T(8,128)S(1)}, u32[]{:S(2)}, u32[]{:S(2)}) %collective-permute-start.11) | collective-permute-done | bytes 131104 | tf_op jit(solution)/shard_map/ppermute | solution.py:326
  55.2 0.5 collective-permute-done.12.refs_6_
  55.6 1.0 %second_section_sent.1 = f32[2,512,128]{2,1,0:T(8,128)S(1)} custom-call(f32[2,4,2,16,128]{4,3,2,1,0:T(8,128)S(1)} %get-tuple-element.42.refs_0_, f32[2,4,2,16,128]{4,3,2,1,0:T(8,128)S(1)} %collective-permute-done.7.refs_1_, f32[2,4,2,16,128]{4,3,2,1,0:T(8,128)S(1)} %collective-permute-done.8.refs_2_, ...), custom_call_target="tpu_custom_call" | custom-call | flops 603979776 | bytes 4194304 | tf_op jit(solution)/shard_map/second_section_sent/pallas_call | solution.py:281
  56.7 0.1 collective-permute-start.14
  56.7 1.0 %second_section_kept.1.kept_ref = f32[2,512,128]{2,1,0:T(8,128)S(1)} custom-call(f32[2,4,2,16,128]{4,3,2,1,0:T(8,128)S(1)} %get-tuple-element.42.refs_0_, f32[2,4,2,16,128]{4,3,2,1,0:T(8,128)S(1)} %collective-permute-done.7.refs_1_, f32[2,4,2,16,128]{4,3,2,1,0:T(8,128)S(1)} %collective-permute-done.8.refs_2_, ...), custom_call_target="tpu_custom_call" | custom-call | flops 603979776 | bytes 4194304 | tf_op jit(solution)/shard_map/second_section_kept/pallas_call | solution.py:281
  57.7 0.9 %collective-permute-done.14.came_ref = f32[2,512,128]{2,1,0:T(8,128)S(1)} collective-permute-done((f32[2,512,128]{2,1,0:T(8,128)S(1)}, f32[2,512,128]{2,1,0:T(8,128)S(1)}, u32[]{:S(2)}, u32[]{:S(2)}) %collective-permute-start.14) | collective-permute-done | bytes 524320 | tf_op jit(solution)/shard_map/ppermute | solution.py:378
  58.6 3.2 %third_section.1 = f32[2048,128]{1,0:T(8,128)} custom-call(f32[2,512,128]{2,1,0:T(8,128)S(1)} %second_section_kept.1.kept_ref, f32[2,512,128]{2,1,0:T(8,128)S(1)} %collective-permute-done.14.came_ref, bf16[256,768]{1,0:T(8,128)(2,1)S(1)} %get-tuple-element.52.refs_0_, bf16[256,768]{1,0:T(8,128)(2,1)S(1)} %get-tuple-element.53.refs_1_, ...), custom_call_target="tpu_custom_call" | custom-call | flops 1610612736 | bytes 4194304 | tf_op jit(solution)/shard_map/third_section/pallas_call | solution.py:281
  (10 shorter events, 0.0 us)
Async XLA Ops:
  0.0 1.2 %copy-start = (f32[2,131072]{1,0:T(2,128)S(1)}, f32[2,131072]{1,0:T(2,128)}, u32[]{:S(2)}) copy-start(f32[2,131072]{1,0:T(2,128)} %param.3) | copy-start | bytes 3145732
  1.3 11.4 %collective-permute-start = (f32[256,128]{1,0:T(8,128)S(1)}, f32[256,128]{1,0:T(8,128)S(1)}, u32[]{:S(2)}, u32[]{:S(2)}) collective-permute-start(f32[256,128]{1,0:T(8,128)S(1)} %get-tuple-element.31), channel_id=1, source_target_pairs={{0,14},{2,12},{4,10},{6,8},{8,6},{10,4},{12,2},{14,0},{1,15},{3,13... | collective-permute-start | bytes 393224 | tf_op jit(solution)/shard_map/ppermute | solution.py:326
  7.4 10.9 %collective-permute-start.1 = (f32[256,128]{1,0:T(8,128)S(1)}, f32[256,128]{1,0:T(8,128)S(1)}, u32[]{:S(2)}, u32[]{:S(2)}) collective-permute-start(f32[256,128]{1,0:T(8,128)S(1)} %get-tuple-element.32), channel_id=1, source_target_pairs={{0,12},{2,14},{4,8},{6,10},{8,4},{10,6},{12,0},{14,2},{1,13},{3,15... | collective-permute-start | bytes 393224 | tf_op jit(solution)/shard_map/ppermute | solution.py:326
  7.6 20.3 %collective-permute-start.2 = (f32[256,128]{1,0:T(8,128)S(1)}, f32[256,128]{1,0:T(8,128)S(1)}, u32[]{:S(2)}, u32[]{:S(2)}) collective-permute-start(f32[256,128]{1,0:T(8,128)S(1)} %get-tuple-element.33), channel_id=1, source_target_pairs={{0,6},{2,4},{4,2},{6,0},{8,14},{10,12},{12,10},{14,8},{1,7},{3,5},... | collective-permute-start | bytes 393224 | tf_op jit(solution)/shard_map/ppermute | solution.py:326
  7.6 20.3 %collective-permute-start.3 = (f32[256,128]{1,0:T(8,128)S(1)}, f32[256,128]{1,0:T(8,128)S(1)}, u32[]{:S(2)}, u32[]{:S(2)}) collective-permute-start(f32[256,128]{1,0:T(8,128)S(1)} %get-tuple-element.34), channel_id=1, source_target_pairs={{0,4},{2,6},{4,0},{6,2},{8,12},{10,14},{12,8},{14,10},{1,5},{3,7},... | collective-permute-start | bytes 393224 | tf_op jit(solution)/shard_map/ppermute | solution.py:326
  9.5 18.5 %collective-permute-start.4 = (f32[256,128]{1,0:T(8,128)S(1)}, f32[256,128]{1,0:T(8,128)S(1)}, u32[]{:S(2)}, u32[]{:S(2)}) collective-permute-start(f32[256,128]{1,0:T(8,128)S(1)} %get-tuple-element.35), channel_id=1, source_target_pairs={{0,10},{2,8},{4,14},{6,12},{8,2},{10,0},{12,6},{14,4},{1,11},{3,9}... | collective-permute-start | bytes 393224 | tf_op jit(solution)/shard_map/ppermute | solution.py:326
  12.7 17.0 %collective-permute-start.5 = (f32[256,128]{1,0:T(8,128)S(1)}, f32[256,128]{1,0:T(8,128)S(1)}, u32[]{:S(2)}, u32[]{:S(2)}) collective-permute-start(f32[256,128]{1,0:T(8,128)S(1)} %get-tuple-element.36), channel_id=1, source_target_pairs={{0,8},{2,10},{4,12},{6,14},{8,0},{10,2},{12,4},{14,6},{1,9},{3,11}... | collective-permute-start | bytes 393224 | tf_op jit(solution)/shard_map/ppermute | solution.py:326
  18.3 11.4 %collective-permute-start.6 = (f32[256,128]{1,0:T(8,128)S(1)}, f32[256,128]{1,0:T(8,128)S(1)}, u32[]{:S(2)}, u32[]{:S(2)}) collective-permute-start(f32[256,128]{1,0:T(8,128)S(1)} %get-tuple-element.37), channel_id=1, source_target_pairs={{0,2},{2,0},{4,6},{6,4},{8,10},{10,8},{12,14},{14,12},{1,3},{3,1},... | collective-permute-start | bytes 393224 | tf_op jit(solution)/shard_map/ppermute | solution.py:326
  19.8 0.7 %copy-start.1 = (s32[18]{0:T(128)S(1)}, s32[18]{0:T(128)}, u32[]{:S(2)}) copy-start(s32[18]{0:T(128)} %bits_ref.1) | copy-start | bytes 220
  32.5 8.9 %collective-permute-start.7 = (f32[2,4,2,16,128]{4,3,2,1,0:T(8,128)S(1)}, f32[2,4,2,16,128]{4,3,2,1,0:T(8,128)S(1)}, u32[]{:S(2)}, u32[]{:S(2)}) collective-permute-start(f32[2,4,2,16,128]{4,3,2,1,0:T(8,128)S(1)} %get-tuple-element.43), channel_id=1, source_target_pairs={{0,14},{2,12},{4,10},{6,8},{8,6},{10,4},{12,2},{14,0},{1,15},{3,13... | collective-permute-start | bytes 393224 | tf_op jit(solution)/shard_map/ppermute | solution.py:326
  35.0 8.3 %collective-permute-start.8 = (f32[2,4,2,16,128]{4,3,2,1,0:T(8,128)S(1)}, f32[2,4,2,16,128]{4,3,2,1,0:T(8,128)S(1)}, u32[]{:S(2)}, u32[]{:S(2)}) collective-permute-start(f32[2,4,2,16,128]{4,3,2,1,0:T(8,128)S(1)} %get-tuple-element.44), channel_id=1, source_target_pairs={{0,12},{2,14},{4,8},{6,10},{8,4},{10,6},{12,0},{14,2},{1,13},{3,15... | collective-permute-start | bytes 393224 | tf_op jit(solution)/shard_map/ppermute | solution.py:326
  36.3 12.2 %collective-permute-start.9 = (f32[2,4,2,16,128]{4,3,2,1,0:T(8,128)S(1)}, f32[2,4,2,16,128]{4,3,2,1,0:T(8,128)S(1)}, u32[]{:S(2)}, u32[]{:S(2)}) collective-permute-start(f32[2,4,2,16,128]{4,3,2,1,0:T(8,128)S(1)} %get-tuple-element.45), channel_id=1, source_target_pairs={{0,6},{2,4},{4,2},{6,0},{8,14},{10,12},{12,10},{14,8},{1,7},{3,5},... | collective-permute-start | bytes 393224 | tf_op jit(solution)/shard_map/ppermute | solution.py:326
  36.3 14.8 %collective-permute-start.10 = (f32[2,4,2,16,128]{4,3,2,1,0:T(8,128)S(1)}, f32[2,4,2,16,128]{4,3,2,1,0:T(8,128)S(1)}, u32[]{:S(2)}, u32[]{:S(2)}) collective-permute-start(f32[2,4,2,16,128]{4,3,2,1,0:T(8,128)S(1)} %get-tuple-element.46), channel_id=1, source_target_pairs={{0,4},{2,6},{4,0},{6,2},{8,12},{10,14},{12,8},{14,10},{1,5},{3,7},... | collective-permute-start | bytes 393224 | tf_op jit(solution)/shard_map/ppermute | solution.py:326
  39.3 15.9 %collective-permute-start.11 = (f32[2,4,2,16,128]{4,3,2,1,0:T(8,128)S(1)}, f32[2,4,2,16,128]{4,3,2,1,0:T(8,128)S(1)}, u32[]{:S(2)}, u32[]{:S(2)}) collective-permute-start(f32[2,4,2,16,128]{4,3,2,1,0:T(8,128)S(1)} %get-tuple-element.47), channel_id=1, source_target_pairs={{0,10},{2,8},{4,14},{6,12},{8,2},{10,0},{12,6},{14,4},{1,11},{3,9}... | collective-permute-start | bytes 393224 | tf_op jit(solution)/shard_map/ppermute | solution.py:326
  41.4 14.2 %collective-permute-start.12 = (f32[2,4,2,16,128]{4,3,2,1,0:T(8,128)S(1)}, f32[2,4,2,16,128]{4,3,2,1,0:T(8,128)S(1)}, u32[]{:S(2)}, u32[]{:S(2)}) collective-permute-start(f32[2,4,2,16,128]{4,3,2,1,0:T(8,128)S(1)} %get-tuple-element.48), channel_id=1, source_target_pairs={{0,8},{2,10},{4,12},{6,14},{8,0},{10,2},{12,4},{14,6},{1,9},{3,11}... | collective-permute-start | bytes 393224 | tf_op jit(solution)/shard_map/ppermute | solution.py:326
  43.3 12.3 %collective-permute-start.13 = (f32[2,4,2,16,128]{4,3,2,1,0:T(8,128)S(1)}, f32[2,4,2,16,128]{4,3,2,1,0:T(8,128)S(1)}, u32[]{:S(2)}, u32[]{:S(2)}) collective-permute-start(f32[2,4,2,16,128]{4,3,2,1,0:T(8,128)S(1)} %get-tuple-element.49), channel_id=1, source_target_pairs={{0,2},{2,0},{4,6},{6,4},{8,10},{10,8},{12,14},{14,12},{1,3},{3,1},... | collective-permute-start | bytes 393224 | tf_op jit(solution)/shard_map/ppermute | solution.py:326
  56.6 2.0 %copy-start.2 = (bf16[512,1536]{1,0:T(8,128)(2,1)S(1)}, bf16[512,1536]{1,0:T(8,128)(2,1)}, u32[]{:S(2)}) copy-start(bf16[512,1536]{1,0:T(8,128)(2,1)} %get-tuple-element.54.refs_2_) | copy-start | bytes 4718596
  56.7 2.0 %collective-permute-start.14 = (f32[2,512,128]{2,1,0:T(8,128)S(1)}, f32[2,512,128]{2,1,0:T(8,128)S(1)}, u32[]{:S(2)}, u32[]{:S(2)}) collective-permute-start(f32[2,512,128]{2,1,0:T(8,128)S(1)} %second_section_sent.1), channel_id=1, source_target_pairs={{0,1},{1,0},{2,3},{3,2},{4,5},{5,4},{6,7},{7,6},{8,9},{9,8},{10,11... | collective-permute-start | bytes 1572872 | tf_op jit(solution)/shard_map/ppermute | solution.py:378

commit v8 on v7

--- a/solution.py
+++ b/solution.py
@@ -78,7 +78,22 @@
     )
 
 
-def prepare_kernel(low, sections, bits_ref, gates_ref, low_ref, *refs):
+def relative(matrix, number, count):
+    dim = matrix.shape[1]
+    column = lax.broadcasted_iota(jnp.int32, matrix.shape, 1)
+    row = lax.broadcasted_iota(jnp.int32, matrix.shape, 0)
+    if number == 0:
+        size = dim // count
+        spot, source = column // size, jnp.zeros_like(column)
+        for index, distance in enumerate(distances_of(count)):
+            source = jnp.where(spot == index, partner(distance), source)
+        natural = source * size + lax.rem(column, size)
+    else:
+        natural = jnp.bitwise_xor(column, lax.axis_index("qb") * (dim // 2))
+    return exact_dot(matrix, jnp.where(row == natural, 1.0, 0.0).astype(F32))
+
+
+def prepare_kernel(low, sections, count, bits_ref, gates_ref, low_ref, *refs):
     *targets, held, wide, sems = refs
     copies = []
     for gate in range(held.shape[0]):
@@ -115,12 +130,18 @@
                             wide[p, c, at, :] = y[p * dim : (p + 1) * dim, c * dim : (c + 1) * dim]
         return [jnp.concatenate([wide[p, 0], wide[p, 1]], axis=1) for p in range(2)]
 
-    targets = iter(targets)
-    for section in sections:
-        for base, _, parts in section:
-            target = next(targets)
-            high, rest = split(block(*(joined(base, parts) if len(parts) > 1 else product(parts[0][1]))))
-            target[...] = jnp.concatenate([high, rest, high], axis=1)
+    for number, section in enumerate(sections):
+        weights, targets = targets[: len(section)], targets[len(section) :]
+        for target, (base, _, parts) in zip(weights, section):
+            if len(parts) > 1:
+                high, rest = split(block(*joined(base, parts)))
+                target[...] = jnp.concatenate([high, rest, high], axis=1)
+                continue
+            pair = product(parts[0][1])
+            if number != 1 and target is weights[0]:
+                pair = [relative(x, number, count) for x in pair]
+            high, rest = split(block(*pair))
+            target[...] = jnp.concatenate([high, rest], axis=0)
     real, imag = product(low)
     high, rest = split(block(real.T, -imag.T))
     low_ref[...] = jnp.concatenate([high, rest, high], axis=0)
@@ -146,14 +167,19 @@
 
 
 def apply_stage(weights_ref, starts, load, store):
-    dim = weights_ref.shape[0] // 2
+    stacked = weights_ref.shape[0] > weights_ref.shape[1]
+    dim = weights_ref.shape[1] // 2 if stacked else weights_ref.shape[0] // 2
     for pair in range(0, len(starts), 2):
         group = starts[pair : pair + 2]
         x = jnp.concatenate(
             [jnp.concatenate([load(part, start) for start in group], axis=1) for part in range(2)], axis=0
         )
         high, rest = split(x)
-        y = bf_dot(weights_ref[...], jnp.concatenate([rest, high, high], axis=0))
+        if stacked:
+            both = bf_dot(weights_ref[...], high)
+            y = bf_dot(weights_ref[: 2 * dim], rest) + both[2 * dim :] + both[: 2 * dim]
+        else:
+            y = bf_dot(weights_ref[...], jnp.concatenate([rest, high, high], axis=0))
         lanes = y.shape[1] // len(group)
         for part in range(2):
             for place, start in enumerate(group):
@@ -184,13 +210,19 @@
 
 
 def run_top_stage(stage, weights_ref, lane_bits, source, halves):
-    dim, stride, starts = stage_starts(stage, lane_bits, source.shape[1])
+    rows = 2 * halves[0].shape[1]
+    dim, stride, starts = stage_starts(stage, lane_bits, rows)
 
     def store(part, start, value):
         for t in range(2):
             halves[t][part, pl.ds(start, dim // 2, stride=stride), :] = value[t * dim // 2 : (t + 1) * dim // 2]
 
-    apply_stage(weights_ref, starts, lambda part, start: source[part, pl.ds(start, dim, stride=stride), :], store)
+    def load(part, start):
+        if not isinstance(source, tuple):
+            return source[part, pl.ds(start, dim, stride=stride), :]
+        return jnp.concatenate([half[part, pl.ds(start, dim // 2, stride=stride), :] for half in source], axis=0)
+
+    apply_stage(weights_ref, starts, load, store)
 
 
 def run_halves(stages, weights, lane_bits, halves, spares, last_store=None):
@@ -204,20 +236,29 @@
     return halves
 
 
-def first_kernel(stages, lane_bits, count, *refs):
-    blocks, refs = refs[:count], refs[count:]
-    low_ref, weights, refs = refs[0], refs[1 : 1 + len(stages)], refs[1 + len(stages) :]
-    outs, (whole, *halves) = refs[:count], refs[count:]
+def low_gate(blocks, low_ref, whole):
     lanes = whole.shape[2]
-    for distance, block_ref in zip(distances_of(count), blocks):
+    for spot, block_ref in blocks:
         size = block_ref.shape[0] // 2
-        start = pl.multiple_of(partner(distance) * size, size)
         real = block_ref[pl.ds(0, size, stride=2), :]
         imag = block_ref[pl.ds(1, size, stride=2), :]
         high, rest = split(jnp.concatenate([real, imag], axis=1))
         y = bf_dot(jnp.concatenate([rest, high, high], axis=1), low_ref[...])
-        whole[0, pl.ds(start, size), :] = y[:, :lanes]
-        whole[1, pl.ds(start, size), :] = y[:, lanes:]
+        whole[0, pl.ds(spot * size, size), :] = y[:, :lanes]
+        whole[1, pl.ds(spot * size, size), :] = y[:, lanes:]
+
+
+def low_kernel(spots, *refs):
+    *blocks, low_ref, whole = refs
+    low_gate(zip(spots, blocks), low_ref, whole)
+
+
+def first_kernel(stages, lane_bits, count, spots, *refs):
+    _, *blocks = refs[: 1 + len(spots)]
+    refs = refs[1 + len(spots) :]
+    low_ref, weights, refs = refs[0], refs[1 : 1 + len(stages)], refs[1 + len(stages) :]
+    outs, (whole, *halves) = refs[:count], refs[count:]
+    low_gate(zip(spots, blocks), low_ref, whole)
     run_top_stage(stages[0], weights[0], lane_bits, whole, halves[:2])
     done = run_halves(stages[1:], weights[1:], lane_bits, halves[:2], halves[2:])
     tops, mids, _, inner, _ = outs[0].shape
@@ -248,13 +289,10 @@
 
 
 def third_kernel(stages, lane_bits, kept_ref, came_ref, *refs):
-    weights, (out_ref, whole, *halves, sems) = refs[: len(stages)], refs[len(stages) :]
+    weights, (out_ref, *halves, sems) = refs[: len(stages)], refs[len(stages) :]
     results = halves[4:]
     half = kept_ref.shape[1]
-    core = lax.axis_index("qb")
-    whole[:, pl.ds(pl.multiple_of(core * half, half), half), :] = kept_ref[...]
-    whole[:, pl.ds(pl.multiple_of((1 - core) * half, half), half), :] = came_ref[...]
-    run_top_stage(stages[0], weights[0], lane_bits, whole, halves[:2])
+    run_top_stage(stages[0], weights[0], lane_bits, (kept_ref, came_ref), halves[:2])
     done = run_halves(stages[1:-1], weights[1:-1], lane_bits, halves[:2], halves[2:4])
     copies = []
     for t in range(2):
@@ -275,7 +313,7 @@
         copy.wait()
 
 
-def call(kernel, name, out_shapes, in_specs, scratch, matmuls, *operands, limit=VMEM_LIMIT, out_spec=None):
+def call(kernel, name, out_shapes, in_specs, scratch, matmuls, *operands, limit=VMEM_LIMIT, out_spec=None, aliases=None):
     many = isinstance(out_shapes, tuple)
     vmem = out_spec or pl.BlockSpec(memory_space=pltpu.VMEM)
     return pl.pallas_call(
@@ -284,6 +322,7 @@
         in_specs=in_specs,
         out_specs=(vmem,) * len(out_shapes) if many else vmem,
         scratch_shapes=scratch,
+        input_output_aliases=aliases or {},
         compiler_params=pltpu.CompilerParams(vmem_limit_bytes=limit),
         cost_estimate=pl.CostEstimate(
             flops=int(matmuls * 3 * 2 * 256 * 256 * 1024), bytes_accessed=4 * 2**20, transcendentals=0
@@ -320,6 +359,10 @@
         state,
     )
 
+    index = jnp.bitwise_xor(lax.axis_index("qa"), distances_of(qa)[1])
+    blocks = list(blocks)
+    blocks[1] = lax.dynamic_index_in_dim(state, index, 0, keepdims=False)
+
     def exchange(blocks):
         came = [blocks[0]]
         for distance, piece in zip(distances_of(qa)[1:], blocks[1:]):
@@ -328,10 +371,14 @@
 
     blocks = exchange(blocks)
     low_w, *weights = call(
-        functools.partial(prepare_kernel, low, sections),
+        functools.partial(prepare_kernel, low, sections, qa),
         "prepare_gates",
         (shape((3 * order, order), BF16),)
-        + tuple(shape((2 * 2**bits, 6 * 2**bits), BF16) for section in sections for _, bits, _ in section),
+        + tuple(
+            shape((2 * 2**bits, 6 * 2**bits) if len(parts) > 1 else (4 * 2**bits, 2 * 2**bits), BF16)
+            for section in sections
+            for _, bits, parts in section
+        ),
         [pl.BlockSpec(memory_space=pltpu.SMEM), hbm],
         [
             pltpu.VMEM((gate_terms.shape[0], 2, dim, dim), F32),
@@ -346,18 +393,32 @@
     counts = [len(section) for section in sections]
     weights = [weights[: counts[0]], weights[counts[0] : counts[0] + counts[1]], weights[counts[0] + counts[1] :]]
     inner = rows // (qa * qa)
-    whole = pltpu.VMEM((2, rows, lanes), F32)
     half = pltpu.VMEM((2, rows // 2, lanes), F32)
-    blocks = call(
-        functools.partial(first_kernel, sections[0], lane_bits, qa),
+    late = [spot for spot, distance in enumerate(distances_of(qa)) if distance in (qa // 2, qa // 2 + 1, 1)]
+    early = [spot for spot in range(qa) if spot not in late]
+    planes = shape((2, rows, lanes), F32)
+    begun = call(
+        functools.partial(low_kernel, early),
+        "low_gate_early",
+        planes,
+        [vmem] * (len(early) + 1),
+        [],
+        1,
+        *[blocks[spot] for spot in early],
+        low_w,
+    )
+    *blocks, _ = call(
+        functools.partial(first_kernel, sections[0], lane_bits, qa, late),
         "first_section",
-        (shape((qb, qa // qb, 2, inner, lanes), F32),) * qa,
-        [vmem] * (qa + 1 + counts[0]),
-        [whole] + [half] * 4,
+        (shape((qb, qa // qb, 2, inner, lanes), F32),) * qa + (planes,),
+        [vmem] * (2 + len(late) + counts[0]),
+        [half] * 4,
         5,
-        *blocks,
+        begun,
+        *[blocks[spot] for spot in late],
         low_w,
         *weights[0],
+        aliases={0: qa},
     )
     blocks = exchange(blocks)
     halves = []
@@ -381,7 +442,7 @@
         "third_section",
         shape((2 * rows, lanes), F32),
         [vmem] * (2 + counts[2]),
-        [whole] + [half] * 4 + [pltpu.VMEM((rows, lanes), F32)] * 2 + [pltpu.SemaphoreType.DMA((2 * PIECES,))],
+        [half] * 4 + [pltpu.VMEM((rows, lanes), F32)] * 2 + [pltpu.SemaphoreType.DMA((2 * PIECES,))],
         4,
         halves[1],
         came,

time: 62 us -> 61.9 us (level)
  starting transfers between devices: 31.6 us -> 29.7 us
  Pallas kernels: 15.4 us -> 16.9 us
  local copies, waits for them, and re-layouts: 1.88 us -> 2.8 us
    ppermute x14, starting transfers between devices: 31.5 us -> 29.7 us  [exchange(): lax.ppermute(piece, 'qa', [(i, i ^ distance) for i in range(qa)])]
    pallas_call x6 -> x7, Pallas kernels: 15.4 us -> 16.9 us  [call(): pl.pallas_call(kernel, out_shape=out_shapes, in_specs=in_specs, out_specs...]
    squeeze x0 -> x1, local copies, waits for them, and re-layouts: none -> 0.91 us  [per_device(): blocks[1] = lax.dynamic_index_in_dim(state, index, 0, keepdims=False)]
  transfers between devices with their start and end apart: 15 -> 15, of which waited for: 8 -> 7; matrix products, arithmetic and copies ran while one was open for 0% -> 0% of each run, Pallas kernels for 14% -> 16%
where the time goes in v8:
time: 61.9 us; the launch traced here: 61.7 us
  starting transfers between devices  29.7 us (48%)
  Pallas kernels  16.9 us (27%)
  waiting for transfers between devices  12.2 us (20%)
  local copies, waits for them, and re-layouts  2.8 us (5%)
    ppermute x14, starting transfers between devices, exchange(): lax.ppermute(piece, 'qa', [(i, i ^ distance) for i in range(qa)])  29.7 us
    pallas_call x7, Pallas kernels, call(): pl.pallas_call(kernel, out_shape=out_shapes, in_specs=in_specs, out_specs...  16.9 us
    ppermute x14, waiting for transfers between devices, exchange(): lax.ppermute(piece, 'qa', [(i, i ^ distance) for i in range(qa)])  11.5 us
    unnamed x6, local copies, waits for them, and re-layouts  1.88 us
  transfers between devices with their start and end apart: 15, of which 7 were waited for; matrix products, arithmetic and copies ran while one was open for 0% of the time, Pallas kernels for 16%

profile of v8, /device:TPU:0, one launch (start us, length us, event | category | flops | bytes accessed | tf_op | source)
XLA Modules:
  0.0 61.7 jit_solution(42992531766900975)
XLA Ops:
  0.0 0.9 %dynamic-slice_bitcast_fusion = f32[256,128]{1,0:T(8,128)S(1)} fusion(f32[8,256,128]{2,1,0:T(8,128)} %bitcast.12, s32[]{:T(128)S(6)} %select_n.4), kind=kLoop, calls=%fused_computation | loop fusion | bytes 262148 | tf_op jit(solution)/shard_map/jit(dynamic_index_in_dim)/squeeze | solution.py:364
  0.9 6.1 %collective-permute-start = (f32[256,128]{1,0:T(8,128)S(1)}, f32[256,128]{1,0:T(8,128)S(1)}, u32[]{:S(2)}, u32[]{:S(2)}) collective-permute-start(f32[256,128]{1,0:T(8,128)S(1)} %dynamic-slice_bitcast_fusion), channel_id=1, source_target_pairs={{0,14},{2,12},{4,10},{6,8},{8,6},{10,4},{12,2},{14,0},{1,15},{3,13... | collective-permute-start | bytes 393224 | tf_op jit(solution)/shard_map/ppermute | solution.py:369
  7.0 1.2 %copy-done = f32[2,131072]{1,0:T(2,128)S(1)} copy-done((f32[2,131072]{1,0:T(2,128)S(1)}, f32[2,131072]{1,0:T(2,128)}, u32[]{:S(2)}) %copy-start) | copy-done | bytes 1048600
  8.2 0.7 %split_state.1 = (f32[256,128]{1,0:T(8,128)S(1)}, f32[256,128]{1,0:T(8,128)}, f32[256,128]{1,0:T(8,128)S(1)}, f32[256,128]{1,0:T(8,128)S(1)}, f32[256,128]{1,0:T...) custom-call(f32[8,256,128]{2,1,0:T(8,128)S(1)} %bitcast.13), custom_call_target="tpu_custom_call" | custom-call | bytes 4194304 | tf_op jit(solution)/shard_map/split_state/pallas_call | solution.py:319
  8.9 0.2 collective-permute-start.1
  9.2 0.0 collective-permute-start.2
  9.2 1.8 %collective-permute-start.3 = (f32[256,128]{1,0:T(8,128)S(1)}, f32[256,128]{1,0:T(8,128)S(1)}, u32[]{:S(2)}, u32[]{:S(2)}) collective-permute-start(f32[256,128]{1,0:T(8,128)S(1)} %get-tuple-element.32), channel_id=1, source_target_pairs={{0,4},{2,6},{4,0},{6,2},{8,12},{10,14},{12,8},{14,10},{1,5},{3,7},... | collective-permute-start | bytes 393224 | tf_op jit(solution)/shard_map/ppermute | solution.py:369
  11.0 3.2 %collective-permute-start.4 = (f32[256,128]{1,0:T(8,128)S(1)}, f32[256,128]{1,0:T(8,128)S(1)}, u32[]{:S(2)}, u32[]{:S(2)}) collective-permute-start(f32[256,128]{1,0:T(8,128)S(1)} %get-tuple-element.34), channel_id=1, source_target_pairs={{0,10},{2,8},{4,14},{6,12},{8,2},{10,0},{12,6},{14,4},{1,11},{3,9}... | collective-permute-start | bytes 393224 | tf_op jit(solution)/shard_map/ppermute | solution.py:369
  14.2 0.0 collective-permute-done.refs_1_
  14.2 3.3 %collective-permute-start.5 = (f32[256,128]{1,0:T(8,128)S(1)}, f32[256,128]{1,0:T(8,128)S(1)}, u32[]{:S(2)}, u32[]{:S(2)}) collective-permute-start(f32[256,128]{1,0:T(8,128)S(1)} %get-tuple-element.35), channel_id=1, source_target_pairs={{0,8},{2,10},{4,12},{6,14},{8,0},{10,2},{12,4},{14,6},{1,9},{3,11}... | collective-permute-start | bytes 393224 | tf_op jit(solution)/shard_map/ppermute | solution.py:369
  17.6 1.5 %collective-permute-start.6 = (f32[256,128]{1,0:T(8,128)S(1)}, f32[256,128]{1,0:T(8,128)S(1)}, u32[]{:S(2)}, u32[]{:S(2)}) collective-permute-start(f32[256,128]{1,0:T(8,128)S(1)} %get-tuple-element.36), channel_id=1, source_target_pairs={{0,2},{2,0},{4,6},{6,4},{8,10},{10,8},{12,14},{14,12},{1,3},{3,1},... | collective-permute-start | bytes 393224 | tf_op jit(solution)/shard_map/ppermute | solution.py:369
  19.1 0.7 %copy-done.1 = s32[18]{0:T(128)S(1)} copy-done((s32[18]{0:T(128)S(1)}, s32[18]{0:T(128)}, u32[]{:S(2)}) %copy-start.1) | copy-done | bytes 96
  19.8 7.6 %prepare_gates.1 = (bf16[768,256]{1,0:T(8,128)(2,1)S(1)}, bf16[512,256]{1,0:T(8,128)(2,1)S(1)}, bf16[512,256]{1,0:T(8,128)(2,1)S(1)}, bf16[512,1536]{1,0:T(8,128...) custom-call(s32[18]{0:T(128)S(1)} %copy-done.1, ...), custom_call_target="tpu_custom_call" | custom-call | flops 3221225472 | bytes 4194304 | tf_op jit(solution)/shard_map/prepare_gates/pallas_call | solution.py:319
  27.4 0.4 low_gate_early.1.refs_0_
  27.9 1.4 %collective-permute-done.5.refs_2_ = f32[256,128]{1,0:T(8,128)S(1)} collective-permute-done((f32[256,128]{1,0:T(8,128)S(1)}, f32[256,128]{1,0:T(8,128)S(1)}, u32[]{:S(2)}, u32[]{:S(2)}) %collective-permute-start.5) | collective-permute-done | bytes 131104 | tf_op jit(solution)/shard_map/ppermute | solution.py:369
  29.3 2.6 %first_section.1 = (f32[2,4,2,16,128]{4,3,2,1,0:T(8,128)S(1)}, f32[2,4,2,16,128]{4,3,2,1,0:T(8,128)S(1)}, f32[2,4,2,16,128]{4,3,2,1,0:T(8,128)S(1)}, f32[2,4,2,1...) custom-call(f32[2,1024,128]{2,1,0:T(8,128)S(1)} %low_gate_early.1.re, ...), custom_call_target="tpu_custom_call", output_to_operand_aliasing={{8}: (0, {})} | custom-call | flops 2013265920 | bytes 4194304 | tf_op jit(solution)/shard_map/first_section/pallas_call | solution.py:319
  31.9 2.5 %collective-permute-start.7 = (f32[2,4,2,16,128]{4,3,2,1,0:T(8,128)S(1)}, f32[2,4,2,16,128]{4,3,2,1,0:T(8,128)S(1)}, u32[]{:S(2)}, u32[]{:S(2)}) collective-permute-start(f32[2,4,2,16,128]{4,3,2,1,0:T(8,128)S(1)} %get-tuple-element.41), channel_id=1, source_target_pairs={{0,14},{2,12},{4,10},{6,8},{8,6},{10,4},{12,2},{14,0},{1,15},{3,13... | collective-permute-start | bytes 393224 | tf_op jit(solution)/shard_map/ppermute | solution.py:369
  34.4 1.3 %collective-permute-start.8 = (f32[2,4,2,16,128]{4,3,2,1,0:T(8,128)S(1)}, f32[2,4,2,16,128]{4,3,2,1,0:T(8,128)S(1)}, u32[]{:S(2)}, u32[]{:S(2)}) collective-permute-start(f32[2,4,2,16,128]{4,3,2,1,0:T(8,128)S(1)} %get-tuple-element.42), channel_id=1, source_target_pairs={{0,12},{2,14},{4,8},{6,10},{8,4},{10,6},{12,0},{14,2},{1,13},{3,15... | collective-permute-start | bytes 393224 | tf_op jit(solution)/shard_map/ppermute | solution.py:369
  35.7 3.0 %collective-permute-start.10 = (f32[2,4,2,16,128]{4,3,2,1,0:T(8,128)S(1)}, f32[2,4,2,16,128]{4,3,2,1,0:T(8,128)S(1)}, u32[]{:S(2)}, u32[]{:S(2)}) collective-permute-start(f32[2,4,2,16,128]{4,3,2,1,0:T(8,128)S(1)} %get-tuple-element.44), channel_id=1, source_target_pairs={{0,4},{2,6},{4,0},{6,2},{8,12},{10,14},{12,8},{14,10},{1,5},{3,7},... | collective-permute-start | bytes 393224 | tf_op jit(solution)/shard_map/ppermute | solution.py:369
  38.7 1.0 %collective-permute-start.11 = (f32[2,4,2,16,128]{4,3,2,1,0:T(8,128)S(1)}, f32[2,4,2,16,128]{4,3,2,1,0:T(8,128)S(1)}, u32[]{:S(2)}, u32[]{:S(2)}) collective-permute-start(f32[2,4,2,16,128]{4,3,2,1,0:T(8,128)S(1)} %get-tuple-element.45), channel_id=1, source_target_pairs={{0,10},{2,8},{4,14},{6,12},{8,2},{10,0},{12,6},{14,4},{1,11},{3,9}... | collective-permute-start | bytes 393224 | tf_op jit(solution)/shard_map/ppermute | solution.py:369
  39.7 0.8 %collective-permute-done.7.refs_1_ = f32[2,4,2,16,128]{4,3,2,1,0:T(8,128)S(1)} collective-permute-done((f32[2,4,2,16,128]{4,3,2,1,0:T(8,128)S(1)}, f32[2,4,2,16,128]{4,3,2,1,0:T(8,128)S(1)}, u32[]{:S(2)}, u32[]{:S(2)}) %collective-permute-start.7) | collective-permute-done | bytes 131104 | tf_op jit(solution)/shard_map/ppermute | solution.py:369
  40.5 2.9 %collective-permute-start.12 = (f32[2,4,2,16,128]{4,3,2,1,0:T(8,128)S(1)}, f32[2,4,2,16,128]{4,3,2,1,0:T(8,128)S(1)}, u32[]{:S(2)}, u32[]{:S(2)}) collective-permute-start(f32[2,4,2,16,128]{4,3,2,1,0:T(8,128)S(1)} %get-tuple-element.46), channel_id=1, source_target_pairs={{0,8},{2,10},{4,12},{6,14},{8,0},{10,2},{12,4},{14,6},{1,9},{3,11}... | collective-permute-start | bytes 393224 | tf_op jit(solution)/shard_map/ppermute | solution.py:369
  43.4 2.7 %collective-permute-start.13 = (f32[2,4,2,16,128]{4,3,2,1,0:T(8,128)S(1)}, f32[2,4,2,16,128]{4,3,2,1,0:T(8,128)S(1)}, u32[]{:S(2)}, u32[]{:S(2)}) collective-permute-start(f32[2,4,2,16,128]{4,3,2,1,0:T(8,128)S(1)} %get-tuple-element.47), channel_id=1, source_target_pairs={{0,2},{2,0},{4,6},{6,4},{8,10},{10,8},{12,14},{14,12},{1,3},{3,1},... | collective-permute-start | bytes 393224 | tf_op jit(solution)/shard_map/ppermute | solution.py:369
  46.2 1.1 %collective-permute-done.9.refs_3_ = f32[2,4,2,16,128]{4,3,2,1,0:T(8,128)S(1)} collective-permute-done((f32[2,4,2,16,128]{4,3,2,1,0:T(8,128)S(1)}, f32[2,4,2,16,128]{4,3,2,1,0:T(8,128)S(1)}, u32[]{:S(2)}, u32[]{:S(2)}) %collective-permute-start.9) | collective-permute-done | bytes 131104 | tf_op jit(solution)/shard_map/ppermute | solution.py:369
  47.3 2.9 %collective-permute-done.10.refs_4_ = f32[2,4,2,16,128]{4,3,2,1,0:T(8,128)S(1)} collective-permute-done((f32[2,4,2,16,128]{4,3,2,1,0:T(8,128)S(1)}, f32[2,4,2,16,128]{4,3,2,1,0:T(8,128)S(1)}, u32[]{:S(2)}, u32[]{:S(2)}) %collective-permute-start.10) | collective-permute-done | bytes 131104 | tf_op jit(solution)/shard_map/ppermute | solution.py:369
  50.1 4.8 %collective-permute-done.11.refs_5_ = f32[2,4,2,16,128]{4,3,2,1,0:T(8,128)S(1)} collective-permute-done((f32[2,4,2,16,128]{4,3,2,1,0:T(8,128)S(1)}, f32[2,4,2,16,128]{4,3,2,1,0:T(8,128)S(1)}, u32[]{:S(2)}, u32[]{:S(2)}) %collective-permute-start.11) | collective-permute-done | bytes 131104 | tf_op jit(solution)/shard_map/ppermute | solution.py:369
  54.9 0.5 collective-permute-done.12.refs_6_
  55.4 1.2 %second_section_sent.1 = f32[2,512,128]{2,1,0:T(8,128)S(1)} custom-call(f32[2,4,2,16,128]{4,3,2,1,0:T(8,128)S(1)} %get-tuple-element.40.refs_0_, f32[2,4,2,16,128]{4,3,2,1,0:T(8,128)S(1)} %collective-permute-done.7.refs_1_, f32[2,4,2,16,128]{4,3,2,1,0:T(8,128)S(1)} %collective-permute-done.8.refs_2_, ...), custom_call_target="tpu_custom_call" | custom-call | flops 603979776 | bytes 4194304 | tf_op jit(solution)/shard_map/second_section_sent/pallas_call | solution.py:319
  56.6 0.1 collective-permute-start.14
  56.7 1.2 %second_section_kept.1.kept_ref = f32[2,512,128]{2,1,0:T(8,128)S(1)} custom-call(f32[2,4,2,16,128]{4,3,2,1,0:T(8,128)S(1)} %get-tuple-element.40.refs_0_, f32[2,4,2,16,128]{4,3,2,1,0:T(8,128)S(1)} %collective-permute-done.7.refs_1_, f32[2,4,2,16,128]{4,3,2,1,0:T(8,128)S(1)} %collective-permute-done.8.refs_2_, ...), custom_call_target="tpu_custom_call" | custom-call | flops 603979776 | bytes 4194304 | tf_op jit(solution)/shard_map/second_section_kept/pallas_call | solution.py:319
  57.9 0.7 %collective-permute-done.14.came_ref = f32[2,512,128]{2,1,0:T(8,128)S(1)} collective-permute-done((f32[2,512,128]{2,1,0:T(8,128)S(1)}, f32[2,512,128]{2,1,0:T(8,128)S(1)}, u32[]{:S(2)}, u32[]{:S(2)}) %collective-permute-start.14) | collective-permute-done | bytes 524320 | tf_op jit(solution)/shard_map/ppermute | solution.py:439
  58.6 3.1 %third_section.1 = f32[2048,128]{1,0:T(8,128)} custom-call(f32[2,512,128]{2,1,0:T(8,128)S(1)} %second_section_kept.1.kept_ref, f32[2,512,128]{2,1,0:T(8,128)S(1)} %collective-permute-done.14.came_ref, bf16[512,256]{1,0:T(8,128)(2,1)S(1)} %get-tuple-element.50.refs_0_, bf16[512,256]{1,0:T(8,128)(2,1)S(1)} %get-tuple-element.51.refs_1_, ...), custom_call_target="tpu_custom_call" | custom-call | flops 1610612736 | bytes 4194304 | tf_op jit(solution)/shard_map/third_section/pallas_call | solution.py:319
  (12 shorter events, 0.0 us)
Async XLA Ops:
  0.9 13.3 %collective-permute-start = (f32[256,128]{1,0:T(8,128)S(1)}, f32[256,128]{1,0:T(8,128)S(1)}, u32[]{:S(2)}, u32[]{:S(2)}) collective-permute-start(f32[256,128]{1,0:T(8,128)S(1)} %dynamic-slice_bitcast_fusion), channel_id=1, source_target_pairs={{0,14},{2,12},{4,10},{6,8},{8,6},{10,4},{12,2},{14,0},{1,15},{3,13... | collective-permute-start | bytes 393224 | tf_op jit(solution)/shard_map/ppermute | solution.py:369
  7.0 1.2 %copy-start = (f32[2,131072]{1,0:T(2,128)S(1)}, f32[2,131072]{1,0:T(2,128)}, u32[]{:S(2)}) copy-start(f32[2,131072]{1,0:T(2,128)} %param.3) | copy-start | bytes 3145732
  8.9 8.6 %collective-permute-start.1 = (f32[256,128]{1,0:T(8,128)S(1)}, f32[256,128]{1,0:T(8,128)S(1)}, u32[]{:S(2)}, u32[]{:S(2)}) collective-permute-start(f32[256,128]{1,0:T(8,128)S(1)} %get-tuple-element.30), channel_id=1, source_target_pairs={{0,12},{2,14},{4,8},{6,10},{8,4},{10,6},{12,0},{14,2},{1,13},{3,15... | collective-permute-start | bytes 393224 | tf_op jit(solution)/shard_map/ppermute | solution.py:369
  9.2 18.2 %collective-permute-start.2 = (f32[256,128]{1,0:T(8,128)S(1)}, f32[256,128]{1,0:T(8,128)S(1)}, u32[]{:S(2)}, u32[]{:S(2)}) collective-permute-start(f32[256,128]{1,0:T(8,128)S(1)} %get-tuple-element.31), channel_id=1, source_target_pairs={{0,6},{2,4},{4,2},{6,0},{8,14},{10,12},{12,10},{14,8},{1,7},{3,5},... | collective-permute-start | bytes 393224 | tf_op jit(solution)/shard_map/ppermute | solution.py:369
  9.2 18.2 %collective-permute-start.3 = (f32[256,128]{1,0:T(8,128)S(1)}, f32[256,128]{1,0:T(8,128)S(1)}, u32[]{:S(2)}, u32[]{:S(2)}) collective-permute-start(f32[256,128]{1,0:T(8,128)S(1)} %get-tuple-element.32), channel_id=1, source_target_pairs={{0,4},{2,6},{4,0},{6,2},{8,12},{10,14},{12,8},{14,10},{1,5},{3,7},... | collective-permute-start | bytes 393224 | tf_op jit(solution)/shard_map/ppermute | solution.py:369
  11.0 16.9 %collective-permute-start.4 = (f32[256,128]{1,0:T(8,128)S(1)}, f32[256,128]{1,0:T(8,128)S(1)}, u32[]{:S(2)}, u32[]{:S(2)}) collective-permute-start(f32[256,128]{1,0:T(8,128)S(1)} %get-tuple-element.34), channel_id=1, source_target_pairs={{0,10},{2,8},{4,14},{6,12},{8,2},{10,0},{12,6},{14,4},{1,11},{3,9}... | collective-permute-start | bytes 393224 | tf_op jit(solution)/shard_map/ppermute | solution.py:369
  14.2 15.1 %collective-permute-start.5 = (f32[256,128]{1,0:T(8,128)S(1)}, f32[256,128]{1,0:T(8,128)S(1)}, u32[]{:S(2)}, u32[]{:S(2)}) collective-permute-start(f32[256,128]{1,0:T(8,128)S(1)} %get-tuple-element.35), channel_id=1, source_target_pairs={{0,8},{2,10},{4,12},{6,14},{8,0},{10,2},{12,4},{14,6},{1,9},{3,11}... | collective-permute-start | bytes 393224 | tf_op jit(solution)/shard_map/ppermute | solution.py:369
  17.6 11.7 %collective-permute-start.6 = (f32[256,128]{1,0:T(8,128)S(1)}, f32[256,128]{1,0:T(8,128)S(1)}, u32[]{:S(2)}, u32[]{:S(2)}) collective-permute-start(f32[256,128]{1,0:T(8,128)S(1)} %get-tuple-element.36), channel_id=1, source_target_pairs={{0,2},{2,0},{4,6},{6,4},{8,10},{10,8},{12,14},{14,12},{1,3},{3,1},... | collective-permute-start | bytes 393224 | tf_op jit(solution)/shard_map/ppermute | solution.py:369
  19.1 0.7 %copy-start.1 = (s32[18]{0:T(128)S(1)}, s32[18]{0:T(128)}, u32[]{:S(2)}) copy-start(s32[18]{0:T(128)} %bits_ref.1) | copy-start | bytes 220
  31.9 8.7 %collective-permute-start.7 = (f32[2,4,2,16,128]{4,3,2,1,0:T(8,128)S(1)}, f32[2,4,2,16,128]{4,3,2,1,0:T(8,128)S(1)}, u32[]{:S(2)}, u32[]{:S(2)}) collective-permute-start(f32[2,4,2,16,128]{4,3,2,1,0:T(8,128)S(1)} %get-tuple-element.41), channel_id=1, source_target_pairs={{0,14},{2,12},{4,10},{6,8},{8,6},{10,4},{12,2},{14,0},{1,15},{3,13... | collective-permute-start | bytes 393224 | tf_op jit(solution)/shard_map/ppermute | solution.py:369
  34.4 9.1 %collective-permute-start.8 = (f32[2,4,2,16,128]{4,3,2,1,0:T(8,128)S(1)}, f32[2,4,2,16,128]{4,3,2,1,0:T(8,128)S(1)}, u32[]{:S(2)}, u32[]{:S(2)}) collective-permute-start(f32[2,4,2,16,128]{4,3,2,1,0:T(8,128)S(1)} %get-tuple-element.42), channel_id=1, source_target_pairs={{0,12},{2,14},{4,8},{6,10},{8,4},{10,6},{12,0},{14,2},{1,13},{3,15... | collective-permute-start | bytes 393224 | tf_op jit(solution)/shard_map/ppermute | solution.py:369
  35.7 11.5 %collective-permute-start.9 = (f32[2,4,2,16,128]{4,3,2,1,0:T(8,128)S(1)}, f32[2,4,2,16,128]{4,3,2,1,0:T(8,128)S(1)}, u32[]{:S(2)}, u32[]{:S(2)}) collective-permute-start(f32[2,4,2,16,128]{4,3,2,1,0:T(8,128)S(1)} %get-tuple-element.43), channel_id=1, source_target_pairs={{0,6},{2,4},{4,2},{6,0},{8,14},{10,12},{12,10},{14,8},{1,7},{3,5},... | collective-permute-start | bytes 393224 | tf_op jit(solution)/shard_map/ppermute | solution.py:369
  35.7 14.4 %collective-permute-start.10 = (f32[2,4,2,16,128]{4,3,2,1,0:T(8,128)S(1)}, f32[2,4,2,16,128]{4,3,2,1,0:T(8,128)S(1)}, u32[]{:S(2)}, u32[]{:S(2)}) collective-permute-start(f32[2,4,2,16,128]{4,3,2,1,0:T(8,128)S(1)} %get-tuple-element.44), channel_id=1, source_target_pairs={{0,4},{2,6},{4,0},{6,2},{8,12},{10,14},{12,8},{14,10},{1,5},{3,7},... | collective-permute-start | bytes 393224 | tf_op jit(solution)/shard_map/ppermute | solution.py:369
  38.7 16.2 %collective-permute-start.11 = (f32[2,4,2,16,128]{4,3,2,1,0:T(8,128)S(1)}, f32[2,4,2,16,128]{4,3,2,1,0:T(8,128)S(1)}, u32[]{:S(2)}, u32[]{:S(2)}) collective-permute-start(f32[2,4,2,16,128]{4,3,2,1,0:T(8,128)S(1)} %get-tuple-element.45), channel_id=1, source_target_pairs={{0,10},{2,8},{4,14},{6,12},{8,2},{10,0},{12,6},{14,4},{1,11},{3,9}... | collective-permute-start | bytes 393224 | tf_op jit(solution)/shard_map/ppermute | solution.py:369
  40.5 14.8 %collective-permute-start.12 = (f32[2,4,2,16,128]{4,3,2,1,0:T(8,128)S(1)}, f32[2,4,2,16,128]{4,3,2,1,0:T(8,128)S(1)}, u32[]{:S(2)}, u32[]{:S(2)}) collective-permute-start(f32[2,4,2,16,128]{4,3,2,1,0:T(8,128)S(1)} %get-tuple-element.46), channel_id=1, source_target_pairs={{0,8},{2,10},{4,12},{6,14},{8,0},{10,2},{12,4},{14,6},{1,9},{3,11}... | collective-permute-start | bytes 393224 | tf_op jit(solution)/shard_map/ppermute | solution.py:369
  43.4 11.9 %collective-permute-start.13 = (f32[2,4,2,16,128]{4,3,2,1,0:T(8,128)S(1)}, f32[2,4,2,16,128]{4,3,2,1,0:T(8,128)S(1)}, u32[]{:S(2)}, u32[]{:S(2)}) collective-permute-start(f32[2,4,2,16,128]{4,3,2,1,0:T(8,128)S(1)} %get-tuple-element.47), channel_id=1, source_target_pairs={{0,2},{2,0},{4,6},{6,4},{8,10},{10,8},{12,14},{14,12},{1,3},{3,1},... | collective-permute-start | bytes 393224 | tf_op jit(solution)/shard_map/ppermute | solution.py:369
  56.6 2.0 %copy-start.2 = (bf16[512,1536]{1,0:T(8,128)(2,1)S(1)}, bf16[512,1536]{1,0:T(8,128)(2,1)}, u32[]{:S(2)}) copy-start(bf16[512,1536]{1,0:T(8,128)(2,1)} %get-tuple-element.52.refs_2_) | copy-start | bytes 4718596
  56.6 2.0 %collective-permute-start.14 = (f32[2,512,128]{2,1,0:T(8,128)S(1)}, f32[2,512,128]{2,1,0:T(8,128)S(1)}, u32[]{:S(2)}, u32[]{:S(2)}) collective-permute-start(f32[2,512,128]{2,1,0:T(8,128)S(1)} %second_section_sent.1), channel_id=1, source_target_pairs={{0,1},{1,0},{2,3},{3,2},{4,5},{5,4},{6,7},{7,6},{8,9},{9,8},{10,11... | collective-permute-start | bytes 1572872 | tf_op jit(solution)/shard_map/ppermute | solution.py:439

commit v9 on v8

--- a/solution.py
+++ b/solution.py
@@ -13,6 +13,7 @@
 VMEM_LIMIT = 14 * 1024 * 1024
 LARGE_VMEM = 48 * 1024 * 1024
 PIECES = 4
+ORDER = [(1, 0), (2, 0), (1, 1), (2, 1), (3, 0), (3, 1), (0, 1)]
 
 
 def window_offsets(span, gate_bits):
@@ -85,8 +86,8 @@
     if number == 0:
         size = dim // count
         spot, source = column // size, jnp.zeros_like(column)
-        for index, distance in enumerate(distances_of(count)):
-            source = jnp.where(spot == index, partner(distance), source)
+        for index, partner in enumerate(sources_of(count)):
+            source = jnp.where(spot == index, partner, source)
         natural = source * size + lax.rem(column, size)
     else:
         natural = jnp.bitwise_xor(column, lax.axis_index("qb") * (dim // 2))
@@ -133,53 +134,65 @@
     for number, section in enumerate(sections):
         weights, targets = targets[: len(section)], targets[len(section) :]
         for target, (base, _, parts) in zip(weights, section):
-            if len(parts) > 1:
-                high, rest = split(block(*joined(base, parts)))
-                target[...] = jnp.concatenate([high, rest, high], axis=1)
-                continue
-            pair = product(parts[0][1])
+            pair = joined(base, parts) if len(parts) > 1 else product(parts[0][1])
             if number != 1 and target is weights[0]:
                 pair = [relative(x, number, count) for x in pair]
             high, rest = split(block(*pair))
-            target[...] = jnp.concatenate([high, rest], axis=0)
+            target[...] = jnp.concatenate([high, rest, high], axis=1)
     real, imag = product(low)
     high, rest = split(block(real.T, -imag.T))
     low_ref[...] = jnp.concatenate([high, rest, high], axis=0)
 
 
-def distances_of(count):
+def partners_of(count):
+    if count == 8:
+        cycle = [0, 1, 3, 2]
+        tables = [list(range(count))]
+        for shift, crossed in ORDER:
+            line = [cycle[(cycle.index(z) + shift) % 4] for z in range(4)]
+            tables.append([2 * line[i // 2] + (i % 2 ^ crossed) for i in range(count)])
+        return tables
     half = count // 2
     far, near = list(range(count - 1, half - 1, -1)), list(range(half - 1, 0, -1))
     order = [0]
     while far or near:
         order += far[:2] + near[:2]
         far, near = far[2:], near[2:]
-    return order
-
-
-def partner(distance):
-    return jnp.bitwise_xor(lax.axis_index("qa"), distance)
+    return [[i ^ distance for i in range(count)] for distance in order]
+
+
+def look_up(table):
+    me = lax.axis_index("qa")
+    if table == [i ^ table[0] for i in range(len(table))]:
+        return jnp.bitwise_xor(me, table[0])
+    found = jnp.int32(table[0])
+    for index in range(1, len(table)):
+        found = jnp.where(me == index, jnp.int32(table[index]), found)
+    return found
+
+
+def dests_of(count):
+    return [look_up(table) for table in partners_of(count)]
+
+
+def sources_of(count):
+    return [look_up([table.index(i) for i in range(count)]) for table in partners_of(count)]
 
 
 def split_kernel(x_ref, *outs):
-    for distance, out_ref in zip(distances_of(len(outs)), outs):
-        out_ref[...] = x_ref[partner(distance)]
+    for dest, out_ref in zip(dests_of(len(outs)), outs):
+        out_ref[...] = x_ref[dest]
 
 
 def apply_stage(weights_ref, starts, load, store):
-    stacked = weights_ref.shape[0] > weights_ref.shape[1]
-    dim = weights_ref.shape[1] // 2 if stacked else weights_ref.shape[0] // 2
+    dim = weights_ref.shape[0] // 2
     for pair in range(0, len(starts), 2):
         group = starts[pair : pair + 2]
         x = jnp.concatenate(
             [jnp.concatenate([load(part, start) for start in group], axis=1) for part in range(2)], axis=0
         )
         high, rest = split(x)
-        if stacked:
-            both = bf_dot(weights_ref[...], high)
-            y = bf_dot(weights_ref[: 2 * dim], rest) + both[2 * dim :] + both[: 2 * dim]
-        else:
-            y = bf_dot(weights_ref[...], jnp.concatenate([rest, high, high], axis=0))
+        y = bf_dot(weights_ref[...], jnp.concatenate([rest, high, high], axis=0))
         lanes = y.shape[1] // len(group)
         for part in range(2):
             for place, start in enumerate(group):
@@ -262,9 +275,9 @@
     run_top_stage(stages[0], weights[0], lane_bits, whole, halves[:2])
     done = run_halves(stages[1:], weights[1:], lane_bits, halves[:2], halves[2:])
     tops, mids, _, inner, _ = outs[0].shape
+    dests = dests_of(count)
     for top in range(tops):
-        for distance, out_ref in zip(distances_of(count), outs):
-            dest = partner(distance)
+        for dest, out_ref in zip(dests, outs):
             for mid in range(mids):
                 start = pl.multiple_of((mid * count + dest) * inner, inner)
                 for part in range(2):
@@ -276,8 +289,7 @@
     out_ref, one, two = refs
     core = lax.axis_index("qb")
     top = core if stays else 1 - core
-    for distance, block_ref in zip(distances_of(count), blocks):
-        source = partner(distance)
+    for source, block_ref in zip(sources_of(count), blocks):
         _, mids, _, inner, _ = block_ref.shape
         for mid in range(mids):
             start = pl.multiple_of((mid * count + source) * inner, inner)
@@ -359,14 +371,13 @@
         state,
     )
 
-    index = jnp.bitwise_xor(lax.axis_index("qa"), distances_of(qa)[1])
     blocks = list(blocks)
-    blocks[1] = lax.dynamic_index_in_dim(state, index, 0, keepdims=False)
+    blocks[1] = lax.dynamic_index_in_dim(state, look_up(partners_of(qa)[1]), 0, keepdims=False)
 
     def exchange(blocks):
         came = [blocks[0]]
-        for distance, piece in zip(distances_of(qa)[1:], blocks[1:]):
-            came.append(lax.ppermute(piece, "qa", [(i, i ^ distance) for i in range(qa)]))
+        for table, piece in zip(partners_of(qa)[1:], blocks[1:]):
+            came.append(lax.ppermute(piece, "qa", list(enumerate(table))))
         return came
 
     blocks = exchange(blocks)
@@ -374,11 +385,7 @@
         functools.partial(prepare_kernel, low, sections, qa),
         "prepare_gates",
         (shape((3 * order, order), BF16),)
-        + tuple(
-            shape((2 * 2**bits, 6 * 2**bits) if len(parts) > 1 else (4 * 2**bits, 2 * 2**bits), BF16)
-            for section in sections
-            for _, bits, parts in section
-        ),
+        + tuple(shape((2 * 2**bits, 6 * 2**bits), BF16) for section in sections for _, bits, _ in section),
         [pl.BlockSpec(memory_space=pltpu.SMEM), hbm],
         [
             pltpu.VMEM((gate_terms.shape[0], 2, dim, dim), F32),
@@ -394,8 +401,7 @@
     weights = [weights[: counts[0]], weights[counts[0] : counts[0] + counts[1]], weights[counts[0] + counts[1] :]]
     inner = rows // (qa * qa)
     half = pltpu.VMEM((2, rows // 2, lanes), F32)
-    late = [spot for spot, distance in enumerate(distances_of(qa)) if distance in (qa // 2, qa // 2 + 1, 1)]
-    early = [spot for spot in range(qa) if spot not in late]
+    early, late = list(range(qa - 3)), list(range(qa - 3, qa))
     planes = shape((2, rows, lanes), F32)
     begun = call(
         functools.partial(low_kernel, early),

time: 61.9 us -> 64.2 us (1.037); the launches traced: 61.7 us -> 63 us
  waiting for transfers between devices: 12.2 us -> 16.4 us
  starting transfers between devices: 29.7 us -> 27.3 us
    ppermute x14, waiting for transfers between devices: 11.5 us -> 15.5 us  [exchange(): came.append(lax.ppermute(piece, 'qa', list(enumerate(table))))]
    ppermute x14, starting transfers between devices: 29.7 us -> 27.2 us  [exchange(): came.append(lax.ppermute(piece, 'qa', list(enumerate(table))))]
  transfers between devices with their start and end apart: 15 -> 15, of which waited for: 7 -> 5; matrix products, arithmetic and copies ran while one was open for 0% -> 0% of each run, Pallas kernels for 16% -> 16%
where the time goes in v9:
time: 64.2 us; the launch traced here: 63 us
  starting transfers between devices  27.3 us (43%)
  Pallas kernels  16.4 us (26%)
  waiting for transfers between devices  16.4 us (26%)
  local copies, waits for them, and re-layouts  2.8 us (4%)
    ppermute x14, starting transfers between devices, exchange(): came.append(lax.ppermute(piece, 'qa', list(enumerate(table))))  27.2 us
    pallas_call x7, Pallas kernels, call(): pl.pallas_call(kernel, out_shape=out_shapes, in_specs=in_specs, out_specs...  16.4 us
    ppermute x14, waiting for transfers between devices, exchange(): came.append(lax.ppermute(piece, 'qa', list(enumerate(table))))  15.5 us
    unnamed x6, local copies, waits for them, and re-layouts  1.88 us
  transfers between devices with their start and end apart: 15, of which 5 were waited for; matrix products, arithmetic and copies ran while one was open for 0% of the time, Pallas kernels for 16%

profile of v9, /device:TPU:0, one launch (start us, length us, event | category | flops | bytes accessed | tf_op | source)
XLA Modules:
  0.0 63.0 jit_solution(3455142264704532054)
XLA Ops:
  0.0 0.9 %dynamic-slice_bitcast_fusion = f32[256,128]{1,0:T(8,128)S(1)} fusion(f32[8,256,128]{2,1,0:T(8,128)} %bitcast.12, s32[]{:T(128)S(6)} %select_n.30), kind=kLoop, calls=%fused_computation | loop fusion | bytes 262148 | tf_op jit(solution)/shard_map/jit(dynamic_index_in_dim)/squeeze | solution.py:375
  0.9 3.1 %collective-permute-start = (f32[256,128]{1,0:T(8,128)S(1)}, f32[256,128]{1,0:T(8,128)S(1)}, u32[]{:S(2)}, u32[]{:S(2)}) collective-permute-start(f32[256,128]{1,0:T(8,128)S(1)} %dynamic-slice_bitcast_fusion), channel_id=1, source_target_pairs={{0,4},{2,6},{4,12},{6,14},{8,0},{10,2},{12,8},{14,10},{1,5},{3,7},... | collective-permute-start | bytes 393224 | tf_op jit(solution)/shard_map/ppermute | solution.py:380
  4.0 1.2 %copy-done = f32[2,131072]{1,0:T(2,128)S(1)} copy-done((f32[2,131072]{1,0:T(2,128)S(1)}, f32[2,131072]{1,0:T(2,128)}, u32[]{:S(2)}) %copy-start) | copy-done | bytes 1048600
  5.2 0.7 %split_state.1 = (f32[256,128]{1,0:T(8,128)S(1)}, f32[256,128]{1,0:T(8,128)}, f32[256,128]{1,0:T(8,128)S(1)}, f32[256,128]{1,0:T(8,128)S(1)}, f32[256,128]{1,0:T...) custom-call(f32[8,256,128]{2,1,0:T(8,128)S(1)} %bitcast.13), custom_call_target="tpu_custom_call" | custom-call | bytes 4194304 | tf_op jit(solution)/shard_map/split_state/pallas_call | solution.py:331
  5.9 2.5 %collective-permute-start.1 = (f32[256,128]{1,0:T(8,128)S(1)}, f32[256,128]{1,0:T(8,128)S(1)}, u32[]{:S(2)}, u32[]{:S(2)}) collective-permute-start(f32[256,128]{1,0:T(8,128)S(1)} %get-tuple-element.30), channel_id=1, source_target_pairs={{0,12},{2,14},{4,8},{6,10},{8,4},{10,6},{12,0},{14,2},{1,13},{3,15... | collective-permute-start | bytes 393224 | tf_op jit(solution)/shard_map/ppermute | solution.py:380
  8.4 1.1 %collective-permute-start.2 = (f32[256,128]{1,0:T(8,128)S(1)}, f32[256,128]{1,0:T(8,128)S(1)}, u32[]{:S(2)}, u32[]{:S(2)}) collective-permute-start(f32[256,128]{1,0:T(8,128)S(1)} %get-tuple-element.31), channel_id=1, source_target_pairs={{0,6},{2,4},{4,14},{6,12},{8,2},{10,0},{12,10},{14,8},{1,7},{3,5},... | collective-permute-start | bytes 393224 | tf_op jit(solution)/shard_map/ppermute | solution.py:380
  9.5 2.9 %collective-permute-start.3 = (f32[256,128]{1,0:T(8,128)S(1)}, f32[256,128]{1,0:T(8,128)S(1)}, u32[]{:S(2)}, u32[]{:S(2)}) collective-permute-start(f32[256,128]{1,0:T(8,128)S(1)} %get-tuple-element.32), channel_id=1, source_target_pairs={{0,14},{2,12},{4,10},{6,8},{8,6},{10,4},{12,2},{14,0},{1,15},{3,13... | collective-permute-start | bytes 393224 | tf_op jit(solution)/shard_map/ppermute | solution.py:380
  12.4 0.3 collective-permute-start.4
  12.7 2.1 %collective-permute-start.5 = (f32[256,128]{1,0:T(8,128)S(1)}, f32[256,128]{1,0:T(8,128)S(1)}, u32[]{:S(2)}, u32[]{:S(2)}) collective-permute-start(f32[256,128]{1,0:T(8,128)S(1)} %get-tuple-element.35), channel_id=1, source_target_pairs={{0,10},{2,8},{4,2},{6,0},{8,14},{10,12},{12,6},{14,4},{1,11},{3,9}... | collective-permute-start | bytes 393224 | tf_op jit(solution)/shard_map/ppermute | solution.py:380
  14.8 1.0 %collective-permute-start.6 = (f32[256,128]{1,0:T(8,128)S(1)}, f32[256,128]{1,0:T(8,128)S(1)}, u32[]{:S(2)}, u32[]{:S(2)}) collective-permute-start(f32[256,128]{1,0:T(8,128)S(1)} %get-tuple-element.36), channel_id=1, source_target_pairs={{0,2},{2,0},{4,6},{6,4},{8,10},{10,8},{12,14},{14,12},{1,3},{3,1},... | collective-permute-start | bytes 393224 | tf_op jit(solution)/shard_map/ppermute | solution.py:380
  15.8 0.7 %copy-done.1 = s32[18]{0:T(128)S(1)} copy-done((s32[18]{0:T(128)S(1)}, s32[18]{0:T(128)}, u32[]{:S(2)}) %copy-start.1) | copy-done | bytes 96
  16.4 7.6 %prepare_gates.1 = (bf16[768,256]{1,0:T(8,128)(2,1)S(1)}, bf16[256,768]{1,0:T(8,128)(2,1)S(1)}, bf16[256,768]{1,0:T(8,128)(2,1)S(1)}, bf16[512,1536]{1,0:T(8,128...) custom-call(s32[18]{0:T(128)S(1)} %copy-done.1, ...), custom_call_target="tpu_custom_call" | custom-call | flops 3221225472 | bytes 4194304 | tf_op jit(solution)/shard_map/prepare_gates/pallas_call | solution.py:331
  24.1 3.8 %collective-permute-done.2.refs_3_ = f32[256,128]{1,0:T(8,128)S(1)} collective-permute-done((f32[256,128]{1,0:T(8,128)S(1)}, f32[256,128]{1,0:T(8,128)S(1)}, u32[]{:S(2)}, u32[]{:S(2)}) %collective-permute-start.2) | collective-permute-done | bytes 131104 | tf_op jit(solution)/shard_map/ppermute | solution.py:380
  27.8 0.4 low_gate_early.1.refs_0_
  28.3 0.0 collective-permute-done.4.refs_1_
  28.3 0.0 collective-permute-done.5.refs_2_
  28.3 2.5 %first_section.1 = (f32[2,4,2,16,128]{4,3,2,1,0:T(8,128)S(1)}, f32[2,4,2,16,128]{4,3,2,1,0:T(8,128)S(1)}, f32[2,4,2,16,128]{4,3,2,1,0:T(8,128)S(1)}, f32[2,4,2,1...) custom-call(f32[2,1024,128]{2,1,0:T(8,128)S(1)} %low_gate_early.1.re, ...), custom_call_target="tpu_custom_call", output_to_operand_aliasing={{8}: (0, {})} | custom-call | flops 2013265920 | bytes 4194304 | tf_op jit(solution)/shard_map/first_section/pallas_call | solution.py:331
  30.8 6.7 %collective-permute-start.7 = (f32[2,4,2,16,128]{4,3,2,1,0:T(8,128)S(1)}, f32[2,4,2,16,128]{4,3,2,1,0:T(8,128)S(1)}, u32[]{:S(2)}, u32[]{:S(2)}) collective-permute-start(f32[2,4,2,16,128]{4,3,2,1,0:T(8,128)S(1)} %get-tuple-element.41), channel_id=1, source_target_pairs={{0,4},{2,6},{4,12},{6,14},{8,0},{10,2},{12,8},{14,10},{1,5},{3,7},... | collective-permute-start | bytes 393224 | tf_op jit(solution)/shard_map/ppermute | solution.py:380
  37.5 3.0 %collective-permute-start.8 = (f32[2,4,2,16,128]{4,3,2,1,0:T(8,128)S(1)}, f32[2,4,2,16,128]{4,3,2,1,0:T(8,128)S(1)}, u32[]{:S(2)}, u32[]{:S(2)}) collective-permute-start(f32[2,4,2,16,128]{4,3,2,1,0:T(8,128)S(1)} %get-tuple-element.42), channel_id=1, source_target_pairs={{0,12},{2,14},{4,8},{6,10},{8,4},{10,6},{12,0},{14,2},{1,13},{3,15... | collective-permute-start | bytes 393224 | tf_op jit(solution)/shard_map/ppermute | solution.py:380
  40.5 0.0 collective-permute-start.9
  40.5 1.0 %collective-permute-start.10 = (f32[2,4,2,16,128]{4,3,2,1,0:T(8,128)S(1)}, f32[2,4,2,16,128]{4,3,2,1,0:T(8,128)S(1)}, u32[]{:S(2)}, u32[]{:S(2)}) collective-permute-start(f32[2,4,2,16,128]{4,3,2,1,0:T(8,128)S(1)} %get-tuple-element.44), channel_id=1, source_target_pairs={{0,14},{2,12},{4,10},{6,8},{8,6},{10,4},{12,2},{14,0},{1,15},{3,13... | collective-permute-start | bytes 393224 | tf_op jit(solution)/shard_map/ppermute | solution.py:380
  41.6 2.7 %collective-permute-start.11 = (f32[2,4,2,16,128]{4,3,2,1,0:T(8,128)S(1)}, f32[2,4,2,16,128]{4,3,2,1,0:T(8,128)S(1)}, u32[]{:S(2)}, u32[]{:S(2)}) collective-permute-start(f32[2,4,2,16,128]{4,3,2,1,0:T(8,128)S(1)} %get-tuple-element.45), channel_id=1, source_target_pairs={{0,8},{2,10},{4,0},{6,2},{8,12},{10,14},{12,4},{14,6},{1,9},{3,11}... | collective-permute-start | bytes 393224 | tf_op jit(solution)/shard_map/ppermute | solution.py:380
  44.3 4.9 %collective-permute-done.7.refs_1_ = f32[2,4,2,16,128]{4,3,2,1,0:T(8,128)S(1)} collective-permute-done((f32[2,4,2,16,128]{4,3,2,1,0:T(8,128)S(1)}, f32[2,4,2,16,128]{4,3,2,1,0:T(8,128)S(1)}, u32[]{:S(2)}, u32[]{:S(2)}) %collective-permute-start.7) | collective-permute-done | bytes 131104 | tf_op jit(solution)/shard_map/ppermute | solution.py:380
  49.1 0.0 collective-permute-done.8.refs_2_
  49.1 0.9 %collective-permute-start.13 = (f32[2,4,2,16,128]{4,3,2,1,0:T(8,128)S(1)}, f32[2,4,2,16,128]{4,3,2,1,0:T(8,128)S(1)}, u32[]{:S(2)}, u32[]{:S(2)}) collective-permute-start(f32[2,4,2,16,128]{4,3,2,1,0:T(8,128)S(1)} %get-tuple-element.47), channel_id=1, source_target_pairs={{0,2},{2,0},{4,6},{6,4},{8,10},{10,8},{12,14},{14,12},{1,3},{3,1},... | collective-permute-start | bytes 393224 | tf_op jit(solution)/shard_map/ppermute | solution.py:380
  50.0 6.6 %collective-permute-done.9.refs_3_ = f32[2,4,2,16,128]{4,3,2,1,0:T(8,128)S(1)} collective-permute-done((f32[2,4,2,16,128]{4,3,2,1,0:T(8,128)S(1)}, f32[2,4,2,16,128]{4,3,2,1,0:T(8,128)S(1)}, u32[]{:S(2)}, u32[]{:S(2)}) %collective-permute-start.9) | collective-permute-done | bytes 131104 | tf_op jit(solution)/shard_map/ppermute | solution.py:380
  56.6 0.3 collective-permute-done.13.refs_7_
  56.9 1.0 %second_section_sent.1 = f32[2,512,128]{2,1,0:T(8,128)S(1)} custom-call(f32[2,4,2,16,128]{4,3,2,1,0:T(8,128)S(1)} %get-tuple-element.40.refs_0_, f32[2,4,2,16,128]{4,3,2,1,0:T(8,128)S(1)} %collective-permute-done.7.refs_1_, f32[2,4,2,16,128]{4,3,2,1,0:T(8,128)S(1)} %collective-permute-done.8.refs_2_, ...), custom_call_target="tpu_custom_call" | custom-call | flops 603979776 | bytes 4194304 | tf_op jit(solution)/shard_map/second_section_sent/pallas_call | solution.py:331
  57.9 0.1 collective-permute-start.14
  58.0 1.0 %second_section_kept.1.kept_ref = f32[2,512,128]{2,1,0:T(8,128)S(1)} custom-call(f32[2,4,2,16,128]{4,3,2,1,0:T(8,128)S(1)} %get-tuple-element.40.refs_0_, f32[2,4,2,16,128]{4,3,2,1,0:T(8,128)S(1)} %collective-permute-done.7.refs_1_, f32[2,4,2,16,128]{4,3,2,1,0:T(8,128)S(1)} %collective-permute-done.8.refs_2_, ...), custom_call_target="tpu_custom_call" | custom-call | flops 603979776 | bytes 4194304 | tf_op jit(solution)/shard_map/second_section_kept/pallas_call | solution.py:331
  59.0 0.9 %collective-permute-done.14.came_ref = f32[2,512,128]{2,1,0:T(8,128)S(1)} collective-permute-done((f32[2,512,128]{2,1,0:T(8,128)S(1)}, f32[2,512,128]{2,1,0:T(8,128)S(1)}, u32[]{:S(2)}, u32[]{:S(2)}) %collective-permute-start.14) | collective-permute-done | bytes 524320 | tf_op jit(solution)/shard_map/ppermute | solution.py:445
  59.9 3.1 %third_section.1 = f32[2048,128]{1,0:T(8,128)} custom-call(f32[2,512,128]{2,1,0:T(8,128)S(1)} %second_section_kept.1.kept_ref, f32[2,512,128]{2,1,0:T(8,128)S(1)} %collective-permute-done.14.came_ref, bf16[256,768]{1,0:T(8,128)(2,1)S(1)} %get-tuple-element.50.refs_0_, bf16[256,768]{1,0:T(8,128)(2,1)S(1)} %get-tuple-element.51.refs_1_, ...), custom_call_target="tpu_custom_call" | custom-call | flops 1610612736 | bytes 4194304 | tf_op jit(solution)/shard_map/third_section/pallas_call | solution.py:331
  (12 shorter events, 0.0 us)
Async XLA Ops:
  0.9 11.8 %collective-permute-start = (f32[256,128]{1,0:T(8,128)S(1)}, f32[256,128]{1,0:T(8,128)S(1)}, u32[]{:S(2)}, u32[]{:S(2)}) collective-permute-start(f32[256,128]{1,0:T(8,128)S(1)} %dynamic-slice_bitcast_fusion), channel_id=1, source_target_pairs={{0,4},{2,6},{4,12},{6,14},{8,0},{10,2},{12,8},{14,10},{1,5},{3,7},... | collective-permute-start | bytes 393224 | tf_op jit(solution)/shard_map/ppermute | solution.py:380
  4.0 1.2 %copy-start = (f32[2,131072]{1,0:T(2,128)S(1)}, f32[2,131072]{1,0:T(2,128)}, u32[]{:S(2)}) copy-start(f32[2,131072]{1,0:T(2,128)} %param.3) | copy-start | bytes 3145732
  5.9 8.8 %collective-permute-start.1 = (f32[256,128]{1,0:T(8,128)S(1)}, f32[256,128]{1,0:T(8,128)S(1)}, u32[]{:S(2)}, u32[]{:S(2)}) collective-permute-start(f32[256,128]{1,0:T(8,128)S(1)} %get-tuple-element.30), channel_id=1, source_target_pairs={{0,12},{2,14},{4,8},{6,10},{8,4},{10,6},{12,0},{14,2},{1,13},{3,15... | collective-permute-start | bytes 393224 | tf_op jit(solution)/shard_map/ppermute | solution.py:380
  8.4 19.4 %collective-permute-start.2 = (f32[256,128]{1,0:T(8,128)S(1)}, f32[256,128]{1,0:T(8,128)S(1)}, u32[]{:S(2)}, u32[]{:S(2)}) collective-permute-start(f32[256,128]{1,0:T(8,128)S(1)} %get-tuple-element.31), channel_id=1, source_target_pairs={{0,6},{2,4},{4,14},{6,12},{8,2},{10,0},{12,10},{14,8},{1,7},{3,5},... | collective-permute-start | bytes 393224 | tf_op jit(solution)/shard_map/ppermute | solution.py:380
  9.5 18.4 %collective-permute-start.3 = (f32[256,128]{1,0:T(8,128)S(1)}, f32[256,128]{1,0:T(8,128)S(1)}, u32[]{:S(2)}, u32[]{:S(2)}) collective-permute-start(f32[256,128]{1,0:T(8,128)S(1)} %get-tuple-element.32), channel_id=1, source_target_pairs={{0,14},{2,12},{4,10},{6,8},{8,6},{10,4},{12,2},{14,0},{1,15},{3,13... | collective-permute-start | bytes 393224 | tf_op jit(solution)/shard_map/ppermute | solution.py:380
  12.4 15.9 %collective-permute-start.4 = (f32[256,128]{1,0:T(8,128)S(1)}, f32[256,128]{1,0:T(8,128)S(1)}, u32[]{:S(2)}, u32[]{:S(2)}) collective-permute-start(f32[256,128]{1,0:T(8,128)S(1)} %get-tuple-element.34), channel_id=1, source_target_pairs={{0,8},{2,10},{4,0},{6,2},{8,12},{10,14},{12,4},{14,6},{1,9},{3,11}... | collective-permute-start | bytes 393224 | tf_op jit(solution)/shard_map/ppermute | solution.py:380
  12.7 15.6 %collective-permute-start.5 = (f32[256,128]{1,0:T(8,128)S(1)}, f32[256,128]{1,0:T(8,128)S(1)}, u32[]{:S(2)}, u32[]{:S(2)}) collective-permute-start(f32[256,128]{1,0:T(8,128)S(1)} %get-tuple-element.35), channel_id=1, source_target_pairs={{0,10},{2,8},{4,2},{6,0},{8,14},{10,12},{12,6},{14,4},{1,11},{3,9}... | collective-permute-start | bytes 393224 | tf_op jit(solution)/shard_map/ppermute | solution.py:380
  14.8 13.5 %collective-permute-start.6 = (f32[256,128]{1,0:T(8,128)S(1)}, f32[256,128]{1,0:T(8,128)S(1)}, u32[]{:S(2)}, u32[]{:S(2)}) collective-permute-start(f32[256,128]{1,0:T(8,128)S(1)} %get-tuple-element.36), channel_id=1, source_target_pairs={{0,2},{2,0},{4,6},{6,4},{8,10},{10,8},{12,14},{14,12},{1,3},{3,1},... | collective-permute-start | bytes 393224 | tf_op jit(solution)/shard_map/ppermute | solution.py:380
  15.8 0.7 %copy-start.1 = (s32[18]{0:T(128)S(1)}, s32[18]{0:T(128)}, u32[]{:S(2)}) copy-start(s32[18]{0:T(128)} %bits_ref.1) | copy-start | bytes 220
  30.8 18.3 %collective-permute-start.7 = (f32[2,4,2,16,128]{4,3,2,1,0:T(8,128)S(1)}, f32[2,4,2,16,128]{4,3,2,1,0:T(8,128)S(1)}, u32[]{:S(2)}, u32[]{:S(2)}) collective-permute-start(f32[2,4,2,16,128]{4,3,2,1,0:T(8,128)S(1)} %get-tuple-element.41), channel_id=1, source_target_pairs={{0,4},{2,6},{4,12},{6,14},{8,0},{10,2},{12,8},{14,10},{1,5},{3,7},... | collective-permute-start | bytes 393224 | tf_op jit(solution)/shard_map/ppermute | solution.py:380
  37.5 11.6 %collective-permute-start.8 = (f32[2,4,2,16,128]{4,3,2,1,0:T(8,128)S(1)}, f32[2,4,2,16,128]{4,3,2,1,0:T(8,128)S(1)}, u32[]{:S(2)}, u32[]{:S(2)}) collective-permute-start(f32[2,4,2,16,128]{4,3,2,1,0:T(8,128)S(1)} %get-tuple-element.42), channel_id=1, source_target_pairs={{0,12},{2,14},{4,8},{6,10},{8,4},{10,6},{12,0},{14,2},{1,13},{3,15... | collective-permute-start | bytes 393224 | tf_op jit(solution)/shard_map/ppermute | solution.py:380
  40.5 16.0 %collective-permute-start.9 = (f32[2,4,2,16,128]{4,3,2,1,0:T(8,128)S(1)}, f32[2,4,2,16,128]{4,3,2,1,0:T(8,128)S(1)}, u32[]{:S(2)}, u32[]{:S(2)}) collective-permute-start(f32[2,4,2,16,128]{4,3,2,1,0:T(8,128)S(1)} %get-tuple-element.43), channel_id=1, source_target_pairs={{0,6},{2,4},{4,14},{6,12},{8,2},{10,0},{12,10},{14,8},{1,7},{3,5},... | collective-permute-start | bytes 393224 | tf_op jit(solution)/shard_map/ppermute | solution.py:380
  40.5 16.0 %collective-permute-start.10 = (f32[2,4,2,16,128]{4,3,2,1,0:T(8,128)S(1)}, f32[2,4,2,16,128]{4,3,2,1,0:T(8,128)S(1)}, u32[]{:S(2)}, u32[]{:S(2)}) collective-permute-start(f32[2,4,2,16,128]{4,3,2,1,0:T(8,128)S(1)} %get-tuple-element.44), channel_id=1, source_target_pairs={{0,14},{2,12},{4,10},{6,8},{8,6},{10,4},{12,2},{14,0},{1,15},{3,13... | collective-permute-start | bytes 393224 | tf_op jit(solution)/shard_map/ppermute | solution.py:380
  41.6 15.0 %collective-permute-start.11 = (f32[2,4,2,16,128]{4,3,2,1,0:T(8,128)S(1)}, f32[2,4,2,16,128]{4,3,2,1,0:T(8,128)S(1)}, u32[]{:S(2)}, u32[]{:S(2)}) collective-permute-start(f32[2,4,2,16,128]{4,3,2,1,0:T(8,128)S(1)} %get-tuple-element.45), channel_id=1, source_target_pairs={{0,8},{2,10},{4,0},{6,2},{8,12},{10,14},{12,4},{14,6},{1,9},{3,11}... | collective-permute-start | bytes 393224 | tf_op jit(solution)/shard_map/ppermute | solution.py:380
  49.1 7.4 %collective-permute-start.12 = (f32[2,4,2,16,128]{4,3,2,1,0:T(8,128)S(1)}, f32[2,4,2,16,128]{4,3,2,1,0:T(8,128)S(1)}, u32[]{:S(2)}, u32[]{:S(2)}) collective-permute-start(f32[2,4,2,16,128]{4,3,2,1,0:T(8,128)S(1)} %get-tuple-element.46), channel_id=1, source_target_pairs={{0,10},{2,8},{4,2},{6,0},{8,14},{10,12},{12,6},{14,4},{1,11},{3,9}... | collective-permute-start | bytes 393224 | tf_op jit(solution)/shard_map/ppermute | solution.py:380
  49.1 7.8 %collective-permute-start.13 = (f32[2,4,2,16,128]{4,3,2,1,0:T(8,128)S(1)}, f32[2,4,2,16,128]{4,3,2,1,0:T(8,128)S(1)}, u32[]{:S(2)}, u32[]{:S(2)}) collective-permute-start(f32[2,4,2,16,128]{4,3,2,1,0:T(8,128)S(1)} %get-tuple-element.47), channel_id=1, source_target_pairs={{0,2},{2,0},{4,6},{6,4},{8,10},{10,8},{12,14},{14,12},{1,3},{3,1},... | collective-permute-start | bytes 393224 | tf_op jit(solution)/shard_map/ppermute | solution.py:380
  57.9 2.0 %copy-start.2 = (bf16[512,1536]{1,0:T(8,128)(2,1)S(1)}, bf16[512,1536]{1,0:T(8,128)(2,1)}, u32[]{:S(2)}) copy-start(bf16[512,1536]{1,0:T(8,128)(2,1)} %get-tuple-element.52.refs_2_) | copy-start | bytes 4718596
  57.9 2.0 %collective-permute-start.14 = (f32[2,512,128]{2,1,0:T(8,128)S(1)}, f32[2,512,128]{2,1,0:T(8,128)S(1)}, u32[]{:S(2)}, u32[]{:S(2)}) collective-permute-start(f32[2,512,128]{2,1,0:T(8,128)S(1)} %second_section_sent.1), channel_id=1, source_target_pairs={{0,1},{1,0},{2,3},{3,2},{4,5},{5,4},{6,7},{7,6},{8,9},{9,8},{10,11... | collective-permute-start | bytes 1572872 | tf_op jit(solution)/shard_map/ppermute | solution.py:445

commit v10 on v9

--- a/solution.py
+++ b/solution.py
@@ -13,7 +13,12 @@
 VMEM_LIMIT = 14 * 1024 * 1024
 LARGE_VMEM = 48 * 1024 * 1024
 PIECES = 4
-ORDER = [(1, 0), (2, 0), (1, 1), (2, 1), (3, 0), (3, 1), (0, 1)]
+ORDERS = {
+    (0, 1): [7, 6, 3, 2, 5, 4, 1],
+    (0, 0): [7, 1, 3, 2, 5, 4, 6],
+    (1, 1): [3, 7, 6, 2, 5, 4, 1],
+    (1, 0): [3, 7, 1, 2, 5, 4, 6],
+}
 
 
 def window_offsets(span, gate_bits):
@@ -86,7 +91,7 @@
     if number == 0:
         size = dim // count
         spot, source = column // size, jnp.zeros_like(column)
-        for index, partner in enumerate(sources_of(count)):
+        for index, partner in enumerate(partners_of(count)):
             source = jnp.where(spot == index, partner, source)
         natural = source * size + lax.rem(column, size)
     else:
@@ -144,43 +149,53 @@
     low_ref[...] = jnp.concatenate([high, rest, high], axis=0)
 
 
-def partners_of(count):
+def orders_of(count):
     if count == 8:
-        cycle = [0, 1, 3, 2]
-        tables = [list(range(count))]
-        for shift, crossed in ORDER:
-            line = [cycle[(cycle.index(z) + shift) % 4] for z in range(4)]
-            tables.append([2 * line[i // 2] + (i % 2 ^ crossed) for i in range(count)])
-        return tables
+        return ORDERS
     half = count // 2
     far, near = list(range(count - 1, half - 1, -1)), list(range(half - 1, 0, -1))
-    order = [0]
+    order = []
     while far or near:
         order += far[:2] + near[:2]
         far, near = far[2:], near[2:]
-    return [[i ^ distance for i in range(count)] for distance in order]
-
-
-def look_up(table):
-    me = lax.axis_index("qa")
-    if table == [i ^ table[0] for i in range(len(table))]:
-        return jnp.bitwise_xor(me, table[0])
-    found = jnp.int32(table[0])
-    for index in range(1, len(table)):
-        found = jnp.where(me == index, jnp.int32(table[index]), found)
+    return {(core, 0): order for core in range(2)}
+
+
+def place_of(index, count):
+    return int(index // 2 in (0, 3)) if count == 8 else 0
+
+
+def tables_of(count, cores):
+    orders = orders_of(count)
+    return [
+        [
+            (index ^ orders[core, place_of(index, count)][spot]) * cores + core
+            for index in range(count)
+            for core in range(cores)
+        ]
+        for spot in range(count - 1)
+    ]
+
+
+def partners_of(count):
+    me, core = lax.axis_index("qa"), lax.axis_index("qb")
+    orders = orders_of(count)
+    places = sorted({place for _, place in orders})
+    found = [me]
+    for spot in range(count - 1):
+        per_core = []
+        for c in range(2):
+            distance = jnp.int32(orders[c, places[0]][spot])
+            if len(places) > 1:
+                at_end = jnp.logical_or(me < 2, me >= 6)
+                distance = jnp.where(at_end, jnp.int32(orders[c, 1][spot]), distance)
+            per_core.append(distance)
+        found.append(jnp.bitwise_xor(me, jnp.where(core == 0, per_core[0], per_core[1])))
     return found
 
 
-def dests_of(count):
-    return [look_up(table) for table in partners_of(count)]
-
-
-def sources_of(count):
-    return [look_up([table.index(i) for i in range(count)]) for table in partners_of(count)]
-
-
 def split_kernel(x_ref, *outs):
-    for dest, out_ref in zip(dests_of(len(outs)), outs):
+    for dest, out_ref in zip(partners_of(len(outs)), outs):
         out_ref[...] = x_ref[dest]
 
 
@@ -275,7 +290,7 @@
     run_top_stage(stages[0], weights[0], lane_bits, whole, halves[:2])
     done = run_halves(stages[1:], weights[1:], lane_bits, halves[:2], halves[2:])
     tops, mids, _, inner, _ = outs[0].shape
-    dests = dests_of(count)
+    dests = partners_of(count)
     for top in range(tops):
         for dest, out_ref in zip(dests, outs):
             for mid in range(mids):
@@ -289,7 +304,7 @@
     out_ref, one, two = refs
     core = lax.axis_index("qb")
     top = core if stays else 1 - core
-    for source, block_ref in zip(sources_of(count), blocks):
+    for source, block_ref in zip(partners_of(count), blocks):
         _, mids, _, inner, _ = block_ref.shape
         for mid in range(mids):
             start = pl.multiple_of((mid * count + source) * inner, inner)
@@ -372,12 +387,12 @@
     )
 
     blocks = list(blocks)
-    blocks[1] = lax.dynamic_index_in_dim(state, look_up(partners_of(qa)[1]), 0, keepdims=False)
+    blocks[1] = lax.dynamic_index_in_dim(state, partners_of(qa)[1], 0, keepdims=False)
 
     def exchange(blocks):
         came = [blocks[0]]
-        for table, piece in zip(partners_of(qa)[1:], blocks[1:]):
-            came.append(lax.ppermute(piece, "qa", list(enumerate(table))))
+        for table, piece in zip(tables_of(qa, qb), blocks[1:]):
+            came.append(lax.ppermute(piece, ("qa", "qb"), list(enumerate(table))))
         return came
 
     blocks = exchange(blocks)

time: 64.2 us -> 62.7 us (0.977); the launches traced: 63 us -> 62.2 us
  waiting for transfers between devices: 16.4 us -> 12.9 us
  starting transfers between devices: 27.3 us -> 30 us
    ppermute x14, waiting for transfers between devices: 15.5 us -> 12 us  [exchange(): came.append(lax.ppermute(piece, ('qa', 'qb'), list(enumerate(table))))]
    ppermute x14, starting transfers between devices: 27.2 us -> 29.9 us  [exchange(): came.append(lax.ppermute(piece, ('qa', 'qb'), list(enumerate(table))))]
  transfers between devices with their start and end apart: 15 -> 15, of which waited for: 5 -> 7; matrix products, arithmetic and copies ran while one was open for 0% -> 0% of each run, Pallas kernels for 16% -> 16%
where the time goes in v10:
time: 62.7 us; the launch traced here: 62.2 us
  starting transfers between devices  30 us (48%)
  Pallas kernels  16.4 us (26%)
  waiting for transfers between devices  12.9 us (21%)
  local copies, waits for them, and re-layouts  2.8 us (4%)
    ppermute x14, starting transfers between devices, exchange(): came.append(lax.ppermute(piece, ('qa', 'qb'), list(enumerate(table))))  29.9 us
    pallas_call x7, Pallas kernels, call(): pl.pallas_call(kernel, out_shape=out_shapes, in_specs=in_specs, out_specs...  16.4 us
    ppermute x14, waiting for transfers between devices, exchange(): came.append(lax.ppermute(piece, ('qa', 'qb'), list(enumerate(table))))  12 us
    unnamed x6, local copies, waits for them, and re-layouts  1.88 us
  transfers between devices with their start and end apart: 15, of which 7 were waited for; matrix products, arithmetic and copies ran while one was open for 0% of the time, Pallas kernels for 16%

profile of v10, /device:TPU:0, one launch (start us, length us, event | category | flops | bytes accessed | tf_op | source)
XLA Modules:
  0.0 62.2 jit_solution(16582457316766321015)
XLA Ops:
  0.0 0.9 %dynamic-slice_bitcast_fusion = f32[256,128]{1,0:T(8,128)S(1)} fusion(f32[8,256,128]{2,1,0:T(8,128)} %bitcast.12, s32[]{:T(128)S(6)} %select_n.11), kind=kLoop, calls=%fused_computation | loop fusion | bytes 262148 | tf_op jit(solution)/shard_map/jit(dynamic_index_in_dim)/squeeze | solution.py:390
  0.9 6.1 %collective-permute-start = (f32[256,128]{1,0:T(8,128)S(1)}, f32[256,128]{1,0:T(8,128)S(1)}, u32[]{:S(2)}, u32[]{:S(2)}) collective-permute-start(f32[256,128]{1,0:T(8,128)S(1)} %dynamic-slice_bitcast_fusion), channel_id=1, source_target_pairs={{0,14},{1,7},{2,12},{3,5},{4,10},{5,3},{6,8},{7,1},{8,6},{9,15},{1... | collective-permute-start | bytes 393224 | tf_op jit(solution)/shard_map/ppermute | solution.py:395
  7.0 1.2 %copy-done = f32[2,131072]{1,0:T(2,128)S(1)} copy-done((f32[2,131072]{1,0:T(2,128)S(1)}, f32[2,131072]{1,0:T(2,128)}, u32[]{:S(2)}) %copy-start) | copy-done | bytes 1048600
  8.2 0.7 %split_state.1 = (f32[256,128]{1,0:T(8,128)S(1)}, f32[256,128]{1,0:T(8,128)}, f32[256,128]{1,0:T(8,128)S(1)}, f32[256,128]{1,0:T(8,128)S(1)}, f32[256,128]{1,0:T...) custom-call(f32[8,256,128]{2,1,0:T(8,128)S(1)} %bitcast.13), custom_call_target="tpu_custom_call" | custom-call | bytes 4194304 | tf_op jit(solution)/shard_map/split_state/pallas_call | solution.py:346
  8.9 0.2 collective-permute-start.1
  9.2 0.8 %collective-permute-start.2 = (f32[256,128]{1,0:T(8,128)S(1)}, f32[256,128]{1,0:T(8,128)S(1)}, u32[]{:S(2)}, u32[]{:S(2)}) collective-permute-start(f32[256,128]{1,0:T(8,128)S(1)} %get-tuple-element.31), channel_id=1, source_target_pairs={{0,6},{1,13},{2,4},{3,15},{4,2},{5,7},{6,0},{7,5},{8,14},{9,11},{1... | collective-permute-start | bytes 393224 | tf_op jit(solution)/shard_map/ppermute | solution.py:395
  9.9 1.0 %collective-permute-start.3 = (f32[256,128]{1,0:T(8,128)S(1)}, f32[256,128]{1,0:T(8,128)S(1)}, u32[]{:S(2)}, u32[]{:S(2)}) collective-permute-start(f32[256,128]{1,0:T(8,128)S(1)} %get-tuple-element.32), channel_id=1, source_target_pairs={{0,4},{1,5},{2,6},{3,7},{4,0},{5,1},{6,2},{7,3},{8,12},{9,13},{10,... | collective-permute-start | bytes 393224 | tf_op jit(solution)/shard_map/ppermute | solution.py:395
  11.0 3.2 %collective-permute-start.4 = (f32[256,128]{1,0:T(8,128)S(1)}, f32[256,128]{1,0:T(8,128)S(1)}, u32[]{:S(2)}, u32[]{:S(2)}) collective-permute-start(f32[256,128]{1,0:T(8,128)S(1)} %get-tuple-element.34), channel_id=1, source_target_pairs={{0,10},{1,11},{2,8},{3,9},{4,14},{5,15},{6,12},{7,13},{8,2},{9,3},... | collective-permute-start | bytes 393224 | tf_op jit(solution)/shard_map/ppermute | solution.py:395
  14.2 0.8 %collective-permute-start.5 = (f32[256,128]{1,0:T(8,128)S(1)}, f32[256,128]{1,0:T(8,128)S(1)}, u32[]{:S(2)}, u32[]{:S(2)}) collective-permute-start(f32[256,128]{1,0:T(8,128)S(1)} %get-tuple-element.35), channel_id=1, source_target_pairs={{0,8},{1,9},{2,10},{3,11},{4,12},{5,13},{6,14},{7,15},{8,0},{9,1},... | collective-permute-start | bytes 393224 | tf_op jit(solution)/shard_map/ppermute | solution.py:395
  15.0 2.1 %collective-permute-done.1.refs_2_ = f32[256,128]{1,0:T(8,128)S(1)} collective-permute-done((f32[256,128]{1,0:T(8,128)S(1)}, f32[256,128]{1,0:T(8,128)S(1)}, u32[]{:S(2)}, u32[]{:S(2)}) %collective-permute-start.1) | collective-permute-done | bytes 131104 | tf_op jit(solution)/shard_map/ppermute | solution.py:395
  17.1 0.6 collective-permute-start.6
  17.8 0.7 %copy-done.1 = s32[18]{0:T(128)S(1)} copy-done((s32[18]{0:T(128)S(1)}, s32[18]{0:T(128)}, u32[]{:S(2)}) %copy-start.1) | copy-done | bytes 96
  18.4 7.6 %prepare_gates.1 = (bf16[768,256]{1,0:T(8,128)(2,1)S(1)}, bf16[256,768]{1,0:T(8,128)(2,1)S(1)}, bf16[256,768]{1,0:T(8,128)(2,1)S(1)}, bf16[512,1536]{1,0:T(8,128...) custom-call(s32[18]{0:T(128)S(1)} %copy-done.1, ...), custom_call_target="tpu_custom_call" | custom-call | flops 3221225472 | bytes 4194304 | tf_op jit(solution)/shard_map/prepare_gates/pallas_call | solution.py:346
  26.1 0.4 low_gate_early.1.refs_0_
  26.5 1.6 %collective-permute-done.5.refs_2_ = f32[256,128]{1,0:T(8,128)S(1)} collective-permute-done((f32[256,128]{1,0:T(8,128)S(1)}, f32[256,128]{1,0:T(8,128)S(1)}, u32[]{:S(2)}, u32[]{:S(2)}) %collective-permute-start.5) | collective-permute-done | bytes 131104 | tf_op jit(solution)/shard_map/ppermute | solution.py:395
  28.1 0.0 collective-permute-done.6.refs_3_
  28.1 2.5 %first_section.1 = (f32[2,4,2,16,128]{4,3,2,1,0:T(8,128)S(1)}, f32[2,4,2,16,128]{4,3,2,1,0:T(8,128)S(1)}, f32[2,4,2,16,128]{4,3,2,1,0:T(8,128)S(1)}, f32[2,4,2,1...) custom-call(f32[2,1024,128]{2,1,0:T(8,128)S(1)} %low_gate_early.1.re, ...), custom_call_target="tpu_custom_call", output_to_operand_aliasing={{8}: (0, {})} | custom-call | flops 2013265920 | bytes 4194304 | tf_op jit(solution)/shard_map/first_section/pallas_call | solution.py:346
  30.7 3.3 %collective-permute-start.7 = (f32[2,4,2,16,128]{4,3,2,1,0:T(8,128)S(1)}, f32[2,4,2,16,128]{4,3,2,1,0:T(8,128)S(1)}, u32[]{:S(2)}, u32[]{:S(2)}) collective-permute-start(f32[2,4,2,16,128]{4,3,2,1,0:T(8,128)S(1)} %get-tuple-element.41), channel_id=1, source_target_pairs={{0,14},{1,7},{2,12},{3,5},{4,10},{5,3},{6,8},{7,1},{8,6},{9,15},{1... | collective-permute-start | bytes 393224 | tf_op jit(solution)/shard_map/ppermute | solution.py:395
  34.0 0.6 collective-permute-start.8
  34.6 2.5 %collective-permute-start.9 = (f32[2,4,2,16,128]{4,3,2,1,0:T(8,128)S(1)}, f32[2,4,2,16,128]{4,3,2,1,0:T(8,128)S(1)}, u32[]{:S(2)}, u32[]{:S(2)}) collective-permute-start(f32[2,4,2,16,128]{4,3,2,1,0:T(8,128)S(1)} %get-tuple-element.43), channel_id=1, source_target_pairs={{0,6},{1,13},{2,4},{3,15},{4,2},{5,7},{6,0},{7,5},{8,14},{9,11},{1... | collective-permute-start | bytes 393224 | tf_op jit(solution)/shard_map/ppermute | solution.py:395
  37.1 0.4 collective-permute-start.10
  37.5 2.0 %collective-permute-start.11 = (f32[2,4,2,16,128]{4,3,2,1,0:T(8,128)S(1)}, f32[2,4,2,16,128]{4,3,2,1,0:T(8,128)S(1)}, u32[]{:S(2)}, u32[]{:S(2)}) collective-permute-start(f32[2,4,2,16,128]{4,3,2,1,0:T(8,128)S(1)} %get-tuple-element.45), channel_id=1, source_target_pairs={{0,10},{1,11},{2,8},{3,9},{4,14},{5,15},{6,12},{7,13},{8,2},{9,3},... | collective-permute-start | bytes 393224 | tf_op jit(solution)/shard_map/ppermute | solution.py:395
  39.4 0.1 collective-permute-done.7.refs_1_
  39.5 8.4 %collective-permute-start.12 = (f32[2,4,2,16,128]{4,3,2,1,0:T(8,128)S(1)}, f32[2,4,2,16,128]{4,3,2,1,0:T(8,128)S(1)}, u32[]{:S(2)}, u32[]{:S(2)}) collective-permute-start(f32[2,4,2,16,128]{4,3,2,1,0:T(8,128)S(1)} %get-tuple-element.46), channel_id=1, source_target_pairs={{0,8},{1,9},{2,10},{3,11},{4,12},{5,13},{6,14},{7,15},{8,0},{9,1},... | collective-permute-start | bytes 393224 | tf_op jit(solution)/shard_map/ppermute | solution.py:395
  48.0 1.4 %collective-permute-done.9.refs_3_ = f32[2,4,2,16,128]{4,3,2,1,0:T(8,128)S(1)} collective-permute-done((f32[2,4,2,16,128]{4,3,2,1,0:T(8,128)S(1)}, f32[2,4,2,16,128]{4,3,2,1,0:T(8,128)S(1)}, u32[]{:S(2)}, u32[]{:S(2)}) %collective-permute-start.9) | collective-permute-done | bytes 131104 | tf_op jit(solution)/shard_map/ppermute | solution.py:395
  49.4 0.9 %collective-permute-done.10.refs_4_ = f32[2,4,2,16,128]{4,3,2,1,0:T(8,128)S(1)} collective-permute-done((f32[2,4,2,16,128]{4,3,2,1,0:T(8,128)S(1)}, f32[2,4,2,16,128]{4,3,2,1,0:T(8,128)S(1)}, u32[]{:S(2)}, u32[]{:S(2)}) %collective-permute-start.10) | collective-permute-done | bytes 131104 | tf_op jit(solution)/shard_map/ppermute | solution.py:395
  50.3 5.8 %collective-permute-done.12.refs_6_ = f32[2,4,2,16,128]{4,3,2,1,0:T(8,128)S(1)} collective-permute-done((f32[2,4,2,16,128]{4,3,2,1,0:T(8,128)S(1)}, f32[2,4,2,16,128]{4,3,2,1,0:T(8,128)S(1)}, u32[]{:S(2)}, u32[]{:S(2)}) %collective-permute-start.12) | collective-permute-done | bytes 131104 | tf_op jit(solution)/shard_map/ppermute | solution.py:395
  56.1 1.0 %second_section_sent.1 = f32[2,512,128]{2,1,0:T(8,128)S(1)} custom-call(f32[2,4,2,16,128]{4,3,2,1,0:T(8,128)S(1)} %get-tuple-element.40.refs_0_, f32[2,4,2,16,128]{4,3,2,1,0:T(8,128)S(1)} %collective-permute-done.7.refs_1_, f32[2,4,2,16,128]{4,3,2,1,0:T(8,128)S(1)} %collective-permute-done.8.refs_2_, ...), custom_call_target="tpu_custom_call" | custom-call | flops 603979776 | bytes 4194304 | tf_op jit(solution)/shard_map/second_section_sent/pallas_call | solution.py:346
  57.1 0.1 collective-permute-start.14
  57.2 1.0 %second_section_kept.1.kept_ref = f32[2,512,128]{2,1,0:T(8,128)S(1)} custom-call(f32[2,4,2,16,128]{4,3,2,1,0:T(8,128)S(1)} %get-tuple-element.40.refs_0_, f32[2,4,2,16,128]{4,3,2,1,0:T(8,128)S(1)} %collective-permute-done.7.refs_1_, f32[2,4,2,16,128]{4,3,2,1,0:T(8,128)S(1)} %collective-permute-done.8.refs_2_, ...), custom_call_target="tpu_custom_call" | custom-call | flops 603979776 | bytes 4194304 | tf_op jit(solution)/shard_map/second_section_kept/pallas_call | solution.py:346
  58.2 0.9 %collective-permute-done.14.came_ref = f32[2,512,128]{2,1,0:T(8,128)S(1)} collective-permute-done((f32[2,512,128]{2,1,0:T(8,128)S(1)}, f32[2,512,128]{2,1,0:T(8,128)S(1)}, u32[]{:S(2)}, u32[]{:S(2)}) %collective-permute-start.14) | collective-permute-done | bytes 524320 | tf_op jit(solution)/shard_map/ppermute | solution.py:460
  59.1 3.1 %third_section.1 = f32[2048,128]{1,0:T(8,128)} custom-call(f32[2,512,128]{2,1,0:T(8,128)S(1)} %second_section_kept.1.kept_ref, f32[2,512,128]{2,1,0:T(8,128)S(1)} %collective-permute-done.14.came_ref, bf16[256,768]{1,0:T(8,128)(2,1)S(1)} %get-tuple-element.50.refs_0_, bf16[256,768]{1,0:T(8,128)(2,1)S(1)} %get-tuple-element.51.refs_1_, ...), custom_call_target="tpu_custom_call" | custom-call | flops 1610612736 | bytes 4194304 | tf_op jit(solution)/shard_map/third_section/pallas_call | solution.py:346
  (12 shorter events, 0.0 us)
Async XLA Ops:
  0.9 13.3 %collective-permute-start = (f32[256,128]{1,0:T(8,128)S(1)}, f32[256,128]{1,0:T(8,128)S(1)}, u32[]{:S(2)}, u32[]{:S(2)}) collective-permute-start(f32[256,128]{1,0:T(8,128)S(1)} %dynamic-slice_bitcast_fusion), channel_id=1, source_target_pairs={{0,14},{1,7},{2,12},{3,5},{4,10},{5,3},{6,8},{7,1},{8,6},{9,15},{1... | collective-permute-start | bytes 393224 | tf_op jit(solution)/shard_map/ppermute | solution.py:395
  7.0 1.2 %copy-start = (f32[2,131072]{1,0:T(2,128)S(1)}, f32[2,131072]{1,0:T(2,128)}, u32[]{:S(2)}) copy-start(f32[2,131072]{1,0:T(2,128)} %param.3) | copy-start | bytes 3145732
  8.9 8.2 %collective-permute-start.1 = (f32[256,128]{1,0:T(8,128)S(1)}, f32[256,128]{1,0:T(8,128)S(1)}, u32[]{:S(2)}, u32[]{:S(2)}) collective-permute-start(f32[256,128]{1,0:T(8,128)S(1)} %get-tuple-element.30), channel_id=1, source_target_pairs={{0,12},{1,15},{2,14},{3,13},{4,6},{5,11},{6,4},{7,9},{8,10},{9,7},... | collective-permute-start | bytes 393224 | tf_op jit(solution)/shard_map/ppermute | solution.py:395
  9.2 16.9 %collective-permute-start.2 = (f32[256,128]{1,0:T(8,128)S(1)}, f32[256,128]{1,0:T(8,128)S(1)}, u32[]{:S(2)}, u32[]{:S(2)}) collective-permute-start(f32[256,128]{1,0:T(8,128)S(1)} %get-tuple-element.31), channel_id=1, source_target_pairs={{0,6},{1,13},{2,4},{3,15},{4,2},{5,7},{6,0},{7,5},{8,14},{9,11},{1... | collective-permute-start | bytes 393224 | tf_op jit(solution)/shard_map/ppermute | solution.py:395
  9.9 16.1 %collective-permute-start.3 = (f32[256,128]{1,0:T(8,128)S(1)}, f32[256,128]{1,0:T(8,128)S(1)}, u32[]{:S(2)}, u32[]{:S(2)}) collective-permute-start(f32[256,128]{1,0:T(8,128)S(1)} %get-tuple-element.32), channel_id=1, source_target_pairs={{0,4},{1,5},{2,6},{3,7},{4,0},{5,1},{6,2},{7,3},{8,12},{9,13},{10,... | collective-permute-start | bytes 393224 | tf_op jit(solution)/shard_map/ppermute | solution.py:395
  11.0 15.5 %collective-permute-start.4 = (f32[256,128]{1,0:T(8,128)S(1)}, f32[256,128]{1,0:T(8,128)S(1)}, u32[]{:S(2)}, u32[]{:S(2)}) collective-permute-start(f32[256,128]{1,0:T(8,128)S(1)} %get-tuple-element.34), channel_id=1, source_target_pairs={{0,10},{1,11},{2,8},{3,9},{4,14},{5,15},{6,12},{7,13},{8,2},{9,3},... | collective-permute-start | bytes 393224 | tf_op jit(solution)/shard_map/ppermute | solution.py:395
  14.2 13.9 %collective-permute-start.5 = (f32[256,128]{1,0:T(8,128)S(1)}, f32[256,128]{1,0:T(8,128)S(1)}, u32[]{:S(2)}, u32[]{:S(2)}) collective-permute-start(f32[256,128]{1,0:T(8,128)S(1)} %get-tuple-element.35), channel_id=1, source_target_pairs={{0,8},{1,9},{2,10},{3,11},{4,12},{5,13},{6,14},{7,15},{8,0},{9,1},... | collective-permute-start | bytes 393224 | tf_op jit(solution)/shard_map/ppermute | solution.py:395
  17.1 11.0 %collective-permute-start.6 = (f32[256,128]{1,0:T(8,128)S(1)}, f32[256,128]{1,0:T(8,128)S(1)}, u32[]{:S(2)}, u32[]{:S(2)}) collective-permute-start(f32[256,128]{1,0:T(8,128)S(1)} %get-tuple-element.36), channel_id=1, source_target_pairs={{0,2},{1,3},{2,0},{3,1},{4,8},{5,9},{6,10},{7,11},{8,4},{9,5},{10,... | collective-permute-start | bytes 393224 | tf_op jit(solution)/shard_map/ppermute | solution.py:395
  17.8 0.7 %copy-start.1 = (s32[18]{0:T(128)S(1)}, s32[18]{0:T(128)}, u32[]{:S(2)}) copy-start(s32[18]{0:T(128)} %bits_ref.1) | copy-start | bytes 220
  30.7 8.9 %collective-permute-start.7 = (f32[2,4,2,16,128]{4,3,2,1,0:T(8,128)S(1)}, f32[2,4,2,16,128]{4,3,2,1,0:T(8,128)S(1)}, u32[]{:S(2)}, u32[]{:S(2)}) collective-permute-start(f32[2,4,2,16,128]{4,3,2,1,0:T(8,128)S(1)} %get-tuple-element.41), channel_id=1, source_target_pairs={{0,14},{1,7},{2,12},{3,5},{4,10},{5,3},{6,8},{7,1},{8,6},{9,15},{1... | collective-permute-start | bytes 393224 | tf_op jit(solution)/shard_map/ppermute | solution.py:395
  34.0 14.0 %collective-permute-start.8 = (f32[2,4,2,16,128]{4,3,2,1,0:T(8,128)S(1)}, f32[2,4,2,16,128]{4,3,2,1,0:T(8,128)S(1)}, u32[]{:S(2)}, u32[]{:S(2)}) collective-permute-start(f32[2,4,2,16,128]{4,3,2,1,0:T(8,128)S(1)} %get-tuple-element.42), channel_id=1, source_target_pairs={{0,12},{1,15},{2,14},{3,13},{4,6},{5,11},{6,4},{7,9},{8,10},{9,7},... | collective-permute-start | bytes 393224 | tf_op jit(solution)/shard_map/ppermute | solution.py:395
  34.6 14.8 %collective-permute-start.9 = (f32[2,4,2,16,128]{4,3,2,1,0:T(8,128)S(1)}, f32[2,4,2,16,128]{4,3,2,1,0:T(8,128)S(1)}, u32[]{:S(2)}, u32[]{:S(2)}) collective-permute-start(f32[2,4,2,16,128]{4,3,2,1,0:T(8,128)S(1)} %get-tuple-element.43), channel_id=1, source_target_pairs={{0,6},{1,13},{2,4},{3,15},{4,2},{5,7},{6,0},{7,5},{8,14},{9,11},{1... | collective-permute-start | bytes 393224 | tf_op jit(solution)/shard_map/ppermute | solution.py:395
  37.1 13.2 %collective-permute-start.10 = (f32[2,4,2,16,128]{4,3,2,1,0:T(8,128)S(1)}, f32[2,4,2,16,128]{4,3,2,1,0:T(8,128)S(1)}, u32[]{:S(2)}, u32[]{:S(2)}) collective-permute-start(f32[2,4,2,16,128]{4,3,2,1,0:T(8,128)S(1)} %get-tuple-element.44), channel_id=1, source_target_pairs={{0,4},{1,5},{2,6},{3,7},{4,0},{5,1},{6,2},{7,3},{8,12},{9,13},{10,... | collective-permute-start | bytes 393224 | tf_op jit(solution)/shard_map/ppermute | solution.py:395
  37.5 12.8 %collective-permute-start.11 = (f32[2,4,2,16,128]{4,3,2,1,0:T(8,128)S(1)}, f32[2,4,2,16,128]{4,3,2,1,0:T(8,128)S(1)}, u32[]{:S(2)}, u32[]{:S(2)}) collective-permute-start(f32[2,4,2,16,128]{4,3,2,1,0:T(8,128)S(1)} %get-tuple-element.45), channel_id=1, source_target_pairs={{0,10},{1,11},{2,8},{3,9},{4,14},{5,15},{6,12},{7,13},{8,2},{9,3},... | collective-permute-start | bytes 393224 | tf_op jit(solution)/shard_map/ppermute | solution.py:395
  39.5 16.6 %collective-permute-start.12 = (f32[2,4,2,16,128]{4,3,2,1,0:T(8,128)S(1)}, f32[2,4,2,16,128]{4,3,2,1,0:T(8,128)S(1)}, u32[]{:S(2)}, u32[]{:S(2)}) collective-permute-start(f32[2,4,2,16,128]{4,3,2,1,0:T(8,128)S(1)} %get-tuple-element.46), channel_id=1, source_target_pairs={{0,8},{1,9},{2,10},{3,11},{4,12},{5,13},{6,14},{7,15},{8,0},{9,1},... | collective-permute-start | bytes 393224 | tf_op jit(solution)/shard_map/ppermute | solution.py:395
  48.0 8.1 %collective-permute-start.13 = (f32[2,4,2,16,128]{4,3,2,1,0:T(8,128)S(1)}, f32[2,4,2,16,128]{4,3,2,1,0:T(8,128)S(1)}, u32[]{:S(2)}, u32[]{:S(2)}) collective-permute-start(f32[2,4,2,16,128]{4,3,2,1,0:T(8,128)S(1)} %get-tuple-element.47), channel_id=1, source_target_pairs={{0,2},{1,3},{2,0},{3,1},{4,8},{5,9},{6,10},{7,11},{8,4},{9,5},{10,... | collective-permute-start | bytes 393224 | tf_op jit(solution)/shard_map/ppermute | solution.py:395
  57.1 2.0 %copy-start.2 = (bf16[512,1536]{1,0:T(8,128)(2,1)S(1)}, bf16[512,1536]{1,0:T(8,128)(2,1)}, u32[]{:S(2)}) copy-start(bf16[512,1536]{1,0:T(8,128)(2,1)} %get-tuple-element.52.refs_2_) | copy-start | bytes 4718596
  57.1 2.0 %collective-permute-start.14 = (f32[2,512,128]{2,1,0:T(8,128)S(1)}, f32[2,512,128]{2,1,0:T(8,128)S(1)}, u32[]{:S(2)}, u32[]{:S(2)}) collective-permute-start(f32[2,512,128]{2,1,0:T(8,128)S(1)} %second_section_sent.1), channel_id=1, source_target_pairs={{0,1},{1,0},{2,3},{3,2},{4,5},{5,4},{6,7},{7,6},{8,9},{9,8},{10,11... | collective-permute-start | bytes 1572872 | tf_op jit(solution)/shard_map/ppermute | solution.py:460

commit v11 on v9

--- a/solution.py
+++ b/solution.py
@@ -13,7 +13,6 @@
 VMEM_LIMIT = 14 * 1024 * 1024
 LARGE_VMEM = 48 * 1024 * 1024
 PIECES = 4
-ORDER = [(1, 0), (2, 0), (1, 1), (2, 1), (3, 0), (3, 1), (0, 1)]
 
 
 def window_offsets(span, gate_bits):
@@ -86,7 +85,7 @@
     if number == 0:
         size = dim // count
         spot, source = column // size, jnp.zeros_like(column)
-        for index, partner in enumerate(sources_of(count)):
+        for index, partner in enumerate(partners_of(count)):
             source = jnp.where(spot == index, partner, source)
         natural = source * size + lax.rem(column, size)
     else:
@@ -144,43 +143,23 @@
     low_ref[...] = jnp.concatenate([high, rest, high], axis=0)
 
 
-def partners_of(count):
-    if count == 8:
-        cycle = [0, 1, 3, 2]
-        tables = [list(range(count))]
-        for shift, crossed in ORDER:
-            line = [cycle[(cycle.index(z) + shift) % 4] for z in range(4)]
-            tables.append([2 * line[i // 2] + (i % 2 ^ crossed) for i in range(count)])
-        return tables
+def distances_of(count):
     half = count // 2
     far, near = list(range(count - 1, half - 1, -1)), list(range(half - 1, 0, -1))
     order = [0]
     while far or near:
         order += far[:2] + near[:2]
         far, near = far[2:], near[2:]
-    return [[i ^ distance for i in range(count)] for distance in order]
-
-
-def look_up(table):
+    return order
+
+
+def partners_of(count):
     me = lax.axis_index("qa")
-    if table == [i ^ table[0] for i in range(len(table))]:
-        return jnp.bitwise_xor(me, table[0])
-    found = jnp.int32(table[0])
-    for index in range(1, len(table)):
-        found = jnp.where(me == index, jnp.int32(table[index]), found)
-    return found
-
-
-def dests_of(count):
-    return [look_up(table) for table in partners_of(count)]
-
-
-def sources_of(count):
-    return [look_up([table.index(i) for i in range(count)]) for table in partners_of(count)]
+    return [jnp.bitwise_xor(me, distance) for distance in distances_of(count)]
 
 
 def split_kernel(x_ref, *outs):
-    for dest, out_ref in zip(dests_of(len(outs)), outs):
+    for dest, out_ref in zip(partners_of(len(outs)), outs):
         out_ref[...] = x_ref[dest]
 
 
@@ -233,7 +212,7 @@
     def load(part, start):
         if not isinstance(source, tuple):
             return source[part, pl.ds(start, dim, stride=stride), :]
-        return jnp.concatenate([half[part, pl.ds(start, dim // 2, stride=stride), :] for half in source], axis=0)
+        return jnp.concatenate([half[part][pl.ds(start, dim // 2, stride=stride), :] for half in source], axis=0)
 
     apply_stage(weights_ref, starts, load, store)
 
@@ -275,7 +254,7 @@
     run_top_stage(stages[0], weights[0], lane_bits, whole, halves[:2])
     done = run_halves(stages[1:], weights[1:], lane_bits, halves[:2], halves[2:])
     tops, mids, _, inner, _ = outs[0].shape
-    dests = dests_of(count)
+    dests = partners_of(count)
     for top in range(tops):
         for dest, out_ref in zip(dests, outs):
             for mid in range(mids):
@@ -286,25 +265,32 @@
 
 def second_kernel(stages, lane_bits, count, stays, *refs):
     blocks, weights, refs = refs[:count], refs[count : count + len(stages)], refs[count + len(stages) :]
-    out_ref, one, two = refs
+    *outs, one, two = refs
     core = lax.axis_index("qb")
     top = core if stays else 1 - core
-    for source, block_ref in zip(sources_of(count), blocks):
+    for source, block_ref in zip(partners_of(count), blocks):
         _, mids, _, inner, _ = block_ref.shape
         for mid in range(mids):
             start = pl.multiple_of((mid * count + source) * inner, inner)
             for part in range(2):
                 one[part, pl.ds(start, inner), :] = block_ref[top, mid, part]
-    for index, (stage, weights_ref) in enumerate(zip(stages, weights)):
-        run_stage(stage, weights_ref, lane_bits, one, out_ref if index == len(stages) - 1 else two)
+    for stage, weights_ref in zip(stages[:-1], weights):
+        run_stage(stage, weights_ref, lane_bits, one, two)
         one, two = two, one
-
-
-def third_kernel(stages, lane_bits, kept_ref, came_ref, *refs):
+    dim, stride, _ = stage_starts(stages[-1], lane_bits, one.shape[1])
+
+    def store(part, start, value):
+        outs[part][pl.ds(start, dim, stride=stride), :] = value
+
+    run_stage(stages[-1], weights[-1], lane_bits, one, store=store)
+
+
+def third_kernel(stages, lane_bits, *refs):
+    kept, came, refs = refs[:2], refs[2:4], refs[4:]
     weights, (out_ref, *halves, sems) = refs[: len(stages)], refs[len(stages) :]
     results = halves[4:]
-    half = kept_ref.shape[1]
-    run_top_stage(stages[0], weights[0], lane_bits, (kept_ref, came_ref), halves[:2])
+    half = kept[0].shape[0]
+    run_top_stage(stages[0], weights[0], lane_bits, (kept, came), halves[:2])
     done = run_halves(stages[1:-1], weights[1:-1], lane_bits, halves[:2], halves[2:4])
     copies = []
     for t in range(2):
@@ -372,12 +358,12 @@
     )
 
     blocks = list(blocks)
-    blocks[1] = lax.dynamic_index_in_dim(state, look_up(partners_of(qa)[1]), 0, keepdims=False)
+    blocks[1] = lax.dynamic_index_in_dim(state, partners_of(qa)[1], 0, keepdims=False)
 
     def exchange(blocks):
         came = [blocks[0]]
-        for table, piece in zip(partners_of(qa)[1:], blocks[1:]):
-            came.append(lax.ppermute(piece, "qa", list(enumerate(table))))
+        for distance, piece in zip(distances_of(qa)[1:], blocks[1:]):
+            came.append(lax.ppermute(piece, "qa", [(i, i ^ distance) for i in range(qa)]))
         return came
 
     blocks = exchange(blocks)
@@ -433,7 +419,7 @@
             call(
                 functools.partial(second_kernel, sections[1], lane_bits, qa, stays),
                 "second_section_kept" if stays else "second_section_sent",
-                shape((2, rows // qb, lanes), F32),
+                (shape((rows // qb, lanes), F32),) * 2,
                 [vmem] * (qa + counts[1]),
                 [half] * 2,
                 1.5,
@@ -442,16 +428,16 @@
             )
         )
         if not stays:
-            came = lax.ppermute(halves[0], "qb", [(i, 1 - i) for i in range(qb)])
+            came = [lax.ppermute(part, "qb", [(i, 1 - i) for i in range(qb)]) for part in halves[0]]
     final = call(
         functools.partial(third_kernel, sections[2], lane_bits),
         "third_section",
         shape((2 * rows, lanes), F32),
-        [vmem] * (2 + counts[2]),
+        [vmem] * (4 + counts[2]),
         [half] * 4 + [pltpu.VMEM((rows, lanes), F32)] * 2 + [pltpu.SemaphoreType.DMA((2 * PIECES,))],
         4,
-        halves[1],
-        came,
+        *halves[1],
+        *came,
         *weights[2],
         out_spec=hbm,
     )

time: 64.2 us -> 61.6 us (0.960); the launches traced: 63 us -> 61.3 us
  waiting for transfers between devices: 16.4 us -> 11.8 us
  starting transfers between devices: 27.3 us -> 30.3 us
    ppermute x15 -> x16, waiting for transfers between devices: 16.4 us -> 11.8 us  [the longest x14 11.4 us: exchange(): lax.ppermute(piece, 'qa', [(i, i ^ distance) for i in range(qa)])]
    ppermute x15 -> x16, starting transfers between devices: 27.3 us -> 30.3 us  [the longest x14 29.7 us: exchange(): lax.ppermute(piece, 'qa', [(i, i ^ distance) for i in range(qa)])]
  transfers between devices with their start and end apart: 15 -> 16, of which waited for: 5 -> 7; matrix products, arithmetic and copies ran while one was open for 0% -> 0% of each run, Pallas kernels for 16% -> 16%
where the time goes in v11:
time: 61.6 us; the launch traced here: 61.3 us
  starting transfers between devices  30.3 us (49%)
  Pallas kernels  16.4 us (27%)
  waiting for transfers between devices  11.8 us (19%)
  local copies, waits for them, and re-layouts  2.8 us (5%)
    ppermute x14, starting transfers between devices, exchange(): lax.ppermute(piece, 'qa', [(i, i ^ distance) for i in range(qa)])  29.7 us
    pallas_call x7, Pallas kernels, call(): pl.pallas_call(kernel, out_shape=out_shapes, in_specs=in_specs, out_specs...  16.4 us
    ppermute x14, waiting for transfers between devices, exchange(): lax.ppermute(piece, 'qa', [(i, i ^ distance) for i in range(qa)])  11.4 us
    unnamed x6, local copies, waits for them, and re-layouts  1.88 us
  transfers between devices with their start and end apart: 16, of which 7 were waited for; matrix products, arithmetic and copies ran while one was open for 0% of the time, Pallas kernels for 16%

profile of v11, /device:TPU:0, one launch (start us, length us, event | category | flops | bytes accessed | tf_op | source)
XLA Modules:
  0.0 61.3 jit_solution(12550133325054370068)
XLA Ops:
  0.0 0.9 %dynamic-slice_bitcast_fusion = f32[256,128]{1,0:T(8,128)S(1)} fusion(f32[8,256,128]{2,1,0:T(8,128)} %bitcast.12, s32[]{:T(128)S(6)} %select_n.4), kind=kLoop, calls=%fused_computation | loop fusion | bytes 262148 | tf_op jit(solution)/shard_map/jit(dynamic_index_in_dim)/squeeze | solution.py:361
  0.9 6.1 %collective-permute-start = (f32[256,128]{1,0:T(8,128)S(1)}, f32[256,128]{1,0:T(8,128)S(1)}, u32[]{:S(2)}, u32[]{:S(2)}) collective-permute-start(f32[256,128]{1,0:T(8,128)S(1)} %dynamic-slice_bitcast_fusion), channel_id=1, source_target_pairs={{0,14},{2,12},{4,10},{6,8},{8,6},{10,4},{12,2},{14,0},{1,15},{3,13... | collective-permute-start | bytes 393224 | tf_op jit(solution)/shard_map/ppermute | solution.py:366
  7.0 1.2 %copy-done = f32[2,131072]{1,0:T(2,128)S(1)} copy-done((f32[2,131072]{1,0:T(2,128)S(1)}, f32[2,131072]{1,0:T(2,128)}, u32[]{:S(2)}) %copy-start) | copy-done | bytes 1048600
  8.2 0.7 %split_state.1 = (f32[256,128]{1,0:T(8,128)S(1)}, f32[256,128]{1,0:T(8,128)}, f32[256,128]{1,0:T(8,128)S(1)}, f32[256,128]{1,0:T(8,128)S(1)}, f32[256,128]{1,0:T...) custom-call(f32[8,256,128]{2,1,0:T(8,128)S(1)} %bitcast.13), custom_call_target="tpu_custom_call" | custom-call | bytes 4194304 | tf_op jit(solution)/shard_map/split_state/pallas_call | solution.py:317
  8.9 0.2 collective-permute-start.1
  9.2 1.8 %collective-permute-start.3 = (f32[256,128]{1,0:T(8,128)S(1)}, f32[256,128]{1,0:T(8,128)S(1)}, u32[]{:S(2)}, u32[]{:S(2)}) collective-permute-start(f32[256,128]{1,0:T(8,128)S(1)} %get-tuple-element.36), channel_id=1, source_target_pairs={{0,4},{2,6},{4,0},{6,2},{8,12},{10,14},{12,8},{14,10},{1,5},{3,7},... | collective-permute-start | bytes 393224 | tf_op jit(solution)/shard_map/ppermute | solution.py:366
  11.0 3.2 %collective-permute-start.4 = (f32[256,128]{1,0:T(8,128)S(1)}, f32[256,128]{1,0:T(8,128)S(1)}, u32[]{:S(2)}, u32[]{:S(2)}) collective-permute-start(f32[256,128]{1,0:T(8,128)S(1)} %get-tuple-element.38), channel_id=1, source_target_pairs={{0,10},{2,8},{4,14},{6,12},{8,2},{10,0},{12,6},{14,4},{1,11},{3,9}... | collective-permute-start | bytes 393224 | tf_op jit(solution)/shard_map/ppermute | solution.py:366
  14.2 3.3 %collective-permute-start.5 = (f32[256,128]{1,0:T(8,128)S(1)}, f32[256,128]{1,0:T(8,128)S(1)}, u32[]{:S(2)}, u32[]{:S(2)}) collective-permute-start(f32[256,128]{1,0:T(8,128)S(1)} %get-tuple-element.39), channel_id=1, source_target_pairs={{0,8},{2,10},{4,12},{6,14},{8,0},{10,2},{12,4},{14,6},{1,9},{3,11}... | collective-permute-start | bytes 393224 | tf_op jit(solution)/shard_map/ppermute | solution.py:366
  17.6 1.5 %collective-permute-start.6 = (f32[256,128]{1,0:T(8,128)S(1)}, f32[256,128]{1,0:T(8,128)S(1)}, u32[]{:S(2)}, u32[]{:S(2)}) collective-permute-start(f32[256,128]{1,0:T(8,128)S(1)} %get-tuple-element.40), channel_id=1, source_target_pairs={{0,2},{2,0},{4,6},{6,4},{8,10},{10,8},{12,14},{14,12},{1,3},{3,1},... | collective-permute-start | bytes 393224 | tf_op jit(solution)/shard_map/ppermute | solution.py:366
  19.1 0.7 %copy-done.1 = s32[18]{0:T(128)S(1)} copy-done((s32[18]{0:T(128)S(1)}, s32[18]{0:T(128)}, u32[]{:S(2)}) %copy-start.1) | copy-done | bytes 96
  19.8 7.7 %prepare_gates.1 = (bf16[768,256]{1,0:T(8,128)(2,1)S(1)}, bf16[256,768]{1,0:T(8,128)(2,1)S(1)}, bf16[256,768]{1,0:T(8,128)(2,1)S(1)}, bf16[512,1536]{1,0:T(8,128...) custom-call(s32[18]{0:T(128)S(1)} %copy-done.1, ...), custom_call_target="tpu_custom_call" | custom-call | flops 3221225472 | bytes 4194304 | tf_op jit(solution)/shard_map/prepare_gates/pallas_call | solution.py:317
  27.4 0.4 low_gate_early.1.refs_0_
  27.9 1.4 %collective-permute-done.5.refs_2_ = f32[256,128]{1,0:T(8,128)S(1)} collective-permute-done((f32[256,128]{1,0:T(8,128)S(1)}, f32[256,128]{1,0:T(8,128)S(1)}, u32[]{:S(2)}, u32[]{:S(2)}) %collective-permute-start.5) | collective-permute-done | bytes 131104 | tf_op jit(solution)/shard_map/ppermute | solution.py:366
  29.3 2.5 %first_section.1 = (f32[2,4,2,16,128]{4,3,2,1,0:T(8,128)S(1)}, f32[2,4,2,16,128]{4,3,2,1,0:T(8,128)S(1)}, f32[2,4,2,16,128]{4,3,2,1,0:T(8,128)S(1)}, f32[2,4,2,1...) custom-call(f32[2,1024,128]{2,1,0:T(8,128)S(1)} %low_gate_early.1.re, ...), custom_call_target="tpu_custom_call", output_to_operand_aliasing={{8}: (0, {})} | custom-call | flops 2013265920 | bytes 4194304 | tf_op jit(solution)/shard_map/first_section/pallas_call | solution.py:317
  31.8 2.5 %collective-permute-start.7 = (f32[2,4,2,16,128]{4,3,2,1,0:T(8,128)S(1)}, f32[2,4,2,16,128]{4,3,2,1,0:T(8,128)S(1)}, u32[]{:S(2)}, u32[]{:S(2)}) collective-permute-start(f32[2,4,2,16,128]{4,3,2,1,0:T(8,128)S(1)} %get-tuple-element.45), channel_id=1, source_target_pairs={{0,14},{2,12},{4,10},{6,8},{8,6},{10,4},{12,2},{14,0},{1,15},{3,13... | collective-permute-start | bytes 393224 | tf_op jit(solution)/shard_map/ppermute | solution.py:366
  34.3 1.3 %collective-permute-start.8 = (f32[2,4,2,16,128]{4,3,2,1,0:T(8,128)S(1)}, f32[2,4,2,16,128]{4,3,2,1,0:T(8,128)S(1)}, u32[]{:S(2)}, u32[]{:S(2)}) collective-permute-start(f32[2,4,2,16,128]{4,3,2,1,0:T(8,128)S(1)} %get-tuple-element.46), channel_id=1, source_target_pairs={{0,12},{2,14},{4,8},{6,10},{8,4},{10,6},{12,0},{14,2},{1,13},{3,15... | collective-permute-start | bytes 393224 | tf_op jit(solution)/shard_map/ppermute | solution.py:366
  35.6 3.0 %collective-permute-start.10 = (f32[2,4,2,16,128]{4,3,2,1,0:T(8,128)S(1)}, f32[2,4,2,16,128]{4,3,2,1,0:T(8,128)S(1)}, u32[]{:S(2)}, u32[]{:S(2)}) collective-permute-start(f32[2,4,2,16,128]{4,3,2,1,0:T(8,128)S(1)} %get-tuple-element.48), channel_id=1, source_target_pairs={{0,4},{2,6},{4,0},{6,2},{8,12},{10,14},{12,8},{14,10},{1,5},{3,7},... | collective-permute-start | bytes 393224 | tf_op jit(solution)/shard_map/ppermute | solution.py:366
  38.6 1.0 %collective-permute-start.11 = (f32[2,4,2,16,128]{4,3,2,1,0:T(8,128)S(1)}, f32[2,4,2,16,128]{4,3,2,1,0:T(8,128)S(1)}, u32[]{:S(2)}, u32[]{:S(2)}) collective-permute-start(f32[2,4,2,16,128]{4,3,2,1,0:T(8,128)S(1)} %get-tuple-element.49), channel_id=1, source_target_pairs={{0,10},{2,8},{4,14},{6,12},{8,2},{10,0},{12,6},{14,4},{1,11},{3,9}... | collective-permute-start | bytes 393224 | tf_op jit(solution)/shard_map/ppermute | solution.py:366
  39.6 0.8 %collective-permute-done.7.refs_1_ = f32[2,4,2,16,128]{4,3,2,1,0:T(8,128)S(1)} collective-permute-done((f32[2,4,2,16,128]{4,3,2,1,0:T(8,128)S(1)}, f32[2,4,2,16,128]{4,3,2,1,0:T(8,128)S(1)}, u32[]{:S(2)}, u32[]{:S(2)}) %collective-permute-start.7) | collective-permute-done | bytes 131104 | tf_op jit(solution)/shard_map/ppermute | solution.py:366
  40.5 2.9 %collective-permute-start.12 = (f32[2,4,2,16,128]{4,3,2,1,0:T(8,128)S(1)}, f32[2,4,2,16,128]{4,3,2,1,0:T(8,128)S(1)}, u32[]{:S(2)}, u32[]{:S(2)}) collective-permute-start(f32[2,4,2,16,128]{4,3,2,1,0:T(8,128)S(1)} %get-tuple-element.50), channel_id=1, source_target_pairs={{0,8},{2,10},{4,12},{6,14},{8,0},{10,2},{12,4},{14,6},{1,9},{3,11}... | collective-permute-start | bytes 393224 | tf_op jit(solution)/shard_map/ppermute | solution.py:366
  43.4 2.8 %collective-permute-start.13 = (f32[2,4,2,16,128]{4,3,2,1,0:T(8,128)S(1)}, f32[2,4,2,16,128]{4,3,2,1,0:T(8,128)S(1)}, u32[]{:S(2)}, u32[]{:S(2)}) collective-permute-start(f32[2,4,2,16,128]{4,3,2,1,0:T(8,128)S(1)} %get-tuple-element.51), channel_id=1, source_target_pairs={{0,2},{2,0},{4,6},{6,4},{8,10},{10,8},{12,14},{14,12},{1,3},{3,1},... | collective-permute-start | bytes 393224 | tf_op jit(solution)/shard_map/ppermute | solution.py:366
  46.1 1.1 %collective-permute-done.9.refs_3_ = f32[2,4,2,16,128]{4,3,2,1,0:T(8,128)S(1)} collective-permute-done((f32[2,4,2,16,128]{4,3,2,1,0:T(8,128)S(1)}, f32[2,4,2,16,128]{4,3,2,1,0:T(8,128)S(1)}, u32[]{:S(2)}, u32[]{:S(2)}) %collective-permute-start.9) | collective-permute-done | bytes 131104 | tf_op jit(solution)/shard_map/ppermute | solution.py:366
  47.2 2.9 %collective-permute-done.10.refs_4_ = f32[2,4,2,16,128]{4,3,2,1,0:T(8,128)S(1)} collective-permute-done((f32[2,4,2,16,128]{4,3,2,1,0:T(8,128)S(1)}, f32[2,4,2,16,128]{4,3,2,1,0:T(8,128)S(1)}, u32[]{:S(2)}, u32[]{:S(2)}) %collective-permute-start.10) | collective-permute-done | bytes 131104 | tf_op jit(solution)/shard_map/ppermute | solution.py:366
  50.1 4.8 %collective-permute-done.11.refs_5_ = f32[2,4,2,16,128]{4,3,2,1,0:T(8,128)S(1)} collective-permute-done((f32[2,4,2,16,128]{4,3,2,1,0:T(8,128)S(1)}, f32[2,4,2,16,128]{4,3,2,1,0:T(8,128)S(1)}, u32[]{:S(2)}, u32[]{:S(2)}) %collective-permute-start.11) | collective-permute-done | bytes 131104 | tf_op jit(solution)/shard_map/ppermute | solution.py:366
  54.8 0.5 collective-permute-done.12.refs_6_
  55.3 1.0 %second_section_sent.1 = (f32[512,128]{1,0:T(8,128)S(1)}, f32[512,128]{1,0:T(8,128)S(1)}) custom-call(f32[2,4,2,16,128]{4,3,2,1,0:T(8,128)S(1)} %get-tuple-element.44.refs_0_, f32[2,4,2,16,128]{4,3,2,1,0:T(8,128)S(1)} %collective-permute-done.7.refs_1_, f32[2,4,2,16,128]{4,3,2,1,0:T(8,128)S(1)} %collective-permute-done.8.refs_2_, ...), custom_call_target="tpu_custom_call" | custom-call | flops 603979776 | bytes 4194304 | tf_op jit(solution)/shard_map/second_section_sent/pallas_call | solution.py:317
  56.3 0.1 collective-permute-start.14
  56.4 0.5 collective-permute-start.15
  56.9 1.0 %second_section_kept.1 = (f32[512,128]{1,0:T(8,128)S(1)}, f32[512,128]{1,0:T(8,128)S(1)}) custom-call(f32[2,4,2,16,128]{4,3,2,1,0:T(8,128)S(1)} %get-tuple-element.44.refs_0_, f32[2,4,2,16,128]{4,3,2,1,0:T(8,128)S(1)} %collective-permute-done.7.refs_1_, f32[2,4,2,16,128]{4,3,2,1,0:T(8,128)S(1)} %collective-permute-done.8.refs_2_, ...), custom_call_target="tpu_custom_call" | custom-call | flops 603979776 | bytes 4194304 | tf_op jit(solution)/shard_map/second_section_kept/pallas_call | solution.py:317
  57.9 0.0 collective-permute-done.14.refs_2_
  57.9 0.4 collective-permute-done.15.refs_3_
  58.3 3.1 %third_section.1 = f32[2048,128]{1,0:T(8,128)} custom-call(f32[512,128]{1,0:T(8,128)S(1)} %get-tuple-element.54.refs_0_, f32[512,128]{1,0:T(8,128)S(1)} %get-tuple-element.55.refs_1_, f32[512,128]{1,0:T(8,128)S(1)} %collective-permute-done.14.refs_2_, f32[512,128]{1,0:T(8,128)S(1)} %collective-permute-done.15.refs_3_, ...), custom_call_target="tpu_custom_call" | custom-call | flops 1610612736 | bytes 4194304 | tf_op jit(solution)/shard_map/third_section/pallas_call | solution.py:317
  (14 shorter events, 0.0 us)
Async XLA Ops:
  0.9 13.3 %collective-permute-start = (f32[256,128]{1,0:T(8,128)S(1)}, f32[256,128]{1,0:T(8,128)S(1)}, u32[]{:S(2)}, u32[]{:S(2)}) collective-permute-start(f32[256,128]{1,0:T(8,128)S(1)} %dynamic-slice_bitcast_fusion), channel_id=1, source_target_pairs={{0,14},{2,12},{4,10},{6,8},{8,6},{10,4},{12,2},{14,0},{1,15},{3,13... | collective-permute-start | bytes 393224 | tf_op jit(solution)/shard_map/ppermute | solution.py:366
  7.0 1.2 %copy-start = (f32[2,131072]{1,0:T(2,128)S(1)}, f32[2,131072]{1,0:T(2,128)}, u32[]{:S(2)}) copy-start(f32[2,131072]{1,0:T(2,128)} %param.3) | copy-start | bytes 3145732
  8.9 8.6 %collective-permute-start.1 = (f32[256,128]{1,0:T(8,128)S(1)}, f32[256,128]{1,0:T(8,128)S(1)}, u32[]{:S(2)}, u32[]{:S(2)}) collective-permute-start(f32[256,128]{1,0:T(8,128)S(1)} %get-tuple-element.34), channel_id=1, source_target_pairs={{0,12},{2,14},{4,8},{6,10},{8,4},{10,6},{12,0},{14,2},{1,13},{3,15... | collective-permute-start | bytes 393224 | tf_op jit(solution)/shard_map/ppermute | solution.py:366
  9.2 18.3 %collective-permute-start.2 = (f32[256,128]{1,0:T(8,128)S(1)}, f32[256,128]{1,0:T(8,128)S(1)}, u32[]{:S(2)}, u32[]{:S(2)}) collective-permute-start(f32[256,128]{1,0:T(8,128)S(1)} %get-tuple-element.35), channel_id=1, source_target_pairs={{0,6},{2,4},{4,2},{6,0},{8,14},{10,12},{12,10},{14,8},{1,7},{3,5},... | collective-permute-start | bytes 393224 | tf_op jit(solution)/shard_map/ppermute | solution.py:366
  9.2 18.3 %collective-permute-start.3 = (f32[256,128]{1,0:T(8,128)S(1)}, f32[256,128]{1,0:T(8,128)S(1)}, u32[]{:S(2)}, u32[]{:S(2)}) collective-permute-start(f32[256,128]{1,0:T(8,128)S(1)} %get-tuple-element.36), channel_id=1, source_target_pairs={{0,4},{2,6},{4,0},{6,2},{8,12},{10,14},{12,8},{14,10},{1,5},{3,7},... | collective-permute-start | bytes 393224 | tf_op jit(solution)/shard_map/ppermute | solution.py:366
  11.0 16.9 %collective-permute-start.4 = (f32[256,128]{1,0:T(8,128)S(1)}, f32[256,128]{1,0:T(8,128)S(1)}, u32[]{:S(2)}, u32[]{:S(2)}) collective-permute-start(f32[256,128]{1,0:T(8,128)S(1)} %get-tuple-element.38), channel_id=1, source_target_pairs={{0,10},{2,8},{4,14},{6,12},{8,2},{10,0},{12,6},{14,4},{1,11},{3,9}... | collective-permute-start | bytes 393224 | tf_op jit(solution)/shard_map/ppermute | solution.py:366
  14.2 15.1 %collective-permute-start.5 = (f32[256,128]{1,0:T(8,128)S(1)}, f32[256,128]{1,0:T(8,128)S(1)}, u32[]{:S(2)}, u32[]{:S(2)}) collective-permute-start(f32[256,128]{1,0:T(8,128)S(1)} %get-tuple-element.39), channel_id=1, source_target_pairs={{0,8},{2,10},{4,12},{6,14},{8,0},{10,2},{12,4},{14,6},{1,9},{3,11}... | collective-permute-start | bytes 393224 | tf_op jit(solution)/shard_map/ppermute | solution.py:366
  17.6 11.7 %collective-permute-start.6 = (f32[256,128]{1,0:T(8,128)S(1)}, f32[256,128]{1,0:T(8,128)S(1)}, u32[]{:S(2)}, u32[]{:S(2)}) collective-permute-start(f32[256,128]{1,0:T(8,128)S(1)} %get-tuple-element.40), channel_id=1, source_target_pairs={{0,2},{2,0},{4,6},{6,4},{8,10},{10,8},{12,14},{14,12},{1,3},{3,1},... | collective-permute-start | bytes 393224 | tf_op jit(solution)/shard_map/ppermute | solution.py:366
  19.1 0.7 %copy-start.1 = (s32[18]{0:T(128)S(1)}, s32[18]{0:T(128)}, u32[]{:S(2)}) copy-start(s32[18]{0:T(128)} %bits_ref.1) | copy-start | bytes 220
  31.8 8.7 %collective-permute-start.7 = (f32[2,4,2,16,128]{4,3,2,1,0:T(8,128)S(1)}, f32[2,4,2,16,128]{4,3,2,1,0:T(8,128)S(1)}, u32[]{:S(2)}, u32[]{:S(2)}) collective-permute-start(f32[2,4,2,16,128]{4,3,2,1,0:T(8,128)S(1)} %get-tuple-element.45), channel_id=1, source_target_pairs={{0,14},{2,12},{4,10},{6,8},{8,6},{10,4},{12,2},{14,0},{1,15},{3,13... | collective-permute-start | bytes 393224 | tf_op jit(solution)/shard_map/ppermute | solution.py:366
  34.3 9.1 %collective-permute-start.8 = (f32[2,4,2,16,128]{4,3,2,1,0:T(8,128)S(1)}, f32[2,4,2,16,128]{4,3,2,1,0:T(8,128)S(1)}, u32[]{:S(2)}, u32[]{:S(2)}) collective-permute-start(f32[2,4,2,16,128]{4,3,2,1,0:T(8,128)S(1)} %get-tuple-element.46), channel_id=1, source_target_pairs={{0,12},{2,14},{4,8},{6,10},{8,4},{10,6},{12,0},{14,2},{1,13},{3,15... | collective-permute-start | bytes 393224 | tf_op jit(solution)/shard_map/ppermute | solution.py:366
  35.6 11.6 %collective-permute-start.9 = (f32[2,4,2,16,128]{4,3,2,1,0:T(8,128)S(1)}, f32[2,4,2,16,128]{4,3,2,1,0:T(8,128)S(1)}, u32[]{:S(2)}, u32[]{:S(2)}) collective-permute-start(f32[2,4,2,16,128]{4,3,2,1,0:T(8,128)S(1)} %get-tuple-element.47), channel_id=1, source_target_pairs={{0,6},{2,4},{4,2},{6,0},{8,14},{10,12},{12,10},{14,8},{1,7},{3,5},... | collective-permute-start | bytes 393224 | tf_op jit(solution)/shard_map/ppermute | solution.py:366
  35.6 14.4 %collective-permute-start.10 = (f32[2,4,2,16,128]{4,3,2,1,0:T(8,128)S(1)}, f32[2,4,2,16,128]{4,3,2,1,0:T(8,128)S(1)}, u32[]{:S(2)}, u32[]{:S(2)}) collective-permute-start(f32[2,4,2,16,128]{4,3,2,1,0:T(8,128)S(1)} %get-tuple-element.48), channel_id=1, source_target_pairs={{0,4},{2,6},{4,0},{6,2},{8,12},{10,14},{12,8},{14,10},{1,5},{3,7},... | collective-permute-start | bytes 393224 | tf_op jit(solution)/shard_map/ppermute | solution.py:366
  38.6 16.2 %collective-permute-start.11 = (f32[2,4,2,16,128]{4,3,2,1,0:T(8,128)S(1)}, f32[2,4,2,16,128]{4,3,2,1,0:T(8,128)S(1)}, u32[]{:S(2)}, u32[]{:S(2)}) collective-permute-start(f32[2,4,2,16,128]{4,3,2,1,0:T(8,128)S(1)} %get-tuple-element.49), channel_id=1, source_target_pairs={{0,10},{2,8},{4,14},{6,12},{8,2},{10,0},{12,6},{14,4},{1,11},{3,9}... | collective-permute-start | bytes 393224 | tf_op jit(solution)/shard_map/ppermute | solution.py:366
  40.5 14.8 %collective-permute-start.12 = (f32[2,4,2,16,128]{4,3,2,1,0:T(8,128)S(1)}, f32[2,4,2,16,128]{4,3,2,1,0:T(8,128)S(1)}, u32[]{:S(2)}, u32[]{:S(2)}) collective-permute-start(f32[2,4,2,16,128]{4,3,2,1,0:T(8,128)S(1)} %get-tuple-element.50), channel_id=1, source_target_pairs={{0,8},{2,10},{4,12},{6,14},{8,0},{10,2},{12,4},{14,6},{1,9},{3,11}... | collective-permute-start | bytes 393224 | tf_op jit(solution)/shard_map/ppermute | solution.py:366
  43.4 11.9 %collective-permute-start.13 = (f32[2,4,2,16,128]{4,3,2,1,0:T(8,128)S(1)}, f32[2,4,2,16,128]{4,3,2,1,0:T(8,128)S(1)}, u32[]{:S(2)}, u32[]{:S(2)}) collective-permute-start(f32[2,4,2,16,128]{4,3,2,1,0:T(8,128)S(1)} %get-tuple-element.51), channel_id=1, source_target_pairs={{0,2},{2,0},{4,6},{6,4},{8,10},{10,8},{12,14},{14,12},{1,3},{3,1},... | collective-permute-start | bytes 393224 | tf_op jit(solution)/shard_map/ppermute | solution.py:366
  56.3 2.0 %copy-start.2 = (bf16[512,1536]{1,0:T(8,128)(2,1)S(1)}, bf16[512,1536]{1,0:T(8,128)(2,1)}, u32[]{:S(2)}) copy-start(bf16[512,1536]{1,0:T(8,128)(2,1)} %get-tuple-element.60.refs_6_) | copy-start | bytes 4718596
  56.3 1.6 %collective-permute-start.14 = (f32[512,128]{1,0:T(8,128)S(1)}, f32[512,128]{1,0:T(8,128)S(1)}, u32[]{:S(2)}, u32[]{:S(2)}) collective-permute-start(f32[512,128]{1,0:T(8,128)S(1)} %get-tuple-element.56), channel_id=1, source_target_pairs={{0,1},{1,0},{2,3},{3,2},{4,5},{5,4},{6,7},{7,6},{8,9},{9,8},{10,11... | collective-permute-start | bytes 786440 | tf_op jit(solution)/shard_map/ppermute | solution.py:431
  56.4 1.9 %collective-permute-start.15 = (f32[512,128]{1,0:T(8,128)S(1)}, f32[512,128]{1,0:T(8,128)S(1)}, u32[]{:S(2)}, u32[]{:S(2)}) collective-permute-start(f32[512,128]{1,0:T(8,128)S(1)} %get-tuple-element.57), channel_id=1, source_target_pairs={{0,1},{1,0},{2,3},{3,2},{4,5},{5,4},{6,7},{7,6},{8,9},{9,8},{10,11... | collective-permute-start | bytes 786440 | tf_op jit(solution)/shard_map/ppermute | solution.py:431

commit v12 on v10

--- a/solution.py
+++ b/solution.py
@@ -14,10 +14,10 @@
 LARGE_VMEM = 48 * 1024 * 1024
 PIECES = 4
 ORDERS = {
-    (0, 1): [7, 6, 3, 2, 5, 4, 1],
-    (0, 0): [7, 1, 3, 2, 5, 4, 6],
-    (1, 1): [3, 7, 6, 2, 5, 4, 1],
-    (1, 0): [3, 7, 1, 2, 5, 4, 6],
+    (0, 1): [7, 6, 3, 2, 1, 5, 4],
+    (0, 0): [7, 1, 3, 2, 6, 5, 4],
+    (1, 1): [7, 1, 3, 2, 6, 5, 4],
+    (1, 0): [7, 1, 3, 2, 6, 5, 4],
 }
 
 

time: 62.7 us -> 63.4 us (1.011)
  waiting for transfers between devices: 12.9 us -> 22.5 us
  starting transfers between devices: 30 us -> 21.5 us
    ppermute x14, waiting for transfers between devices: 12 us -> 21.6 us  [exchange(): came.append(lax.ppermute(piece, ('qa', 'qb'), list(enumerate(table))))]
    ppermute x14, starting transfers between devices: 29.9 us -> 21.4 us  [exchange(): came.append(lax.ppermute(piece, ('qa', 'qb'), list(enumerate(table))))]
  transfers between devices with their start and end apart: 15 -> 15, of which waited for: 7 -> 10; matrix products, arithmetic and copies ran while one was open for 0% -> 0% of each run, Pallas kernels for 16% -> 16%
where the time goes in v12:
time: 63.4 us; the launch traced here: 63.2 us
  waiting for transfers between devices  22.5 us (35%)
  starting transfers between devices  21.5 us (34%)
  Pallas kernels  16.4 us (26%)
  local copies, waits for them, and re-layouts  2.8 us (4%)
    ppermute x14, waiting for transfers between devices, exchange(): came.append(lax.ppermute(piece, ('qa', 'qb'), list(enumerate(table))))  21.6 us
    ppermute x14, starting transfers between devices, exchange(): came.append(lax.ppermute(piece, ('qa', 'qb'), list(enumerate(table))))  21.4 us
    pallas_call x7, Pallas kernels, call(): pl.pallas_call(kernel, out_shape=out_shapes, in_specs=in_specs, out_specs...  16.4 us
    unnamed x6, local copies, waits for them, and re-layouts  1.88 us
  transfers between devices with their start and end apart: 15, of which 10 were waited for; matrix products, arithmetic and copies ran while one was open for 0% of the time, Pallas kernels for 16%

profile of v12, /device:TPU:0, one launch (start us, length us, event | category | flops | bytes accessed | tf_op | source)
XLA Modules:
  0.0 63.2 jit_solution(8024615161782201918)
XLA Ops:
  0.0 0.9 %dynamic-slice_bitcast_fusion = f32[256,128]{1,0:T(8,128)S(1)} fusion(f32[8,256,128]{2,1,0:T(8,128)} %bitcast.12, s32[]{:T(128)S(6)} %select_n.8), kind=kLoop, calls=%fused_computation | loop fusion | bytes 262148 | tf_op jit(solution)/shard_map/jit(dynamic_index_in_dim)/squeeze | solution.py:390
  0.9 6.1 %collective-permute-start = (f32[256,128]{1,0:T(8,128)S(1)}, f32[256,128]{1,0:T(8,128)S(1)}, u32[]{:S(2)}, u32[]{:S(2)}) collective-permute-start(f32[256,128]{1,0:T(8,128)S(1)} %dynamic-slice_bitcast_fusion), channel_id=1, source_target_pairs={{0,14},{1,15},{2,12},{3,13},{4,10},{5,11},{6,8},{7,9},{8,6},{9,7},... | collective-permute-start | bytes 393224 | tf_op jit(solution)/shard_map/ppermute | solution.py:395
  7.0 1.2 %copy-done = f32[2,131072]{1,0:T(2,128)S(1)} copy-done((f32[2,131072]{1,0:T(2,128)S(1)}, f32[2,131072]{1,0:T(2,128)}, u32[]{:S(2)}) %copy-start) | copy-done | bytes 1048600
  8.2 0.7 %split_state.1 = (f32[256,128]{1,0:T(8,128)S(1)}, f32[256,128]{1,0:T(8,128)}, f32[256,128]{1,0:T(8,128)S(1)}, f32[256,128]{1,0:T(8,128)S(1)}, f32[256,128]{1,0:T...) custom-call(f32[8,256,128]{2,1,0:T(8,128)S(1)} %bitcast.13), custom_call_target="tpu_custom_call" | custom-call | bytes 4194304 | tf_op jit(solution)/shard_map/split_state/pallas_call | solution.py:346
  8.9 0.2 collective-permute-start.1
  9.2 0.8 %collective-permute-start.2 = (f32[256,128]{1,0:T(8,128)S(1)}, f32[256,128]{1,0:T(8,128)S(1)}, u32[]{:S(2)}, u32[]{:S(2)}) collective-permute-start(f32[256,128]{1,0:T(8,128)S(1)} %get-tuple-element.31), channel_id=1, source_target_pairs={{0,6},{1,7},{2,4},{3,5},{4,2},{5,3},{6,0},{7,1},{8,14},{9,15},{10,... | collective-permute-start | bytes 393224 | tf_op jit(solution)/shard_map/ppermute | solution.py:395
  9.9 1.0 %collective-permute-start.3 = (f32[256,128]{1,0:T(8,128)S(1)}, f32[256,128]{1,0:T(8,128)S(1)}, u32[]{:S(2)}, u32[]{:S(2)}) collective-permute-start(f32[256,128]{1,0:T(8,128)S(1)} %get-tuple-element.32), channel_id=1, source_target_pairs={{0,4},{1,5},{2,6},{3,7},{4,0},{5,1},{6,2},{7,3},{8,12},{9,13},{10,... | collective-permute-start | bytes 393224 | tf_op jit(solution)/shard_map/ppermute | solution.py:395
  11.0 1.7 %collective-permute-start.4 = (f32[256,128]{1,0:T(8,128)S(1)}, f32[256,128]{1,0:T(8,128)S(1)}, u32[]{:S(2)}, u32[]{:S(2)}) collective-permute-start(f32[256,128]{1,0:T(8,128)S(1)} %get-tuple-element.34), channel_id=1, source_target_pairs={{0,2},{1,13},{2,0},{3,15},{4,8},{5,9},{6,10},{7,11},{8,4},{9,5},{1... | collective-permute-start | bytes 393224 | tf_op jit(solution)/shard_map/ppermute | solution.py:395
  12.7 3.2 %collective-permute-start.5 = (f32[256,128]{1,0:T(8,128)S(1)}, f32[256,128]{1,0:T(8,128)S(1)}, u32[]{:S(2)}, u32[]{:S(2)}) collective-permute-start(f32[256,128]{1,0:T(8,128)S(1)} %get-tuple-element.35), channel_id=1, source_target_pairs={{0,10},{1,11},{2,8},{3,9},{4,14},{5,15},{6,12},{7,13},{8,2},{9,3},... | collective-permute-start | bytes 393224 | tf_op jit(solution)/shard_map/ppermute | solution.py:395
  15.9 0.1 collective-permute-done.1.refs_2_
  16.0 0.7 %copy-done.1 = s32[18]{0:T(128)S(1)} copy-done((s32[18]{0:T(128)S(1)}, s32[18]{0:T(128)}, u32[]{:S(2)}) %copy-start.1) | copy-done | bytes 96
  16.6 7.6 %prepare_gates.1 = (bf16[768,256]{1,0:T(8,128)(2,1)S(1)}, bf16[256,768]{1,0:T(8,128)(2,1)S(1)}, bf16[256,768]{1,0:T(8,128)(2,1)S(1)}, bf16[512,1536]{1,0:T(8,128...) custom-call(s32[18]{0:T(128)S(1)} %copy-done.1, ...), custom_call_target="tpu_custom_call" | custom-call | flops 3221225472 | bytes 4194304 | tf_op jit(solution)/shard_map/prepare_gates/pallas_call | solution.py:346
  24.3 0.4 low_gate_early.1.refs_0_
  24.8 3.7 %collective-permute-done.5.refs_2_ = f32[256,128]{1,0:T(8,128)S(1)} collective-permute-done((f32[256,128]{1,0:T(8,128)S(1)}, f32[256,128]{1,0:T(8,128)S(1)}, u32[]{:S(2)}, u32[]{:S(2)}) %collective-permute-start.5) | collective-permute-done | bytes 131104 | tf_op jit(solution)/shard_map/ppermute | solution.py:395
  28.4 1.9 %collective-permute-done.6.refs_3_ = f32[256,128]{1,0:T(8,128)S(1)} collective-permute-done((f32[256,128]{1,0:T(8,128)S(1)}, f32[256,128]{1,0:T(8,128)S(1)}, u32[]{:S(2)}, u32[]{:S(2)}) %collective-permute-start.6) | collective-permute-done | bytes 131104 | tf_op jit(solution)/shard_map/ppermute | solution.py:395
  30.3 2.5 %first_section.1 = (f32[2,4,2,16,128]{4,3,2,1,0:T(8,128)S(1)}, f32[2,4,2,16,128]{4,3,2,1,0:T(8,128)S(1)}, f32[2,4,2,16,128]{4,3,2,1,0:T(8,128)S(1)}, f32[2,4,2,1...) custom-call(f32[2,1024,128]{2,1,0:T(8,128)S(1)} %low_gate_early.1.re, ...), custom_call_target="tpu_custom_call", output_to_operand_aliasing={{8}: (0, {})} | custom-call | flops 2013265920 | bytes 4194304 | tf_op jit(solution)/shard_map/first_section/pallas_call | solution.py:346
  32.8 2.5 %collective-permute-start.7 = (f32[2,4,2,16,128]{4,3,2,1,0:T(8,128)S(1)}, f32[2,4,2,16,128]{4,3,2,1,0:T(8,128)S(1)}, u32[]{:S(2)}, u32[]{:S(2)}) collective-permute-start(f32[2,4,2,16,128]{4,3,2,1,0:T(8,128)S(1)} %get-tuple-element.41), channel_id=1, source_target_pairs={{0,14},{1,15},{2,12},{3,13},{4,10},{5,11},{6,8},{7,9},{8,6},{9,7},... | collective-permute-start | bytes 393224 | tf_op jit(solution)/shard_map/ppermute | solution.py:395
  35.3 1.4 %collective-permute-start.8 = (f32[2,4,2,16,128]{4,3,2,1,0:T(8,128)S(1)}, f32[2,4,2,16,128]{4,3,2,1,0:T(8,128)S(1)}, u32[]{:S(2)}, u32[]{:S(2)}) collective-permute-start(f32[2,4,2,16,128]{4,3,2,1,0:T(8,128)S(1)} %get-tuple-element.42), channel_id=1, source_target_pairs={{0,12},{1,3},{2,14},{3,1},{4,6},{5,7},{6,4},{7,5},{8,10},{9,11},{1... | collective-permute-start | bytes 393224 | tf_op jit(solution)/shard_map/ppermute | solution.py:395
  36.7 2.9 %collective-permute-start.10 = (f32[2,4,2,16,128]{4,3,2,1,0:T(8,128)S(1)}, f32[2,4,2,16,128]{4,3,2,1,0:T(8,128)S(1)}, u32[]{:S(2)}, u32[]{:S(2)}) collective-permute-start(f32[2,4,2,16,128]{4,3,2,1,0:T(8,128)S(1)} %get-tuple-element.44), channel_id=1, source_target_pairs={{0,4},{1,5},{2,6},{3,7},{4,0},{5,1},{6,2},{7,3},{8,12},{9,13},{10,... | collective-permute-start | bytes 393224 | tf_op jit(solution)/shard_map/ppermute | solution.py:395
  39.6 0.6 collective-permute-start.11
  40.2 1.8 %collective-permute-done.7.refs_1_ = f32[2,4,2,16,128]{4,3,2,1,0:T(8,128)S(1)} collective-permute-done((f32[2,4,2,16,128]{4,3,2,1,0:T(8,128)S(1)}, f32[2,4,2,16,128]{4,3,2,1,0:T(8,128)S(1)}, u32[]{:S(2)}, u32[]{:S(2)}) %collective-permute-start.7) | collective-permute-done | bytes 131104 | tf_op jit(solution)/shard_map/ppermute | solution.py:395
  42.0 1.9 %collective-permute-done.8.refs_2_ = f32[2,4,2,16,128]{4,3,2,1,0:T(8,128)S(1)} collective-permute-done((f32[2,4,2,16,128]{4,3,2,1,0:T(8,128)S(1)}, f32[2,4,2,16,128]{4,3,2,1,0:T(8,128)S(1)}, u32[]{:S(2)}, u32[]{:S(2)}) %collective-permute-start.8) | collective-permute-done | bytes 131104 | tf_op jit(solution)/shard_map/ppermute | solution.py:395
  43.9 1.0 %collective-permute-start.13 = (f32[2,4,2,16,128]{4,3,2,1,0:T(8,128)S(1)}, f32[2,4,2,16,128]{4,3,2,1,0:T(8,128)S(1)}, u32[]{:S(2)}, u32[]{:S(2)}) collective-permute-start(f32[2,4,2,16,128]{4,3,2,1,0:T(8,128)S(1)} %get-tuple-element.47), channel_id=1, source_target_pairs={{0,8},{1,9},{2,10},{3,11},{4,12},{5,13},{6,14},{7,15},{8,0},{9,1},... | collective-permute-start | bytes 393224 | tf_op jit(solution)/shard_map/ppermute | solution.py:395
  44.9 3.2 %collective-permute-done.9.refs_3_ = f32[2,4,2,16,128]{4,3,2,1,0:T(8,128)S(1)} collective-permute-done((f32[2,4,2,16,128]{4,3,2,1,0:T(8,128)S(1)}, f32[2,4,2,16,128]{4,3,2,1,0:T(8,128)S(1)}, u32[]{:S(2)}, u32[]{:S(2)}) %collective-permute-start.9) | collective-permute-done | bytes 131104 | tf_op jit(solution)/shard_map/ppermute | solution.py:395
  48.2 1.4 %collective-permute-done.10.refs_4_ = f32[2,4,2,16,128]{4,3,2,1,0:T(8,128)S(1)} collective-permute-done((f32[2,4,2,16,128]{4,3,2,1,0:T(8,128)S(1)}, f32[2,4,2,16,128]{4,3,2,1,0:T(8,128)S(1)}, u32[]{:S(2)}, u32[]{:S(2)}) %collective-permute-start.10) | collective-permute-done | bytes 131104 | tf_op jit(solution)/shard_map/ppermute | solution.py:395
  49.6 6.6 %collective-permute-done.12.refs_6_ = f32[2,4,2,16,128]{4,3,2,1,0:T(8,128)S(1)} collective-permute-done((f32[2,4,2,16,128]{4,3,2,1,0:T(8,128)S(1)}, f32[2,4,2,16,128]{4,3,2,1,0:T(8,128)S(1)}, u32[]{:S(2)}, u32[]{:S(2)}) %collective-permute-start.12) | collective-permute-done | bytes 131104 | tf_op jit(solution)/shard_map/ppermute | solution.py:395
  56.1 1.0 %collective-permute-done.13.refs_7_ = f32[2,4,2,16,128]{4,3,2,1,0:T(8,128)S(1)} collective-permute-done((f32[2,4,2,16,128]{4,3,2,1,0:T(8,128)S(1)}, f32[2,4,2,16,128]{4,3,2,1,0:T(8,128)S(1)}, u32[]{:S(2)}, u32[]{:S(2)}) %collective-permute-start.13) | collective-permute-done | bytes 131104 | tf_op jit(solution)/shard_map/ppermute | solution.py:395
  57.1 1.0 %second_section_sent.1 = f32[2,512,128]{2,1,0:T(8,128)S(1)} custom-call(f32[2,4,2,16,128]{4,3,2,1,0:T(8,128)S(1)} %get-tuple-element.40.refs_0_, f32[2,4,2,16,128]{4,3,2,1,0:T(8,128)S(1)} %collective-permute-done.7.refs_1_, f32[2,4,2,16,128]{4,3,2,1,0:T(8,128)S(1)} %collective-permute-done.8.refs_2_, ...), custom_call_target="tpu_custom_call" | custom-call | flops 603979776 | bytes 4194304 | tf_op jit(solution)/shard_map/second_section_sent/pallas_call | solution.py:346
  58.2 0.1 collective-permute-start.14
  58.2 1.0 %second_section_kept.1.kept_ref = f32[2,512,128]{2,1,0:T(8,128)S(1)} custom-call(f32[2,4,2,16,128]{4,3,2,1,0:T(8,128)S(1)} %get-tuple-element.40.refs_0_, f32[2,4,2,16,128]{4,3,2,1,0:T(8,128)S(1)} %collective-permute-done.7.refs_1_, f32[2,4,2,16,128]{4,3,2,1,0:T(8,128)S(1)} %collective-permute-done.8.refs_2_, ...), custom_call_target="tpu_custom_call" | custom-call | flops 603979776 | bytes 4194304 | tf_op jit(solution)/shard_map/second_section_kept/pallas_call | solution.py:346
  59.3 0.9 %collective-permute-done.14.came_ref = f32[2,512,128]{2,1,0:T(8,128)S(1)} collective-permute-done((f32[2,512,128]{2,1,0:T(8,128)S(1)}, f32[2,512,128]{2,1,0:T(8,128)S(1)}, u32[]{:S(2)}, u32[]{:S(2)}) %collective-permute-start.14) | collective-permute-done | bytes 524320 | tf_op jit(solution)/shard_map/ppermute | solution.py:460
  60.1 3.1 %third_section.1 = f32[2048,128]{1,0:T(8,128)} custom-call(f32[2,512,128]{2,1,0:T(8,128)S(1)} %second_section_kept.1.kept_ref, f32[2,512,128]{2,1,0:T(8,128)S(1)} %collective-permute-done.14.came_ref, bf16[256,768]{1,0:T(8,128)(2,1)S(1)} %get-tuple-element.50.refs_0_, bf16[256,768]{1,0:T(8,128)(2,1)S(1)} %get-tuple-element.51.refs_1_, ...), custom_call_target="tpu_custom_call" | custom-call | flops 1610612736 | bytes 4194304 | tf_op jit(solution)/shard_map/third_section/pallas_call | solution.py:346
  (12 shorter events, 0.0 us)
Async XLA Ops:
  0.9 11.7 %collective-permute-start = (f32[256,128]{1,0:T(8,128)S(1)}, f32[256,128]{1,0:T(8,128)S(1)}, u32[]{:S(2)}, u32[]{:S(2)}) collective-permute-start(f32[256,128]{1,0:T(8,128)S(1)} %dynamic-slice_bitcast_fusion), channel_id=1, source_target_pairs={{0,14},{1,15},{2,12},{3,13},{4,10},{5,11},{6,8},{7,9},{8,6},{9,7},... | collective-permute-start | bytes 393224 | tf_op jit(solution)/shard_map/ppermute | solution.py:395
  7.0 1.2 %copy-start = (f32[2,131072]{1,0:T(2,128)S(1)}, f32[2,131072]{1,0:T(2,128)}, u32[]{:S(2)}) copy-start(f32[2,131072]{1,0:T(2,128)} %param.3) | copy-start | bytes 3145732
  8.9 7.0 %collective-permute-start.1 = (f32[256,128]{1,0:T(8,128)S(1)}, f32[256,128]{1,0:T(8,128)S(1)}, u32[]{:S(2)}, u32[]{:S(2)}) collective-permute-start(f32[256,128]{1,0:T(8,128)S(1)} %get-tuple-element.30), channel_id=1, source_target_pairs={{0,12},{1,3},{2,14},{3,1},{4,6},{5,7},{6,4},{7,5},{8,10},{9,11},{1... | collective-permute-start | bytes 393224 | tf_op jit(solution)/shard_map/ppermute | solution.py:395
  9.2 15.1 %collective-permute-start.2 = (f32[256,128]{1,0:T(8,128)S(1)}, f32[256,128]{1,0:T(8,128)S(1)}, u32[]{:S(2)}, u32[]{:S(2)}) collective-permute-start(f32[256,128]{1,0:T(8,128)S(1)} %get-tuple-element.31), channel_id=1, source_target_pairs={{0,6},{1,7},{2,4},{3,5},{4,2},{5,3},{6,0},{7,1},{8,14},{9,15},{10,... | collective-permute-start | bytes 393224 | tf_op jit(solution)/shard_map/ppermute | solution.py:395
  9.9 14.4 %collective-permute-start.3 = (f32[256,128]{1,0:T(8,128)S(1)}, f32[256,128]{1,0:T(8,128)S(1)}, u32[]{:S(2)}, u32[]{:S(2)}) collective-permute-start(f32[256,128]{1,0:T(8,128)S(1)} %get-tuple-element.32), channel_id=1, source_target_pairs={{0,4},{1,5},{2,6},{3,7},{4,0},{5,1},{6,2},{7,3},{8,12},{9,13},{10,... | collective-permute-start | bytes 393224 | tf_op jit(solution)/shard_map/ppermute | solution.py:395
  11.0 13.8 %collective-permute-start.4 = (f32[256,128]{1,0:T(8,128)S(1)}, f32[256,128]{1,0:T(8,128)S(1)}, u32[]{:S(2)}, u32[]{:S(2)}) collective-permute-start(f32[256,128]{1,0:T(8,128)S(1)} %get-tuple-element.34), channel_id=1, source_target_pairs={{0,2},{1,13},{2,0},{3,15},{4,8},{5,9},{6,10},{7,11},{8,4},{9,5},{1... | collective-permute-start | bytes 393224 | tf_op jit(solution)/shard_map/ppermute | solution.py:395
  12.7 15.8 %collective-permute-start.5 = (f32[256,128]{1,0:T(8,128)S(1)}, f32[256,128]{1,0:T(8,128)S(1)}, u32[]{:S(2)}, u32[]{:S(2)}) collective-permute-start(f32[256,128]{1,0:T(8,128)S(1)} %get-tuple-element.35), channel_id=1, source_target_pairs={{0,10},{1,11},{2,8},{3,9},{4,14},{5,15},{6,12},{7,13},{8,2},{9,3},... | collective-permute-start | bytes 393224 | tf_op jit(solution)/shard_map/ppermute | solution.py:395
  16.0 14.3 %collective-permute-start.6 = (f32[256,128]{1,0:T(8,128)S(1)}, f32[256,128]{1,0:T(8,128)S(1)}, u32[]{:S(2)}, u32[]{:S(2)}) collective-permute-start(f32[256,128]{1,0:T(8,128)S(1)} %get-tuple-element.36), channel_id=1, source_target_pairs={{0,8},{1,9},{2,10},{3,11},{4,12},{5,13},{6,14},{7,15},{8,0},{9,1},... | collective-permute-start | bytes 393224 | tf_op jit(solution)/shard_map/ppermute | solution.py:395
  16.0 0.7 %copy-start.1 = (s32[18]{0:T(128)S(1)}, s32[18]{0:T(128)}, u32[]{:S(2)}) copy-start(s32[18]{0:T(128)} %bits_ref.1) | copy-start | bytes 220
  32.8 9.2 %collective-permute-start.7 = (f32[2,4,2,16,128]{4,3,2,1,0:T(8,128)S(1)}, f32[2,4,2,16,128]{4,3,2,1,0:T(8,128)S(1)}, u32[]{:S(2)}, u32[]{:S(2)}) collective-permute-start(f32[2,4,2,16,128]{4,3,2,1,0:T(8,128)S(1)} %get-tuple-element.41), channel_id=1, source_target_pairs={{0,14},{1,15},{2,12},{3,13},{4,10},{5,11},{6,8},{7,9},{8,6},{9,7},... | collective-permute-start | bytes 393224 | tf_op jit(solution)/shard_map/ppermute | solution.py:395
  35.3 8.6 %collective-permute-start.8 = (f32[2,4,2,16,128]{4,3,2,1,0:T(8,128)S(1)}, f32[2,4,2,16,128]{4,3,2,1,0:T(8,128)S(1)}, u32[]{:S(2)}, u32[]{:S(2)}) collective-permute-start(f32[2,4,2,16,128]{4,3,2,1,0:T(8,128)S(1)} %get-tuple-element.42), channel_id=1, source_target_pairs={{0,12},{1,3},{2,14},{3,1},{4,6},{5,7},{6,4},{7,5},{8,10},{9,11},{1... | collective-permute-start | bytes 393224 | tf_op jit(solution)/shard_map/ppermute | solution.py:395
  36.7 11.5 %collective-permute-start.9 = (f32[2,4,2,16,128]{4,3,2,1,0:T(8,128)S(1)}, f32[2,4,2,16,128]{4,3,2,1,0:T(8,128)S(1)}, u32[]{:S(2)}, u32[]{:S(2)}) collective-permute-start(f32[2,4,2,16,128]{4,3,2,1,0:T(8,128)S(1)} %get-tuple-element.43), channel_id=1, source_target_pairs={{0,6},{1,7},{2,4},{3,5},{4,2},{5,3},{6,0},{7,1},{8,14},{9,15},{10,... | collective-permute-start | bytes 393224 | tf_op jit(solution)/shard_map/ppermute | solution.py:395
  36.7 12.9 %collective-permute-start.10 = (f32[2,4,2,16,128]{4,3,2,1,0:T(8,128)S(1)}, f32[2,4,2,16,128]{4,3,2,1,0:T(8,128)S(1)}, u32[]{:S(2)}, u32[]{:S(2)}) collective-permute-start(f32[2,4,2,16,128]{4,3,2,1,0:T(8,128)S(1)} %get-tuple-element.44), channel_id=1, source_target_pairs={{0,4},{1,5},{2,6},{3,7},{4,0},{5,1},{6,2},{7,3},{8,12},{9,13},{10,... | collective-permute-start | bytes 393224 | tf_op jit(solution)/shard_map/ppermute | solution.py:395
  39.6 9.9 %collective-permute-start.11 = (f32[2,4,2,16,128]{4,3,2,1,0:T(8,128)S(1)}, f32[2,4,2,16,128]{4,3,2,1,0:T(8,128)S(1)}, u32[]{:S(2)}, u32[]{:S(2)}) collective-permute-start(f32[2,4,2,16,128]{4,3,2,1,0:T(8,128)S(1)} %get-tuple-element.45), channel_id=1, source_target_pairs={{0,2},{1,13},{2,0},{3,15},{4,8},{5,9},{6,10},{7,11},{8,4},{9,5},{1... | collective-permute-start | bytes 393224 | tf_op jit(solution)/shard_map/ppermute | solution.py:395
  42.0 14.1 %collective-permute-start.12 = (f32[2,4,2,16,128]{4,3,2,1,0:T(8,128)S(1)}, f32[2,4,2,16,128]{4,3,2,1,0:T(8,128)S(1)}, u32[]{:S(2)}, u32[]{:S(2)}) collective-permute-start(f32[2,4,2,16,128]{4,3,2,1,0:T(8,128)S(1)} %get-tuple-element.46), channel_id=1, source_target_pairs={{0,10},{1,11},{2,8},{3,9},{4,14},{5,15},{6,12},{7,13},{8,2},{9,3},... | collective-permute-start | bytes 393224 | tf_op jit(solution)/shard_map/ppermute | solution.py:395
  43.9 13.2 %collective-permute-start.13 = (f32[2,4,2,16,128]{4,3,2,1,0:T(8,128)S(1)}, f32[2,4,2,16,128]{4,3,2,1,0:T(8,128)S(1)}, u32[]{:S(2)}, u32[]{:S(2)}) collective-permute-start(f32[2,4,2,16,128]{4,3,2,1,0:T(8,128)S(1)} %get-tuple-element.47), channel_id=1, source_target_pairs={{0,8},{1,9},{2,10},{3,11},{4,12},{5,13},{6,14},{7,15},{8,0},{9,1},... | collective-permute-start | bytes 393224 | tf_op jit(solution)/shard_map/ppermute | solution.py:395
  58.1 2.0 %copy-start.2 = (bf16[512,1536]{1,0:T(8,128)(2,1)S(1)}, bf16[512,1536]{1,0:T(8,128)(2,1)}, u32[]{:S(2)}) copy-start(bf16[512,1536]{1,0:T(8,128)(2,1)} %get-tuple-element.52.refs_2_) | copy-start | bytes 4718596
  58.2 2.0 %collective-permute-start.14 = (f32[2,512,128]{2,1,0:T(8,128)S(1)}, f32[2,512,128]{2,1,0:T(8,128)S(1)}, u32[]{:S(2)}, u32[]{:S(2)}) collective-permute-start(f32[2,512,128]{2,1,0:T(8,128)S(1)} %second_section_sent.1), channel_id=1, source_target_pairs={{0,1},{1,0},{2,3},{3,2},{4,5},{5,4},{6,7},{7,6},{8,9},{9,8},{10,11... | collective-permute-start | bytes 1572872 | tf_op jit(solution)/shard_map/ppermute | solution.py:460

commit v13 on v11

--- a/solution.py
+++ b/solution.py
@@ -90,7 +90,11 @@
         natural = source * size + lax.rem(column, size)
     else:
         natural = jnp.bitwise_xor(column, lax.axis_index("qb") * (dim // 2))
-    return exact_dot(matrix, jnp.where(row == natural, 1.0, 0.0).astype(F32))
+    matrix = exact_dot(matrix, jnp.where(row == natural, 1.0, 0.0).astype(F32))
+    if number == 0:
+        swapped = jnp.bitwise_xor(row, (1 - lax.axis_index("qb")) * (dim // 2))
+        matrix = exact_dot(jnp.where(column == swapped, 1.0, 0.0).astype(F32), matrix)
+    return matrix
 
 
 def prepare_kernel(low, sections, count, bits_ref, gates_ref, low_ref, *refs):
@@ -212,7 +216,7 @@
     def load(part, start):
         if not isinstance(source, tuple):
             return source[part, pl.ds(start, dim, stride=stride), :]
-        return jnp.concatenate([half[part][pl.ds(start, dim // 2, stride=stride), :] for half in source], axis=0)
+        return jnp.concatenate([half[part, pl.ds(start, dim // 2, stride=stride), :] for half in source], axis=0)
 
     apply_stage(weights_ref, starts, load, store)
 
@@ -245,52 +249,71 @@
     low_gate(zip(spots, blocks), low_ref, whole)
 
 
-def first_kernel(stages, lane_bits, count, spots, *refs):
-    _, *blocks = refs[: 1 + len(spots)]
-    refs = refs[1 + len(spots) :]
-    low_ref, weights, refs = refs[0], refs[1 : 1 + len(stages)], refs[1 + len(stages) :]
-    outs, (whole, *halves) = refs[:count], refs[count:]
+def first_top_kernel(stage, lane_bits, spots, *refs):
+    blocks, (low_ref, weights_ref, away_ref, stay_ref, whole) = refs[1 : 1 + len(spots)], refs[1 + len(spots) :]
     low_gate(zip(spots, blocks), low_ref, whole)
-    run_top_stage(stages[0], weights[0], lane_bits, whole, halves[:2])
-    done = run_halves(stages[1:], weights[1:], lane_bits, halves[:2], halves[2:])
-    tops, mids, _, inner, _ = outs[0].shape
+    run_top_stage(stage, weights_ref, lane_bits, whole, (away_ref, stay_ref))
+
+
+def pieces_for(done, dest, count, piece):
+    mids, _, inner, _ = piece.shape
+    for mid in range(mids):
+        start = pl.multiple_of((mid * count + dest) * inner, inner)
+        for part in range(2):
+            piece[mid, part] = done[part, pl.ds(start, inner), :]
+
+
+def far_spots(count):
+    return [spot for spot, distance in enumerate(distances_of(count)) if distance >= count // 2]
+
+
+def near_spots(count):
+    return [spot for spot, distance in enumerate(distances_of(count)) if distance < count // 2]
+
+
+def first_rest_kernel(stages, lane_bits, count, *refs):
+    half_ref, weights, refs = refs[0], refs[1 : 1 + len(stages)], refs[1 + len(stages) :]
+    *outs, done, spare = refs
+    buffers = [half_ref, spare] if len(stages) == 2 else None
+    for index, (stage, weights_ref) in enumerate(zip(stages, weights)):
+        run_stage(stage, weights_ref, lane_bits, buffers[index], done if index == len(stages) - 1 else spare)
     dests = partners_of(count)
-    for top in range(tops):
-        for dest, out_ref in zip(dests, outs):
-            for mid in range(mids):
-                start = pl.multiple_of((mid * count + dest) * inner, inner)
-                for part in range(2):
-                    out_ref[top, mid, part] = done[top][part, pl.ds(start, inner), :]
-
-
-def second_kernel(stages, lane_bits, count, stays, *refs):
+    for spot, out_ref in zip(far_spots(count), outs):
+        pieces_for(done, dests[spot], count, out_ref)
+
+
+def first_last_kernel(stages, lane_bits, count, half_ref, before_ref, *refs):
+    weights, refs = refs[: len(stages)], refs[len(stages) :]
+    *outs, done, spare = refs
+    first_rest_kernel(stages, lane_bits, count, half_ref, *weights, *outs[: count // 2], done, spare)
+    dests = partners_of(count)
+    for spot, out_ref in zip(near_spots(count), outs[count // 2 :]):
+        pieces_for(before_ref, dests[spot], count, out_ref.at[0])
+        pieces_for(done, dests[spot], count, out_ref.at[1])
+
+
+def second_kernel(stages, lane_bits, count, which, *refs):
     blocks, weights, refs = refs[:count], refs[count : count + len(stages)], refs[count + len(stages) :]
-    *outs, one, two = refs
-    core = lax.axis_index("qb")
-    top = core if stays else 1 - core
-    for source, block_ref in zip(partners_of(count), blocks):
-        _, mids, _, inner, _ = block_ref.shape
+    out_ref, one, two = refs
+    sources = partners_of(count)
+    half = count // 2
+    pieces = [block_ref.at[which] for block_ref in blocks[:half]] + list(blocks[half:])
+    for spot, piece in zip(near_spots(count) + far_spots(count), pieces):
+        mids, _, inner, _ = piece.shape
         for mid in range(mids):
-            start = pl.multiple_of((mid * count + source) * inner, inner)
+            start = pl.multiple_of((mid * count + sources[spot]) * inner, inner)
             for part in range(2):
-                one[part, pl.ds(start, inner), :] = block_ref[top, mid, part]
-    for stage, weights_ref in zip(stages[:-1], weights):
-        run_stage(stage, weights_ref, lane_bits, one, two)
+                one[part, pl.ds(start, inner), :] = piece[mid, part]
+    for index, (stage, weights_ref) in enumerate(zip(stages, weights)):
+        run_stage(stage, weights_ref, lane_bits, one, out_ref if index == len(stages) - 1 else two)
         one, two = two, one
-    dim, stride, _ = stage_starts(stages[-1], lane_bits, one.shape[1])
-
-    def store(part, start, value):
-        outs[part][pl.ds(start, dim, stride=stride), :] = value
-
-    run_stage(stages[-1], weights[-1], lane_bits, one, store=store)
-
-
-def third_kernel(stages, lane_bits, *refs):
-    kept, came, refs = refs[:2], refs[2:4], refs[4:]
+
+
+def third_kernel(stages, lane_bits, kept_ref, came_ref, *refs):
     weights, (out_ref, *halves, sems) = refs[: len(stages)], refs[len(stages) :]
     results = halves[4:]
-    half = kept[0].shape[0]
-    run_top_stage(stages[0], weights[0], lane_bits, (kept, came), halves[:2])
+    half = kept_ref.shape[1]
+    run_top_stage(stages[0], weights[0], lane_bits, (kept_ref, came_ref), halves[:2])
     done = run_halves(stages[1:-1], weights[1:-1], lane_bits, halves[:2], halves[2:4])
     copies = []
     for t in range(2):
@@ -399,45 +422,80 @@
         *[blocks[spot] for spot in early],
         low_w,
     )
-    *blocks, _ = call(
-        functools.partial(first_kernel, sections[0], lane_bits, qa, late),
-        "first_section",
-        (shape((qb, qa // qb, 2, inner, lanes), F32),) * qa + (planes,),
-        [vmem] * (2 + len(late) + counts[0]),
-        [half] * 4,
-        5,
+    part = shape((2, rows // qb, lanes), F32)
+    away, stay, _ = call(
+        functools.partial(first_top_kernel, sections[0][0], lane_bits, late),
+        "first_section_top",
+        (part, part, planes),
+        [vmem] * (3 + len(late)),
+        [],
+        1.5,
         begun,
         *[blocks[spot] for spot in late],
         low_w,
-        *weights[0],
-        aliases={0: qa},
-    )
-    blocks = exchange(blocks)
+        weights[0][0],
+        aliases={0: 2},
+    )
+    far_block = shape((qa // qb, 2, inner, lanes), F32)
+    near_block = shape((qb, qa // qb, 2, inner, lanes), F32)
+    *far_away, done = call(
+        functools.partial(first_rest_kernel, sections[0][1:], lane_bits, qa),
+        "first_section_away",
+        (far_block,) * (qa // 2) + (part,),
+        [vmem] * counts[0],
+        [half],
+        1.5,
+        away,
+        *weights[0][1:],
+    )
+    outs = call(
+        functools.partial(first_last_kernel, sections[0][1:], lane_bits, qa),
+        "first_section_stay",
+        (far_block,) * (qa // 2) + (near_block,) * (qa // 2),
+        [vmem] * (1 + counts[0]),
+        [half] * 2,
+        1.5,
+        stay,
+        done,
+        *weights[0][1:],
+    )
+    far_stay, near_both = outs[: qa // 2], outs[qa // 2 :]
+
+    def send(pieces, spots):
+        return [
+            lax.ppermute(piece, "qa", [(i, i ^ distances_of(qa)[spot]) for i in range(qa)]) if spot else piece
+            for spot, piece in zip(spots, pieces)
+        ]
+
+    far_away = send(far_away, far_spots(qa))
+    near_both = send(near_both, near_spots(qa))
+    far_stay = send(far_stay, far_spots(qa))
     halves = []
-    for stays in (False, True):
+    for which, far in enumerate((far_away, far_stay)):
         halves.append(
             call(
-                functools.partial(second_kernel, sections[1], lane_bits, qa, stays),
-                "second_section_kept" if stays else "second_section_sent",
-                (shape((rows // qb, lanes), F32),) * 2,
+                functools.partial(second_kernel, sections[1], lane_bits, qa, which),
+                ("second_section_away", "second_section_stay")[which],
+                part,
                 [vmem] * (qa + counts[1]),
                 [half] * 2,
-                1.5,
-                *blocks,
+                (0.001, 100)[which],
+                *near_both,
+                *far,
                 *weights[1],
             )
         )
-        if not stays:
-            came = [lax.ppermute(part, "qb", [(i, 1 - i) for i in range(qb)]) for part in halves[0]]
+        if which == 0:
+            came = lax.ppermute(halves[0], "qb", [(i, 1 - i) for i in range(qb)])
     final = call(
         functools.partial(third_kernel, sections[2], lane_bits),
         "third_section",
         shape((2 * rows, lanes), F32),
-        [vmem] * (4 + counts[2]),
+        [vmem] * (2 + counts[2]),
         [half] * 4 + [pltpu.VMEM((rows, lanes), F32)] * 2 + [pltpu.SemaphoreType.DMA((2 * PIECES,))],
         4,
-        *halves[1],
-        *came,
+        halves[1],
+        came,
         *weights[2],
         out_spec=hbm,
     )

time: 61.6 us -> 63.7 us (1.034)
  starting transfers between devices: 30.3 us -> 36.9 us
  waiting for transfers between devices: 11.8 us -> 6.5 us
  Pallas kernels: 16.4 us -> 17.2 us
    ppermute x2 -> x12, starting transfers between devices: 0.57 us -> 20.7 us  [the longest x11 20.6 us: send(): lax.ppermute(piece, 'qa', [(i, i ^ distances_of(qa)[spot]) for i in range...]
    ppermute x14 -> x7, starting transfers between devices: 29.7 us -> 16.2 us  [exchange(): lax.ppermute(piece, 'qa', [(i, i ^ distance) for i in range(qa)])]
    ppermute x14 -> x7, waiting for transfers between devices: 11.4 us -> 1.16 us  [exchange(): lax.ppermute(piece, 'qa', [(i, i ^ distance) for i in range(qa)])]
    ppermute x2 -> x12, waiting for transfers between devices: 0.4 us -> 5.33 us  [the longest x11 5.33 us: send(): lax.ppermute(piece, 'qa', [(i, i ^ distances_of(qa)[spot]) for i in range...]
    pallas_call x7 -> x9, Pallas kernels: 16.4 us -> 17.2 us  [call(): pl.pallas_call(kernel, out_shape=out_shapes, in_specs=in_specs, out_specs...]
  transfers between devices with their start and end apart: 16 -> 19, of which waited for: 7 -> 4; matrix products, arithmetic and copies ran while one was open for 0% -> 0% of each run, Pallas kernels for 16% -> 19%
where the time goes in v13:
time: 63.7 us; the launch traced here: 63.5 us
  starting transfers between devices  36.9 us (58%)
  Pallas kernels  17.2 us (27%)
  waiting for transfers between devices  6.5 us (10%)
  local copies, waits for them, and re-layouts  2.8 us (4%)
    ppermute x11, starting transfers between devices, send(): lax.ppermute(piece, 'qa', [(i, i ^ distances_of(qa)[spot]) for i in range...  20.6 us
    pallas_call x9, Pallas kernels, call(): pl.pallas_call(kernel, out_shape=out_shapes, in_specs=in_specs, out_specs...  17.2 us
    ppermute x7, starting transfers between devices, exchange(): lax.ppermute(piece, 'qa', [(i, i ^ distance) for i in range(qa)])  16.2 us
    ppermute x11, waiting for transfers between devices, send(): lax.ppermute(piece, 'qa', [(i, i ^ distances_of(qa)[spot]) for i in range...  5.33 us
    unnamed x6, local copies, waits for them, and re-layouts  1.88 us
  transfers between devices with their start and end apart: 19, of which 4 were waited for; matrix products, arithmetic and copies ran while one was open for 0% of the time, Pallas kernels for 19%

profile of v13, /device:TPU:0, one launch (start us, length us, event | category | flops | bytes accessed | tf_op | source)
XLA Modules:
  0.0 63.5 jit_solution(11434439924949021220)
XLA Ops:
  0.0 0.9 %dynamic-slice_bitcast_fusion = f32[256,128]{1,0:T(8,128)S(1)} fusion(f32[8,256,128]{2,1,0:T(8,128)} %bitcast.12, s32[]{:T(128)S(6)} %select_n.4), kind=kLoop, calls=%fused_computation | loop fusion | bytes 262148 | tf_op jit(solution)/shard_map/jit(dynamic_index_in_dim)/squeeze | solution.py:384
  0.9 6.1 %collective-permute-start = (f32[256,128]{1,0:T(8,128)S(1)}, f32[256,128]{1,0:T(8,128)S(1)}, u32[]{:S(2)}, u32[]{:S(2)}) collective-permute-start(f32[256,128]{1,0:T(8,128)S(1)} %dynamic-slice_bitcast_fusion), channel_id=1, source_target_pairs={{0,14},{2,12},{4,10},{6,8},{8,6},{10,4},{12,2},{14,0},{1,15},{3,13... | collective-permute-start | bytes 393224 | tf_op jit(solution)/shard_map/ppermute | solution.py:389
  7.0 1.2 %copy-done = f32[2,131072]{1,0:T(2,128)S(1)} copy-done((f32[2,131072]{1,0:T(2,128)S(1)}, f32[2,131072]{1,0:T(2,128)}, u32[]{:S(2)}) %copy-start) | copy-done | bytes 1048600
  8.2 0.7 %split_state.1 = (f32[256,128]{1,0:T(8,128)S(1)}, f32[256,128]{1,0:T(8,128)}, f32[256,128]{1,0:T(8,128)S(1)}, f32[256,128]{1,0:T(8,128)S(1)}, f32[256,128]{1,0:T...) custom-call(f32[8,256,128]{2,1,0:T(8,128)S(1)} %bitcast.13), custom_call_target="tpu_custom_call" | custom-call | bytes 4194304 | tf_op jit(solution)/shard_map/split_state/pallas_call | solution.py:340
  8.9 0.2 collective-permute-start.1
  9.2 1.8 %collective-permute-start.3 = (f32[256,128]{1,0:T(8,128)S(1)}, f32[256,128]{1,0:T(8,128)S(1)}, u32[]{:S(2)}, u32[]{:S(2)}) collective-permute-start(f32[256,128]{1,0:T(8,128)S(1)} %get-tuple-element.39), channel_id=1, source_target_pairs={{0,4},{2,6},{4,0},{6,2},{8,12},{10,14},{12,8},{14,10},{1,5},{3,7},... | collective-permute-start | bytes 393224 | tf_op jit(solution)/shard_map/ppermute | solution.py:389
  11.0 3.2 %collective-permute-start.4 = (f32[256,128]{1,0:T(8,128)S(1)}, f32[256,128]{1,0:T(8,128)S(1)}, u32[]{:S(2)}, u32[]{:S(2)}) collective-permute-start(f32[256,128]{1,0:T(8,128)S(1)} %get-tuple-element.41), channel_id=1, source_target_pairs={{0,10},{2,8},{4,14},{6,12},{8,2},{10,0},{12,6},{14,4},{1,11},{3,9}... | collective-permute-start | bytes 393224 | tf_op jit(solution)/shard_map/ppermute | solution.py:389
  14.2 3.3 %collective-permute-start.5 = (f32[256,128]{1,0:T(8,128)S(1)}, f32[256,128]{1,0:T(8,128)S(1)}, u32[]{:S(2)}, u32[]{:S(2)}) collective-permute-start(f32[256,128]{1,0:T(8,128)S(1)} %get-tuple-element.42), channel_id=1, source_target_pairs={{0,8},{2,10},{4,12},{6,14},{8,0},{10,2},{12,4},{14,6},{1,9},{3,11}... | collective-permute-start | bytes 393224 | tf_op jit(solution)/shard_map/ppermute | solution.py:389
  17.6 1.5 %collective-permute-start.6 = (f32[256,128]{1,0:T(8,128)S(1)}, f32[256,128]{1,0:T(8,128)S(1)}, u32[]{:S(2)}, u32[]{:S(2)}) collective-permute-start(f32[256,128]{1,0:T(8,128)S(1)} %get-tuple-element.43), channel_id=1, source_target_pairs={{0,2},{2,0},{4,6},{6,4},{8,10},{10,8},{12,14},{14,12},{1,3},{3,1},... | collective-permute-start | bytes 393224 | tf_op jit(solution)/shard_map/ppermute | solution.py:389
  19.1 0.7 %copy-done.1 = s32[18]{0:T(128)S(1)} copy-done((s32[18]{0:T(128)S(1)}, s32[18]{0:T(128)}, u32[]{:S(2)}) %copy-start.1) | copy-done | bytes 96
  19.8 7.9 %prepare_gates.1 = (bf16[768,256]{1,0:T(8,128)(2,1)S(1)}, bf16[256,768]{1,0:T(8,128)(2,1)S(1)}, bf16[256,768]{1,0:T(8,128)(2,1)S(1)}, bf16[512,1536]{1,0:T(8,128...) custom-call(s32[18]{0:T(128)S(1)} %copy-done.1, ...), custom_call_target="tpu_custom_call" | custom-call | flops 3221225472 | bytes 4194304 | tf_op jit(solution)/shard_map/prepare_gates/pallas_call | solution.py:340
  27.7 0.4 low_gate_early.1.refs_0_
  28.1 1.1 %collective-permute-done.5.refs_2_ = f32[256,128]{1,0:T(8,128)S(1)} collective-permute-done((f32[256,128]{1,0:T(8,128)S(1)}, f32[256,128]{1,0:T(8,128)S(1)}, u32[]{:S(2)}, u32[]{:S(2)}) %collective-permute-start.5) | collective-permute-done | bytes 131104 | tf_op jit(solution)/shard_map/ppermute | solution.py:389
  29.3 1.0 %first_section_top.1 = (f32[2,512,128]{2,1,0:T(8,128)S(1)}, f32[2,512,128]{2,1,0:T(8,128)S(1)}, f32[2,1024,128]{2,1,0:T(8,128)S(1)}) custom-call(f32[2,1024,128]{2,1,0:T(8,128)S(1)} %low_gate_early.1.refs_0_, f32[256,128]{1,0:T(8,128)S(1)} %collective-permute-done.4.refs_1_, ...), custom_call_target="tpu_custom_call", output_to_operand_aliasing={{2}: (0, {})} | custom-call | flops 603979776 | bytes 4194304 | tf_op jit(solution)/shard_map/first_section_top/pallas_call | solution.py:340
  30.3 1.0 %first_section_away.1 = (f32[4,2,16,128]{3,2,1,0:T(8,128)S(1)}, f32[4,2,16,128]{3,2,1,0:T(8,128)S(1)}, f32[4,2,16,128]{3,2,1,0:T(8,128)S(1)}, f32[4,2,16,128]{3,2,1,0:T(8,128)S(1)}, f32[2,512,128]{2,1,0:T(8,128)S(1)}) custom-call(f32[2,512,128]{2,1,0:T(8,128)S(1)} %get-tuple-element.46.refs_0_, bf16[256,768]{1,0:T(8,128)(2,1)S(1)} %get-tuple-element.47.refs_1_.refs_0_, ...), custom_call_target="tpu_custom_call" | custom-call | flops 603979776 | bytes 4194304 | tf_op jit(solution)/shard_map/first_section_away/pallas_call | solution.py:340
  31.3 2.5 %collective-permute-start.14 = (f32[4,2,16,128]{3,2,1,0:T(8,128)S(1)}, f32[4,2,16,128]{3,2,1,0:T(8,128)S(1)}, u32[]{:S(2)}, u32[]{:S(2)}) collective-permute-start(f32[4,2,16,128]{3,2,1,0:T(8,128)S(1)} %get-tuple-element.60), channel_id=1, source_target_pairs={{0,14},{2,12},{4,10},{6,8},{8,6},{10,4},{12,2},{14,0},{1,15},{3,13... | collective-permute-start | bytes 196616 | tf_op jit(solution)/shard_map/ppermute | solution.py:466
  33.8 1.4 %collective-permute-start.15 = (f32[4,2,16,128]{3,2,1,0:T(8,128)S(1)}, f32[4,2,16,128]{3,2,1,0:T(8,128)S(1)}, u32[]{:S(2)}, u32[]{:S(2)}) collective-permute-start(f32[4,2,16,128]{3,2,1,0:T(8,128)S(1)} %get-tuple-element.61), channel_id=1, source_target_pairs={{0,12},{2,14},{4,8},{6,10},{8,4},{10,6},{12,0},{14,2},{1,13},{3,15... | collective-permute-start | bytes 196616 | tf_op jit(solution)/shard_map/ppermute | solution.py:466
  35.2 1.0 %first_section_stay.1 = (f32[4,2,16,128]{3,2,1,0:T(8,128)S(1)}, f32[4,2,16,128]{3,2,1,0:T(8,128)S(1)}, f32[4,2,16,128]{3,2,1,0:T(8,128)S(1)}, f32[4,2,16,128]{3,...) custom-call(f32[2,512,128]{2,1,0:T(8,128)S(1)} %get-tuple-element.45, ...), custom_call_target="tpu_custom_call" | custom-call | flops 603979776 | bytes 4194304 | tf_op jit(solution)/shard_map/first_section_stay/pallas_call | solution.py:340
  36.3 3.0 %collective-permute-start.8 = (f32[2,4,2,16,128]{4,3,2,1,0:T(8,128)S(1)}, f32[2,4,2,16,128]{4,3,2,1,0:T(8,128)S(1)}, u32[]{:S(2)}, u32[]{:S(2)}) collective-permute-start(f32[2,4,2,16,128]{4,3,2,1,0:T(8,128)S(1)} %get-tuple-element.52), channel_id=1, source_target_pairs={{0,4},{2,6},{4,0},{6,2},{8,12},{10,14},{12,8},{14,10},{1,5},{3,7},... | collective-permute-start | bytes 393224 | tf_op jit(solution)/shard_map/ppermute | solution.py:466
  39.2 1.1 %collective-permute-start.16 = (f32[4,2,16,128]{3,2,1,0:T(8,128)S(1)}, f32[4,2,16,128]{3,2,1,0:T(8,128)S(1)}, u32[]{:S(2)}, u32[]{:S(2)}) collective-permute-start(f32[4,2,16,128]{3,2,1,0:T(8,128)S(1)} %get-tuple-element.62), channel_id=1, source_target_pairs={{0,10},{2,8},{4,14},{6,12},{8,2},{10,0},{12,6},{14,4},{1,11},{3,9}... | collective-permute-start | bytes 196616 | tf_op jit(solution)/shard_map/ppermute | solution.py:466
  40.3 1.4 %collective-permute-start.9 = (f32[2,4,2,16,128]{4,3,2,1,0:T(8,128)S(1)}, f32[2,4,2,16,128]{4,3,2,1,0:T(8,128)S(1)}, u32[]{:S(2)}, u32[]{:S(2)}) collective-permute-start(f32[2,4,2,16,128]{4,3,2,1,0:T(8,128)S(1)} %get-tuple-element.53), channel_id=1, source_target_pairs={{0,2},{2,0},{4,6},{6,4},{8,10},{10,8},{12,14},{14,12},{1,3},{3,1},... | collective-permute-start | bytes 393224 | tf_op jit(solution)/shard_map/ppermute | solution.py:466
  41.7 1.9 %collective-permute-start.17 = (f32[4,2,16,128]{3,2,1,0:T(8,128)S(1)}, f32[4,2,16,128]{3,2,1,0:T(8,128)S(1)}, u32[]{:S(2)}, u32[]{:S(2)}) collective-permute-start(f32[4,2,16,128]{3,2,1,0:T(8,128)S(1)} %get-tuple-element.63), channel_id=1, source_target_pairs={{0,8},{2,10},{4,12},{6,14},{8,0},{10,2},{12,4},{14,6},{1,9},{3,11}... | collective-permute-start | bytes 196616 | tf_op jit(solution)/shard_map/ppermute | solution.py:466
  43.6 2.4 %collective-permute-done.16.refs_6_ = f32[4,2,16,128]{3,2,1,0:T(8,128)S(1)} collective-permute-done((f32[4,2,16,128]{3,2,1,0:T(8,128)S(1)}, f32[4,2,16,128]{3,2,1,0:T(8,128)S(1)}, u32[]{:S(2)}, u32[]{:S(2)}) %collective-permute-start.16) | collective-permute-done | bytes 65568 | tf_op jit(solution)/shard_map/ppermute | solution.py:466
  46.0 2.5 %collective-permute-start.10 = (f32[4,2,16,128]{3,2,1,0:T(8,128)S(1)}, f32[4,2,16,128]{3,2,1,0:T(8,128)S(1)}, u32[]{:S(2)}, u32[]{:S(2)}) collective-permute-start(f32[4,2,16,128]{3,2,1,0:T(8,128)S(1)} %get-tuple-element.54), channel_id=1, source_target_pairs={{0,14},{2,12},{4,10},{6,8},{8,6},{10,4},{12,2},{14,0},{1,15},{3,13... | collective-permute-start | bytes 196616 | tf_op jit(solution)/shard_map/ppermute | solution.py:466
  48.4 2.1 %collective-permute-start.11 = (f32[4,2,16,128]{3,2,1,0:T(8,128)S(1)}, f32[4,2,16,128]{3,2,1,0:T(8,128)S(1)}, u32[]{:S(2)}, u32[]{:S(2)}) collective-permute-start(f32[4,2,16,128]{3,2,1,0:T(8,128)S(1)} %get-tuple-element.55), channel_id=1, source_target_pairs={{0,12},{2,14},{4,8},{6,10},{8,4},{10,6},{12,0},{14,2},{1,13},{3,15... | collective-permute-start | bytes 196616 | tf_op jit(solution)/shard_map/ppermute | solution.py:466
  50.6 0.8 %collective-permute-start.12 = (f32[4,2,16,128]{3,2,1,0:T(8,128)S(1)}, f32[4,2,16,128]{3,2,1,0:T(8,128)S(1)}, u32[]{:S(2)}, u32[]{:S(2)}) collective-permute-start(f32[4,2,16,128]{3,2,1,0:T(8,128)S(1)} %get-tuple-element.56), channel_id=1, source_target_pairs={{0,10},{2,8},{4,14},{6,12},{8,2},{10,0},{12,6},{14,4},{1,11},{3,9}... | collective-permute-start | bytes 196616 | tf_op jit(solution)/shard_map/ppermute | solution.py:466
  51.4 3.9 %collective-permute-start.13 = (f32[4,2,16,128]{3,2,1,0:T(8,128)S(1)}, f32[4,2,16,128]{3,2,1,0:T(8,128)S(1)}, u32[]{:S(2)}, u32[]{:S(2)}) collective-permute-start(f32[4,2,16,128]{3,2,1,0:T(8,128)S(1)} %get-tuple-element.57), channel_id=1, source_target_pairs={{0,8},{2,10},{4,12},{6,14},{8,0},{10,2},{12,4},{14,6},{1,9},{3,11}... | collective-permute-start | bytes 196616 | tf_op jit(solution)/shard_map/ppermute | solution.py:466
  55.3 1.0 %second_section_away.1 = f32[2,512,128]{2,1,0:T(8,128)S(1)} custom-call(f32[2,4,2,16,128]{4,3,2,1,0:T(8,128)S(1)} %get-tuple-element.50.refs_0_, f32[2,4,2,16,128]{4,3,2,1,0:T(8,128)S(1)} %collective-permute-done.7.refs_1_, f32[2,4,2,16,128]{4,3,2,1,0:T(8,128)S(1)} %collective-permute-done.8.refs_2_, ...), custom_call_target="tpu_custom_call" | custom-call | flops 402653 | bytes 4194304 | tf_op jit(solution)/shard_map/second_section_away/pallas_call | solution.py:340
  56.5 2.7 %collective-permute-done.12.refs_6_ = f32[4,2,16,128]{3,2,1,0:T(8,128)S(1)} collective-permute-done((f32[4,2,16,128]{3,2,1,0:T(8,128)S(1)}, f32[4,2,16,128]{3,2,1,0:T(8,128)S(1)}, u32[]{:S(2)}, u32[]{:S(2)}) %collective-permute-start.12) | collective-permute-done | bytes 65568 | tf_op jit(solution)/shard_map/ppermute | solution.py:466
  59.2 0.2 collective-permute-done.13.refs_7_
  59.4 1.0 %second_section_stay.1.kept_ref = f32[2,512,128]{2,1,0:T(8,128)S(1)} custom-call(f32[2,4,2,16,128]{4,3,2,1,0:T(8,128)S(1)} %get-tuple-element.50.refs_0_, f32[2,4,2,16,128]{4,3,2,1,0:T(8,128)S(1)} %collective-permute-done.7.refs_1_, f32[2,4,2,16,128]{4,3,2,1,0:T(8,128)S(1)} %collective-permute-done.8.refs_2_, ...), custom_call_target="tpu_custom_call" | custom-call | flops 40265318400 | bytes 4194304 | tf_op jit(solution)/shard_map/second_section_stay/pallas_call | solution.py:340
  60.4 3.1 %third_section.1 = f32[2048,128]{1,0:T(8,128)} custom-call(f32[2,512,128]{2,1,0:T(8,128)S(1)} %second_section_stay.1.kept_ref, f32[2,512,128]{2,1,0:T(8,128)S(1)} %collective-permute-done.18.came_ref, bf16[256,768]{1,0:T(8,128)(2,1)S(1)} %get-tuple-element.64.refs_0_, bf16[256,768]{1,0:T(8,128)(2,1)S(1)} %get-tuple-element.65.refs_1_, ...), custom_call_target="tpu_custom_call" | custom-call | flops 1610612736 | bytes 4194304 | tf_op jit(solution)/shard_map/third_section/pallas_call | solution.py:340
  (22 shorter events, 0.2 us)
Async XLA Ops:
  0.9 13.3 %collective-permute-start = (f32[256,128]{1,0:T(8,128)S(1)}, f32[256,128]{1,0:T(8,128)S(1)}, u32[]{:S(2)}, u32[]{:S(2)}) collective-permute-start(f32[256,128]{1,0:T(8,128)S(1)} %dynamic-slice_bitcast_fusion), channel_id=1, source_target_pairs={{0,14},{2,12},{4,10},{6,8},{8,6},{10,4},{12,2},{14,0},{1,15},{3,13... | collective-permute-start | bytes 393224 | tf_op jit(solution)/shard_map/ppermute | solution.py:389
  7.0 1.2 %copy-start = (f32[2,131072]{1,0:T(2,128)S(1)}, f32[2,131072]{1,0:T(2,128)}, u32[]{:S(2)}) copy-start(f32[2,131072]{1,0:T(2,128)} %param.3) | copy-start | bytes 3145732
  8.9 8.6 %collective-permute-start.1 = (f32[256,128]{1,0:T(8,128)S(1)}, f32[256,128]{1,0:T(8,128)S(1)}, u32[]{:S(2)}, u32[]{:S(2)}) collective-permute-start(f32[256,128]{1,0:T(8,128)S(1)} %get-tuple-element.37), channel_id=1, source_target_pairs={{0,12},{2,14},{4,8},{6,10},{8,4},{10,6},{12,0},{14,2},{1,13},{3,15... | collective-permute-start | bytes 393224 | tf_op jit(solution)/shard_map/ppermute | solution.py:389
  9.2 18.5 %collective-permute-start.2 = (f32[256,128]{1,0:T(8,128)S(1)}, f32[256,128]{1,0:T(8,128)S(1)}, u32[]{:S(2)}, u32[]{:S(2)}) collective-permute-start(f32[256,128]{1,0:T(8,128)S(1)} %get-tuple-element.38), channel_id=1, source_target_pairs={{0,6},{2,4},{4,2},{6,0},{8,14},{10,12},{12,10},{14,8},{1,7},{3,5},... | collective-permute-start | bytes 393224 | tf_op jit(solution)/shard_map/ppermute | solution.py:389
  9.2 18.5 %collective-permute-start.3 = (f32[256,128]{1,0:T(8,128)S(1)}, f32[256,128]{1,0:T(8,128)S(1)}, u32[]{:S(2)}, u32[]{:S(2)}) collective-permute-start(f32[256,128]{1,0:T(8,128)S(1)} %get-tuple-element.39), channel_id=1, source_target_pairs={{0,4},{2,6},{4,0},{6,2},{8,12},{10,14},{12,8},{14,10},{1,5},{3,7},... | collective-permute-start | bytes 393224 | tf_op jit(solution)/shard_map/ppermute | solution.py:389
  11.0 17.2 %collective-permute-start.4 = (f32[256,128]{1,0:T(8,128)S(1)}, f32[256,128]{1,0:T(8,128)S(1)}, u32[]{:S(2)}, u32[]{:S(2)}) collective-permute-start(f32[256,128]{1,0:T(8,128)S(1)} %get-tuple-element.41), channel_id=1, source_target_pairs={{0,10},{2,8},{4,14},{6,12},{8,2},{10,0},{12,6},{14,4},{1,11},{3,9}... | collective-permute-start | bytes 393224 | tf_op jit(solution)/shard_map/ppermute | solution.py:389
  14.2 15.1 %collective-permute-start.5 = (f32[256,128]{1,0:T(8,128)S(1)}, f32[256,128]{1,0:T(8,128)S(1)}, u32[]{:S(2)}, u32[]{:S(2)}) collective-permute-start(f32[256,128]{1,0:T(8,128)S(1)} %get-tuple-element.42), channel_id=1, source_target_pairs={{0,8},{2,10},{4,12},{6,14},{8,0},{10,2},{12,4},{14,6},{1,9},{3,11}... | collective-permute-start | bytes 393224 | tf_op jit(solution)/shard_map/ppermute | solution.py:389
  17.6 11.7 %collective-permute-start.6 = (f32[256,128]{1,0:T(8,128)S(1)}, f32[256,128]{1,0:T(8,128)S(1)}, u32[]{:S(2)}, u32[]{:S(2)}) collective-permute-start(f32[256,128]{1,0:T(8,128)S(1)} %get-tuple-element.43), channel_id=1, source_target_pairs={{0,2},{2,0},{4,6},{6,4},{8,10},{10,8},{12,14},{14,12},{1,3},{3,1},... | collective-permute-start | bytes 393224 | tf_op jit(solution)/shard_map/ppermute | solution.py:389
  19.1 0.7 %copy-start.1 = (s32[18]{0:T(128)S(1)}, s32[18]{0:T(128)}, u32[]{:S(2)}) copy-start(s32[18]{0:T(128)} %bits_ref.1) | copy-start | bytes 220
  31.3 9.0 %collective-permute-start.14 = (f32[4,2,16,128]{3,2,1,0:T(8,128)S(1)}, f32[4,2,16,128]{3,2,1,0:T(8,128)S(1)}, u32[]{:S(2)}, u32[]{:S(2)}) collective-permute-start(f32[4,2,16,128]{3,2,1,0:T(8,128)S(1)} %get-tuple-element.60), channel_id=1, source_target_pairs={{0,14},{2,12},{4,10},{6,8},{8,6},{10,4},{12,2},{14,0},{1,15},{3,13... | collective-permute-start | bytes 196616 | tf_op jit(solution)/shard_map/ppermute | solution.py:466
  33.8 7.9 %collective-permute-start.15 = (f32[4,2,16,128]{3,2,1,0:T(8,128)S(1)}, f32[4,2,16,128]{3,2,1,0:T(8,128)S(1)}, u32[]{:S(2)}, u32[]{:S(2)}) collective-permute-start(f32[4,2,16,128]{3,2,1,0:T(8,128)S(1)} %get-tuple-element.61), channel_id=1, source_target_pairs={{0,12},{2,14},{4,8},{6,10},{8,4},{10,6},{12,0},{14,2},{1,13},{3,15... | collective-permute-start | bytes 196616 | tf_op jit(solution)/shard_map/ppermute | solution.py:466
  36.2 14.4 %collective-permute-start.7 = (f32[2,4,2,16,128]{4,3,2,1,0:T(8,128)S(1)}, f32[2,4,2,16,128]{4,3,2,1,0:T(8,128)S(1)}, u32[]{:S(2)}, u32[]{:S(2)}) collective-permute-start(f32[2,4,2,16,128]{4,3,2,1,0:T(8,128)S(1)} %get-tuple-element.51), channel_id=1, source_target_pairs={{0,6},{2,4},{4,2},{6,0},{8,14},{10,12},{12,10},{14,8},{1,7},{3,5},... | collective-permute-start | bytes 393224 | tf_op jit(solution)/shard_map/ppermute | solution.py:466
  36.3 15.2 %collective-permute-start.8 = (f32[2,4,2,16,128]{4,3,2,1,0:T(8,128)S(1)}, f32[2,4,2,16,128]{4,3,2,1,0:T(8,128)S(1)}, u32[]{:S(2)}, u32[]{:S(2)}) collective-permute-start(f32[2,4,2,16,128]{4,3,2,1,0:T(8,128)S(1)} %get-tuple-element.52), channel_id=1, source_target_pairs={{0,4},{2,6},{4,0},{6,2},{8,12},{10,14},{12,8},{14,10},{1,5},{3,7},... | collective-permute-start | bytes 393224 | tf_op jit(solution)/shard_map/ppermute | solution.py:466
  39.2 6.8 %collective-permute-start.16 = (f32[4,2,16,128]{3,2,1,0:T(8,128)S(1)}, f32[4,2,16,128]{3,2,1,0:T(8,128)S(1)}, u32[]{:S(2)}, u32[]{:S(2)}) collective-permute-start(f32[4,2,16,128]{3,2,1,0:T(8,128)S(1)} %get-tuple-element.62), channel_id=1, source_target_pairs={{0,10},{2,8},{4,14},{6,12},{8,2},{10,0},{12,6},{14,4},{1,11},{3,9}... | collective-permute-start | bytes 196616 | tf_op jit(solution)/shard_map/ppermute | solution.py:466
  40.3 15.0 %collective-permute-start.9 = (f32[2,4,2,16,128]{4,3,2,1,0:T(8,128)S(1)}, f32[2,4,2,16,128]{4,3,2,1,0:T(8,128)S(1)}, u32[]{:S(2)}, u32[]{:S(2)}) collective-permute-start(f32[2,4,2,16,128]{4,3,2,1,0:T(8,128)S(1)} %get-tuple-element.53), channel_id=1, source_target_pairs={{0,2},{2,0},{4,6},{6,4},{8,10},{10,8},{12,14},{14,12},{1,3},{3,1},... | collective-permute-start | bytes 393224 | tf_op jit(solution)/shard_map/ppermute | solution.py:466
  41.7 6.7 %collective-permute-start.17 = (f32[4,2,16,128]{3,2,1,0:T(8,128)S(1)}, f32[4,2,16,128]{3,2,1,0:T(8,128)S(1)}, u32[]{:S(2)}, u32[]{:S(2)}) collective-permute-start(f32[4,2,16,128]{3,2,1,0:T(8,128)S(1)} %get-tuple-element.63), channel_id=1, source_target_pairs={{0,8},{2,10},{4,12},{6,14},{8,0},{10,2},{12,4},{14,6},{1,9},{3,11}... | collective-permute-start | bytes 196616 | tf_op jit(solution)/shard_map/ppermute | solution.py:466
  46.0 10.5 %collective-permute-start.10 = (f32[4,2,16,128]{3,2,1,0:T(8,128)S(1)}, f32[4,2,16,128]{3,2,1,0:T(8,128)S(1)}, u32[]{:S(2)}, u32[]{:S(2)}) collective-permute-start(f32[4,2,16,128]{3,2,1,0:T(8,128)S(1)} %get-tuple-element.54), channel_id=1, source_target_pairs={{0,14},{2,12},{4,10},{6,8},{8,6},{10,4},{12,2},{14,0},{1,15},{3,13... | collective-permute-start | bytes 196616 | tf_op jit(solution)/shard_map/ppermute | solution.py:466
  48.4 8.0 %collective-permute-start.11 = (f32[4,2,16,128]{3,2,1,0:T(8,128)S(1)}, f32[4,2,16,128]{3,2,1,0:T(8,128)S(1)}, u32[]{:S(2)}, u32[]{:S(2)}) collective-permute-start(f32[4,2,16,128]{3,2,1,0:T(8,128)S(1)} %get-tuple-element.55), channel_id=1, source_target_pairs={{0,12},{2,14},{4,8},{6,10},{8,4},{10,6},{12,0},{14,2},{1,13},{3,15... | collective-permute-start | bytes 196616 | tf_op jit(solution)/shard_map/ppermute | solution.py:466
  50.6 8.6 %collective-permute-start.12 = (f32[4,2,16,128]{3,2,1,0:T(8,128)S(1)}, f32[4,2,16,128]{3,2,1,0:T(8,128)S(1)}, u32[]{:S(2)}, u32[]{:S(2)}) collective-permute-start(f32[4,2,16,128]{3,2,1,0:T(8,128)S(1)} %get-tuple-element.56), channel_id=1, source_target_pairs={{0,10},{2,8},{4,14},{6,12},{8,2},{10,0},{12,6},{14,4},{1,11},{3,9}... | collective-permute-start | bytes 196616 | tf_op jit(solution)/shard_map/ppermute | solution.py:466
  51.4 8.0 %collective-permute-start.13 = (f32[4,2,16,128]{3,2,1,0:T(8,128)S(1)}, f32[4,2,16,128]{3,2,1,0:T(8,128)S(1)}, u32[]{:S(2)}, u32[]{:S(2)}) collective-permute-start(f32[4,2,16,128]{3,2,1,0:T(8,128)S(1)} %get-tuple-element.57), channel_id=1, source_target_pairs={{0,8},{2,10},{4,12},{6,14},{8,0},{10,2},{12,4},{14,6},{1,9},{3,11}... | collective-permute-start | bytes 196616 | tf_op jit(solution)/shard_map/ppermute | solution.py:466
  56.4 4.1 %copy-start.2 = (bf16[512,1536]{1,0:T(8,128)(2,1)S(1)}, bf16[512,1536]{1,0:T(8,128)(2,1)}, u32[]{:S(2)}) copy-start(bf16[512,1536]{1,0:T(8,128)(2,1)} %get-tuple-element.66.refs_2_) | copy-start | bytes 4718596
  56.4 4.1 %collective-permute-start.18 = (f32[2,512,128]{2,1,0:T(8,128)S(1)}, f32[2,512,128]{2,1,0:T(8,128)S(1)}, u32[]{:S(2)}, u32[]{:S(2)}) collective-permute-start(f32[2,512,128]{2,1,0:T(8,128)S(1)} %second_section_away.1), channel_id=1, source_target_pairs={{0,1},{1,0},{2,3},{3,2},{4,5},{5,4},{6,7},{7,6},{8,9},{9,8},{10,11... | collective-permute-start | bytes 1572872 | tf_op jit(solution)/shard_map/ppermute | solution.py:489

commit v14 on v11

--- a/solution.py
+++ b/solution.py
@@ -57,12 +57,6 @@
     return parts[0][0] != base
 
 
-def exact_dot(a, b):
-    return lax.dot_general(
-        a, b, (((1,), (0,)), ((), ())), precision=lax.Precision.HIGHEST, preferred_element_type=F32
-    )
-
-
 def split(x):
     high = x.astype(BF16)
     return high, (x - high.astype(F32)).astype(BF16)
@@ -72,6 +66,11 @@
     return jnp.dot(a, b, preferred_element_type=F32)
 
 
+def pair_dot(a, b):
+    (a_high, a_rest), (b_high, b_rest) = split(a), split(b)
+    return bf_dot(a_high, b_rest) + bf_dot(a_rest, b_high) + bf_dot(a_high, b_high)
+
+
 def block(real, imag):
     return jnp.concatenate(
         [jnp.concatenate([real, -imag], axis=1), jnp.concatenate([imag, real], axis=1)], axis=0
@@ -79,40 +78,42 @@
 
 
 def relative(matrix, number, count):
-    dim = matrix.shape[1]
-    column = lax.broadcasted_iota(jnp.int32, matrix.shape, 1)
-    row = lax.broadcasted_iota(jnp.int32, matrix.shape, 0)
+    order = matrix.shape[1]
+    dim = order // 2
+    column = lax.broadcasted_iota(jnp.int32, (order, order), 1)
+    row = lax.broadcasted_iota(jnp.int32, (order, order), 0)
+    within = lax.rem(column, dim)
     if number == 0:
         size = dim // count
-        spot, source = column // size, jnp.zeros_like(column)
+        spot, source = within // size, jnp.zeros_like(column)
         for index, partner in enumerate(partners_of(count)):
             source = jnp.where(spot == index, partner, source)
-        natural = source * size + lax.rem(column, size)
+        natural = source * size + lax.rem(within, size)
     else:
-        natural = jnp.bitwise_xor(column, lax.axis_index("qb") * (dim // 2))
-    return exact_dot(matrix, jnp.where(row == natural, 1.0, 0.0).astype(F32))
+        natural = jnp.bitwise_xor(within, lax.axis_index("qb") * (dim // 2))
+    picked = jnp.where(row == natural + (column - within), 1.0, 0.0).astype(BF16)
+    return bf_dot(matrix, picked).astype(BF16)
 
 
 def prepare_kernel(low, sections, count, bits_ref, gates_ref, low_ref, *refs):
-    *targets, held, wide, sems = refs
-    copies = []
-    for gate in range(held.shape[0]):
-        copy = pltpu.make_async_copy(gates_ref.at[gate, bits_ref[gate]], held.at[gate], sems.at[gate])
-        copy.start()
-        copies.append(copy)
-    for copy in copies:
-        copy.wait()
+    *targets, held, wides, sems = refs
+    copies = {}
+    for gate in [gate for section in sections for _, _, parts in section for _, gates in parts for gate in gates] + low:
+        copies[gate] = pltpu.make_async_copy(gates_ref.at[gate, bits_ref[gate]], held.at[gate], sems.at[gate])
+        copies[gate].start()
     dim = held.shape[-1]
 
     def product(gates):
+        for gate in gates:
+            copies.pop(gate).wait()
         real, imag = held[gates[0], 0], held[gates[0], 1]
         for gate in gates[1:]:
-            column = exact_dot(block(held[gate, 0], held[gate, 1]), jnp.concatenate([real, imag], axis=0))
+            column = pair_dot(block(held[gate, 0], held[gate, 1]), jnp.concatenate([real, imag], axis=0))
             real, imag = column[:dim], column[dim:]
         return real, imag
 
-    def joined(base, parts):
-        wide[...] = jnp.zeros_like(wide)
+    def joined(wide, base, parts):
+        wide[...] = jnp.zeros(wide.shape, F32)
         for index, (offset, gates) in enumerate(parts):
             real, imag = product(gates)
             for t in range(2):
@@ -124,7 +125,7 @@
                     x = jnp.concatenate(
                         [jnp.concatenate([wide[p, c, at, :] for c in range(2)], axis=1) for p in range(2)], axis=0
                     )
-                    y = exact_dot(block(real, imag), x)
+                    y = pair_dot(block(real, imag), x)
                     for p in range(2):
                         for c in range(2):
                             wide[p, c, at, :] = y[p * dim : (p + 1) * dim, c * dim : (c + 1) * dim]
@@ -133,10 +134,9 @@
     for number, section in enumerate(sections):
         weights, targets = targets[: len(section)], targets[len(section) :]
         for target, (base, _, parts) in zip(weights, section):
-            pair = joined(base, parts) if len(parts) > 1 else product(parts[0][1])
+            high, rest = split(block(*(joined(wides.at[number], base, parts) if len(parts) > 1 else product(parts[0][1]))))
             if number != 1 and target is weights[0]:
-                pair = [relative(x, number, count) for x in pair]
-            high, rest = split(block(*pair))
+                high, rest = relative(high, number, count), relative(rest, number, count)
             target[...] = jnp.concatenate([high, rest, high], axis=1)
     real, imag = product(low)
     high, rest = split(block(real.T, -imag.T))
@@ -212,7 +212,7 @@
     def load(part, start):
         if not isinstance(source, tuple):
             return source[part, pl.ds(start, dim, stride=stride), :]
-        return jnp.concatenate([half[part][pl.ds(start, dim // 2, stride=stride), :] for half in source], axis=0)
+        return jnp.concatenate([half[part, pl.ds(start, dim // 2, stride=stride), :] for half in source], axis=0)
 
     apply_stage(weights_ref, starts, load, store)
 
@@ -265,7 +265,7 @@
 
 def second_kernel(stages, lane_bits, count, stays, *refs):
     blocks, weights, refs = refs[:count], refs[count : count + len(stages)], refs[count + len(stages) :]
-    *outs, one, two = refs
+    out_ref, one, two = refs
     core = lax.axis_index("qb")
     top = core if stays else 1 - core
     for source, block_ref in zip(partners_of(count), blocks):
@@ -274,23 +274,16 @@
             start = pl.multiple_of((mid * count + source) * inner, inner)
             for part in range(2):
                 one[part, pl.ds(start, inner), :] = block_ref[top, mid, part]
-    for stage, weights_ref in zip(stages[:-1], weights):
-        run_stage(stage, weights_ref, lane_bits, one, two)
+    for index, (stage, weights_ref) in enumerate(zip(stages, weights)):
+        run_stage(stage, weights_ref, lane_bits, one, out_ref if index == len(stages) - 1 else two)
         one, two = two, one
-    dim, stride, _ = stage_starts(stages[-1], lane_bits, one.shape[1])
-
-    def store(part, start, value):
-        outs[part][pl.ds(start, dim, stride=stride), :] = value
-
-    run_stage(stages[-1], weights[-1], lane_bits, one, store=store)
-
-
-def third_kernel(stages, lane_bits, *refs):
-    kept, came, refs = refs[:2], refs[2:4], refs[4:]
+
+
+def third_kernel(stages, lane_bits, kept_ref, came_ref, *refs):
     weights, (out_ref, *halves, sems) = refs[: len(stages)], refs[len(stages) :]
     results = halves[4:]
-    half = kept[0].shape[0]
-    run_top_stage(stages[0], weights[0], lane_bits, (kept, came), halves[:2])
+    half = kept_ref.shape[1]
+    run_top_stage(stages[0], weights[0], lane_bits, (kept_ref, came_ref), halves[:2])
     done = run_halves(stages[1:-1], weights[1:-1], lane_bits, halves[:2], halves[2:4])
     copies = []
     for t in range(2):
@@ -375,7 +368,7 @@
         [pl.BlockSpec(memory_space=pltpu.SMEM), hbm],
         [
             pltpu.VMEM((gate_terms.shape[0], 2, dim, dim), F32),
-            pltpu.VMEM((2, 2, 2 * dim, dim), F32),
+            pltpu.VMEM((len(sections), 2, 2, 2 * dim, dim), F32),
             pltpu.SemaphoreType.DMA((gate_terms.shape[0],)),
         ],
         8,
@@ -419,7 +412,7 @@
             call(
                 functools.partial(second_kernel, sections[1], lane_bits, qa, stays),
                 "second_section_kept" if stays else "second_section_sent",
-                (shape((rows // qb, lanes), F32),) * 2,
+                shape((2, rows // qb, lanes), F32),
                 [vmem] * (qa + counts[1]),
                 [half] * 2,
                 1.5,
@@ -428,16 +421,16 @@
             )
         )
         if not stays:
-            came = [lax.ppermute(part, "qb", [(i, 1 - i) for i in range(qb)]) for part in halves[0]]
+            came = lax.ppermute(halves[0], "qb", [(i, 1 - i) for i in range(qb)])
     final = call(
         functools.partial(third_kernel, sections[2], lane_bits),
         "third_section",
         shape((2 * rows, lanes), F32),
-        [vmem] * (4 + counts[2]),
+        [vmem] * (2 + counts[2]),
         [half] * 4 + [pltpu.VMEM((rows, lanes), F32)] * 2 + [pltpu.SemaphoreType.DMA((2 * PIECES,))],
         4,
-        *halves[1],
-        *came,
+        halves[1],
+        came,
         *weights[2],
         out_spec=hbm,
     )

time: 61.6 us -> 61.5 us (level)
  waiting for transfers between devices: 11.8 us -> 16.1 us
  starting transfers between devices: 30.3 us -> 27.7 us
  Pallas kernels: 16.4 us -> 14.7 us
    ppermute x14, waiting for transfers between devices: 11.4 us -> 15.2 us  [exchange(): lax.ppermute(piece, 'qa', [(i, i ^ distance) for i in range(qa)])]
    ppermute x14, starting transfers between devices: 29.7 us -> 27.6 us  [exchange(): lax.ppermute(piece, 'qa', [(i, i ^ distance) for i in range(qa)])]
    pallas_call x7, Pallas kernels: 16.4 us -> 14.7 us  [call(): pl.pallas_call(kernel, out_shape=out_shapes, in_specs=in_specs, out_specs...]
  transfers between devices with their start and end apart: 16 -> 15, of which waited for: 7 -> 8; matrix products, arithmetic and copies ran while one was open for 0% -> 0% of each run, Pallas kernels for 16% -> 13%
where the time goes in v14:
time: 61.5 us; the launch traced here: 61.3 us
  starting transfers between devices  27.7 us (45%)
  waiting for transfers between devices  16.1 us (26%)
  Pallas kernels  14.7 us (24%)
  local copies, waits for them, and re-layouts  2.8 us (5%)
    ppermute x14, starting transfers between devices, exchange(): lax.ppermute(piece, 'qa', [(i, i ^ distance) for i in range(qa)])  27.6 us
    ppermute x14, waiting for transfers between devices, exchange(): lax.ppermute(piece, 'qa', [(i, i ^ distance) for i in range(qa)])  15.2 us
    pallas_call x7, Pallas kernels, call(): pl.pallas_call(kernel, out_shape=out_shapes, in_specs=in_specs, out_specs...  14.7 us
    unnamed x6, local copies, waits for them, and re-layouts  1.88 us
  transfers between devices with their start and end apart: 15, of which 8 were waited for; matrix products, arithmetic and copies ran while one was open for 0% of the time, Pallas kernels for 13%

profile of v14, /device:TPU:0, one launch (start us, length us, event | category | flops | bytes accessed | tf_op | source)
XLA Modules:
  0.0 61.3 jit_solution(7221775473692726964)
XLA Ops:
  0.0 0.9 %dynamic-slice_bitcast_fusion = f32[256,128]{1,0:T(8,128)S(1)} fusion(f32[8,256,128]{2,1,0:T(8,128)} %bitcast.12, s32[]{:T(128)S(6)} %select_n.4), kind=kLoop, calls=%fused_computation | loop fusion | bytes 262148 | tf_op jit(solution)/shard_map/jit(dynamic_index_in_dim)/squeeze | solution.py:354
  0.9 6.1 %collective-permute-start = (f32[256,128]{1,0:T(8,128)S(1)}, f32[256,128]{1,0:T(8,128)S(1)}, u32[]{:S(2)}, u32[]{:S(2)}) collective-permute-start(f32[256,128]{1,0:T(8,128)S(1)} %dynamic-slice_bitcast_fusion), channel_id=1, source_target_pairs={{0,14},{2,12},{4,10},{6,8},{8,6},{10,4},{12,2},{14,0},{1,15},{3,13... | collective-permute-start | bytes 393224 | tf_op jit(solution)/shard_map/ppermute | solution.py:359
  7.0 1.2 %copy-done = f32[2,131072]{1,0:T(2,128)S(1)} copy-done((f32[2,131072]{1,0:T(2,128)S(1)}, f32[2,131072]{1,0:T(2,128)}, u32[]{:S(2)}) %copy-start) | copy-done | bytes 1048600
  8.2 0.7 %split_state.1 = (f32[256,128]{1,0:T(8,128)S(1)}, f32[256,128]{1,0:T(8,128)}, f32[256,128]{1,0:T(8,128)S(1)}, f32[256,128]{1,0:T(8,128)S(1)}, f32[256,128]{1,0:T...) custom-call(f32[8,256,128]{2,1,0:T(8,128)S(1)} %bitcast.13), custom_call_target="tpu_custom_call" | custom-call | bytes 4194304 | tf_op jit(solution)/shard_map/split_state/pallas_call | solution.py:310
  8.9 0.2 collective-permute-start.1
  9.2 1.8 %collective-permute-start.3 = (f32[256,128]{1,0:T(8,128)S(1)}, f32[256,128]{1,0:T(8,128)S(1)}, u32[]{:S(2)}, u32[]{:S(2)}) collective-permute-start(f32[256,128]{1,0:T(8,128)S(1)} %get-tuple-element.32), channel_id=1, source_target_pairs={{0,4},{2,6},{4,0},{6,2},{8,12},{10,14},{12,8},{14,10},{1,5},{3,7},... | collective-permute-start | bytes 393224 | tf_op jit(solution)/shard_map/ppermute | solution.py:359
  11.0 3.2 %collective-permute-start.4 = (f32[256,128]{1,0:T(8,128)S(1)}, f32[256,128]{1,0:T(8,128)S(1)}, u32[]{:S(2)}, u32[]{:S(2)}) collective-permute-start(f32[256,128]{1,0:T(8,128)S(1)} %get-tuple-element.34), channel_id=1, source_target_pairs={{0,10},{2,8},{4,14},{6,12},{8,2},{10,0},{12,6},{14,4},{1,11},{3,9}... | collective-permute-start | bytes 393224 | tf_op jit(solution)/shard_map/ppermute | solution.py:359
  14.2 3.3 %collective-permute-start.5 = (f32[256,128]{1,0:T(8,128)S(1)}, f32[256,128]{1,0:T(8,128)S(1)}, u32[]{:S(2)}, u32[]{:S(2)}) collective-permute-start(f32[256,128]{1,0:T(8,128)S(1)} %get-tuple-element.35), channel_id=1, source_target_pairs={{0,8},{2,10},{4,12},{6,14},{8,0},{10,2},{12,4},{14,6},{1,9},{3,11}... | collective-permute-start | bytes 393224 | tf_op jit(solution)/shard_map/ppermute | solution.py:359
  17.6 1.5 %collective-permute-start.6 = (f32[256,128]{1,0:T(8,128)S(1)}, f32[256,128]{1,0:T(8,128)S(1)}, u32[]{:S(2)}, u32[]{:S(2)}) collective-permute-start(f32[256,128]{1,0:T(8,128)S(1)} %get-tuple-element.36), channel_id=1, source_target_pairs={{0,2},{2,0},{4,6},{6,4},{8,10},{10,8},{12,14},{14,12},{1,3},{3,1},... | collective-permute-start | bytes 393224 | tf_op jit(solution)/shard_map/ppermute | solution.py:359
  19.1 0.7 %copy-done.1 = s32[18]{0:T(128)S(1)} copy-done((s32[18]{0:T(128)S(1)}, s32[18]{0:T(128)}, u32[]{:S(2)}) %copy-start.1) | copy-done | bytes 96
  19.8 6.0 %prepare_gates.1 = (bf16[768,256]{1,0:T(8,128)(2,1)S(1)}, bf16[256,768]{1,0:T(8,128)(2,1)S(1)}, bf16[256,768]{1,0:T(8,128)(2,1)S(1)}, bf16[512,1536]{1,0:T(8,128...) custom-call(s32[18]{0:T(128)S(1)} %copy-done.1, ...), custom_call_target="tpu_custom_call" | custom-call | flops 3221225472 | bytes 4194304 | tf_op jit(solution)/shard_map/prepare_gates/pallas_call | solution.py:310
  25.8 0.4 low_gate_early.1.refs_0_
  26.2 1.2 %collective-permute-done.4.refs_1_ = f32[256,128]{1,0:T(8,128)S(1)} collective-permute-done((f32[256,128]{1,0:T(8,128)S(1)}, f32[256,128]{1,0:T(8,128)S(1)}, u32[]{:S(2)}, u32[]{:S(2)}) %collective-permute-start.4) | collective-permute-done | bytes 131104 | tf_op jit(solution)/shard_map/ppermute | solution.py:359
  27.5 1.8 %collective-permute-done.5.refs_2_ = f32[256,128]{1,0:T(8,128)S(1)} collective-permute-done((f32[256,128]{1,0:T(8,128)S(1)}, f32[256,128]{1,0:T(8,128)S(1)}, u32[]{:S(2)}, u32[]{:S(2)}) %collective-permute-start.5) | collective-permute-done | bytes 131104 | tf_op jit(solution)/shard_map/ppermute | solution.py:359
  29.3 2.5 %first_section.1 = (f32[2,4,2,16,128]{4,3,2,1,0:T(8,128)S(1)}, f32[2,4,2,16,128]{4,3,2,1,0:T(8,128)S(1)}, f32[2,4,2,16,128]{4,3,2,1,0:T(8,128)S(1)}, f32[2,4,2,1...) custom-call(f32[2,1024,128]{2,1,0:T(8,128)S(1)} %low_gate_early.1.re, ...), custom_call_target="tpu_custom_call", output_to_operand_aliasing={{8}: (0, {})} | custom-call | flops 2013265920 | bytes 4194304 | tf_op jit(solution)/shard_map/first_section/pallas_call | solution.py:310
  31.8 2.5 %collective-permute-start.7 = (f32[2,4,2,16,128]{4,3,2,1,0:T(8,128)S(1)}, f32[2,4,2,16,128]{4,3,2,1,0:T(8,128)S(1)}, u32[]{:S(2)}, u32[]{:S(2)}) collective-permute-start(f32[2,4,2,16,128]{4,3,2,1,0:T(8,128)S(1)} %get-tuple-element.41), channel_id=1, source_target_pairs={{0,14},{2,12},{4,10},{6,8},{8,6},{10,4},{12,2},{14,0},{1,15},{3,13... | collective-permute-start | bytes 393224 | tf_op jit(solution)/shard_map/ppermute | solution.py:359
  34.3 1.3 %collective-permute-start.8 = (f32[2,4,2,16,128]{4,3,2,1,0:T(8,128)S(1)}, f32[2,4,2,16,128]{4,3,2,1,0:T(8,128)S(1)}, u32[]{:S(2)}, u32[]{:S(2)}) collective-permute-start(f32[2,4,2,16,128]{4,3,2,1,0:T(8,128)S(1)} %get-tuple-element.42), channel_id=1, source_target_pairs={{0,12},{2,14},{4,8},{6,10},{8,4},{10,6},{12,0},{14,2},{1,13},{3,15... | collective-permute-start | bytes 393224 | tf_op jit(solution)/shard_map/ppermute | solution.py:359
  35.6 3.0 %collective-permute-start.10 = (f32[2,4,2,16,128]{4,3,2,1,0:T(8,128)S(1)}, f32[2,4,2,16,128]{4,3,2,1,0:T(8,128)S(1)}, u32[]{:S(2)}, u32[]{:S(2)}) collective-permute-start(f32[2,4,2,16,128]{4,3,2,1,0:T(8,128)S(1)} %get-tuple-element.44), channel_id=1, source_target_pairs={{0,4},{2,6},{4,0},{6,2},{8,12},{10,14},{12,8},{14,10},{1,5},{3,7},... | collective-permute-start | bytes 393224 | tf_op jit(solution)/shard_map/ppermute | solution.py:359
  38.6 1.0 %collective-permute-start.11 = (f32[2,4,2,16,128]{4,3,2,1,0:T(8,128)S(1)}, f32[2,4,2,16,128]{4,3,2,1,0:T(8,128)S(1)}, u32[]{:S(2)}, u32[]{:S(2)}) collective-permute-start(f32[2,4,2,16,128]{4,3,2,1,0:T(8,128)S(1)} %get-tuple-element.45), channel_id=1, source_target_pairs={{0,10},{2,8},{4,14},{6,12},{8,2},{10,0},{12,6},{14,4},{1,11},{3,9}... | collective-permute-start | bytes 393224 | tf_op jit(solution)/shard_map/ppermute | solution.py:359
  39.6 0.8 %collective-permute-done.7.refs_1_ = f32[2,4,2,16,128]{4,3,2,1,0:T(8,128)S(1)} collective-permute-done((f32[2,4,2,16,128]{4,3,2,1,0:T(8,128)S(1)}, f32[2,4,2,16,128]{4,3,2,1,0:T(8,128)S(1)}, u32[]{:S(2)}, u32[]{:S(2)}) %collective-permute-start.7) | collective-permute-done | bytes 131104 | tf_op jit(solution)/shard_map/ppermute | solution.py:359
  40.5 2.0 %collective-permute-start.12 = (f32[2,4,2,16,128]{4,3,2,1,0:T(8,128)S(1)}, f32[2,4,2,16,128]{4,3,2,1,0:T(8,128)S(1)}, u32[]{:S(2)}, u32[]{:S(2)}) collective-permute-start(f32[2,4,2,16,128]{4,3,2,1,0:T(8,128)S(1)} %get-tuple-element.46), channel_id=1, source_target_pairs={{0,8},{2,10},{4,12},{6,14},{8,0},{10,2},{12,4},{14,6},{1,9},{3,11}... | collective-permute-start | bytes 393224 | tf_op jit(solution)/shard_map/ppermute | solution.py:359
  42.5 0.0 collective-permute-done.8.refs_2_
  42.5 1.5 %collective-permute-start.13 = (f32[2,4,2,16,128]{4,3,2,1,0:T(8,128)S(1)}, f32[2,4,2,16,128]{4,3,2,1,0:T(8,128)S(1)}, u32[]{:S(2)}, u32[]{:S(2)}) collective-permute-start(f32[2,4,2,16,128]{4,3,2,1,0:T(8,128)S(1)} %get-tuple-element.47), channel_id=1, source_target_pairs={{0,2},{2,0},{4,6},{6,4},{8,10},{10,8},{12,14},{14,12},{1,3},{3,1},... | collective-permute-start | bytes 393224 | tf_op jit(solution)/shard_map/ppermute | solution.py:359
  44.1 3.2 %collective-permute-done.9.refs_3_ = f32[2,4,2,16,128]{4,3,2,1,0:T(8,128)S(1)} collective-permute-done((f32[2,4,2,16,128]{4,3,2,1,0:T(8,128)S(1)}, f32[2,4,2,16,128]{4,3,2,1,0:T(8,128)S(1)}, u32[]{:S(2)}, u32[]{:S(2)}) %collective-permute-start.9) | collective-permute-done | bytes 131104 | tf_op jit(solution)/shard_map/ppermute | solution.py:359
  47.2 2.9 %collective-permute-done.10.refs_4_ = f32[2,4,2,16,128]{4,3,2,1,0:T(8,128)S(1)} collective-permute-done((f32[2,4,2,16,128]{4,3,2,1,0:T(8,128)S(1)}, f32[2,4,2,16,128]{4,3,2,1,0:T(8,128)S(1)}, u32[]{:S(2)}, u32[]{:S(2)}) %collective-permute-start.10) | collective-permute-done | bytes 131104 | tf_op jit(solution)/shard_map/ppermute | solution.py:359
  50.1 4.7 %collective-permute-done.11.refs_5_ = f32[2,4,2,16,128]{4,3,2,1,0:T(8,128)S(1)} collective-permute-done((f32[2,4,2,16,128]{4,3,2,1,0:T(8,128)S(1)}, f32[2,4,2,16,128]{4,3,2,1,0:T(8,128)S(1)}, u32[]{:S(2)}, u32[]{:S(2)}) %collective-permute-start.11) | collective-permute-done | bytes 131104 | tf_op jit(solution)/shard_map/ppermute | solution.py:359
  54.8 0.5 collective-permute-done.12.refs_6_
  55.3 1.0 %second_section_sent.1 = f32[2,512,128]{2,1,0:T(8,128)S(1)} custom-call(f32[2,4,2,16,128]{4,3,2,1,0:T(8,128)S(1)} %get-tuple-element.40.refs_0_, f32[2,4,2,16,128]{4,3,2,1,0:T(8,128)S(1)} %collective-permute-done.7.refs_1_, f32[2,4,2,16,128]{4,3,2,1,0:T(8,128)S(1)} %collective-permute-done.8.refs_2_, ...), custom_call_target="tpu_custom_call" | custom-call | flops 603979776 | bytes 4194304 | tf_op jit(solution)/shard_map/second_section_sent/pallas_call | solution.py:310
  56.3 0.1 collective-permute-start.14
  56.4 1.0 %second_section_kept.1.kept_ref = f32[2,512,128]{2,1,0:T(8,128)S(1)} custom-call(f32[2,4,2,16,128]{4,3,2,1,0:T(8,128)S(1)} %get-tuple-element.40.refs_0_, f32[2,4,2,16,128]{4,3,2,1,0:T(8,128)S(1)} %collective-permute-done.7.refs_1_, f32[2,4,2,16,128]{4,3,2,1,0:T(8,128)S(1)} %collective-permute-done.8.refs_2_, ...), custom_call_target="tpu_custom_call" | custom-call | flops 603979776 | bytes 4194304 | tf_op jit(solution)/shard_map/second_section_kept/pallas_call | solution.py:310
  57.4 0.9 %collective-permute-done.14.came_ref = f32[2,512,128]{2,1,0:T(8,128)S(1)} collective-permute-done((f32[2,512,128]{2,1,0:T(8,128)S(1)}, f32[2,512,128]{2,1,0:T(8,128)S(1)}, u32[]{:S(2)}, u32[]{:S(2)}) %collective-permute-start.14) | collective-permute-done | bytes 524320 | tf_op jit(solution)/shard_map/ppermute | solution.py:424
  58.3 3.1 %third_section.1 = f32[2048,128]{1,0:T(8,128)} custom-call(f32[2,512,128]{2,1,0:T(8,128)S(1)} %second_section_kept.1.kept_ref, f32[2,512,128]{2,1,0:T(8,128)S(1)} %collective-permute-done.14.came_ref, bf16[256,768]{1,0:T(8,128)(2,1)S(1)} %get-tuple-element.50.refs_0_, bf16[256,768]{1,0:T(8,128)(2,1)S(1)} %get-tuple-element.51.refs_1_, ...), custom_call_target="tpu_custom_call" | custom-call | flops 1610612736 | bytes 4194304 | tf_op jit(solution)/shard_map/third_section/pallas_call | solution.py:310
  (12 shorter events, 0.0 us)
Async XLA Ops:
  0.9 13.3 %collective-permute-start = (f32[256,128]{1,0:T(8,128)S(1)}, f32[256,128]{1,0:T(8,128)S(1)}, u32[]{:S(2)}, u32[]{:S(2)}) collective-permute-start(f32[256,128]{1,0:T(8,128)S(1)} %dynamic-slice_bitcast_fusion), channel_id=1, source_target_pairs={{0,14},{2,12},{4,10},{6,8},{8,6},{10,4},{12,2},{14,0},{1,15},{3,13... | collective-permute-start | bytes 393224 | tf_op jit(solution)/shard_map/ppermute | solution.py:359
  7.0 1.2 %copy-start = (f32[2,131072]{1,0:T(2,128)S(1)}, f32[2,131072]{1,0:T(2,128)}, u32[]{:S(2)}) copy-start(f32[2,131072]{1,0:T(2,128)} %param.3) | copy-start | bytes 3145732
  8.9 8.6 %collective-permute-start.1 = (f32[256,128]{1,0:T(8,128)S(1)}, f32[256,128]{1,0:T(8,128)S(1)}, u32[]{:S(2)}, u32[]{:S(2)}) collective-permute-start(f32[256,128]{1,0:T(8,128)S(1)} %get-tuple-element.30), channel_id=1, source_target_pairs={{0,12},{2,14},{4,8},{6,10},{8,4},{10,6},{12,0},{14,2},{1,13},{3,15... | collective-permute-start | bytes 393224 | tf_op jit(solution)/shard_map/ppermute | solution.py:359
  9.2 16.6 %collective-permute-start.2 = (f32[256,128]{1,0:T(8,128)S(1)}, f32[256,128]{1,0:T(8,128)S(1)}, u32[]{:S(2)}, u32[]{:S(2)}) collective-permute-start(f32[256,128]{1,0:T(8,128)S(1)} %get-tuple-element.31), channel_id=1, source_target_pairs={{0,6},{2,4},{4,2},{6,0},{8,14},{10,12},{12,10},{14,8},{1,7},{3,5},... | collective-permute-start | bytes 393224 | tf_op jit(solution)/shard_map/ppermute | solution.py:359
  9.2 16.6 %collective-permute-start.3 = (f32[256,128]{1,0:T(8,128)S(1)}, f32[256,128]{1,0:T(8,128)S(1)}, u32[]{:S(2)}, u32[]{:S(2)}) collective-permute-start(f32[256,128]{1,0:T(8,128)S(1)} %get-tuple-element.32), channel_id=1, source_target_pairs={{0,4},{2,6},{4,0},{6,2},{8,12},{10,14},{12,8},{14,10},{1,5},{3,7},... | collective-permute-start | bytes 393224 | tf_op jit(solution)/shard_map/ppermute | solution.py:359
  11.0 16.5 %collective-permute-start.4 = (f32[256,128]{1,0:T(8,128)S(1)}, f32[256,128]{1,0:T(8,128)S(1)}, u32[]{:S(2)}, u32[]{:S(2)}) collective-permute-start(f32[256,128]{1,0:T(8,128)S(1)} %get-tuple-element.34), channel_id=1, source_target_pairs={{0,10},{2,8},{4,14},{6,12},{8,2},{10,0},{12,6},{14,4},{1,11},{3,9}... | collective-permute-start | bytes 393224 | tf_op jit(solution)/shard_map/ppermute | solution.py:359
  14.2 15.1 %collective-permute-start.5 = (f32[256,128]{1,0:T(8,128)S(1)}, f32[256,128]{1,0:T(8,128)S(1)}, u32[]{:S(2)}, u32[]{:S(2)}) collective-permute-start(f32[256,128]{1,0:T(8,128)S(1)} %get-tuple-element.35), channel_id=1, source_target_pairs={{0,8},{2,10},{4,12},{6,14},{8,0},{10,2},{12,4},{14,6},{1,9},{3,11}... | collective-permute-start | bytes 393224 | tf_op jit(solution)/shard_map/ppermute | solution.py:359
  17.6 11.7 %collective-permute-start.6 = (f32[256,128]{1,0:T(8,128)S(1)}, f32[256,128]{1,0:T(8,128)S(1)}, u32[]{:S(2)}, u32[]{:S(2)}) collective-permute-start(f32[256,128]{1,0:T(8,128)S(1)} %get-tuple-element.36), channel_id=1, source_target_pairs={{0,2},{2,0},{4,6},{6,4},{8,10},{10,8},{12,14},{14,12},{1,3},{3,1},... | collective-permute-start | bytes 393224 | tf_op jit(solution)/shard_map/ppermute | solution.py:359
  19.1 0.7 %copy-start.1 = (s32[18]{0:T(128)S(1)}, s32[18]{0:T(128)}, u32[]{:S(2)}) copy-start(s32[18]{0:T(128)} %bits_ref.1) | copy-start | bytes 220
  31.8 8.7 %collective-permute-start.7 = (f32[2,4,2,16,128]{4,3,2,1,0:T(8,128)S(1)}, f32[2,4,2,16,128]{4,3,2,1,0:T(8,128)S(1)}, u32[]{:S(2)}, u32[]{:S(2)}) collective-permute-start(f32[2,4,2,16,128]{4,3,2,1,0:T(8,128)S(1)} %get-tuple-element.41), channel_id=1, source_target_pairs={{0,14},{2,12},{4,10},{6,8},{8,6},{10,4},{12,2},{14,0},{1,15},{3,13... | collective-permute-start | bytes 393224 | tf_op jit(solution)/shard_map/ppermute | solution.py:359
  34.3 8.2 %collective-permute-start.8 = (f32[2,4,2,16,128]{4,3,2,1,0:T(8,128)S(1)}, f32[2,4,2,16,128]{4,3,2,1,0:T(8,128)S(1)}, u32[]{:S(2)}, u32[]{:S(2)}) collective-permute-start(f32[2,4,2,16,128]{4,3,2,1,0:T(8,128)S(1)} %get-tuple-element.42), channel_id=1, source_target_pairs={{0,12},{2,14},{4,8},{6,10},{8,4},{10,6},{12,0},{14,2},{1,13},{3,15... | collective-permute-start | bytes 393224 | tf_op jit(solution)/shard_map/ppermute | solution.py:359
  35.6 11.6 %collective-permute-start.9 = (f32[2,4,2,16,128]{4,3,2,1,0:T(8,128)S(1)}, f32[2,4,2,16,128]{4,3,2,1,0:T(8,128)S(1)}, u32[]{:S(2)}, u32[]{:S(2)}) collective-permute-start(f32[2,4,2,16,128]{4,3,2,1,0:T(8,128)S(1)} %get-tuple-element.43), channel_id=1, source_target_pairs={{0,6},{2,4},{4,2},{6,0},{8,14},{10,12},{12,10},{14,8},{1,7},{3,5},... | collective-permute-start | bytes 393224 | tf_op jit(solution)/shard_map/ppermute | solution.py:359
  35.6 14.5 %collective-permute-start.10 = (f32[2,4,2,16,128]{4,3,2,1,0:T(8,128)S(1)}, f32[2,4,2,16,128]{4,3,2,1,0:T(8,128)S(1)}, u32[]{:S(2)}, u32[]{:S(2)}) collective-permute-start(f32[2,4,2,16,128]{4,3,2,1,0:T(8,128)S(1)} %get-tuple-element.44), channel_id=1, source_target_pairs={{0,4},{2,6},{4,0},{6,2},{8,12},{10,14},{12,8},{14,10},{1,5},{3,7},... | collective-permute-start | bytes 393224 | tf_op jit(solution)/shard_map/ppermute | solution.py:359
  38.6 16.2 %collective-permute-start.11 = (f32[2,4,2,16,128]{4,3,2,1,0:T(8,128)S(1)}, f32[2,4,2,16,128]{4,3,2,1,0:T(8,128)S(1)}, u32[]{:S(2)}, u32[]{:S(2)}) collective-permute-start(f32[2,4,2,16,128]{4,3,2,1,0:T(8,128)S(1)} %get-tuple-element.45), channel_id=1, source_target_pairs={{0,10},{2,8},{4,14},{6,12},{8,2},{10,0},{12,6},{14,4},{1,11},{3,9}... | collective-permute-start | bytes 393224 | tf_op jit(solution)/shard_map/ppermute | solution.py:359
  40.5 14.8 %collective-permute-start.12 = (f32[2,4,2,16,128]{4,3,2,1,0:T(8,128)S(1)}, f32[2,4,2,16,128]{4,3,2,1,0:T(8,128)S(1)}, u32[]{:S(2)}, u32[]{:S(2)}) collective-permute-start(f32[2,4,2,16,128]{4,3,2,1,0:T(8,128)S(1)} %get-tuple-element.46), channel_id=1, source_target_pairs={{0,8},{2,10},{4,12},{6,14},{8,0},{10,2},{12,4},{14,6},{1,9},{3,11}... | collective-permute-start | bytes 393224 | tf_op jit(solution)/shard_map/ppermute | solution.py:359
  42.5 12.8 %collective-permute-start.13 = (f32[2,4,2,16,128]{4,3,2,1,0:T(8,128)S(1)}, f32[2,4,2,16,128]{4,3,2,1,0:T(8,128)S(1)}, u32[]{:S(2)}, u32[]{:S(2)}) collective-permute-start(f32[2,4,2,16,128]{4,3,2,1,0:T(8,128)S(1)} %get-tuple-element.47), channel_id=1, source_target_pairs={{0,2},{2,0},{4,6},{6,4},{8,10},{10,8},{12,14},{14,12},{1,3},{3,1},... | collective-permute-start | bytes 393224 | tf_op jit(solution)/shard_map/ppermute | solution.py:359
  56.3 2.0 %copy-start.2 = (bf16[512,1536]{1,0:T(8,128)(2,1)S(1)}, bf16[512,1536]{1,0:T(8,128)(2,1)}, u32[]{:S(2)}) copy-start(bf16[512,1536]{1,0:T(8,128)(2,1)} %get-tuple-element.52.refs_2_) | copy-start | bytes 4718596
  56.3 2.0 %collective-permute-start.14 = (f32[2,512,128]{2,1,0:T(8,128)S(1)}, f32[2,512,128]{2,1,0:T(8,128)S(1)}, u32[]{:S(2)}, u32[]{:S(2)}) collective-permute-start(f32[2,512,128]{2,1,0:T(8,128)S(1)} %second_section_sent.1), channel_id=1, source_target_pairs={{0,1},{1,0},{2,3},{3,2},{4,5},{5,4},{6,7},{7,6},{8,9},{9,8},{10,11... | collective-permute-start | bytes 1572872 | tf_op jit(solution)/shard_map/ppermute | solution.py:424

commit v15 on v14

--- a/solution.py
+++ b/solution.py
@@ -145,7 +145,9 @@
 
 def distances_of(count):
     half = count // 2
-    far, near = list(range(count - 1, half - 1, -1)), list(range(half - 1, 0, -1))
+    middle = half + half // 2
+    far = [*range(middle - 1, half - 1, -1), *range(count - 1, middle - 1, -1)]
+    near = list(range(half - 1, 0, -1))
     order = [0]
     while far or near:
         order += far[:2] + near[:2]

time: 61.5 us -> 62.2 us (1.011)
  the two profiles are of different devices: /device:TPU:0 before, /device:TPU:25 now
where the time goes in v15:
time: 62.2 us; the launch traced here: 62 us
  starting transfers between devices  28.6 us (46%)
  waiting for transfers between devices  15.8 us (25%)
  Pallas kernels  14.7 us (24%)
  local copies, waits for them, and re-layouts  2.8 us (5%)
    ppermute x14, starting transfers between devices, exchange(): lax.ppermute(piece, 'qa', [(i, i ^ distance) for i in range(qa)])  22.1 us
    ppermute x14, waiting for transfers between devices, exchange(): lax.ppermute(piece, 'qa', [(i, i ^ distance) for i in range(qa)])  15.3 us
    pallas_call x7, Pallas kernels, call(): pl.pallas_call(kernel, out_shape=out_shapes, in_specs=in_specs, out_specs...  14.7 us
    ppermute x1, starting transfers between devices, per_device(): came = lax.ppermute(halves[0], 'qb', [(i, 1 - i) for i in range(qb)])  6.44 us
    unnamed x6, local copies, waits for them, and re-layouts  1.88 us
  transfers between devices with their start and end apart: 15, of which 5 were waited for; matrix products, arithmetic and copies ran while one was open for 0% of the time, Pallas kernels for 13%

profile of v15, /device:TPU:25, one launch (start us, length us, event | category | flops | bytes accessed | tf_op | source)
XLA Modules:
  0.0 62.0 jit_solution(12517011094415237098)
XLA Ops:
  0.0 0.9 %dynamic-slice_bitcast_fusion = f32[256,128]{1,0:T(8,128)S(1)} fusion(f32[8,256,128]{2,1,0:T(8,128)} %bitcast.12, s32[]{:T(128)S(6)} %select_n.4), kind=kLoop, calls=%fused_computation | loop fusion | bytes 262148 | tf_op jit(solution)/shard_map/jit(dynamic_index_in_dim)/squeeze | solution.py:356
  0.9 1.1 %collective-permute-start = (f32[256,128]{1,0:T(8,128)S(1)}, f32[256,128]{1,0:T(8,128)S(1)}, u32[]{:S(2)}, u32[]{:S(2)}) collective-permute-start(f32[256,128]{1,0:T(8,128)S(1)} %dynamic-slice_bitcast_fusion), channel_id=1, source_target_pairs={{0,10},{2,8},{4,14},{6,12},{8,2},{10,0},{12,6},{14,4},{1,11},{3,9}... | collective-permute-start | bytes 393224 | tf_op jit(solution)/shard_map/ppermute | solution.py:361
  2.0 1.2 %copy-done = f32[2,131072]{1,0:T(2,128)S(1)} copy-done((f32[2,131072]{1,0:T(2,128)S(1)}, f32[2,131072]{1,0:T(2,128)}, u32[]{:S(2)}) %copy-start) | copy-done | bytes 1048600
  3.2 0.7 %split_state.1 = (f32[256,128]{1,0:T(8,128)S(1)}, f32[256,128]{1,0:T(8,128)}, f32[256,128]{1,0:T(8,128)S(1)}, f32[256,128]{1,0:T(8,128)S(1)}, f32[256,128]{1,0:T...) custom-call(f32[8,256,128]{2,1,0:T(8,128)S(1)} %bitcast.13), custom_call_target="tpu_custom_call" | custom-call | bytes 4194304 | tf_op jit(solution)/shard_map/split_state/pallas_call | solution.py:312
  3.9 2.3 %collective-permute-start.1 = (f32[256,128]{1,0:T(8,128)S(1)}, f32[256,128]{1,0:T(8,128)S(1)}, u32[]{:S(2)}, u32[]{:S(2)}) collective-permute-start(f32[256,128]{1,0:T(8,128)S(1)} %get-tuple-element.30), channel_id=1, source_target_pairs={{0,8},{2,10},{4,12},{6,14},{8,0},{10,2},{12,4},{14,6},{1,9},{3,11}... | collective-permute-start | bytes 393224 | tf_op jit(solution)/shard_map/ppermute | solution.py:361
  6.3 0.1 collective-permute-start.2
  6.4 1.3 %collective-permute-start.3 = (f32[256,128]{1,0:T(8,128)S(1)}, f32[256,128]{1,0:T(8,128)S(1)}, u32[]{:S(2)}, u32[]{:S(2)}) collective-permute-start(f32[256,128]{1,0:T(8,128)S(1)} %get-tuple-element.32), channel_id=1, source_target_pairs={{0,4},{2,6},{4,0},{6,2},{8,12},{10,14},{12,8},{14,10},{1,5},{3,7},... | collective-permute-start | bytes 393224 | tf_op jit(solution)/shard_map/ppermute | solution.py:361
  7.7 0.9 %collective-permute-start.4 = (f32[256,128]{1,0:T(8,128)S(1)}, f32[256,128]{1,0:T(8,128)S(1)}, u32[]{:S(2)}, u32[]{:S(2)}) collective-permute-start(f32[256,128]{1,0:T(8,128)S(1)} %get-tuple-element.34), channel_id=1, source_target_pairs={{0,14},{2,12},{4,10},{6,8},{8,6},{10,4},{12,2},{14,0},{1,15},{3,13... | collective-permute-start | bytes 393224 | tf_op jit(solution)/shard_map/ppermute | solution.py:361
  8.6 5.2 %collective-permute-done.refs_1_ = f32[256,128]{1,0:T(8,128)S(1)} collective-permute-done((f32[256,128]{1,0:T(8,128)S(1)}, f32[256,128]{1,0:T(8,128)S(1)}, u32[]{:S(2)}, u32[]{:S(2)}) %collective-permute-start) | collective-permute-done | bytes 131104 | tf_op jit(solution)/shard_map/ppermute | solution.py:361
  13.7 0.0 collective-permute-start.5
  13.8 3.6 %collective-permute-done.1.refs_2_ = f32[256,128]{1,0:T(8,128)S(1)} collective-permute-done((f32[256,128]{1,0:T(8,128)S(1)}, f32[256,128]{1,0:T(8,128)S(1)}, u32[]{:S(2)}, u32[]{:S(2)}) %collective-permute-start.1) | collective-permute-done | bytes 131104 | tf_op jit(solution)/shard_map/ppermute | solution.py:361
  17.4 0.2 collective-permute-start.6
  17.6 0.7 %copy-done.1 = s32[18]{0:T(128)S(1)} copy-done((s32[18]{0:T(128)S(1)}, s32[18]{0:T(128)}, u32[]{:S(2)}) %copy-start.1) | copy-done | bytes 96
  18.2 6.0 %prepare_gates.1 = (bf16[768,256]{1,0:T(8,128)(2,1)S(1)}, bf16[256,768]{1,0:T(8,128)(2,1)S(1)}, bf16[256,768]{1,0:T(8,128)(2,1)S(1)}, bf16[512,1536]{1,0:T(8,128...) custom-call(s32[18]{0:T(128)S(1)} %copy-done.1, ...), custom_call_target="tpu_custom_call" | custom-call | flops 3221225472 | bytes 4194304 | tf_op jit(solution)/shard_map/prepare_gates/pallas_call | solution.py:312
  24.3 0.4 low_gate_early.1.refs_0_
  24.7 0.0 collective-permute-done.5.refs_2_
  24.7 0.0 collective-permute-done.6.refs_3_
  24.7 2.5 %first_section.1 = (f32[2,4,2,16,128]{4,3,2,1,0:T(8,128)S(1)}, f32[2,4,2,16,128]{4,3,2,1,0:T(8,128)S(1)}, f32[2,4,2,16,128]{4,3,2,1,0:T(8,128)S(1)}, f32[2,4,2,1...) custom-call(f32[2,1024,128]{2,1,0:T(8,128)S(1)} %low_gate_early.1.re, ...), custom_call_target="tpu_custom_call", output_to_operand_aliasing={{8}: (0, {})} | custom-call | flops 2013265920 | bytes 4194304 | tf_op jit(solution)/shard_map/first_section/pallas_call | solution.py:312
  27.3 2.4 %collective-permute-start.7 = (f32[2,4,2,16,128]{4,3,2,1,0:T(8,128)S(1)}, f32[2,4,2,16,128]{4,3,2,1,0:T(8,128)S(1)}, u32[]{:S(2)}, u32[]{:S(2)}) collective-permute-start(f32[2,4,2,16,128]{4,3,2,1,0:T(8,128)S(1)} %get-tuple-element.41), channel_id=1, source_target_pairs={{0,10},{2,8},{4,14},{6,12},{8,2},{10,0},{12,6},{14,4},{1,11},{3,9}... | collective-permute-start | bytes 393224 | tf_op jit(solution)/shard_map/ppermute | solution.py:361
  29.6 1.3 %collective-permute-start.8 = (f32[2,4,2,16,128]{4,3,2,1,0:T(8,128)S(1)}, f32[2,4,2,16,128]{4,3,2,1,0:T(8,128)S(1)}, u32[]{:S(2)}, u32[]{:S(2)}) collective-permute-start(f32[2,4,2,16,128]{4,3,2,1,0:T(8,128)S(1)} %get-tuple-element.42), channel_id=1, source_target_pairs={{0,8},{2,10},{4,12},{6,14},{8,0},{10,2},{12,4},{14,6},{1,9},{3,11}... | collective-permute-start | bytes 393224 | tf_op jit(solution)/shard_map/ppermute | solution.py:361
  30.9 3.1 %collective-permute-start.9 = (f32[2,4,2,16,128]{4,3,2,1,0:T(8,128)S(1)}, f32[2,4,2,16,128]{4,3,2,1,0:T(8,128)S(1)}, u32[]{:S(2)}, u32[]{:S(2)}) collective-permute-start(f32[2,4,2,16,128]{4,3,2,1,0:T(8,128)S(1)} %get-tuple-element.43), channel_id=1, source_target_pairs={{0,6},{2,4},{4,2},{6,0},{8,14},{10,12},{12,10},{14,8},{1,7},{3,5},... | collective-permute-start | bytes 393224 | tf_op jit(solution)/shard_map/ppermute | solution.py:361
  34.0 0.0 collective-permute-start.10
  34.0 1.3 %collective-permute-start.11 = (f32[2,4,2,16,128]{4,3,2,1,0:T(8,128)S(1)}, f32[2,4,2,16,128]{4,3,2,1,0:T(8,128)S(1)}, u32[]{:S(2)}, u32[]{:S(2)}) collective-permute-start(f32[2,4,2,16,128]{4,3,2,1,0:T(8,128)S(1)} %get-tuple-element.45), channel_id=1, source_target_pairs={{0,14},{2,12},{4,10},{6,8},{8,6},{10,4},{12,2},{14,0},{1,15},{3,13... | collective-permute-start | bytes 393224 | tf_op jit(solution)/shard_map/ppermute | solution.py:361
  35.2 6.5 %collective-permute-start.12 = (f32[2,4,2,16,128]{4,3,2,1,0:T(8,128)S(1)}, f32[2,4,2,16,128]{4,3,2,1,0:T(8,128)S(1)}, u32[]{:S(2)}, u32[]{:S(2)}) collective-permute-start(f32[2,4,2,16,128]{4,3,2,1,0:T(8,128)S(1)} %get-tuple-element.46), channel_id=1, source_target_pairs={{0,12},{2,14},{4,8},{6,10},{8,4},{10,6},{12,0},{14,2},{1,13},{3,15... | collective-permute-start | bytes 393224 | tf_op jit(solution)/shard_map/ppermute | solution.py:361
  41.8 1.7 %collective-permute-start.13 = (f32[2,4,2,16,128]{4,3,2,1,0:T(8,128)S(1)}, f32[2,4,2,16,128]{4,3,2,1,0:T(8,128)S(1)}, u32[]{:S(2)}, u32[]{:S(2)}) collective-permute-start(f32[2,4,2,16,128]{4,3,2,1,0:T(8,128)S(1)} %get-tuple-element.47), channel_id=1, source_target_pairs={{0,2},{2,0},{4,6},{6,4},{8,10},{10,8},{12,14},{14,12},{1,3},{3,1},... | collective-permute-start | bytes 393224 | tf_op jit(solution)/shard_map/ppermute | solution.py:361
  43.5 4.6 %collective-permute-done.11.refs_5_ = f32[2,4,2,16,128]{4,3,2,1,0:T(8,128)S(1)} collective-permute-done((f32[2,4,2,16,128]{4,3,2,1,0:T(8,128)S(1)}, f32[2,4,2,16,128]{4,3,2,1,0:T(8,128)S(1)}, u32[]{:S(2)}, u32[]{:S(2)}) %collective-permute-start.11) | collective-permute-done | bytes 131104 | tf_op jit(solution)/shard_map/ppermute | solution.py:361
  48.1 1.9 %collective-permute-done.12.refs_6_ = f32[2,4,2,16,128]{4,3,2,1,0:T(8,128)S(1)} collective-permute-done((f32[2,4,2,16,128]{4,3,2,1,0:T(8,128)S(1)}, f32[2,4,2,16,128]{4,3,2,1,0:T(8,128)S(1)}, u32[]{:S(2)}, u32[]{:S(2)}) %collective-permute-start.12) | collective-permute-done | bytes 131104 | tf_op jit(solution)/shard_map/ppermute | solution.py:361
  50.0 1.0 %second_section_sent.1 = f32[2,512,128]{2,1,0:T(8,128)S(1)} custom-call(f32[2,4,2,16,128]{4,3,2,1,0:T(8,128)S(1)} %get-tuple-element.40.refs_0_, f32[2,4,2,16,128]{4,3,2,1,0:T(8,128)S(1)} %collective-permute-done.7.refs_1_, f32[2,4,2,16,128]{4,3,2,1,0:T(8,128)S(1)} %collective-permute-done.8.refs_2_, ...), custom_call_target="tpu_custom_call" | custom-call | flops 603979776 | bytes 4194304 | tf_op jit(solution)/shard_map/second_section_sent/pallas_call | solution.py:312
  51.0 6.4 %collective-permute-start.14 = (f32[2,512,128]{2,1,0:T(8,128)S(1)}, f32[2,512,128]{2,1,0:T(8,128)S(1)}, u32[]{:S(2)}, u32[]{:S(2)}) collective-permute-start(f32[2,512,128]{2,1,0:T(8,128)S(1)} %second_section_sent.1), channel_id=1, source_target_pairs={{0,1},{1,0},{2,3},{3,2},{4,5},{5,4},{6,7},{7,6},{8,9},{9,8},{10,11... | collective-permute-start | bytes 1572872 | tf_op jit(solution)/shard_map/ppermute | solution.py:426
  57.4 1.0 %second_section_kept.1.kept_ref = f32[2,512,128]{2,1,0:T(8,128)S(1)} custom-call(f32[2,4,2,16,128]{4,3,2,1,0:T(8,128)S(1)} %get-tuple-element.40.refs_0_, f32[2,4,2,16,128]{4,3,2,1,0:T(8,128)S(1)} %collective-permute-done.7.refs_1_, f32[2,4,2,16,128]{4,3,2,1,0:T(8,128)S(1)} %collective-permute-done.8.refs_2_, ...), custom_call_target="tpu_custom_call" | custom-call | flops 603979776 | bytes 4194304 | tf_op jit(solution)/shard_map/second_section_kept/pallas_call | solution.py:312
  58.4 0.5 collective-permute-done.14.came_ref
  59.0 3.1 %third_section.1 = f32[2048,128]{1,0:T(8,128)} custom-call(f32[2,512,128]{2,1,0:T(8,128)S(1)} %second_section_kept.1.kept_ref, f32[2,512,128]{2,1,0:T(8,128)S(1)} %collective-permute-done.14.came_ref, bf16[256,768]{1,0:T(8,128)(2,1)S(1)} %get-tuple-element.50.refs_0_, bf16[256,768]{1,0:T(8,128)(2,1)S(1)} %get-tuple-element.51.refs_1_, ...), custom_call_target="tpu_custom_call" | custom-call | flops 1610612736 | bytes 4194304 | tf_op jit(solution)/shard_map/third_section/pallas_call | solution.py:312
  (12 shorter events, 0.0 us)
Async XLA Ops:
  0.9 12.8 %collective-permute-start = (f32[256,128]{1,0:T(8,128)S(1)}, f32[256,128]{1,0:T(8,128)S(1)}, u32[]{:S(2)}, u32[]{:S(2)}) collective-permute-start(f32[256,128]{1,0:T(8,128)S(1)} %dynamic-slice_bitcast_fusion), channel_id=1, source_target_pairs={{0,10},{2,8},{4,14},{6,12},{8,2},{10,0},{12,6},{14,4},{1,11},{3,9}... | collective-permute-start | bytes 393224 | tf_op jit(solution)/shard_map/ppermute | solution.py:361
  2.0 1.2 %copy-start = (f32[2,131072]{1,0:T(2,128)S(1)}, f32[2,131072]{1,0:T(2,128)}, u32[]{:S(2)}) copy-start(f32[2,131072]{1,0:T(2,128)} %param.3) | copy-start | bytes 3145732
  3.9 13.4 %collective-permute-start.1 = (f32[256,128]{1,0:T(8,128)S(1)}, f32[256,128]{1,0:T(8,128)S(1)}, u32[]{:S(2)}, u32[]{:S(2)}) collective-permute-start(f32[256,128]{1,0:T(8,128)S(1)} %get-tuple-element.30), channel_id=1, source_target_pairs={{0,8},{2,10},{4,12},{6,14},{8,0},{10,2},{12,4},{14,6},{1,9},{3,11}... | collective-permute-start | bytes 393224 | tf_op jit(solution)/shard_map/ppermute | solution.py:361
  6.3 18.0 %collective-permute-start.2 = (f32[256,128]{1,0:T(8,128)S(1)}, f32[256,128]{1,0:T(8,128)S(1)}, u32[]{:S(2)}, u32[]{:S(2)}) collective-permute-start(f32[256,128]{1,0:T(8,128)S(1)} %get-tuple-element.31), channel_id=1, source_target_pairs={{0,6},{2,4},{4,2},{6,0},{8,14},{10,12},{12,10},{14,8},{1,7},{3,5},... | collective-permute-start | bytes 393224 | tf_op jit(solution)/shard_map/ppermute | solution.py:361
  6.4 17.9 %collective-permute-start.3 = (f32[256,128]{1,0:T(8,128)S(1)}, f32[256,128]{1,0:T(8,128)S(1)}, u32[]{:S(2)}, u32[]{:S(2)}) collective-permute-start(f32[256,128]{1,0:T(8,128)S(1)} %get-tuple-element.32), channel_id=1, source_target_pairs={{0,4},{2,6},{4,0},{6,2},{8,12},{10,14},{12,8},{14,10},{1,5},{3,7},... | collective-permute-start | bytes 393224 | tf_op jit(solution)/shard_map/ppermute | solution.py:361
  7.7 17.1 %collective-permute-start.4 = (f32[256,128]{1,0:T(8,128)S(1)}, f32[256,128]{1,0:T(8,128)S(1)}, u32[]{:S(2)}, u32[]{:S(2)}) collective-permute-start(f32[256,128]{1,0:T(8,128)S(1)} %get-tuple-element.34), channel_id=1, source_target_pairs={{0,14},{2,12},{4,10},{6,8},{8,6},{10,4},{12,2},{14,0},{1,15},{3,13... | collective-permute-start | bytes 393224 | tf_op jit(solution)/shard_map/ppermute | solution.py:361
  13.7 11.0 %collective-permute-start.5 = (f32[256,128]{1,0:T(8,128)S(1)}, f32[256,128]{1,0:T(8,128)S(1)}, u32[]{:S(2)}, u32[]{:S(2)}) collective-permute-start(f32[256,128]{1,0:T(8,128)S(1)} %get-tuple-element.35), channel_id=1, source_target_pairs={{0,12},{2,14},{4,8},{6,10},{8,4},{10,6},{12,0},{14,2},{1,13},{3,15... | collective-permute-start | bytes 393224 | tf_op jit(solution)/shard_map/ppermute | solution.py:361
  17.4 7.4 %collective-permute-start.6 = (f32[256,128]{1,0:T(8,128)S(1)}, f32[256,128]{1,0:T(8,128)S(1)}, u32[]{:S(2)}, u32[]{:S(2)}) collective-permute-start(f32[256,128]{1,0:T(8,128)S(1)} %get-tuple-element.36), channel_id=1, source_target_pairs={{0,2},{2,0},{4,6},{6,4},{8,10},{10,8},{12,14},{14,12},{1,3},{3,1},... | collective-permute-start | bytes 393224 | tf_op jit(solution)/shard_map/ppermute | solution.py:361
  17.6 0.7 %copy-start.1 = (s32[18]{0:T(128)S(1)}, s32[18]{0:T(128)}, u32[]{:S(2)}) copy-start(s32[18]{0:T(128)} %bits_ref.1) | copy-start | bytes 220
  27.3 8.0 %collective-permute-start.7 = (f32[2,4,2,16,128]{4,3,2,1,0:T(8,128)S(1)}, f32[2,4,2,16,128]{4,3,2,1,0:T(8,128)S(1)}, u32[]{:S(2)}, u32[]{:S(2)}) collective-permute-start(f32[2,4,2,16,128]{4,3,2,1,0:T(8,128)S(1)} %get-tuple-element.41), channel_id=1, source_target_pairs={{0,10},{2,8},{4,14},{6,12},{8,2},{10,0},{12,6},{14,4},{1,11},{3,9}... | collective-permute-start | bytes 393224 | tf_op jit(solution)/shard_map/ppermute | solution.py:361
  29.6 12.1 %collective-permute-start.8 = (f32[2,4,2,16,128]{4,3,2,1,0:T(8,128)S(1)}, f32[2,4,2,16,128]{4,3,2,1,0:T(8,128)S(1)}, u32[]{:S(2)}, u32[]{:S(2)}) collective-permute-start(f32[2,4,2,16,128]{4,3,2,1,0:T(8,128)S(1)} %get-tuple-element.42), channel_id=1, source_target_pairs={{0,8},{2,10},{4,12},{6,14},{8,0},{10,2},{12,4},{14,6},{1,9},{3,11}... | collective-permute-start | bytes 393224 | tf_op jit(solution)/shard_map/ppermute | solution.py:361
  30.9 12.6 %collective-permute-start.9 = (f32[2,4,2,16,128]{4,3,2,1,0:T(8,128)S(1)}, f32[2,4,2,16,128]{4,3,2,1,0:T(8,128)S(1)}, u32[]{:S(2)}, u32[]{:S(2)}) collective-permute-start(f32[2,4,2,16,128]{4,3,2,1,0:T(8,128)S(1)} %get-tuple-element.43), channel_id=1, source_target_pairs={{0,6},{2,4},{4,2},{6,0},{8,14},{10,12},{12,10},{14,8},{1,7},{3,5},... | collective-permute-start | bytes 393224 | tf_op jit(solution)/shard_map/ppermute | solution.py:361
  34.0 9.5 %collective-permute-start.10 = (f32[2,4,2,16,128]{4,3,2,1,0:T(8,128)S(1)}, f32[2,4,2,16,128]{4,3,2,1,0:T(8,128)S(1)}, u32[]{:S(2)}, u32[]{:S(2)}) collective-permute-start(f32[2,4,2,16,128]{4,3,2,1,0:T(8,128)S(1)} %get-tuple-element.44), channel_id=1, source_target_pairs={{0,4},{2,6},{4,0},{6,2},{8,12},{10,14},{12,8},{14,10},{1,5},{3,7},... | collective-permute-start | bytes 393224 | tf_op jit(solution)/shard_map/ppermute | solution.py:361
  34.0 14.1 %collective-permute-start.11 = (f32[2,4,2,16,128]{4,3,2,1,0:T(8,128)S(1)}, f32[2,4,2,16,128]{4,3,2,1,0:T(8,128)S(1)}, u32[]{:S(2)}, u32[]{:S(2)}) collective-permute-start(f32[2,4,2,16,128]{4,3,2,1,0:T(8,128)S(1)} %get-tuple-element.45), channel_id=1, source_target_pairs={{0,14},{2,12},{4,10},{6,8},{8,6},{10,4},{12,2},{14,0},{1,15},{3,13... | collective-permute-start | bytes 393224 | tf_op jit(solution)/shard_map/ppermute | solution.py:361
  35.2 14.7 %collective-permute-start.12 = (f32[2,4,2,16,128]{4,3,2,1,0:T(8,128)S(1)}, f32[2,4,2,16,128]{4,3,2,1,0:T(8,128)S(1)}, u32[]{:S(2)}, u32[]{:S(2)}) collective-permute-start(f32[2,4,2,16,128]{4,3,2,1,0:T(8,128)S(1)} %get-tuple-element.46), channel_id=1, source_target_pairs={{0,12},{2,14},{4,8},{6,10},{8,4},{10,6},{12,0},{14,2},{1,13},{3,15... | collective-permute-start | bytes 393224 | tf_op jit(solution)/shard_map/ppermute | solution.py:361
  41.8 8.2 %collective-permute-start.13 = (f32[2,4,2,16,128]{4,3,2,1,0:T(8,128)S(1)}, f32[2,4,2,16,128]{4,3,2,1,0:T(8,128)S(1)}, u32[]{:S(2)}, u32[]{:S(2)}) collective-permute-start(f32[2,4,2,16,128]{4,3,2,1,0:T(8,128)S(1)} %get-tuple-element.47), channel_id=1, source_target_pairs={{0,2},{2,0},{4,6},{6,4},{8,10},{10,8},{12,14},{14,12},{1,3},{3,1},... | collective-permute-start | bytes 393224 | tf_op jit(solution)/shard_map/ppermute | solution.py:361
  51.0 8.0 %copy-start.2 = (bf16[512,1536]{1,0:T(8,128)(2,1)S(1)}, bf16[512,1536]{1,0:T(8,128)(2,1)}, u32[]{:S(2)}) copy-start(bf16[512,1536]{1,0:T(8,128)(2,1)} %get-tuple-element.52.refs_2_) | copy-start | bytes 4718596
  51.0 8.0 %collective-permute-start.14 = (f32[2,512,128]{2,1,0:T(8,128)S(1)}, f32[2,512,128]{2,1,0:T(8,128)S(1)}, u32[]{:S(2)}, u32[]{:S(2)}) collective-permute-start(f32[2,512,128]{2,1,0:T(8,128)S(1)} %second_section_sent.1), channel_id=1, source_target_pairs={{0,1},{1,0},{2,3},{3,2},{4,5},{5,4},{6,7},{7,6},{8,9},{9,8},{10,11... | collective-permute-start | bytes 1572872 | tf_op jit(solution)/shard_map/ppermute | solution.py:426

commit v16 on v15

--- a/solution.py
+++ b/solution.py
@@ -86,7 +86,7 @@
     if number == 0:
         size = dim // count
         spot, source = within // size, jnp.zeros_like(column)
-        for index, partner in enumerate(partners_of(count)):
+        for index, partner in enumerate(partners_of(count, 1)):
             source = jnp.where(spot == index, partner, source)
         natural = source * size + lax.rem(within, size)
     else:
@@ -143,10 +143,12 @@
     low_ref[...] = jnp.concatenate([high, rest, high], axis=0)
 
 
-def distances_of(count):
+def distances_of(count, exchange):
     half = count // 2
     middle = half + half // 2
     far = [*range(middle - 1, half - 1, -1), *range(count - 1, middle - 1, -1)]
+    if exchange == 2:
+        far.sort(reverse=True)
     near = list(range(half - 1, 0, -1))
     order = [0]
     while far or near:
@@ -155,13 +157,13 @@
     return order
 
 
-def partners_of(count):
+def partners_of(count, exchange):
     me = lax.axis_index("qa")
-    return [jnp.bitwise_xor(me, distance) for distance in distances_of(count)]
+    return [jnp.bitwise_xor(me, distance) for distance in distances_of(count, exchange)]
 
 
 def split_kernel(x_ref, *outs):
-    for dest, out_ref in zip(partners_of(len(outs)), outs):
+    for dest, out_ref in zip(partners_of(len(outs), 1), outs):
         out_ref[...] = x_ref[dest]
 
 
@@ -256,7 +258,7 @@
     run_top_stage(stages[0], weights[0], lane_bits, whole, halves[:2])
     done = run_halves(stages[1:], weights[1:], lane_bits, halves[:2], halves[2:])
     tops, mids, _, inner, _ = outs[0].shape
-    dests = partners_of(count)
+    dests = partners_of(count, 2)
     for top in range(tops):
         for dest, out_ref in zip(dests, outs):
             for mid in range(mids):
@@ -270,7 +272,7 @@
     out_ref, one, two = refs
     core = lax.axis_index("qb")
     top = core if stays else 1 - core
-    for source, block_ref in zip(partners_of(count), blocks):
+    for source, block_ref in zip(partners_of(count, 2), blocks):
         _, mids, _, inner, _ = block_ref.shape
         for mid in range(mids):
             start = pl.multiple_of((mid * count + source) * inner, inner)
@@ -353,15 +355,15 @@
     )
 
     blocks = list(blocks)
-    blocks[1] = lax.dynamic_index_in_dim(state, partners_of(qa)[1], 0, keepdims=False)
-
-    def exchange(blocks):
+    blocks[1] = lax.dynamic_index_in_dim(state, partners_of(qa, 1)[1], 0, keepdims=False)
+
+    def exchange(blocks, which):
         came = [blocks[0]]
-        for distance, piece in zip(distances_of(qa)[1:], blocks[1:]):
+        for distance, piece in zip(distances_of(qa, which)[1:], blocks[1:]):
             came.append(lax.ppermute(piece, "qa", [(i, i ^ distance) for i in range(qa)]))
         return came
 
-    blocks = exchange(blocks)
+    blocks = exchange(blocks, 1)
     low_w, *weights = call(
         functools.partial(prepare_kernel, low, sections, qa),
         "prepare_gates",
@@ -407,7 +409,7 @@
         *weights[0],
         aliases={0: qa},
     )
-    blocks = exchange(blocks)
+    blocks = exchange(blocks, 2)
     halves = []
     for stays in (False, True):
         halves.append(

time: 62.2 us -> 62.6 us (level)
  the two profiles are of different devices: /device:TPU:25 before, /device:TPU:0 now
where the time goes in v16:
time: 62.6 us; the launch traced here: 62.4 us
  starting transfers between devices  33.5 us (54%)
  Pallas kernels  14.7 us (23%)
  waiting for transfers between devices  11.3 us (18%)
  local copies, waits for them, and re-layouts  2.8 us (4%)
    ppermute x14, starting transfers between devices, exchange(): lax.ppermute(piece, 'qa', [(i, i ^ distance) for i in range(qa)])  33.4 us
    pallas_call x7, Pallas kernels, call(): pl.pallas_call(kernel, out_shape=out_shapes, in_specs=in_specs, out_specs...  14.7 us
    ppermute x14, waiting for transfers between devices, exchange(): lax.ppermute(piece, 'qa', [(i, i ^ distance) for i in range(qa)])  10.4 us
    unnamed x6, local copies, waits for them, and re-layouts  1.88 us
  transfers between devices with their start and end apart: 15, of which 5 were waited for; matrix products, arithmetic and copies ran while one was open for 0% of the time, Pallas kernels for 13%

profile of v16, /device:TPU:0, one launch (start us, length us, event | category | flops | bytes accessed | tf_op | source)
XLA Modules:
  0.0 62.4 jit_solution(10923982391942177065)
XLA Ops:
  0.0 0.9 %dynamic-slice_bitcast_fusion = f32[256,128]{1,0:T(8,128)S(1)} fusion(f32[8,256,128]{2,1,0:T(8,128)} %bitcast.12, s32[]{:T(128)S(6)} %select_n.4), kind=kLoop, calls=%fused_computation | loop fusion | bytes 262148 | tf_op jit(solution)/shard_map/jit(dynamic_index_in_dim)/squeeze | solution.py:358
  0.9 5.1 %collective-permute-start = (f32[256,128]{1,0:T(8,128)S(1)}, f32[256,128]{1,0:T(8,128)S(1)}, u32[]{:S(2)}, u32[]{:S(2)}) collective-permute-start(f32[256,128]{1,0:T(8,128)S(1)} %dynamic-slice_bitcast_fusion), channel_id=1, source_target_pairs={{0,10},{2,8},{4,14},{6,12},{8,2},{10,0},{12,6},{14,4},{1,11},{3,9}... | collective-permute-start | bytes 393224 | tf_op jit(solution)/shard_map/ppermute | solution.py:363
  6.0 1.2 %copy-done = f32[2,131072]{1,0:T(2,128)S(1)} copy-done((f32[2,131072]{1,0:T(2,128)S(1)}, f32[2,131072]{1,0:T(2,128)}, u32[]{:S(2)}) %copy-start) | copy-done | bytes 1048600
  7.2 0.7 %split_state.1 = (f32[256,128]{1,0:T(8,128)S(1)}, f32[256,128]{1,0:T(8,128)}, f32[256,128]{1,0:T(8,128)S(1)}, f32[256,128]{1,0:T(8,128)S(1)}, f32[256,128]{1,0:T...) custom-call(f32[8,256,128]{2,1,0:T(8,128)S(1)} %bitcast.13), custom_call_target="tpu_custom_call" | custom-call | bytes 4194304 | tf_op jit(solution)/shard_map/split_state/pallas_call | solution.py:314
  7.9 0.3 collective-permute-start.1
  8.3 1.5 %collective-permute-start.2 = (f32[256,128]{1,0:T(8,128)S(1)}, f32[256,128]{1,0:T(8,128)S(1)}, u32[]{:S(2)}, u32[]{:S(2)}) collective-permute-start(f32[256,128]{1,0:T(8,128)S(1)} %get-tuple-element.31), channel_id=1, source_target_pairs={{0,6},{2,4},{4,2},{6,0},{8,14},{10,12},{12,10},{14,8},{1,7},{3,5},... | collective-permute-start | bytes 393224 | tf_op jit(solution)/shard_map/ppermute | solution.py:363
  9.8 0.2 collective-permute-start.3
  10.0 4.8 %collective-permute-start.4 = (f32[256,128]{1,0:T(8,128)S(1)}, f32[256,128]{1,0:T(8,128)S(1)}, u32[]{:S(2)}, u32[]{:S(2)}) collective-permute-start(f32[256,128]{1,0:T(8,128)S(1)} %get-tuple-element.34), channel_id=1, source_target_pairs={{0,14},{2,12},{4,10},{6,8},{8,6},{10,4},{12,2},{14,0},{1,15},{3,13... | collective-permute-start | bytes 393224 | tf_op jit(solution)/shard_map/ppermute | solution.py:363
  14.8 0.8 %collective-permute-done.refs_1_ = f32[256,128]{1,0:T(8,128)S(1)} collective-permute-done((f32[256,128]{1,0:T(8,128)S(1)}, f32[256,128]{1,0:T(8,128)S(1)}, u32[]{:S(2)}, u32[]{:S(2)}) %collective-permute-start) | collective-permute-done | bytes 131104 | tf_op jit(solution)/shard_map/ppermute | solution.py:363
  15.6 3.1 %collective-permute-start.5 = (f32[256,128]{1,0:T(8,128)S(1)}, f32[256,128]{1,0:T(8,128)S(1)}, u32[]{:S(2)}, u32[]{:S(2)}) collective-permute-start(f32[256,128]{1,0:T(8,128)S(1)} %get-tuple-element.35), channel_id=1, source_target_pairs={{0,12},{2,14},{4,8},{6,10},{8,4},{10,6},{12,0},{14,2},{1,13},{3,15... | collective-permute-start | bytes 393224 | tf_op jit(solution)/shard_map/ppermute | solution.py:363
  18.8 0.4 collective-permute-done.1.refs_2_
  19.2 1.1 %collective-permute-start.6 = (f32[256,128]{1,0:T(8,128)S(1)}, f32[256,128]{1,0:T(8,128)S(1)}, u32[]{:S(2)}, u32[]{:S(2)}) collective-permute-start(f32[256,128]{1,0:T(8,128)S(1)} %get-tuple-element.36), channel_id=1, source_target_pairs={{0,2},{2,0},{4,6},{6,4},{8,10},{10,8},{12,14},{14,12},{1,3},{3,1},... | collective-permute-start | bytes 393224 | tf_op jit(solution)/shard_map/ppermute | solution.py:363
  20.3 0.7 %copy-done.1 = s32[18]{0:T(128)S(1)} copy-done((s32[18]{0:T(128)S(1)}, s32[18]{0:T(128)}, u32[]{:S(2)}) %copy-start.1) | copy-done | bytes 96
  20.9 6.0 %prepare_gates.1 = (bf16[768,256]{1,0:T(8,128)(2,1)S(1)}, bf16[256,768]{1,0:T(8,128)(2,1)S(1)}, bf16[256,768]{1,0:T(8,128)(2,1)S(1)}, bf16[512,1536]{1,0:T(8,128...) custom-call(s32[18]{0:T(128)S(1)} %copy-done.1, ...), custom_call_target="tpu_custom_call" | custom-call | flops 3221225472 | bytes 4194304 | tf_op jit(solution)/shard_map/prepare_gates/pallas_call | solution.py:314
  27.0 0.0 collective-permute-done.2.refs_3_
  27.0 0.0 collective-permute-done.3.refs_4_
  27.0 0.4 low_gate_early.1.refs_0_
  27.4 0.0 collective-permute-done.5.refs_2_
  27.5 2.5 %first_section.1 = (f32[2,4,2,16,128]{4,3,2,1,0:T(8,128)S(1)}, f32[2,4,2,16,128]{4,3,2,1,0:T(8,128)S(1)}, f32[2,4,2,16,128]{4,3,2,1,0:T(8,128)S(1)}, f32[2,4,2,1...) custom-call(f32[2,1024,128]{2,1,0:T(8,128)S(1)} %low_gate_early.1.re, ...), custom_call_target="tpu_custom_call", output_to_operand_aliasing={{8}: (0, {})} | custom-call | flops 2013265920 | bytes 4194304 | tf_op jit(solution)/shard_map/first_section/pallas_call | solution.py:314
  30.0 4.5 %collective-permute-start.7 = (f32[2,4,2,16,128]{4,3,2,1,0:T(8,128)S(1)}, f32[2,4,2,16,128]{4,3,2,1,0:T(8,128)S(1)}, u32[]{:S(2)}, u32[]{:S(2)}) collective-permute-start(f32[2,4,2,16,128]{4,3,2,1,0:T(8,128)S(1)} %get-tuple-element.41), channel_id=1, source_target_pairs={{0,14},{2,12},{4,10},{6,8},{8,6},{10,4},{12,2},{14,0},{1,15},{3,13... | collective-permute-start | bytes 393224 | tf_op jit(solution)/shard_map/ppermute | solution.py:363
  34.4 1.4 %collective-permute-start.9 = (f32[2,4,2,16,128]{4,3,2,1,0:T(8,128)S(1)}, f32[2,4,2,16,128]{4,3,2,1,0:T(8,128)S(1)}, u32[]{:S(2)}, u32[]{:S(2)}) collective-permute-start(f32[2,4,2,16,128]{4,3,2,1,0:T(8,128)S(1)} %get-tuple-element.43), channel_id=1, source_target_pairs={{0,6},{2,4},{4,2},{6,0},{8,14},{10,12},{12,10},{14,8},{1,7},{3,5},... | collective-permute-start | bytes 393224 | tf_op jit(solution)/shard_map/ppermute | solution.py:363
  35.9 0.9 %collective-permute-start.10 = (f32[2,4,2,16,128]{4,3,2,1,0:T(8,128)S(1)}, f32[2,4,2,16,128]{4,3,2,1,0:T(8,128)S(1)}, u32[]{:S(2)}, u32[]{:S(2)}) collective-permute-start(f32[2,4,2,16,128]{4,3,2,1,0:T(8,128)S(1)} %get-tuple-element.44), channel_id=1, source_target_pairs={{0,4},{2,6},{4,0},{6,2},{8,12},{10,14},{12,8},{14,10},{1,5},{3,7},... | collective-permute-start | bytes 393224 | tf_op jit(solution)/shard_map/ppermute | solution.py:363
  36.8 2.9 %collective-permute-start.11 = (f32[2,4,2,16,128]{4,3,2,1,0:T(8,128)S(1)}, f32[2,4,2,16,128]{4,3,2,1,0:T(8,128)S(1)}, u32[]{:S(2)}, u32[]{:S(2)}) collective-permute-start(f32[2,4,2,16,128]{4,3,2,1,0:T(8,128)S(1)} %get-tuple-element.45), channel_id=1, source_target_pairs={{0,10},{2,8},{4,14},{6,12},{8,2},{10,0},{12,6},{14,4},{1,11},{3,9}... | collective-permute-start | bytes 393224 | tf_op jit(solution)/shard_map/ppermute | solution.py:363
  39.7 5.6 %collective-permute-start.12 = (f32[2,4,2,16,128]{4,3,2,1,0:T(8,128)S(1)}, f32[2,4,2,16,128]{4,3,2,1,0:T(8,128)S(1)}, u32[]{:S(2)}, u32[]{:S(2)}) collective-permute-start(f32[2,4,2,16,128]{4,3,2,1,0:T(8,128)S(1)} %get-tuple-element.46), channel_id=1, source_target_pairs={{0,8},{2,10},{4,12},{6,14},{8,0},{10,2},{12,4},{14,6},{1,9},{3,11}... | collective-permute-start | bytes 393224 | tf_op jit(solution)/shard_map/ppermute | solution.py:363
  45.3 1.9 %collective-permute-start.13 = (f32[2,4,2,16,128]{4,3,2,1,0:T(8,128)S(1)}, f32[2,4,2,16,128]{4,3,2,1,0:T(8,128)S(1)}, u32[]{:S(2)}, u32[]{:S(2)}) collective-permute-start(f32[2,4,2,16,128]{4,3,2,1,0:T(8,128)S(1)} %get-tuple-element.47), channel_id=1, source_target_pairs={{0,2},{2,0},{4,6},{6,4},{8,10},{10,8},{12,14},{14,12},{1,3},{3,1},... | collective-permute-start | bytes 393224 | tf_op jit(solution)/shard_map/ppermute | solution.py:363
  47.2 7.3 %collective-permute-done.11.refs_5_ = f32[2,4,2,16,128]{4,3,2,1,0:T(8,128)S(1)} collective-permute-done((f32[2,4,2,16,128]{4,3,2,1,0:T(8,128)S(1)}, f32[2,4,2,16,128]{4,3,2,1,0:T(8,128)S(1)}, u32[]{:S(2)}, u32[]{:S(2)}) %collective-permute-start.11) | collective-permute-done | bytes 131104 | tf_op jit(solution)/shard_map/ppermute | solution.py:363
  54.5 1.8 %collective-permute-done.12.refs_6_ = f32[2,4,2,16,128]{4,3,2,1,0:T(8,128)S(1)} collective-permute-done((f32[2,4,2,16,128]{4,3,2,1,0:T(8,128)S(1)}, f32[2,4,2,16,128]{4,3,2,1,0:T(8,128)S(1)}, u32[]{:S(2)}, u32[]{:S(2)}) %collective-permute-start.12) | collective-permute-done | bytes 131104 | tf_op jit(solution)/shard_map/ppermute | solution.py:363
  56.3 1.0 %second_section_sent.1 = f32[2,512,128]{2,1,0:T(8,128)S(1)} custom-call(f32[2,4,2,16,128]{4,3,2,1,0:T(8,128)S(1)} %get-tuple-element.40.refs_0_, f32[2,4,2,16,128]{4,3,2,1,0:T(8,128)S(1)} %collective-permute-done.7.refs_1_, f32[2,4,2,16,128]{4,3,2,1,0:T(8,128)S(1)} %collective-permute-done.8.refs_2_, ...), custom_call_target="tpu_custom_call" | custom-call | flops 603979776 | bytes 4194304 | tf_op jit(solution)/shard_map/second_section_sent/pallas_call | solution.py:314
  57.3 0.1 collective-permute-start.14
  57.4 1.0 %second_section_kept.1.kept_ref = f32[2,512,128]{2,1,0:T(8,128)S(1)} custom-call(f32[2,4,2,16,128]{4,3,2,1,0:T(8,128)S(1)} %get-tuple-element.40.refs_0_, f32[2,4,2,16,128]{4,3,2,1,0:T(8,128)S(1)} %collective-permute-done.7.refs_1_, f32[2,4,2,16,128]{4,3,2,1,0:T(8,128)S(1)} %collective-permute-done.8.refs_2_, ...), custom_call_target="tpu_custom_call" | custom-call | flops 603979776 | bytes 4194304 | tf_op jit(solution)/shard_map/second_section_kept/pallas_call | solution.py:314
  58.4 0.9 %collective-permute-done.14.came_ref = f32[2,512,128]{2,1,0:T(8,128)S(1)} collective-permute-done((f32[2,512,128]{2,1,0:T(8,128)S(1)}, f32[2,512,128]{2,1,0:T(8,128)S(1)}, u32[]{:S(2)}, u32[]{:S(2)}) %collective-permute-start.14) | collective-permute-done | bytes 524320 | tf_op jit(solution)/shard_map/ppermute | solution.py:428
  59.3 3.1 %third_section.1 = f32[2048,128]{1,0:T(8,128)} custom-call(f32[2,512,128]{2,1,0:T(8,128)S(1)} %second_section_kept.1.kept_ref, f32[2,512,128]{2,1,0:T(8,128)S(1)} %collective-permute-done.14.came_ref, bf16[256,768]{1,0:T(8,128)(2,1)S(1)} %get-tuple-element.50.refs_0_, bf16[256,768]{1,0:T(8,128)(2,1)S(1)} %get-tuple-element.51.refs_1_, ...), custom_call_target="tpu_custom_call" | custom-call | flops 1610612736 | bytes 4194304 | tf_op jit(solution)/shard_map/third_section/pallas_call | solution.py:314
  (12 shorter events, 0.0 us)
Async XLA Ops:
  0.9 14.7 %collective-permute-start = (f32[256,128]{1,0:T(8,128)S(1)}, f32[256,128]{1,0:T(8,128)S(1)}, u32[]{:S(2)}, u32[]{:S(2)}) collective-permute-start(f32[256,128]{1,0:T(8,128)S(1)} %dynamic-slice_bitcast_fusion), channel_id=1, source_target_pairs={{0,10},{2,8},{4,14},{6,12},{8,2},{10,0},{12,6},{14,4},{1,11},{3,9}... | collective-permute-start | bytes 393224 | tf_op jit(solution)/shard_map/ppermute | solution.py:363
  6.0 1.2 %copy-start = (f32[2,131072]{1,0:T(2,128)S(1)}, f32[2,131072]{1,0:T(2,128)}, u32[]{:S(2)}) copy-start(f32[2,131072]{1,0:T(2,128)} %param.3) | copy-start | bytes 3145732
  7.9 11.3 %collective-permute-start.1 = (f32[256,128]{1,0:T(8,128)S(1)}, f32[256,128]{1,0:T(8,128)S(1)}, u32[]{:S(2)}, u32[]{:S(2)}) collective-permute-start(f32[256,128]{1,0:T(8,128)S(1)} %get-tuple-element.30), channel_id=1, source_target_pairs={{0,8},{2,10},{4,12},{6,14},{8,0},{10,2},{12,4},{14,6},{1,9},{3,11}... | collective-permute-start | bytes 393224 | tf_op jit(solution)/shard_map/ppermute | solution.py:363
  8.3 18.7 %collective-permute-start.2 = (f32[256,128]{1,0:T(8,128)S(1)}, f32[256,128]{1,0:T(8,128)S(1)}, u32[]{:S(2)}, u32[]{:S(2)}) collective-permute-start(f32[256,128]{1,0:T(8,128)S(1)} %get-tuple-element.31), channel_id=1, source_target_pairs={{0,6},{2,4},{4,2},{6,0},{8,14},{10,12},{12,10},{14,8},{1,7},{3,5},... | collective-permute-start | bytes 393224 | tf_op jit(solution)/shard_map/ppermute | solution.py:363
  9.8 17.2 %collective-permute-start.3 = (f32[256,128]{1,0:T(8,128)S(1)}, f32[256,128]{1,0:T(8,128)S(1)}, u32[]{:S(2)}, u32[]{:S(2)}) collective-permute-start(f32[256,128]{1,0:T(8,128)S(1)} %get-tuple-element.32), channel_id=1, source_target_pairs={{0,4},{2,6},{4,0},{6,2},{8,12},{10,14},{12,8},{14,10},{1,5},{3,7},... | collective-permute-start | bytes 393224 | tf_op jit(solution)/shard_map/ppermute | solution.py:363
  10.0 17.5 %collective-permute-start.4 = (f32[256,128]{1,0:T(8,128)S(1)}, f32[256,128]{1,0:T(8,128)S(1)}, u32[]{:S(2)}, u32[]{:S(2)}) collective-permute-start(f32[256,128]{1,0:T(8,128)S(1)} %get-tuple-element.34), channel_id=1, source_target_pairs={{0,14},{2,12},{4,10},{6,8},{8,6},{10,4},{12,2},{14,0},{1,15},{3,13... | collective-permute-start | bytes 393224 | tf_op jit(solution)/shard_map/ppermute | solution.py:363
  15.6 11.8 %collective-permute-start.5 = (f32[256,128]{1,0:T(8,128)S(1)}, f32[256,128]{1,0:T(8,128)S(1)}, u32[]{:S(2)}, u32[]{:S(2)}) collective-permute-start(f32[256,128]{1,0:T(8,128)S(1)} %get-tuple-element.35), channel_id=1, source_target_pairs={{0,12},{2,14},{4,8},{6,10},{8,4},{10,6},{12,0},{14,2},{1,13},{3,15... | collective-permute-start | bytes 393224 | tf_op jit(solution)/shard_map/ppermute | solution.py:363
  19.2 8.2 %collective-permute-start.6 = (f32[256,128]{1,0:T(8,128)S(1)}, f32[256,128]{1,0:T(8,128)S(1)}, u32[]{:S(2)}, u32[]{:S(2)}) collective-permute-start(f32[256,128]{1,0:T(8,128)S(1)} %get-tuple-element.36), channel_id=1, source_target_pairs={{0,2},{2,0},{4,6},{6,4},{8,10},{10,8},{12,14},{14,12},{1,3},{3,1},... | collective-permute-start | bytes 393224 | tf_op jit(solution)/shard_map/ppermute | solution.py:363
  20.3 0.7 %copy-start.1 = (s32[18]{0:T(128)S(1)}, s32[18]{0:T(128)}, u32[]{:S(2)}) copy-start(s32[18]{0:T(128)} %bits_ref.1) | copy-start | bytes 220
  30.0 9.8 %collective-permute-start.7 = (f32[2,4,2,16,128]{4,3,2,1,0:T(8,128)S(1)}, f32[2,4,2,16,128]{4,3,2,1,0:T(8,128)S(1)}, u32[]{:S(2)}, u32[]{:S(2)}) collective-permute-start(f32[2,4,2,16,128]{4,3,2,1,0:T(8,128)S(1)} %get-tuple-element.41), channel_id=1, source_target_pairs={{0,14},{2,12},{4,10},{6,8},{8,6},{10,4},{12,2},{14,0},{1,15},{3,13... | collective-permute-start | bytes 393224 | tf_op jit(solution)/shard_map/ppermute | solution.py:363
  34.4 10.9 %collective-permute-start.8 = (f32[2,4,2,16,128]{4,3,2,1,0:T(8,128)S(1)}, f32[2,4,2,16,128]{4,3,2,1,0:T(8,128)S(1)}, u32[]{:S(2)}, u32[]{:S(2)}) collective-permute-start(f32[2,4,2,16,128]{4,3,2,1,0:T(8,128)S(1)} %get-tuple-element.42), channel_id=1, source_target_pairs={{0,12},{2,14},{4,8},{6,10},{8,4},{10,6},{12,0},{14,2},{1,13},{3,15... | collective-permute-start | bytes 393224 | tf_op jit(solution)/shard_map/ppermute | solution.py:363
  34.4 12.8 %collective-permute-start.9 = (f32[2,4,2,16,128]{4,3,2,1,0:T(8,128)S(1)}, f32[2,4,2,16,128]{4,3,2,1,0:T(8,128)S(1)}, u32[]{:S(2)}, u32[]{:S(2)}) collective-permute-start(f32[2,4,2,16,128]{4,3,2,1,0:T(8,128)S(1)} %get-tuple-element.43), channel_id=1, source_target_pairs={{0,6},{2,4},{4,2},{6,0},{8,14},{10,12},{12,10},{14,8},{1,7},{3,5},... | collective-permute-start | bytes 393224 | tf_op jit(solution)/shard_map/ppermute | solution.py:363
  35.9 11.4 %collective-permute-start.10 = (f32[2,4,2,16,128]{4,3,2,1,0:T(8,128)S(1)}, f32[2,4,2,16,128]{4,3,2,1,0:T(8,128)S(1)}, u32[]{:S(2)}, u32[]{:S(2)}) collective-permute-start(f32[2,4,2,16,128]{4,3,2,1,0:T(8,128)S(1)} %get-tuple-element.44), channel_id=1, source_target_pairs={{0,4},{2,6},{4,0},{6,2},{8,12},{10,14},{12,8},{14,10},{1,5},{3,7},... | collective-permute-start | bytes 393224 | tf_op jit(solution)/shard_map/ppermute | solution.py:363
  36.8 17.8 %collective-permute-start.11 = (f32[2,4,2,16,128]{4,3,2,1,0:T(8,128)S(1)}, f32[2,4,2,16,128]{4,3,2,1,0:T(8,128)S(1)}, u32[]{:S(2)}, u32[]{:S(2)}) collective-permute-start(f32[2,4,2,16,128]{4,3,2,1,0:T(8,128)S(1)} %get-tuple-element.45), channel_id=1, source_target_pairs={{0,10},{2,8},{4,14},{6,12},{8,2},{10,0},{12,6},{14,4},{1,11},{3,9}... | collective-permute-start | bytes 393224 | tf_op jit(solution)/shard_map/ppermute | solution.py:363
  39.7 16.6 %collective-permute-start.12 = (f32[2,4,2,16,128]{4,3,2,1,0:T(8,128)S(1)}, f32[2,4,2,16,128]{4,3,2,1,0:T(8,128)S(1)}, u32[]{:S(2)}, u32[]{:S(2)}) collective-permute-start(f32[2,4,2,16,128]{4,3,2,1,0:T(8,128)S(1)} %get-tuple-element.46), channel_id=1, source_target_pairs={{0,8},{2,10},{4,12},{6,14},{8,0},{10,2},{12,4},{14,6},{1,9},{3,11}... | collective-permute-start | bytes 393224 | tf_op jit(solution)/shard_map/ppermute | solution.py:363
  45.3 11.0 %collective-permute-start.13 = (f32[2,4,2,16,128]{4,3,2,1,0:T(8,128)S(1)}, f32[2,4,2,16,128]{4,3,2,1,0:T(8,128)S(1)}, u32[]{:S(2)}, u32[]{:S(2)}) collective-permute-start(f32[2,4,2,16,128]{4,3,2,1,0:T(8,128)S(1)} %get-tuple-element.47), channel_id=1, source_target_pairs={{0,2},{2,0},{4,6},{6,4},{8,10},{10,8},{12,14},{14,12},{1,3},{3,1},... | collective-permute-start | bytes 393224 | tf_op jit(solution)/shard_map/ppermute | solution.py:363
  57.3 2.0 %copy-start.2 = (bf16[512,1536]{1,0:T(8,128)(2,1)S(1)}, bf16[512,1536]{1,0:T(8,128)(2,1)}, u32[]{:S(2)}) copy-start(bf16[512,1536]{1,0:T(8,128)(2,1)} %get-tuple-element.52.refs_2_) | copy-start | bytes 4718596
  57.3 2.0 %collective-permute-start.14 = (f32[2,512,128]{2,1,0:T(8,128)S(1)}, f32[2,512,128]{2,1,0:T(8,128)S(1)}, u32[]{:S(2)}, u32[]{:S(2)}) collective-permute-start(f32[2,512,128]{2,1,0:T(8,128)S(1)} %second_section_sent.1), channel_id=1, source_target_pairs={{0,1},{1,0},{2,3},{3,2},{4,5},{5,4},{6,7},{7,6},{8,9},{9,8},{10,11... | collective-permute-start | bytes 1572872 | tf_op jit(solution)/shard_map/ppermute | solution.py:428

commit v17 on v14

--- a/solution.py
+++ b/solution.py
@@ -77,22 +77,51 @@
     )
 
 
-def relative(matrix, number, count):
-    order = matrix.shape[1]
-    dim = order // 2
-    column = lax.broadcasted_iota(jnp.int32, (order, order), 1)
-    row = lax.broadcasted_iota(jnp.int32, (order, order), 0)
-    within = lax.rem(column, dim)
-    if number == 0:
-        size = dim // count
-        spot, source = within // size, jnp.zeros_like(column)
-        for index, partner in enumerate(partners_of(count)):
-            source = jnp.where(spot == index, partner, source)
-        natural = source * size + lax.rem(within, size)
-    else:
-        natural = jnp.bitwise_xor(within, lax.axis_index("qb") * (dim // 2))
-    picked = jnp.where(row == natural + (column - within), 1.0, 0.0).astype(BF16)
+def iotas(order):
+    return [lax.broadcasted_iota(jnp.int32, (order, order), axis) for axis in (0, 1)]
+
+
+def pick_columns(matrix, natural):
+    row, column = iotas(matrix.shape[1])
+    within = lax.rem(column, matrix.shape[1] // 2)
+    picked = jnp.where(row == natural(within) + (column - within), 1.0, 0.0).astype(BF16)
     return bf_dot(matrix, picked).astype(BF16)
+
+
+def pick_rows(matrix, natural):
+    row, column = iotas(matrix.shape[0])
+    within = lax.rem(row, matrix.shape[0] // 2)
+    picked = jnp.where(column == natural(within) + (row - within), 1.0, 0.0).astype(BF16)
+    return bf_dot(picked, matrix).astype(BF16)
+
+
+def partner_at(spot, count):
+    found = jnp.zeros_like(spot)
+    for index, partner in enumerate(partners_of(count)):
+        found = jnp.where(spot == index, partner, found)
+    return found
+
+
+def by_source(dim, count):
+    size = dim // count
+    return lambda x: partner_at(x // size, count) * size + lax.rem(x, size)
+
+
+def by_core(dim):
+    return lambda x: jnp.bitwise_xor(x, lax.axis_index("qb") * (dim // 2))
+
+
+def straight(count):
+    return count == 8
+
+
+def into_blocks(x):
+    high, low = (x >> 2) & 3, x & 3
+    return high * 64 + partner_at(x >> 5, 8) * 8 + low * 2 + ((x >> 4) & 1)
+
+
+def from_blocks(x):
+    return ((x >> 2) & 3) * 32 + partner_at(x >> 4, 8) * 4 + (x & 3)
 
 
 def prepare_kernel(low, sections, count, bits_ref, gates_ref, low_ref, *refs):
@@ -135,8 +164,12 @@
         weights, targets = targets[: len(section)], targets[len(section) :]
         for target, (base, _, parts) in zip(weights, section):
             high, rest = split(block(*(joined(wides.at[number], base, parts) if len(parts) > 1 else product(parts[0][1]))))
-            if number != 1 and target is weights[0]:
-                high, rest = relative(high, number, count), relative(rest, number, count)
+            if target is weights[0]:
+                order = (by_source(dim, count), from_blocks if straight(count) else None, by_core(dim))[number]
+                if order is not None:
+                    high, rest = pick_columns(high, order), pick_columns(rest, order)
+            elif number == 0 and straight(count) and target is weights[-1]:
+                high, rest = pick_rows(high, into_blocks), pick_rows(rest, into_blocks)
             target[...] = jnp.concatenate([high, rest, high], axis=1)
     real, imag = product(low)
     high, rest = split(block(real.T, -imag.T))
@@ -252,6 +285,16 @@
     outs, (whole, *halves) = refs[:count], refs[count:]
     low_gate(zip(spots, blocks), low_ref, whole)
     run_top_stage(stages[0], weights[0], lane_bits, whole, halves[:2])
+    if straight(count):
+
+        def store(top, part, start, value):
+            for spot, out_ref in enumerate(outs):
+                for bit in range(2):
+                    rows = value[(2 * spot + bit) * 16 : (2 * spot + bit + 1) * 16]
+                    out_ref[top, part, 2 * bit + start] = rows
+
+        run_halves(stages[1:], weights[1:], lane_bits, halves[:2], halves[2:], store)
+        return
     done = run_halves(stages[1:], weights[1:], lane_bits, halves[:2], halves[2:])
     tops, mids, _, inner, _ = outs[0].shape
     dests = partners_of(count)
@@ -268,6 +311,17 @@
     out_ref, one, two = refs
     core = lax.axis_index("qb")
     top = core if stays else 1 - core
+    if straight(count):
+        dim, stride, starts = stage_starts(stages[0], lane_bits, one.shape[1])
+
+        def load(part, start):
+            return jnp.concatenate([block_ref[top, part, start] for block_ref in blocks], axis=0)
+
+        def store(part, start, value):
+            one[part, pl.ds(start, dim, stride=stride), :] = value
+
+        apply_stage(weights[0], starts, load, store)
+        stages, weights, blocks = stages[1:], weights[1:], []
     for source, block_ref in zip(partners_of(count), blocks):
         _, mids, _, inner, _ = block_ref.shape
         for mid in range(mids):
@@ -395,7 +449,7 @@
     *blocks, _ = call(
         functools.partial(first_kernel, sections[0], lane_bits, qa, late),
         "first_section",
-        (shape((qb, qa // qb, 2, inner, lanes), F32),) * qa + (planes,),
+        (shape((qb, 2, 4, 16, lanes) if straight(qa) else (qb, qa // qb, 2, inner, lanes), F32),) * qa + (planes,),
         [vmem] * (2 + len(late) + counts[0]),
         [half] * 4,
         5,

time: 61.5 us -> 61.5 us (level)
  waiting for transfers between devices: 16.1 us -> 15.1 us
  Pallas kernels: 14.7 us -> 15.6 us
    ppermute x14, waiting for transfers between devices: 15.2 us -> 14.2 us  [exchange(): lax.ppermute(piece, 'qa', [(i, i ^ distance) for i in range(qa)])]
    pallas_call x7, Pallas kernels: 14.7 us -> 15.6 us  [call(): pl.pallas_call(kernel, out_shape=out_shapes, in_specs=in_specs, out_specs...]
  transfers between devices with their start and end apart: 15 -> 15, of which waited for: 8 -> 8; matrix products, arithmetic and copies ran while one was open for 0% -> 0% of each run, Pallas kernels for 13% -> 15%
where the time goes in v17:
time: 61.5 us; the launch traced here: 61.3 us
  starting transfers between devices  27.7 us (45%)
  Pallas kernels  15.6 us (25%)
  waiting for transfers between devices  15.1 us (25%)
  local copies, waits for them, and re-layouts  2.8 us (5%)
    ppermute x14, starting transfers between devices, exchange(): lax.ppermute(piece, 'qa', [(i, i ^ distance) for i in range(qa)])  27.6 us
    pallas_call x7, Pallas kernels, call(): pl.pallas_call(kernel, out_shape=out_shapes, in_specs=in_specs, out_specs...  15.6 us
    ppermute x14, waiting for transfers between devices, exchange(): lax.ppermute(piece, 'qa', [(i, i ^ distance) for i in range(qa)])  14.2 us
    unnamed x6, local copies, waits for them, and re-layouts  1.88 us
  transfers between devices with their start and end apart: 15, of which 8 were waited for; matrix products, arithmetic and copies ran while one was open for 0% of the time, Pallas kernels for 15%

profile of v17, /device:TPU:0, one launch (start us, length us, event | category | flops | bytes accessed | tf_op | source)
XLA Modules:
  0.0 61.3 jit_solution(10756535887138244297)
XLA Ops:
  0.0 0.9 %dynamic-slice_bitcast_fusion = f32[256,128]{1,0:T(8,128)S(1)} fusion(f32[8,256,128]{2,1,0:T(8,128)} %bitcast.12, s32[]{:T(128)S(6)} %select_n.4), kind=kLoop, calls=%fused_computation | loop fusion | bytes 262148 | tf_op jit(solution)/shard_map/jit(dynamic_index_in_dim)/squeeze | solution.py:408
  0.9 6.1 %collective-permute-start = (f32[256,128]{1,0:T(8,128)S(1)}, f32[256,128]{1,0:T(8,128)S(1)}, u32[]{:S(2)}, u32[]{:S(2)}) collective-permute-start(f32[256,128]{1,0:T(8,128)S(1)} %dynamic-slice_bitcast_fusion), channel_id=1, source_target_pairs={{0,14},{2,12},{4,10},{6,8},{8,6},{10,4},{12,2},{14,0},{1,15},{3,13... | collective-permute-start | bytes 393224 | tf_op jit(solution)/shard_map/ppermute | solution.py:413
  7.0 1.2 %copy-done = f32[2,131072]{1,0:T(2,128)S(1)} copy-done((f32[2,131072]{1,0:T(2,128)S(1)}, f32[2,131072]{1,0:T(2,128)}, u32[]{:S(2)}) %copy-start) | copy-done | bytes 1048600
  8.2 0.7 %split_state.1 = (f32[256,128]{1,0:T(8,128)S(1)}, f32[256,128]{1,0:T(8,128)}, f32[256,128]{1,0:T(8,128)S(1)}, f32[256,128]{1,0:T(8,128)S(1)}, f32[256,128]{1,0:T...) custom-call(f32[8,256,128]{2,1,0:T(8,128)S(1)} %bitcast.13), custom_call_target="tpu_custom_call" | custom-call | bytes 4194304 | tf_op jit(solution)/shard_map/split_state/pallas_call | solution.py:364
  8.9 0.2 collective-permute-start.1
  9.2 0.0 collective-permute-start.2
  9.2 1.8 %collective-permute-start.3 = (f32[256,128]{1,0:T(8,128)S(1)}, f32[256,128]{1,0:T(8,128)S(1)}, u32[]{:S(2)}, u32[]{:S(2)}) collective-permute-start(f32[256,128]{1,0:T(8,128)S(1)} %get-tuple-element.32), channel_id=1, source_target_pairs={{0,4},{2,6},{4,0},{6,2},{8,12},{10,14},{12,8},{14,10},{1,5},{3,7},... | collective-permute-start | bytes 393224 | tf_op jit(solution)/shard_map/ppermute | solution.py:413
  11.0 3.2 %collective-permute-start.4 = (f32[256,128]{1,0:T(8,128)S(1)}, f32[256,128]{1,0:T(8,128)S(1)}, u32[]{:S(2)}, u32[]{:S(2)}) collective-permute-start(f32[256,128]{1,0:T(8,128)S(1)} %get-tuple-element.34), channel_id=1, source_target_pairs={{0,10},{2,8},{4,14},{6,12},{8,2},{10,0},{12,6},{14,4},{1,11},{3,9}... | collective-permute-start | bytes 393224 | tf_op jit(solution)/shard_map/ppermute | solution.py:413
  14.2 3.3 %collective-permute-start.5 = (f32[256,128]{1,0:T(8,128)S(1)}, f32[256,128]{1,0:T(8,128)S(1)}, u32[]{:S(2)}, u32[]{:S(2)}) collective-permute-start(f32[256,128]{1,0:T(8,128)S(1)} %get-tuple-element.35), channel_id=1, source_target_pairs={{0,8},{2,10},{4,12},{6,14},{8,0},{10,2},{12,4},{14,6},{1,9},{3,11}... | collective-permute-start | bytes 393224 | tf_op jit(solution)/shard_map/ppermute | solution.py:413
  17.6 1.5 %collective-permute-start.6 = (f32[256,128]{1,0:T(8,128)S(1)}, f32[256,128]{1,0:T(8,128)S(1)}, u32[]{:S(2)}, u32[]{:S(2)}) collective-permute-start(f32[256,128]{1,0:T(8,128)S(1)} %get-tuple-element.36), channel_id=1, source_target_pairs={{0,2},{2,0},{4,6},{6,4},{8,10},{10,8},{12,14},{14,12},{1,3},{3,1},... | collective-permute-start | bytes 393224 | tf_op jit(solution)/shard_map/ppermute | solution.py:413
  19.1 0.7 %copy-done.1 = s32[18]{0:T(128)S(1)} copy-done((s32[18]{0:T(128)S(1)}, s32[18]{0:T(128)}, u32[]{:S(2)}) %copy-start.1) | copy-done | bytes 96
  19.8 7.0 %prepare_gates.1 = (bf16[768,256]{1,0:T(8,128)(2,1)S(1)}, bf16[256,768]{1,0:T(8,128)(2,1)S(1)}, bf16[256,768]{1,0:T(8,128)(2,1)S(1)}, bf16[512,1536]{1,0:T(8,128...) custom-call(s32[18]{0:T(128)S(1)} %copy-done.1, ...), custom_call_target="tpu_custom_call" | custom-call | flops 3221225472 | bytes 4194304 | tf_op jit(solution)/shard_map/prepare_gates/pallas_call | solution.py:364
  26.7 0.4 low_gate_early.1.refs_0_
  27.2 0.3 collective-permute-done.4.refs_1_
  27.5 1.8 %collective-permute-done.5.refs_2_ = f32[256,128]{1,0:T(8,128)S(1)} collective-permute-done((f32[256,128]{1,0:T(8,128)S(1)}, f32[256,128]{1,0:T(8,128)S(1)}, u32[]{:S(2)}, u32[]{:S(2)}) %collective-permute-start.5) | collective-permute-done | bytes 131104 | tf_op jit(solution)/shard_map/ppermute | solution.py:413
  29.3 2.5 %first_section.1 = (f32[2,2,4,16,128]{4,3,2,1,0:T(8,128)S(1)}, f32[2,2,4,16,128]{4,3,2,1,0:T(8,128)S(1)}, f32[2,2,4,16,128]{4,3,2,1,0:T(8,128)S(1)}, f32[2,2,4,1...) custom-call(f32[2,1024,128]{2,1,0:T(8,128)S(1)} %low_gate_early.1.re, ...), custom_call_target="tpu_custom_call", output_to_operand_aliasing={{8}: (0, {})} | custom-call | flops 2013265920 | bytes 4194304 | tf_op jit(solution)/shard_map/first_section/pallas_call | solution.py:364
  31.8 2.5 %collective-permute-start.7 = (f32[2,2,4,16,128]{4,3,2,1,0:T(8,128)S(1)}, f32[2,2,4,16,128]{4,3,2,1,0:T(8,128)S(1)}, u32[]{:S(2)}, u32[]{:S(2)}) collective-permute-start(f32[2,2,4,16,128]{4,3,2,1,0:T(8,128)S(1)} %get-tuple-element.41), channel_id=1, source_target_pairs={{0,14},{2,12},{4,10},{6,8},{8,6},{10,4},{12,2},{14,0},{1,15},{3,13... | collective-permute-start | bytes 393224 | tf_op jit(solution)/shard_map/ppermute | solution.py:413
  34.3 1.3 %collective-permute-start.8 = (f32[2,2,4,16,128]{4,3,2,1,0:T(8,128)S(1)}, f32[2,2,4,16,128]{4,3,2,1,0:T(8,128)S(1)}, u32[]{:S(2)}, u32[]{:S(2)}) collective-permute-start(f32[2,2,4,16,128]{4,3,2,1,0:T(8,128)S(1)} %get-tuple-element.42), channel_id=1, source_target_pairs={{0,12},{2,14},{4,8},{6,10},{8,4},{10,6},{12,0},{14,2},{1,13},{3,15... | collective-permute-start | bytes 393224 | tf_op jit(solution)/shard_map/ppermute | solution.py:413
  35.6 3.0 %collective-permute-start.10 = (f32[2,2,4,16,128]{4,3,2,1,0:T(8,128)S(1)}, f32[2,2,4,16,128]{4,3,2,1,0:T(8,128)S(1)}, u32[]{:S(2)}, u32[]{:S(2)}) collective-permute-start(f32[2,2,4,16,128]{4,3,2,1,0:T(8,128)S(1)} %get-tuple-element.44), channel_id=1, source_target_pairs={{0,4},{2,6},{4,0},{6,2},{8,12},{10,14},{12,8},{14,10},{1,5},{3,7},... | collective-permute-start | bytes 393224 | tf_op jit(solution)/shard_map/ppermute | solution.py:413
  38.6 1.0 %collective-permute-start.11 = (f32[2,2,4,16,128]{4,3,2,1,0:T(8,128)S(1)}, f32[2,2,4,16,128]{4,3,2,1,0:T(8,128)S(1)}, u32[]{:S(2)}, u32[]{:S(2)}) collective-permute-start(f32[2,2,4,16,128]{4,3,2,1,0:T(8,128)S(1)} %get-tuple-element.45), channel_id=1, source_target_pairs={{0,10},{2,8},{4,14},{6,12},{8,2},{10,0},{12,6},{14,4},{1,11},{3,9}... | collective-permute-start | bytes 393224 | tf_op jit(solution)/shard_map/ppermute | solution.py:413
  39.6 0.8 %collective-permute-done.7.refs_1_ = f32[2,2,4,16,128]{4,3,2,1,0:T(8,128)S(1)} collective-permute-done((f32[2,2,4,16,128]{4,3,2,1,0:T(8,128)S(1)}, f32[2,2,4,16,128]{4,3,2,1,0:T(8,128)S(1)}, u32[]{:S(2)}, u32[]{:S(2)}) %collective-permute-start.7) | collective-permute-done | bytes 131104 | tf_op jit(solution)/shard_map/ppermute | solution.py:413
  40.4 2.1 %collective-permute-start.12 = (f32[2,2,4,16,128]{4,3,2,1,0:T(8,128)S(1)}, f32[2,2,4,16,128]{4,3,2,1,0:T(8,128)S(1)}, u32[]{:S(2)}, u32[]{:S(2)}) collective-permute-start(f32[2,2,4,16,128]{4,3,2,1,0:T(8,128)S(1)} %get-tuple-element.46), channel_id=1, source_target_pairs={{0,8},{2,10},{4,12},{6,14},{8,0},{10,2},{12,4},{14,6},{1,9},{3,11}... | collective-permute-start | bytes 393224 | tf_op jit(solution)/shard_map/ppermute | solution.py:413
  42.5 1.5 %collective-permute-start.13 = (f32[2,2,4,16,128]{4,3,2,1,0:T(8,128)S(1)}, f32[2,2,4,16,128]{4,3,2,1,0:T(8,128)S(1)}, u32[]{:S(2)}, u32[]{:S(2)}) collective-permute-start(f32[2,2,4,16,128]{4,3,2,1,0:T(8,128)S(1)} %get-tuple-element.47), channel_id=1, source_target_pairs={{0,2},{2,0},{4,6},{6,4},{8,10},{10,8},{12,14},{14,12},{1,3},{3,1},... | collective-permute-start | bytes 393224 | tf_op jit(solution)/shard_map/ppermute | solution.py:413
  44.0 3.2 %collective-permute-done.9.refs_3_ = f32[2,2,4,16,128]{4,3,2,1,0:T(8,128)S(1)} collective-permute-done((f32[2,2,4,16,128]{4,3,2,1,0:T(8,128)S(1)}, f32[2,2,4,16,128]{4,3,2,1,0:T(8,128)S(1)}, u32[]{:S(2)}, u32[]{:S(2)}) %collective-permute-start.9) | collective-permute-done | bytes 131104 | tf_op jit(solution)/shard_map/ppermute | solution.py:413
  47.2 2.9 %collective-permute-done.10.refs_4_ = f32[2,2,4,16,128]{4,3,2,1,0:T(8,128)S(1)} collective-permute-done((f32[2,2,4,16,128]{4,3,2,1,0:T(8,128)S(1)}, f32[2,2,4,16,128]{4,3,2,1,0:T(8,128)S(1)}, u32[]{:S(2)}, u32[]{:S(2)}) %collective-permute-start.10) | collective-permute-done | bytes 131104 | tf_op jit(solution)/shard_map/ppermute | solution.py:413
  50.1 4.7 %collective-permute-done.11.refs_5_ = f32[2,2,4,16,128]{4,3,2,1,0:T(8,128)S(1)} collective-permute-done((f32[2,2,4,16,128]{4,3,2,1,0:T(8,128)S(1)}, f32[2,2,4,16,128]{4,3,2,1,0:T(8,128)S(1)}, u32[]{:S(2)}, u32[]{:S(2)}) %collective-permute-start.11) | collective-permute-done | bytes 131104 | tf_op jit(solution)/shard_map/ppermute | solution.py:413
  54.8 0.5 collective-permute-done.12.refs_6_
  55.3 1.0 %second_section_sent.1 = f32[2,512,128]{2,1,0:T(8,128)S(1)} custom-call(f32[2,2,4,16,128]{4,3,2,1,0:T(8,128)S(1)} %get-tuple-element.40.refs_0_, f32[2,2,4,16,128]{4,3,2,1,0:T(8,128)S(1)} %collective-permute-done.7.refs_1_, f32[2,2,4,16,128]{4,3,2,1,0:T(8,128)S(1)} %collective-permute-done.8.refs_2_, ...), custom_call_target="tpu_custom_call" | custom-call | flops 603979776 | bytes 4194304 | tf_op jit(solution)/shard_map/second_section_sent/pallas_call | solution.py:364
  56.2 0.1 collective-permute-start.14
  56.3 1.0 %second_section_kept.1.kept_ref = f32[2,512,128]{2,1,0:T(8,128)S(1)} custom-call(f32[2,2,4,16,128]{4,3,2,1,0:T(8,128)S(1)} %get-tuple-element.40.refs_0_, f32[2,2,4,16,128]{4,3,2,1,0:T(8,128)S(1)} %collective-permute-done.7.refs_1_, f32[2,2,4,16,128]{4,3,2,1,0:T(8,128)S(1)} %collective-permute-done.8.refs_2_, ...), custom_call_target="tpu_custom_call" | custom-call | flops 603979776 | bytes 4194304 | tf_op jit(solution)/shard_map/second_section_kept/pallas_call | solution.py:364
  57.3 0.9 %collective-permute-done.14.came_ref = f32[2,512,128]{2,1,0:T(8,128)S(1)} collective-permute-done((f32[2,512,128]{2,1,0:T(8,128)S(1)}, f32[2,512,128]{2,1,0:T(8,128)S(1)}, u32[]{:S(2)}, u32[]{:S(2)}) %collective-permute-start.14) | collective-permute-done | bytes 524320 | tf_op jit(solution)/shard_map/ppermute | solution.py:478
  58.2 3.1 %third_section.1 = f32[2048,128]{1,0:T(8,128)} custom-call(f32[2,512,128]{2,1,0:T(8,128)S(1)} %second_section_kept.1.kept_ref, f32[2,512,128]{2,1,0:T(8,128)S(1)} %collective-permute-done.14.came_ref, bf16[256,768]{1,0:T(8,128)(2,1)S(1)} %get-tuple-element.50.refs_0_, bf16[256,768]{1,0:T(8,128)(2,1)S(1)} %get-tuple-element.51.refs_1_, ...), custom_call_target="tpu_custom_call" | custom-call | flops 1610612736 | bytes 4194304 | tf_op jit(solution)/shard_map/third_section/pallas_call | solution.py:364
  (12 shorter events, 0.0 us)
Async XLA Ops:
  0.9 13.3 %collective-permute-start = (f32[256,128]{1,0:T(8,128)S(1)}, f32[256,128]{1,0:T(8,128)S(1)}, u32[]{:S(2)}, u32[]{:S(2)}) collective-permute-start(f32[256,128]{1,0:T(8,128)S(1)} %dynamic-slice_bitcast_fusion), channel_id=1, source_target_pairs={{0,14},{2,12},{4,10},{6,8},{8,6},{10,4},{12,2},{14,0},{1,15},{3,13... | collective-permute-start | bytes 393224 | tf_op jit(solution)/shard_map/ppermute | solution.py:413
  7.0 1.2 %copy-start = (f32[2,131072]{1,0:T(2,128)S(1)}, f32[2,131072]{1,0:T(2,128)}, u32[]{:S(2)}) copy-start(f32[2,131072]{1,0:T(2,128)} %param.3) | copy-start | bytes 3145732
  8.9 8.6 %collective-permute-start.1 = (f32[256,128]{1,0:T(8,128)S(1)}, f32[256,128]{1,0:T(8,128)S(1)}, u32[]{:S(2)}, u32[]{:S(2)}) collective-permute-start(f32[256,128]{1,0:T(8,128)S(1)} %get-tuple-element.30), channel_id=1, source_target_pairs={{0,12},{2,14},{4,8},{6,10},{8,4},{10,6},{12,0},{14,2},{1,13},{3,15... | collective-permute-start | bytes 393224 | tf_op jit(solution)/shard_map/ppermute | solution.py:413
  9.2 17.6 %collective-permute-start.2 = (f32[256,128]{1,0:T(8,128)S(1)}, f32[256,128]{1,0:T(8,128)S(1)}, u32[]{:S(2)}, u32[]{:S(2)}) collective-permute-start(f32[256,128]{1,0:T(8,128)S(1)} %get-tuple-element.31), channel_id=1, source_target_pairs={{0,6},{2,4},{4,2},{6,0},{8,14},{10,12},{12,10},{14,8},{1,7},{3,5},... | collective-permute-start | bytes 393224 | tf_op jit(solution)/shard_map/ppermute | solution.py:413
  9.2 17.6 %collective-permute-start.3 = (f32[256,128]{1,0:T(8,128)S(1)}, f32[256,128]{1,0:T(8,128)S(1)}, u32[]{:S(2)}, u32[]{:S(2)}) collective-permute-start(f32[256,128]{1,0:T(8,128)S(1)} %get-tuple-element.32), channel_id=1, source_target_pairs={{0,4},{2,6},{4,0},{6,2},{8,12},{10,14},{12,8},{14,10},{1,5},{3,7},... | collective-permute-start | bytes 393224 | tf_op jit(solution)/shard_map/ppermute | solution.py:413
  11.0 16.5 %collective-permute-start.4 = (f32[256,128]{1,0:T(8,128)S(1)}, f32[256,128]{1,0:T(8,128)S(1)}, u32[]{:S(2)}, u32[]{:S(2)}) collective-permute-start(f32[256,128]{1,0:T(8,128)S(1)} %get-tuple-element.34), channel_id=1, source_target_pairs={{0,10},{2,8},{4,14},{6,12},{8,2},{10,0},{12,6},{14,4},{1,11},{3,9}... | collective-permute-start | bytes 393224 | tf_op jit(solution)/shard_map/ppermute | solution.py:413
  14.2 15.1 %collective-permute-start.5 = (f32[256,128]{1,0:T(8,128)S(1)}, f32[256,128]{1,0:T(8,128)S(1)}, u32[]{:S(2)}, u32[]{:S(2)}) collective-permute-start(f32[256,128]{1,0:T(8,128)S(1)} %get-tuple-element.35), channel_id=1, source_target_pairs={{0,8},{2,10},{4,12},{6,14},{8,0},{10,2},{12,4},{14,6},{1,9},{3,11}... | collective-permute-start | bytes 393224 | tf_op jit(solution)/shard_map/ppermute | solution.py:413
  17.6 11.7 %collective-permute-start.6 = (f32[256,128]{1,0:T(8,128)S(1)}, f32[256,128]{1,0:T(8,128)S(1)}, u32[]{:S(2)}, u32[]{:S(2)}) collective-permute-start(f32[256,128]{1,0:T(8,128)S(1)} %get-tuple-element.36), channel_id=1, source_target_pairs={{0,2},{2,0},{4,6},{6,4},{8,10},{10,8},{12,14},{14,12},{1,3},{3,1},... | collective-permute-start | bytes 393224 | tf_op jit(solution)/shard_map/ppermute | solution.py:413
  19.1 0.7 %copy-start.1 = (s32[18]{0:T(128)S(1)}, s32[18]{0:T(128)}, u32[]{:S(2)}) copy-start(s32[18]{0:T(128)} %bits_ref.1) | copy-start | bytes 220
  31.8 8.7 %collective-permute-start.7 = (f32[2,2,4,16,128]{4,3,2,1,0:T(8,128)S(1)}, f32[2,2,4,16,128]{4,3,2,1,0:T(8,128)S(1)}, u32[]{:S(2)}, u32[]{:S(2)}) collective-permute-start(f32[2,2,4,16,128]{4,3,2,1,0:T(8,128)S(1)} %get-tuple-element.41), channel_id=1, source_target_pairs={{0,14},{2,12},{4,10},{6,8},{8,6},{10,4},{12,2},{14,0},{1,15},{3,13... | collective-permute-start | bytes 393224 | tf_op jit(solution)/shard_map/ppermute | solution.py:413
  34.3 8.3 %collective-permute-start.8 = (f32[2,2,4,16,128]{4,3,2,1,0:T(8,128)S(1)}, f32[2,2,4,16,128]{4,3,2,1,0:T(8,128)S(1)}, u32[]{:S(2)}, u32[]{:S(2)}) collective-permute-start(f32[2,2,4,16,128]{4,3,2,1,0:T(8,128)S(1)} %get-tuple-element.42), channel_id=1, source_target_pairs={{0,12},{2,14},{4,8},{6,10},{8,4},{10,6},{12,0},{14,2},{1,13},{3,15... | collective-permute-start | bytes 393224 | tf_op jit(solution)/shard_map/ppermute | solution.py:413
  35.6 11.6 %collective-permute-start.9 = (f32[2,2,4,16,128]{4,3,2,1,0:T(8,128)S(1)}, f32[2,2,4,16,128]{4,3,2,1,0:T(8,128)S(1)}, u32[]{:S(2)}, u32[]{:S(2)}) collective-permute-start(f32[2,2,4,16,128]{4,3,2,1,0:T(8,128)S(1)} %get-tuple-element.43), channel_id=1, source_target_pairs={{0,6},{2,4},{4,2},{6,0},{8,14},{10,12},{12,10},{14,8},{1,7},{3,5},... | collective-permute-start | bytes 393224 | tf_op jit(solution)/shard_map/ppermute | solution.py:413
  35.6 14.5 %collective-permute-start.10 = (f32[2,2,4,16,128]{4,3,2,1,0:T(8,128)S(1)}, f32[2,2,4,16,128]{4,3,2,1,0:T(8,128)S(1)}, u32[]{:S(2)}, u32[]{:S(2)}) collective-permute-start(f32[2,2,4,16,128]{4,3,2,1,0:T(8,128)S(1)} %get-tuple-element.44), channel_id=1, source_target_pairs={{0,4},{2,6},{4,0},{6,2},{8,12},{10,14},{12,8},{14,10},{1,5},{3,7},... | collective-permute-start | bytes 393224 | tf_op jit(solution)/shard_map/ppermute | solution.py:413
  38.6 16.2 %collective-permute-start.11 = (f32[2,2,4,16,128]{4,3,2,1,0:T(8,128)S(1)}, f32[2,2,4,16,128]{4,3,2,1,0:T(8,128)S(1)}, u32[]{:S(2)}, u32[]{:S(2)}) collective-permute-start(f32[2,2,4,16,128]{4,3,2,1,0:T(8,128)S(1)} %get-tuple-element.45), channel_id=1, source_target_pairs={{0,10},{2,8},{4,14},{6,12},{8,2},{10,0},{12,6},{14,4},{1,11},{3,9}... | collective-permute-start | bytes 393224 | tf_op jit(solution)/shard_map/ppermute | solution.py:413
  40.4 14.8 %collective-permute-start.12 = (f32[2,2,4,16,128]{4,3,2,1,0:T(8,128)S(1)}, f32[2,2,4,16,128]{4,3,2,1,0:T(8,128)S(1)}, u32[]{:S(2)}, u32[]{:S(2)}) collective-permute-start(f32[2,2,4,16,128]{4,3,2,1,0:T(8,128)S(1)} %get-tuple-element.46), channel_id=1, source_target_pairs={{0,8},{2,10},{4,12},{6,14},{8,0},{10,2},{12,4},{14,6},{1,9},{3,11}... | collective-permute-start | bytes 393224 | tf_op jit(solution)/shard_map/ppermute | solution.py:413
  42.5 12.7 %collective-permute-start.13 = (f32[2,2,4,16,128]{4,3,2,1,0:T(8,128)S(1)}, f32[2,2,4,16,128]{4,3,2,1,0:T(8,128)S(1)}, u32[]{:S(2)}, u32[]{:S(2)}) collective-permute-start(f32[2,2,4,16,128]{4,3,2,1,0:T(8,128)S(1)} %get-tuple-element.47), channel_id=1, source_target_pairs={{0,2},{2,0},{4,6},{6,4},{8,10},{10,8},{12,14},{14,12},{1,3},{3,1},... | collective-permute-start | bytes 393224 | tf_op jit(solution)/shard_map/ppermute | solution.py:413
  56.2 2.0 %copy-start.2 = (bf16[512,1536]{1,0:T(8,128)(2,1)S(1)}, bf16[512,1536]{1,0:T(8,128)(2,1)}, u32[]{:S(2)}) copy-start(bf16[512,1536]{1,0:T(8,128)(2,1)} %get-tuple-element.52.refs_2_) | copy-start | bytes 4718596
  56.2 2.0 %collective-permute-start.14 = (f32[2,512,128]{2,1,0:T(8,128)S(1)}, f32[2,512,128]{2,1,0:T(8,128)S(1)}, u32[]{:S(2)}, u32[]{:S(2)}) collective-permute-start(f32[2,512,128]{2,1,0:T(8,128)S(1)} %second_section_sent.1), channel_id=1, source_target_pairs={{0,1},{1,0},{2,3},{3,2},{4,5},{5,4},{6,7},{7,6},{8,9},{9,8},{10,11... | collective-permute-start | bytes 1572872 | tf_op jit(solution)/shard_map/ppermute | solution.py:478

commit v18 on v17

--- a/solution.py
+++ b/solution.py
@@ -109,6 +109,20 @@
 
 def by_core(dim):
     return lambda x: jnp.bitwise_xor(x, lax.axis_index("qb") * (dim // 2))
+
+
+def away_first(dim):
+    return lambda x: jnp.bitwise_xor(x, (1 - lax.axis_index("qb")) * (dim // 2))
+
+
+def last_far(count):
+    return max(spot for spot, distance in enumerate(distances_of(count)) if distance >= count // 2)
+
+
+def piece_of(blocks, other, spot, half):
+    if spot != last_far(len(blocks)):
+        return blocks[spot].at[half]
+    return other if half else blocks[spot]
 
 
 def straight(count):
@@ -168,6 +182,8 @@
                 order = (by_source(dim, count), from_blocks if straight(count) else None, by_core(dim))[number]
                 if order is not None:
                     high, rest = pick_columns(high, order), pick_columns(rest, order)
+                if number == 0:
+                    high, rest = pick_rows(high, away_first(dim)), pick_rows(rest, away_first(dim))
             elif number == 0 and straight(count) and target is weights[-1]:
                 high, rest = pick_rows(high, into_blocks), pick_rows(rest, into_blocks)
             target[...] = jnp.concatenate([high, rest, high], axis=1)
@@ -282,16 +298,16 @@
     _, *blocks = refs[: 1 + len(spots)]
     refs = refs[1 + len(spots) :]
     low_ref, weights, refs = refs[0], refs[1 : 1 + len(stages)], refs[1 + len(stages) :]
-    outs, (whole, *halves) = refs[:count], refs[count:]
+    outs, (other, whole, *halves) = refs[:count], refs[count:]
     low_gate(zip(spots, blocks), low_ref, whole)
     run_top_stage(stages[0], weights[0], lane_bits, whole, halves[:2])
     if straight(count):
 
         def store(top, part, start, value):
-            for spot, out_ref in enumerate(outs):
+            for spot in range(count):
                 for bit in range(2):
                     rows = value[(2 * spot + bit) * 16 : (2 * spot + bit + 1) * 16]
-                    out_ref[top, part, 2 * bit + start] = rows
+                    piece_of(outs, other, spot, top)[part, 2 * bit + start] = rows
 
         run_halves(stages[1:], weights[1:], lane_bits, halves[:2], halves[2:], store)
         return
@@ -299,35 +315,35 @@
     tops, mids, _, inner, _ = outs[0].shape
     dests = partners_of(count)
     for top in range(tops):
-        for dest, out_ref in zip(dests, outs):
+        for spot, dest in enumerate(dests):
+            piece = piece_of(outs, other, spot, top)
             for mid in range(mids):
                 start = pl.multiple_of((mid * count + dest) * inner, inner)
                 for part in range(2):
-                    out_ref[top, mid, part] = done[top][part, pl.ds(start, inner), :]
+                    piece[mid, part] = done[top][part, pl.ds(start, inner), :]
 
 
 def second_kernel(stages, lane_bits, count, stays, *refs):
     blocks, weights, refs = refs[:count], refs[count : count + len(stages)], refs[count + len(stages) :]
     out_ref, one, two = refs
-    core = lax.axis_index("qb")
-    top = core if stays else 1 - core
+    pieces = [piece_of(blocks, blocks[last_far(count)], spot, int(stays)) for spot in range(count)]
     if straight(count):
         dim, stride, starts = stage_starts(stages[0], lane_bits, one.shape[1])
 
         def load(part, start):
-            return jnp.concatenate([block_ref[top, part, start] for block_ref in blocks], axis=0)
+            return jnp.concatenate([piece[part, start] for piece in pieces], axis=0)
 
         def store(part, start, value):
             one[part, pl.ds(start, dim, stride=stride), :] = value
 
         apply_stage(weights[0], starts, load, store)
-        stages, weights, blocks = stages[1:], weights[1:], []
-    for source, block_ref in zip(partners_of(count), blocks):
-        _, mids, _, inner, _ = block_ref.shape
+        stages, weights, pieces = stages[1:], weights[1:], []
+    for source, piece in zip(partners_of(count), pieces):
+        mids, _, inner, _ = piece.shape
         for mid in range(mids):
             start = pl.multiple_of((mid * count + source) * inner, inner)
             for part in range(2):
-                one[part, pl.ds(start, inner), :] = block_ref[top, mid, part]
+                one[part, pl.ds(start, inner), :] = piece[mid, part]
     for index, (stage, weights_ref) in enumerate(zip(stages, weights)):
         run_stage(stage, weights_ref, lane_bits, one, out_ref if index == len(stages) - 1 else two)
         one, two = two, one
@@ -446,10 +462,12 @@
         *[blocks[spot] for spot in early],
         low_w,
     )
-    *blocks, _ = call(
+    view = (2, 4, 16, lanes) if straight(qa) else (qa // qb, 2, inner, lanes)
+    views = [shape(view if spot == last_far(qa) else (qb,) + view, F32) for spot in range(qa)]
+    *blocks, other, _ = call(
         functools.partial(first_kernel, sections[0], lane_bits, qa, late),
         "first_section",
-        (shape((qb, 2, 4, 16, lanes) if straight(qa) else (qb, qa // qb, 2, inner, lanes), F32),) * qa + (planes,),
+        (*views, shape(view, F32), planes),
         [vmem] * (2 + len(late) + counts[0]),
         [half] * 4,
         5,
@@ -457,9 +475,11 @@
         *[blocks[spot] for spot in late],
         low_w,
         *weights[0],
-        aliases={0: qa},
+        aliases={0: qa + 1},
     )
     blocks = exchange(blocks)
+    distance = distances_of(qa)[last_far(qa)]
+    other = lax.ppermute(other, "qa", [(i, i ^ distance) for i in range(qa)])
     halves = []
     for stays in (False, True):
         halves.append(
@@ -469,8 +489,8 @@
                 shape((2, rows // qb, lanes), F32),
                 [vmem] * (qa + counts[1]),
                 [half] * 2,
-                1.5,
-                *blocks,
+                100 if stays else 0.001,
+                *[other if stays and spot == last_far(qa) else block for spot, block in enumerate(blocks)],
                 *weights[1],
             )
         )

time: 61.5 us -> 62 us (level)
    ppermute x0 -> x1, starting transfers between devices: none -> 3.61 us  [per_device(): other = lax.ppermute(other, 'qa', [(i, i ^ distance) for i in range(qa)])]
    ppermute x14, starting transfers between devices: 27.6 us -> 24.2 us  [exchange(): lax.ppermute(piece, 'qa', [(i, i ^ distance) for i in range(qa)])]
  transfers between devices with their start and end apart: 15 -> 16, of which waited for: 8 -> 5; matrix products, arithmetic and copies ran while one was open for 0% -> 0% of each run, Pallas kernels for 15% -> 17%
where the time goes in v18:
time: 62 us; the launch traced here: 61.8 us
  starting transfers between devices  27.8 us (45%)
  Pallas kernels  15.7 us (25%)
  waiting for transfers between devices  15.3 us (25%)
  local copies, waits for them, and re-layouts  2.8 us (5%)
    ppermute x14, starting transfers between devices, exchange(): lax.ppermute(piece, 'qa', [(i, i ^ distance) for i in range(qa)])  24.2 us
    pallas_call x7, Pallas kernels, call(): pl.pallas_call(kernel, out_shape=out_shapes, in_specs=in_specs, out_specs...  15.7 us
    ppermute x14, waiting for transfers between devices, exchange(): lax.ppermute(piece, 'qa', [(i, i ^ distance) for i in range(qa)])  14.4 us
    ppermute x1, starting transfers between devices, per_device(): other = lax.ppermute(other, 'qa', [(i, i ^ distance) for i in range(qa)])  3.61 us
    unnamed x6, local copies, waits for them, and re-layouts  1.88 us
  transfers between devices with their start and end apart: 16, of which 5 were waited for; matrix products, arithmetic and copies ran while one was open for 0% of the time, Pallas kernels for 17%

profile of v18, /device:TPU:0, one launch (start us, length us, event | category | flops | bytes accessed | tf_op | source)
XLA Modules:
  0.0 61.8 jit_solution(17632020445901627011)
XLA Ops:
  0.0 0.9 %dynamic-slice_bitcast_fusion = f32[256,128]{1,0:T(8,128)S(1)} fusion(f32[8,256,128]{2,1,0:T(8,128)} %bitcast.12, s32[]{:T(128)S(6)} %select_n.4), kind=kLoop, calls=%fused_computation | loop fusion | bytes 262148 | tf_op jit(solution)/shard_map/jit(dynamic_index_in_dim)/squeeze | solution.py:424
  0.9 6.1 %collective-permute-start = (f32[256,128]{1,0:T(8,128)S(1)}, f32[256,128]{1,0:T(8,128)S(1)}, u32[]{:S(2)}, u32[]{:S(2)}) collective-permute-start(f32[256,128]{1,0:T(8,128)S(1)} %dynamic-slice_bitcast_fusion), channel_id=1, source_target_pairs={{0,14},{2,12},{4,10},{6,8},{8,6},{10,4},{12,2},{14,0},{1,15},{3,13... | collective-permute-start | bytes 393224 | tf_op jit(solution)/shard_map/ppermute | solution.py:429
  7.0 1.2 %copy-done = f32[2,131072]{1,0:T(2,128)S(1)} copy-done((f32[2,131072]{1,0:T(2,128)S(1)}, f32[2,131072]{1,0:T(2,128)}, u32[]{:S(2)}) %copy-start) | copy-done | bytes 1048600
  8.2 0.7 %split_state.1 = (f32[256,128]{1,0:T(8,128)S(1)}, f32[256,128]{1,0:T(8,128)}, f32[256,128]{1,0:T(8,128)S(1)}, f32[256,128]{1,0:T(8,128)S(1)}, f32[256,128]{1,0:T...) custom-call(f32[8,256,128]{2,1,0:T(8,128)S(1)} %bitcast.13), custom_call_target="tpu_custom_call" | custom-call | bytes 4194304 | tf_op jit(solution)/shard_map/split_state/pallas_call | solution.py:380
  8.9 0.2 collective-permute-start.1
  9.2 1.8 %collective-permute-start.3 = (f32[256,128]{1,0:T(8,128)S(1)}, f32[256,128]{1,0:T(8,128)S(1)}, u32[]{:S(2)}, u32[]{:S(2)}) collective-permute-start(f32[256,128]{1,0:T(8,128)S(1)} %get-tuple-element.33), channel_id=1, source_target_pairs={{0,4},{2,6},{4,0},{6,2},{8,12},{10,14},{12,8},{14,10},{1,5},{3,7},... | collective-permute-start | bytes 393224 | tf_op jit(solution)/shard_map/ppermute | solution.py:429
  11.0 3.2 %collective-permute-start.4 = (f32[256,128]{1,0:T(8,128)S(1)}, f32[256,128]{1,0:T(8,128)S(1)}, u32[]{:S(2)}, u32[]{:S(2)}) collective-permute-start(f32[256,128]{1,0:T(8,128)S(1)} %get-tuple-element.35), channel_id=1, source_target_pairs={{0,10},{2,8},{4,14},{6,12},{8,2},{10,0},{12,6},{14,4},{1,11},{3,9}... | collective-permute-start | bytes 393224 | tf_op jit(solution)/shard_map/ppermute | solution.py:429
  14.2 3.3 %collective-permute-start.5 = (f32[256,128]{1,0:T(8,128)S(1)}, f32[256,128]{1,0:T(8,128)S(1)}, u32[]{:S(2)}, u32[]{:S(2)}) collective-permute-start(f32[256,128]{1,0:T(8,128)S(1)} %get-tuple-element.36), channel_id=1, source_target_pairs={{0,8},{2,10},{4,12},{6,14},{8,0},{10,2},{12,4},{14,6},{1,9},{3,11}... | collective-permute-start | bytes 393224 | tf_op jit(solution)/shard_map/ppermute | solution.py:429
  17.6 1.5 %collective-permute-start.6 = (f32[256,128]{1,0:T(8,128)S(1)}, f32[256,128]{1,0:T(8,128)S(1)}, u32[]{:S(2)}, u32[]{:S(2)}) collective-permute-start(f32[256,128]{1,0:T(8,128)S(1)} %get-tuple-element.37), channel_id=1, source_target_pairs={{0,2},{2,0},{4,6},{6,4},{8,10},{10,8},{12,14},{14,12},{1,3},{3,1},... | collective-permute-start | bytes 393224 | tf_op jit(solution)/shard_map/ppermute | solution.py:429
  19.1 0.7 %copy-done.1 = s32[18]{0:T(128)S(1)} copy-done((s32[18]{0:T(128)S(1)}, s32[18]{0:T(128)}, u32[]{:S(2)}) %copy-start.1) | copy-done | bytes 96
  19.8 7.1 %prepare_gates.1 = (bf16[768,256]{1,0:T(8,128)(2,1)S(1)}, bf16[256,768]{1,0:T(8,128)(2,1)S(1)}, bf16[256,768]{1,0:T(8,128)(2,1)S(1)}, bf16[512,1536]{1,0:T(8,128...) custom-call(s32[18]{0:T(128)S(1)} %copy-done.1, ...), custom_call_target="tpu_custom_call" | custom-call | flops 3221225472 | bytes 4194304 | tf_op jit(solution)/shard_map/prepare_gates/pallas_call | solution.py:380
  26.9 0.0 collective-permute-done.2.refs_3_
  26.9 0.4 low_gate_early.1.refs_0_
  27.4 0.1 collective-permute-done.4.refs_1_
  27.5 1.8 %collective-permute-done.5.refs_2_ = f32[256,128]{1,0:T(8,128)S(1)} collective-permute-done((f32[256,128]{1,0:T(8,128)S(1)}, f32[256,128]{1,0:T(8,128)S(1)}, u32[]{:S(2)}, u32[]{:S(2)}) %collective-permute-start.5) | collective-permute-done | bytes 131104 | tf_op jit(solution)/shard_map/ppermute | solution.py:429
  29.3 2.5 %first_section.1 = (f32[2,2,4,16,128]{4,3,2,1,0:T(8,128)S(1)}, f32[2,2,4,16,128]{4,3,2,1,0:T(8,128)S(1)}, f32[2,2,4,16,128]{4,3,2,1,0:T(8,128)S(1)}, f32[2,2,4,1...) custom-call(f32[2,1024,128]{2,1,0:T(8,128)S(1)} %low_gate_early.1.re, ...), custom_call_target="tpu_custom_call", output_to_operand_aliasing={{9}: (0, {})} | custom-call | flops 2013265920 | bytes 4194304 | tf_op jit(solution)/shard_map/first_section/pallas_call | solution.py:380
  31.8 2.5 %collective-permute-start.7 = (f32[2,2,4,16,128]{4,3,2,1,0:T(8,128)S(1)}, f32[2,2,4,16,128]{4,3,2,1,0:T(8,128)S(1)}, u32[]{:S(2)}, u32[]{:S(2)}) collective-permute-start(f32[2,2,4,16,128]{4,3,2,1,0:T(8,128)S(1)} %get-tuple-element.42), channel_id=1, source_target_pairs={{0,14},{2,12},{4,10},{6,8},{8,6},{10,4},{12,2},{14,0},{1,15},{3,13... | collective-permute-start | bytes 393224 | tf_op jit(solution)/shard_map/ppermute | solution.py:429
  34.3 0.0 collective-permute-start.14
  34.3 1.4 %collective-permute-start.8 = (f32[2,2,4,16,128]{4,3,2,1,0:T(8,128)S(1)}, f32[2,2,4,16,128]{4,3,2,1,0:T(8,128)S(1)}, u32[]{:S(2)}, u32[]{:S(2)}) collective-permute-start(f32[2,2,4,16,128]{4,3,2,1,0:T(8,128)S(1)} %get-tuple-element.43), channel_id=1, source_target_pairs={{0,12},{2,14},{4,8},{6,10},{8,4},{10,6},{12,0},{14,2},{1,13},{3,15... | collective-permute-start | bytes 393224 | tf_op jit(solution)/shard_map/ppermute | solution.py:429
  35.7 3.0 %collective-permute-start.9 = (f32[2,2,4,16,128]{4,3,2,1,0:T(8,128)S(1)}, f32[2,2,4,16,128]{4,3,2,1,0:T(8,128)S(1)}, u32[]{:S(2)}, u32[]{:S(2)}) collective-permute-start(f32[2,2,4,16,128]{4,3,2,1,0:T(8,128)S(1)} %get-tuple-element.44), channel_id=1, source_target_pairs={{0,6},{2,4},{4,2},{6,0},{8,14},{10,12},{12,10},{14,8},{1,7},{3,5},... | collective-permute-start | bytes 393224 | tf_op jit(solution)/shard_map/ppermute | solution.py:429
  38.7 0.0 collective-permute-start.10
  38.7 6.8 %collective-permute-done.14.refs_6_ = f32[2,4,16,128]{3,2,1,0:T(8,128)S(1)} collective-permute-done((f32[2,4,16,128]{3,2,1,0:T(8,128)S(1)}, f32[2,4,16,128]{3,2,1,0:T(8,128)S(1)}, u32[]{:S(2)}, u32[]{:S(2)}) %collective-permute-start.14) | collective-permute-done | bytes 65568 | tf_op jit(solution)/shard_map/ppermute | solution.py:429
  45.5 1.0 %collective-permute-start.13 = (f32[2,2,4,16,128]{4,3,2,1,0:T(8,128)S(1)}, f32[2,2,4,16,128]{4,3,2,1,0:T(8,128)S(1)}, u32[]{:S(2)}, u32[]{:S(2)}) collective-permute-start(f32[2,2,4,16,128]{4,3,2,1,0:T(8,128)S(1)} %get-tuple-element.48), channel_id=1, source_target_pairs={{0,2},{2,0},{4,6},{6,4},{8,10},{10,8},{12,14},{14,12},{1,3},{3,1},... | collective-permute-start | bytes 393224 | tf_op jit(solution)/shard_map/ppermute | solution.py:429
  46.5 0.0 collective-permute-done.8.refs_2_
  46.5 3.6 %collective-permute-start.12 = (f32[2,4,16,128]{3,2,1,0:T(8,128)S(1)}, f32[2,4,16,128]{3,2,1,0:T(8,128)S(1)}, u32[]{:S(2)}, u32[]{:S(2)}) collective-permute-start(f32[2,4,16,128]{3,2,1,0:T(8,128)S(1)} %get-tuple-element.47), channel_id=1, source_target_pairs={{0,8},{2,10},{4,12},{6,14},{8,0},{10,2},{12,4},{14,6},{1,9},{3,11}... | collective-permute-start | bytes 196616 | tf_op jit(solution)/shard_map/ppermute | solution.py:482
  50.1 5.7 %collective-permute-done.11.refs_5_ = f32[2,2,4,16,128]{4,3,2,1,0:T(8,128)S(1)} collective-permute-done((f32[2,2,4,16,128]{4,3,2,1,0:T(8,128)S(1)}, f32[2,2,4,16,128]{4,3,2,1,0:T(8,128)S(1)}, u32[]{:S(2)}, u32[]{:S(2)}) %collective-permute-start.11) | collective-permute-done | bytes 131104 | tf_op jit(solution)/shard_map/ppermute | solution.py:429
  55.8 0.0 collective-permute-done.13.refs_7_
  55.8 1.0 %second_section_sent.1 = f32[2,512,128]{2,1,0:T(8,128)S(1)} custom-call(f32[2,2,4,16,128]{4,3,2,1,0:T(8,128)S(1)} %get-tuple-element.41.refs_0_, f32[2,2,4,16,128]{4,3,2,1,0:T(8,128)S(1)} %collective-permute-done.7.refs_1_, f32[2,2,4,16,128]{4,3,2,1,0:T(8,128)S(1)} %collective-permute-done.8.refs_2_, ...), custom_call_target="tpu_custom_call" | custom-call | flops 402653 | bytes 4194304 | tf_op jit(solution)/shard_map/second_section_sent/pallas_call | solution.py:380
  56.7 0.1 collective-permute-start.15
  56.8 1.0 %second_section_kept.1.kept_ref = f32[2,512,128]{2,1,0:T(8,128)S(1)} custom-call(f32[2,2,4,16,128]{4,3,2,1,0:T(8,128)S(1)} %get-tuple-element.41.refs_0_, f32[2,2,4,16,128]{4,3,2,1,0:T(8,128)S(1)} %collective-permute-done.7.refs_1_, f32[2,2,4,16,128]{4,3,2,1,0:T(8,128)S(1)} %collective-permute-done.8.refs_2_, ...), custom_call_target="tpu_custom_call" | custom-call | flops 40265318400 | bytes 4194304 | tf_op jit(solution)/shard_map/second_section_kept/pallas_call | solution.py:380
  57.8 0.9 %collective-permute-done.15.came_ref = f32[2,512,128]{2,1,0:T(8,128)S(1)} collective-permute-done((f32[2,512,128]{2,1,0:T(8,128)S(1)}, f32[2,512,128]{2,1,0:T(8,128)S(1)}, u32[]{:S(2)}, u32[]{:S(2)}) %collective-permute-start.15) | collective-permute-done | bytes 524320 | tf_op jit(solution)/shard_map/ppermute | solution.py:498
  58.7 3.1 %third_section.1 = f32[2048,128]{1,0:T(8,128)} custom-call(f32[2,512,128]{2,1,0:T(8,128)S(1)} %second_section_kept.1.kept_ref, f32[2,512,128]{2,1,0:T(8,128)S(1)} %collective-permute-done.15.came_ref, bf16[256,768]{1,0:T(8,128)(2,1)S(1)} %get-tuple-element.52.refs_0_, bf16[256,768]{1,0:T(8,128)(2,1)S(1)} %get-tuple-element.53.refs_1_, ...), custom_call_target="tpu_custom_call" | custom-call | flops 1610612736 | bytes 4194304 | tf_op jit(solution)/shard_map/third_section/pallas_call | solution.py:380
  (14 shorter events, 0.0 us)
Async XLA Ops:
  0.9 13.3 %collective-permute-start = (f32[256,128]{1,0:T(8,128)S(1)}, f32[256,128]{1,0:T(8,128)S(1)}, u32[]{:S(2)}, u32[]{:S(2)}) collective-permute-start(f32[256,128]{1,0:T(8,128)S(1)} %dynamic-slice_bitcast_fusion), channel_id=1, source_target_pairs={{0,14},{2,12},{4,10},{6,8},{8,6},{10,4},{12,2},{14,0},{1,15},{3,13... | collective-permute-start | bytes 393224 | tf_op jit(solution)/shard_map/ppermute | solution.py:429
  7.0 1.2 %copy-start = (f32[2,131072]{1,0:T(2,128)S(1)}, f32[2,131072]{1,0:T(2,128)}, u32[]{:S(2)}) copy-start(f32[2,131072]{1,0:T(2,128)} %param.3) | copy-start | bytes 3145732
  8.9 8.6 %collective-permute-start.1 = (f32[256,128]{1,0:T(8,128)S(1)}, f32[256,128]{1,0:T(8,128)S(1)}, u32[]{:S(2)}, u32[]{:S(2)}) collective-permute-start(f32[256,128]{1,0:T(8,128)S(1)} %get-tuple-element.31), channel_id=1, source_target_pairs={{0,12},{2,14},{4,8},{6,10},{8,4},{10,6},{12,0},{14,2},{1,13},{3,15... | collective-permute-start | bytes 393224 | tf_op jit(solution)/shard_map/ppermute | solution.py:429
  9.2 17.7 %collective-permute-start.2 = (f32[256,128]{1,0:T(8,128)S(1)}, f32[256,128]{1,0:T(8,128)S(1)}, u32[]{:S(2)}, u32[]{:S(2)}) collective-permute-start(f32[256,128]{1,0:T(8,128)S(1)} %get-tuple-element.32), channel_id=1, source_target_pairs={{0,6},{2,4},{4,2},{6,0},{8,14},{10,12},{12,10},{14,8},{1,7},{3,5},... | collective-permute-start | bytes 393224 | tf_op jit(solution)/shard_map/ppermute | solution.py:429
  9.2 17.7 %collective-permute-start.3 = (f32[256,128]{1,0:T(8,128)S(1)}, f32[256,128]{1,0:T(8,128)S(1)}, u32[]{:S(2)}, u32[]{:S(2)}) collective-permute-start(f32[256,128]{1,0:T(8,128)S(1)} %get-tuple-element.33), channel_id=1, source_target_pairs={{0,4},{2,6},{4,0},{6,2},{8,12},{10,14},{12,8},{14,10},{1,5},{3,7},... | collective-permute-start | bytes 393224 | tf_op jit(solution)/shard_map/ppermute | solution.py:429
  11.0 16.5 %collective-permute-start.4 = (f32[256,128]{1,0:T(8,128)S(1)}, f32[256,128]{1,0:T(8,128)S(1)}, u32[]{:S(2)}, u32[]{:S(2)}) collective-permute-start(f32[256,128]{1,0:T(8,128)S(1)} %get-tuple-element.35), channel_id=1, source_target_pairs={{0,10},{2,8},{4,14},{6,12},{8,2},{10,0},{12,6},{14,4},{1,11},{3,9}... | collective-permute-start | bytes 393224 | tf_op jit(solution)/shard_map/ppermute | solution.py:429
  14.2 15.1 %collective-permute-start.5 = (f32[256,128]{1,0:T(8,128)S(1)}, f32[256,128]{1,0:T(8,128)S(1)}, u32[]{:S(2)}, u32[]{:S(2)}) collective-permute-start(f32[256,128]{1,0:T(8,128)S(1)} %get-tuple-element.36), channel_id=1, source_target_pairs={{0,8},{2,10},{4,12},{6,14},{8,0},{10,2},{12,4},{14,6},{1,9},{3,11}... | collective-permute-start | bytes 393224 | tf_op jit(solution)/shard_map/ppermute | solution.py:429
  17.6 11.7 %collective-permute-start.6 = (f32[256,128]{1,0:T(8,128)S(1)}, f32[256,128]{1,0:T(8,128)S(1)}, u32[]{:S(2)}, u32[]{:S(2)}) collective-permute-start(f32[256,128]{1,0:T(8,128)S(1)} %get-tuple-element.37), channel_id=1, source_target_pairs={{0,2},{2,0},{4,6},{6,4},{8,10},{10,8},{12,14},{14,12},{1,3},{3,1},... | collective-permute-start | bytes 393224 | tf_op jit(solution)/shard_map/ppermute | solution.py:429
  19.1 0.7 %copy-start.1 = (s32[18]{0:T(128)S(1)}, s32[18]{0:T(128)}, u32[]{:S(2)}) copy-start(s32[18]{0:T(128)} %bits_ref.1) | copy-start | bytes 220
  31.8 13.7 %collective-permute-start.7 = (f32[2,2,4,16,128]{4,3,2,1,0:T(8,128)S(1)}, f32[2,2,4,16,128]{4,3,2,1,0:T(8,128)S(1)}, u32[]{:S(2)}, u32[]{:S(2)}) collective-permute-start(f32[2,2,4,16,128]{4,3,2,1,0:T(8,128)S(1)} %get-tuple-element.42), channel_id=1, source_target_pairs={{0,14},{2,12},{4,10},{6,8},{8,6},{10,4},{12,2},{14,0},{1,15},{3,13... | collective-permute-start | bytes 393224 | tf_op jit(solution)/shard_map/ppermute | solution.py:429
  34.3 11.2 %collective-permute-start.14 = (f32[2,4,16,128]{3,2,1,0:T(8,128)S(1)}, f32[2,4,16,128]{3,2,1,0:T(8,128)S(1)}, u32[]{:S(2)}, u32[]{:S(2)}) collective-permute-start(f32[2,4,16,128]{3,2,1,0:T(8,128)S(1)} %get-tuple-element.51), channel_id=1, source_target_pairs={{0,8},{2,10},{4,12},{6,14},{8,0},{10,2},{12,4},{14,6},{1,9},{3,11}... | collective-permute-start | bytes 196616 | tf_op jit(solution)/shard_map/ppermute | solution.py:429
  34.3 12.2 %collective-permute-start.8 = (f32[2,2,4,16,128]{4,3,2,1,0:T(8,128)S(1)}, f32[2,2,4,16,128]{4,3,2,1,0:T(8,128)S(1)}, u32[]{:S(2)}, u32[]{:S(2)}) collective-permute-start(f32[2,2,4,16,128]{4,3,2,1,0:T(8,128)S(1)} %get-tuple-element.43), channel_id=1, source_target_pairs={{0,12},{2,14},{4,8},{6,10},{8,4},{10,6},{12,0},{14,2},{1,13},{3,15... | collective-permute-start | bytes 393224 | tf_op jit(solution)/shard_map/ppermute | solution.py:429
  35.7 14.4 %collective-permute-start.9 = (f32[2,2,4,16,128]{4,3,2,1,0:T(8,128)S(1)}, f32[2,2,4,16,128]{4,3,2,1,0:T(8,128)S(1)}, u32[]{:S(2)}, u32[]{:S(2)}) collective-permute-start(f32[2,2,4,16,128]{4,3,2,1,0:T(8,128)S(1)} %get-tuple-element.44), channel_id=1, source_target_pairs={{0,6},{2,4},{4,2},{6,0},{8,14},{10,12},{12,10},{14,8},{1,7},{3,5},... | collective-permute-start | bytes 393224 | tf_op jit(solution)/shard_map/ppermute | solution.py:429
  38.7 11.4 %collective-permute-start.10 = (f32[2,2,4,16,128]{4,3,2,1,0:T(8,128)S(1)}, f32[2,2,4,16,128]{4,3,2,1,0:T(8,128)S(1)}, u32[]{:S(2)}, u32[]{:S(2)}) collective-permute-start(f32[2,2,4,16,128]{4,3,2,1,0:T(8,128)S(1)} %get-tuple-element.45), channel_id=1, source_target_pairs={{0,4},{2,6},{4,0},{6,2},{8,12},{10,14},{12,8},{14,10},{1,5},{3,7},... | collective-permute-start | bytes 393224 | tf_op jit(solution)/shard_map/ppermute | solution.py:429
  45.5 10.3 %collective-permute-start.11 = (f32[2,2,4,16,128]{4,3,2,1,0:T(8,128)S(1)}, f32[2,2,4,16,128]{4,3,2,1,0:T(8,128)S(1)}, u32[]{:S(2)}, u32[]{:S(2)}) collective-permute-start(f32[2,2,4,16,128]{4,3,2,1,0:T(8,128)S(1)} %get-tuple-element.46), channel_id=1, source_target_pairs={{0,10},{2,8},{4,14},{6,12},{8,2},{10,0},{12,6},{14,4},{1,11},{3,9}... | collective-permute-start | bytes 393224 | tf_op jit(solution)/shard_map/ppermute | solution.py:429
  45.5 10.3 %collective-permute-start.13 = (f32[2,2,4,16,128]{4,3,2,1,0:T(8,128)S(1)}, f32[2,2,4,16,128]{4,3,2,1,0:T(8,128)S(1)}, u32[]{:S(2)}, u32[]{:S(2)}) collective-permute-start(f32[2,2,4,16,128]{4,3,2,1,0:T(8,128)S(1)} %get-tuple-element.48), channel_id=1, source_target_pairs={{0,2},{2,0},{4,6},{6,4},{8,10},{10,8},{12,14},{14,12},{1,3},{3,1},... | collective-permute-start | bytes 393224 | tf_op jit(solution)/shard_map/ppermute | solution.py:429
  46.5 10.3 %collective-permute-start.12 = (f32[2,4,16,128]{3,2,1,0:T(8,128)S(1)}, f32[2,4,16,128]{3,2,1,0:T(8,128)S(1)}, u32[]{:S(2)}, u32[]{:S(2)}) collective-permute-start(f32[2,4,16,128]{3,2,1,0:T(8,128)S(1)} %get-tuple-element.47), channel_id=1, source_target_pairs={{0,8},{2,10},{4,12},{6,14},{8,0},{10,2},{12,4},{14,6},{1,9},{3,11}... | collective-permute-start | bytes 196616 | tf_op jit(solution)/shard_map/ppermute | solution.py:482
  56.7 2.0 %copy-start.2 = (bf16[512,1536]{1,0:T(8,128)(2,1)S(1)}, bf16[512,1536]{1,0:T(8,128)(2,1)}, u32[]{:S(2)}) copy-start(bf16[512,1536]{1,0:T(8,128)(2,1)} %get-tuple-element.54.refs_2_) | copy-start | bytes 4718596
  56.7 2.0 %collective-permute-start.15 = (f32[2,512,128]{2,1,0:T(8,128)S(1)}, f32[2,512,128]{2,1,0:T(8,128)S(1)}, u32[]{:S(2)}, u32[]{:S(2)}) collective-permute-start(f32[2,512,128]{2,1,0:T(8,128)S(1)} %second_section_sent.1), channel_id=1, source_target_pairs={{0,1},{1,0},{2,3},{3,2},{4,5},{5,4},{6,7},{7,6},{8,9},{9,8},{10,11... | collective-permute-start | bytes 1572872 | tf_op jit(solution)/shard_map/ppermute | solution.py:498

commit v19 on v14

--- a/solution.py
+++ b/solution.py
@@ -159,7 +159,8 @@
 
 
 def split_kernel(x_ref, *outs):
-    for dest, out_ref in zip(partners_of(len(outs)), outs):
+    me, _, *dests = partners_of(len(outs) + 1)
+    for dest, out_ref in zip([me, *dests], outs):
         out_ref[...] = x_ref[dest]
 
 
@@ -343,15 +344,15 @@
     blocks = call(
         split_kernel,
         "split_state",
-        (shape((2 * rows // qa, lanes), F32),) * qa,
+        (shape((2 * rows // qa, lanes), F32),) * (qa - 1),
         [vmem],
         [],
         0,
         state,
     )
 
-    blocks = list(blocks)
-    blocks[1] = lax.dynamic_index_in_dim(state, partners_of(qa)[1], 0, keepdims=False)
+    first = lax.dynamic_index_in_dim(state, partners_of(qa)[1], 0, keepdims=False)
+    blocks = [blocks[0], first, *blocks[1:]]
 
     def exchange(blocks):
         came = [blocks[0]]

time: 61.5 us -> 61.2 us (level)
  Pallas kernels: 14.7 us -> 14 us
  starting transfers between devices: 27.7 us -> 28.4 us
    ppermute x14, starting transfers between devices: 27.6 us -> 28.3 us  [exchange(): lax.ppermute(piece, 'qa', [(i, i ^ distance) for i in range(qa)])]
    pallas_call x7, Pallas kernels: 14.7 us -> 14 us  [call(): pl.pallas_call(kernel, out_shape=out_shapes, in_specs=in_specs, out_specs...]
  transfers between devices with their start and end apart: 15 -> 15, of which waited for: 8 -> 9; matrix products, arithmetic and copies ran while one was open for 0% -> 0% of each run, Pallas kernels for 13% -> 12%
where the time goes in v19:
time: 61.2 us; the launch traced here: 61 us
  starting transfers between devices  28.4 us (46%)
  waiting for transfers between devices  15.6 us (25%)
  Pallas kernels  14 us (23%)
  local copies, waits for them, and re-layouts  2.8 us (5%)
    ppermute x14, starting transfers between devices, exchange(): lax.ppermute(piece, 'qa', [(i, i ^ distance) for i in range(qa)])  28.3 us
    ppermute x14, waiting for transfers between devices, exchange(): lax.ppermute(piece, 'qa', [(i, i ^ distance) for i in range(qa)])  14.8 us
    pallas_call x7, Pallas kernels, call(): pl.pallas_call(kernel, out_shape=out_shapes, in_specs=in_specs, out_specs...  14 us
    unnamed x6, local copies, waits for them, and re-layouts  1.88 us
  transfers between devices with their start and end apart: 15, of which 9 were waited for; matrix products, arithmetic and copies ran while one was open for 0% of the time, Pallas kernels for 12%

profile of v19, /device:TPU:0, one launch (start us, length us, event | category | flops | bytes accessed | tf_op | source)
XLA Modules:
  0.0 61.0 jit_solution(1414954842186716162)
XLA Ops:
  0.0 0.9 %dynamic-slice_bitcast_fusion = f32[256,128]{1,0:T(8,128)S(1)} fusion(f32[8,256,128]{2,1,0:T(8,128)} %bitcast.12, s32[]{:T(128)S(6)} %select_n.4), kind=kLoop, calls=%fused_computation | loop fusion | bytes 262148 | tf_op jit(solution)/shard_map/jit(dynamic_index_in_dim)/squeeze | solution.py:354
  0.9 6.1 %collective-permute-start = (f32[256,128]{1,0:T(8,128)S(1)}, f32[256,128]{1,0:T(8,128)S(1)}, u32[]{:S(2)}, u32[]{:S(2)}) collective-permute-start(f32[256,128]{1,0:T(8,128)S(1)} %dynamic-slice_bitcast_fusion), channel_id=1, source_target_pairs={{0,14},{2,12},{4,10},{6,8},{8,6},{10,4},{12,2},{14,0},{1,15},{3,13... | collective-permute-start | bytes 393224 | tf_op jit(solution)/shard_map/ppermute | solution.py:360
  7.0 1.2 %copy-done = f32[2,131072]{1,0:T(2,128)S(1)} copy-done((f32[2,131072]{1,0:T(2,128)S(1)}, f32[2,131072]{1,0:T(2,128)}, u32[]{:S(2)}) %copy-start) | copy-done | bytes 1048600
  8.2 0.1 split_state.1
  8.3 0.3 collective-permute-start.1
  8.6 1.8 %collective-permute-start.3 = (f32[256,128]{1,0:T(8,128)S(1)}, f32[256,128]{1,0:T(8,128)S(1)}, u32[]{:S(2)}, u32[]{:S(2)}) collective-permute-start(f32[256,128]{1,0:T(8,128)S(1)} %get-tuple-element.32), channel_id=1, source_target_pairs={{0,4},{2,6},{4,0},{6,2},{8,12},{10,14},{12,8},{14,10},{1,5},{3,7},... | collective-permute-start | bytes 393224 | tf_op jit(solution)/shard_map/ppermute | solution.py:360
  10.4 3.2 %collective-permute-start.4 = (f32[256,128]{1,0:T(8,128)S(1)}, f32[256,128]{1,0:T(8,128)S(1)}, u32[]{:S(2)}, u32[]{:S(2)}) collective-permute-start(f32[256,128]{1,0:T(8,128)S(1)} %get-tuple-element.34), channel_id=1, source_target_pairs={{0,10},{2,8},{4,14},{6,12},{8,2},{10,0},{12,6},{14,4},{1,11},{3,9}... | collective-permute-start | bytes 393224 | tf_op jit(solution)/shard_map/ppermute | solution.py:360
  13.6 4.3 %collective-permute-start.5 = (f32[256,128]{1,0:T(8,128)S(1)}, f32[256,128]{1,0:T(8,128)S(1)}, u32[]{:S(2)}, u32[]{:S(2)}) collective-permute-start(f32[256,128]{1,0:T(8,128)S(1)} %get-tuple-element.35), channel_id=1, source_target_pairs={{0,8},{2,10},{4,12},{6,14},{8,0},{10,2},{12,4},{14,6},{1,9},{3,11}... | collective-permute-start | bytes 393224 | tf_op jit(solution)/shard_map/ppermute | solution.py:360
  17.9 1.5 %collective-permute-start.6 = (f32[256,128]{1,0:T(8,128)S(1)}, f32[256,128]{1,0:T(8,128)S(1)}, u32[]{:S(2)}, u32[]{:S(2)}) collective-permute-start(f32[256,128]{1,0:T(8,128)S(1)} %get-tuple-element.36), channel_id=1, source_target_pairs={{0,2},{2,0},{4,6},{6,4},{8,10},{10,8},{12,14},{14,12},{1,3},{3,1},... | collective-permute-start | bytes 393224 | tf_op jit(solution)/shard_map/ppermute | solution.py:360
  19.4 0.7 %copy-done.1 = s32[18]{0:T(128)S(1)} copy-done((s32[18]{0:T(128)S(1)}, s32[18]{0:T(128)}, u32[]{:S(2)}) %copy-start.1) | copy-done | bytes 96
  20.1 6.0 %prepare_gates.1 = (bf16[768,256]{1,0:T(8,128)(2,1)S(1)}, bf16[256,768]{1,0:T(8,128)(2,1)S(1)}, bf16[256,768]{1,0:T(8,128)(2,1)S(1)}, bf16[512,1536]{1,0:T(8,128...) custom-call(s32[18]{0:T(128)S(1)} %copy-done.1, ...), custom_call_target="tpu_custom_call" | custom-call | flops 3221225472 | bytes 4194304 | tf_op jit(solution)/shard_map/prepare_gates/pallas_call | solution.py:311
  26.1 0.4 low_gate_early.1.refs_0_
  26.6 0.9 %collective-permute-done.4.refs_1_ = f32[256,128]{1,0:T(8,128)S(1)} collective-permute-done((f32[256,128]{1,0:T(8,128)S(1)}, f32[256,128]{1,0:T(8,128)S(1)}, u32[]{:S(2)}, u32[]{:S(2)}) %collective-permute-start.4) | collective-permute-done | bytes 131104 | tf_op jit(solution)/shard_map/ppermute | solution.py:360
  27.5 1.8 %collective-permute-done.5.refs_2_ = f32[256,128]{1,0:T(8,128)S(1)} collective-permute-done((f32[256,128]{1,0:T(8,128)S(1)}, f32[256,128]{1,0:T(8,128)S(1)}, u32[]{:S(2)}, u32[]{:S(2)}) %collective-permute-start.5) | collective-permute-done | bytes 131104 | tf_op jit(solution)/shard_map/ppermute | solution.py:360
  29.3 2.5 %first_section.1 = (f32[2,4,2,16,128]{4,3,2,1,0:T(8,128)S(1)}, f32[2,4,2,16,128]{4,3,2,1,0:T(8,128)S(1)}, f32[2,4,2,16,128]{4,3,2,1,0:T(8,128)S(1)}, f32[2,4,2,1...) custom-call(f32[2,1024,128]{2,1,0:T(8,128)S(1)} %low_gate_early.1.re, ...), custom_call_target="tpu_custom_call", output_to_operand_aliasing={{8}: (0, {})} | custom-call | flops 2013265920 | bytes 4194304 | tf_op jit(solution)/shard_map/first_section/pallas_call | solution.py:311
  31.8 2.5 %collective-permute-start.7 = (f32[2,4,2,16,128]{4,3,2,1,0:T(8,128)S(1)}, f32[2,4,2,16,128]{4,3,2,1,0:T(8,128)S(1)}, u32[]{:S(2)}, u32[]{:S(2)}) collective-permute-start(f32[2,4,2,16,128]{4,3,2,1,0:T(8,128)S(1)} %get-tuple-element.41), channel_id=1, source_target_pairs={{0,14},{2,12},{4,10},{6,8},{8,6},{10,4},{12,2},{14,0},{1,15},{3,13... | collective-permute-start | bytes 393224 | tf_op jit(solution)/shard_map/ppermute | solution.py:360
  34.3 1.3 %collective-permute-start.8 = (f32[2,4,2,16,128]{4,3,2,1,0:T(8,128)S(1)}, f32[2,4,2,16,128]{4,3,2,1,0:T(8,128)S(1)}, u32[]{:S(2)}, u32[]{:S(2)}) collective-permute-start(f32[2,4,2,16,128]{4,3,2,1,0:T(8,128)S(1)} %get-tuple-element.42), channel_id=1, source_target_pairs={{0,12},{2,14},{4,8},{6,10},{8,4},{10,6},{12,0},{14,2},{1,13},{3,15... | collective-permute-start | bytes 393224 | tf_op jit(solution)/shard_map/ppermute | solution.py:360
  35.6 3.0 %collective-permute-start.10 = (f32[2,4,2,16,128]{4,3,2,1,0:T(8,128)S(1)}, f32[2,4,2,16,128]{4,3,2,1,0:T(8,128)S(1)}, u32[]{:S(2)}, u32[]{:S(2)}) collective-permute-start(f32[2,4,2,16,128]{4,3,2,1,0:T(8,128)S(1)} %get-tuple-element.44), channel_id=1, source_target_pairs={{0,4},{2,6},{4,0},{6,2},{8,12},{10,14},{12,8},{14,10},{1,5},{3,7},... | collective-permute-start | bytes 393224 | tf_op jit(solution)/shard_map/ppermute | solution.py:360
  38.6 1.0 %collective-permute-start.11 = (f32[2,4,2,16,128]{4,3,2,1,0:T(8,128)S(1)}, f32[2,4,2,16,128]{4,3,2,1,0:T(8,128)S(1)}, u32[]{:S(2)}, u32[]{:S(2)}) collective-permute-start(f32[2,4,2,16,128]{4,3,2,1,0:T(8,128)S(1)} %get-tuple-element.45), channel_id=1, source_target_pairs={{0,10},{2,8},{4,14},{6,12},{8,2},{10,0},{12,6},{14,4},{1,11},{3,9}... | collective-permute-start | bytes 393224 | tf_op jit(solution)/shard_map/ppermute | solution.py:360
  39.6 1.1 %collective-permute-done.7.refs_1_ = f32[2,4,2,16,128]{4,3,2,1,0:T(8,128)S(1)} collective-permute-done((f32[2,4,2,16,128]{4,3,2,1,0:T(8,128)S(1)}, f32[2,4,2,16,128]{4,3,2,1,0:T(8,128)S(1)}, u32[]{:S(2)}, u32[]{:S(2)}) %collective-permute-start.7) | collective-permute-done | bytes 131104 | tf_op jit(solution)/shard_map/ppermute | solution.py:360
  40.8 1.8 %collective-permute-start.12 = (f32[2,4,2,16,128]{4,3,2,1,0:T(8,128)S(1)}, f32[2,4,2,16,128]{4,3,2,1,0:T(8,128)S(1)}, u32[]{:S(2)}, u32[]{:S(2)}) collective-permute-start(f32[2,4,2,16,128]{4,3,2,1,0:T(8,128)S(1)} %get-tuple-element.46), channel_id=1, source_target_pairs={{0,8},{2,10},{4,12},{6,14},{8,0},{10,2},{12,4},{14,6},{1,9},{3,11}... | collective-permute-start | bytes 393224 | tf_op jit(solution)/shard_map/ppermute | solution.py:360
  42.5 0.1 collective-permute-done.8.refs_2_
  42.6 1.5 %collective-permute-start.13 = (f32[2,4,2,16,128]{4,3,2,1,0:T(8,128)S(1)}, f32[2,4,2,16,128]{4,3,2,1,0:T(8,128)S(1)}, u32[]{:S(2)}, u32[]{:S(2)}) collective-permute-start(f32[2,4,2,16,128]{4,3,2,1,0:T(8,128)S(1)} %get-tuple-element.47), channel_id=1, source_target_pairs={{0,2},{2,0},{4,6},{6,4},{8,10},{10,8},{12,14},{14,12},{1,3},{3,1},... | collective-permute-start | bytes 393224 | tf_op jit(solution)/shard_map/ppermute | solution.py:360
  44.1 3.7 %collective-permute-done.9.refs_3_ = f32[2,4,2,16,128]{4,3,2,1,0:T(8,128)S(1)} collective-permute-done((f32[2,4,2,16,128]{4,3,2,1,0:T(8,128)S(1)}, f32[2,4,2,16,128]{4,3,2,1,0:T(8,128)S(1)}, u32[]{:S(2)}, u32[]{:S(2)}) %collective-permute-start.9) | collective-permute-done | bytes 131104 | tf_op jit(solution)/shard_map/ppermute | solution.py:360
  47.8 2.6 %collective-permute-done.10.refs_4_ = f32[2,4,2,16,128]{4,3,2,1,0:T(8,128)S(1)} collective-permute-done((f32[2,4,2,16,128]{4,3,2,1,0:T(8,128)S(1)}, f32[2,4,2,16,128]{4,3,2,1,0:T(8,128)S(1)}, u32[]{:S(2)}, u32[]{:S(2)}) %collective-permute-start.10) | collective-permute-done | bytes 131104 | tf_op jit(solution)/shard_map/ppermute | solution.py:360
  50.4 4.1 %collective-permute-done.11.refs_5_ = f32[2,4,2,16,128]{4,3,2,1,0:T(8,128)S(1)} collective-permute-done((f32[2,4,2,16,128]{4,3,2,1,0:T(8,128)S(1)}, f32[2,4,2,16,128]{4,3,2,1,0:T(8,128)S(1)}, u32[]{:S(2)}, u32[]{:S(2)}) %collective-permute-start.11) | collective-permute-done | bytes 131104 | tf_op jit(solution)/shard_map/ppermute | solution.py:360
  54.5 0.4 collective-permute-done.12.refs_6_
  54.9 1.0 %second_section_sent.1 = f32[2,512,128]{2,1,0:T(8,128)S(1)} custom-call(f32[2,4,2,16,128]{4,3,2,1,0:T(8,128)S(1)} %get-tuple-element.40.refs_0_, f32[2,4,2,16,128]{4,3,2,1,0:T(8,128)S(1)} %collective-permute-done.7.refs_1_, f32[2,4,2,16,128]{4,3,2,1,0:T(8,128)S(1)} %collective-permute-done.8.refs_2_, ...), custom_call_target="tpu_custom_call" | custom-call | flops 603979776 | bytes 4194304 | tf_op jit(solution)/shard_map/second_section_sent/pallas_call | solution.py:311
  55.9 0.1 collective-permute-start.14
  56.0 1.0 %second_section_kept.1.kept_ref = f32[2,512,128]{2,1,0:T(8,128)S(1)} custom-call(f32[2,4,2,16,128]{4,3,2,1,0:T(8,128)S(1)} %get-tuple-element.40.refs_0_, f32[2,4,2,16,128]{4,3,2,1,0:T(8,128)S(1)} %collective-permute-done.7.refs_1_, f32[2,4,2,16,128]{4,3,2,1,0:T(8,128)S(1)} %collective-permute-done.8.refs_2_, ...), custom_call_target="tpu_custom_call" | custom-call | flops 603979776 | bytes 4194304 | tf_op jit(solution)/shard_map/second_section_kept/pallas_call | solution.py:311
  57.0 0.9 %collective-permute-done.14.came_ref = f32[2,512,128]{2,1,0:T(8,128)S(1)} collective-permute-done((f32[2,512,128]{2,1,0:T(8,128)S(1)}, f32[2,512,128]{2,1,0:T(8,128)S(1)}, u32[]{:S(2)}, u32[]{:S(2)}) %collective-permute-start.14) | collective-permute-done | bytes 524320 | tf_op jit(solution)/shard_map/ppermute | solution.py:425
  57.9 3.1 %third_section.1 = f32[2048,128]{1,0:T(8,128)} custom-call(f32[2,512,128]{2,1,0:T(8,128)S(1)} %second_section_kept.1.kept_ref, f32[2,512,128]{2,1,0:T(8,128)S(1)} %collective-permute-done.14.came_ref, bf16[256,768]{1,0:T(8,128)(2,1)S(1)} %get-tuple-element.50.refs_0_, bf16[256,768]{1,0:T(8,128)(2,1)S(1)} %get-tuple-element.51.refs_1_, ...), custom_call_target="tpu_custom_call" | custom-call | flops 1610612736 | bytes 4194304 | tf_op jit(solution)/shard_map/third_section/pallas_call | solution.py:311
  (12 shorter events, 0.0 us)
Async XLA Ops:
  0.9 12.7 %collective-permute-start = (f32[256,128]{1,0:T(8,128)S(1)}, f32[256,128]{1,0:T(8,128)S(1)}, u32[]{:S(2)}, u32[]{:S(2)}) collective-permute-start(f32[256,128]{1,0:T(8,128)S(1)} %dynamic-slice_bitcast_fusion), channel_id=1, source_target_pairs={{0,14},{2,12},{4,10},{6,8},{8,6},{10,4},{12,2},{14,0},{1,15},{3,13... | collective-permute-start | bytes 393224 | tf_op jit(solution)/shard_map/ppermute | solution.py:360
  7.0 1.2 %copy-start = (f32[2,131072]{1,0:T(2,128)S(1)}, f32[2,131072]{1,0:T(2,128)}, u32[]{:S(2)}) copy-start(f32[2,131072]{1,0:T(2,128)} %param.3) | copy-start | bytes 3145732
  8.3 9.6 %collective-permute-start.1 = (f32[256,128]{1,0:T(8,128)S(1)}, f32[256,128]{1,0:T(8,128)S(1)}, u32[]{:S(2)}, u32[]{:S(2)}) collective-permute-start(f32[256,128]{1,0:T(8,128)S(1)} %get-tuple-element.30), channel_id=1, source_target_pairs={{0,12},{2,14},{4,8},{6,10},{8,4},{10,6},{12,0},{14,2},{1,13},{3,15... | collective-permute-start | bytes 393224 | tf_op jit(solution)/shard_map/ppermute | solution.py:360
  8.6 17.5 %collective-permute-start.2 = (f32[256,128]{1,0:T(8,128)S(1)}, f32[256,128]{1,0:T(8,128)S(1)}, u32[]{:S(2)}, u32[]{:S(2)}) collective-permute-start(f32[256,128]{1,0:T(8,128)S(1)} %get-tuple-element.31), channel_id=1, source_target_pairs={{0,6},{2,4},{4,2},{6,0},{8,14},{10,12},{12,10},{14,8},{1,7},{3,5},... | collective-permute-start | bytes 393224 | tf_op jit(solution)/shard_map/ppermute | solution.py:360
  8.6 17.6 %collective-permute-start.3 = (f32[256,128]{1,0:T(8,128)S(1)}, f32[256,128]{1,0:T(8,128)S(1)}, u32[]{:S(2)}, u32[]{:S(2)}) collective-permute-start(f32[256,128]{1,0:T(8,128)S(1)} %get-tuple-element.32), channel_id=1, source_target_pairs={{0,4},{2,6},{4,0},{6,2},{8,12},{10,14},{12,8},{14,10},{1,5},{3,7},... | collective-permute-start | bytes 393224 | tf_op jit(solution)/shard_map/ppermute | solution.py:360
  10.4 17.1 %collective-permute-start.4 = (f32[256,128]{1,0:T(8,128)S(1)}, f32[256,128]{1,0:T(8,128)S(1)}, u32[]{:S(2)}, u32[]{:S(2)}) collective-permute-start(f32[256,128]{1,0:T(8,128)S(1)} %get-tuple-element.34), channel_id=1, source_target_pairs={{0,10},{2,8},{4,14},{6,12},{8,2},{10,0},{12,6},{14,4},{1,11},{3,9}... | collective-permute-start | bytes 393224 | tf_op jit(solution)/shard_map/ppermute | solution.py:360
  13.6 15.7 %collective-permute-start.5 = (f32[256,128]{1,0:T(8,128)S(1)}, f32[256,128]{1,0:T(8,128)S(1)}, u32[]{:S(2)}, u32[]{:S(2)}) collective-permute-start(f32[256,128]{1,0:T(8,128)S(1)} %get-tuple-element.35), channel_id=1, source_target_pairs={{0,8},{2,10},{4,12},{6,14},{8,0},{10,2},{12,4},{14,6},{1,9},{3,11}... | collective-permute-start | bytes 393224 | tf_op jit(solution)/shard_map/ppermute | solution.py:360
  17.9 11.4 %collective-permute-start.6 = (f32[256,128]{1,0:T(8,128)S(1)}, f32[256,128]{1,0:T(8,128)S(1)}, u32[]{:S(2)}, u32[]{:S(2)}) collective-permute-start(f32[256,128]{1,0:T(8,128)S(1)} %get-tuple-element.36), channel_id=1, source_target_pairs={{0,2},{2,0},{4,6},{6,4},{8,10},{10,8},{12,14},{14,12},{1,3},{3,1},... | collective-permute-start | bytes 393224 | tf_op jit(solution)/shard_map/ppermute | solution.py:360
  19.4 0.7 %copy-start.1 = (s32[18]{0:T(128)S(1)}, s32[18]{0:T(128)}, u32[]{:S(2)}) copy-start(s32[18]{0:T(128)} %bits_ref.1) | copy-start | bytes 220
  31.8 8.9 %collective-permute-start.7 = (f32[2,4,2,16,128]{4,3,2,1,0:T(8,128)S(1)}, f32[2,4,2,16,128]{4,3,2,1,0:T(8,128)S(1)}, u32[]{:S(2)}, u32[]{:S(2)}) collective-permute-start(f32[2,4,2,16,128]{4,3,2,1,0:T(8,128)S(1)} %get-tuple-element.41), channel_id=1, source_target_pairs={{0,14},{2,12},{4,10},{6,8},{8,6},{10,4},{12,2},{14,0},{1,15},{3,13... | collective-permute-start | bytes 393224 | tf_op jit(solution)/shard_map/ppermute | solution.py:360
  34.3 8.3 %collective-permute-start.8 = (f32[2,4,2,16,128]{4,3,2,1,0:T(8,128)S(1)}, f32[2,4,2,16,128]{4,3,2,1,0:T(8,128)S(1)}, u32[]{:S(2)}, u32[]{:S(2)}) collective-permute-start(f32[2,4,2,16,128]{4,3,2,1,0:T(8,128)S(1)} %get-tuple-element.42), channel_id=1, source_target_pairs={{0,12},{2,14},{4,8},{6,10},{8,4},{10,6},{12,0},{14,2},{1,13},{3,15... | collective-permute-start | bytes 393224 | tf_op jit(solution)/shard_map/ppermute | solution.py:360
  35.6 12.2 %collective-permute-start.9 = (f32[2,4,2,16,128]{4,3,2,1,0:T(8,128)S(1)}, f32[2,4,2,16,128]{4,3,2,1,0:T(8,128)S(1)}, u32[]{:S(2)}, u32[]{:S(2)}) collective-permute-start(f32[2,4,2,16,128]{4,3,2,1,0:T(8,128)S(1)} %get-tuple-element.43), channel_id=1, source_target_pairs={{0,6},{2,4},{4,2},{6,0},{8,14},{10,12},{12,10},{14,8},{1,7},{3,5},... | collective-permute-start | bytes 393224 | tf_op jit(solution)/shard_map/ppermute | solution.py:360
  35.6 14.8 %collective-permute-start.10 = (f32[2,4,2,16,128]{4,3,2,1,0:T(8,128)S(1)}, f32[2,4,2,16,128]{4,3,2,1,0:T(8,128)S(1)}, u32[]{:S(2)}, u32[]{:S(2)}) collective-permute-start(f32[2,4,2,16,128]{4,3,2,1,0:T(8,128)S(1)} %get-tuple-element.44), channel_id=1, source_target_pairs={{0,4},{2,6},{4,0},{6,2},{8,12},{10,14},{12,8},{14,10},{1,5},{3,7},... | collective-permute-start | bytes 393224 | tf_op jit(solution)/shard_map/ppermute | solution.py:360
  38.6 15.9 %collective-permute-start.11 = (f32[2,4,2,16,128]{4,3,2,1,0:T(8,128)S(1)}, f32[2,4,2,16,128]{4,3,2,1,0:T(8,128)S(1)}, u32[]{:S(2)}, u32[]{:S(2)}) collective-permute-start(f32[2,4,2,16,128]{4,3,2,1,0:T(8,128)S(1)} %get-tuple-element.45), channel_id=1, source_target_pairs={{0,10},{2,8},{4,14},{6,12},{8,2},{10,0},{12,6},{14,4},{1,11},{3,9}... | collective-permute-start | bytes 393224 | tf_op jit(solution)/shard_map/ppermute | solution.py:360
  40.8 14.2 %collective-permute-start.12 = (f32[2,4,2,16,128]{4,3,2,1,0:T(8,128)S(1)}, f32[2,4,2,16,128]{4,3,2,1,0:T(8,128)S(1)}, u32[]{:S(2)}, u32[]{:S(2)}) collective-permute-start(f32[2,4,2,16,128]{4,3,2,1,0:T(8,128)S(1)} %get-tuple-element.46), channel_id=1, source_target_pairs={{0,8},{2,10},{4,12},{6,14},{8,0},{10,2},{12,4},{14,6},{1,9},{3,11}... | collective-permute-start | bytes 393224 | tf_op jit(solution)/shard_map/ppermute | solution.py:360
  42.6 12.3 %collective-permute-start.13 = (f32[2,4,2,16,128]{4,3,2,1,0:T(8,128)S(1)}, f32[2,4,2,16,128]{4,3,2,1,0:T(8,128)S(1)}, u32[]{:S(2)}, u32[]{:S(2)}) collective-permute-start(f32[2,4,2,16,128]{4,3,2,1,0:T(8,128)S(1)} %get-tuple-element.47), channel_id=1, source_target_pairs={{0,2},{2,0},{4,6},{6,4},{8,10},{10,8},{12,14},{14,12},{1,3},{3,1},... | collective-permute-start | bytes 393224 | tf_op jit(solution)/shard_map/ppermute | solution.py:360
  55.9 2.0 %copy-start.2 = (bf16[512,1536]{1,0:T(8,128)(2,1)S(1)}, bf16[512,1536]{1,0:T(8,128)(2,1)}, u32[]{:S(2)}) copy-start(bf16[512,1536]{1,0:T(8,128)(2,1)} %get-tuple-element.52.refs_2_) | copy-start | bytes 4718596
  55.9 2.0 %collective-permute-start.14 = (f32[2,512,128]{2,1,0:T(8,128)S(1)}, f32[2,512,128]{2,1,0:T(8,128)S(1)}, u32[]{:S(2)}, u32[]{:S(2)}) collective-permute-start(f32[2,512,128]{2,1,0:T(8,128)S(1)} %second_section_sent.1), channel_id=1, source_target_pairs={{0,1},{1,0},{2,3},{3,2},{4,5},{5,4},{6,7},{7,6},{8,9},{9,8},{10,11... | collective-permute-start | bytes 1572872 | tf_op jit(solution)/shard_map/ppermute | solution.py:425

commit v20 on v17

--- a/solution.py
+++ b/solution.py
@@ -100,6 +100,11 @@
     for index, partner in enumerate(partners_of(count)):
         found = jnp.where(spot == index, partner, found)
     return found
+
+
+def in_groups(matrix):
+    size = matrix.shape[0] // 4
+    return jnp.concatenate([matrix[at * size : (at + 1) * size] for at in (0, 2, 1, 3)], axis=0)
 
 
 def by_source(dim, count):
@@ -170,6 +175,8 @@
                     high, rest = pick_columns(high, order), pick_columns(rest, order)
             elif number == 0 and straight(count) and target is weights[-1]:
                 high, rest = pick_rows(high, into_blocks), pick_rows(rest, into_blocks)
+            elif number == 2 and target is weights[-1]:
+                high, rest = in_groups(high), in_groups(rest)
             target[...] = jnp.concatenate([high, rest, high], axis=1)
     real, imag = product(low)
     high, rest = split(block(real.T, -imag.T))
@@ -192,7 +199,8 @@
 
 
 def split_kernel(x_ref, *outs):
-    for dest, out_ref in zip(partners_of(len(outs)), outs):
+    me, _, *dests = partners_of(len(outs) + 1)
+    for dest, out_ref in zip([me, *dests], outs):
         out_ref[...] = x_ref[dest]
 
 
@@ -217,8 +225,8 @@
     return dim, stride, [h * dim * stride + l for h in range(rows // (dim * stride)) for l in range(stride)]
 
 
-def run_stage(stage, weights_ref, lane_bits, source, target=None, store=None):
-    dim, stride, starts = stage_starts(stage, lane_bits, source.shape[1])
+def stage_load(stage, lane_bits, source):
+    dim, stride, _ = stage_starts(stage, lane_bits, source.shape[1])
 
     def load(part, start):
         if not interleaved(stage):
@@ -228,10 +236,16 @@
             [source[part, pl.ds(start + t * stride, half, stride=2 * stride), :] for t in range(2)], axis=0
         )
 
+    return load
+
+
+def run_stage(stage, weights_ref, lane_bits, source, target=None, store=None):
+    dim, stride, starts = stage_starts(stage, lane_bits, source.shape[1])
+
     def plain(part, start, value):
         target[part, pl.ds(start, dim, stride=stride), :] = value
 
-    apply_stage(weights_ref, starts, load, store or plain)
+    apply_stage(weights_ref, starts, stage_load(stage, lane_bits, source), store or plain)
 
 
 def run_top_stage(stage, weights_ref, lane_bits, source, halves):
@@ -340,20 +354,33 @@
     run_top_stage(stages[0], weights[0], lane_bits, (kept_ref, came_ref), halves[:2])
     done = run_halves(stages[1:-1], weights[1:-1], lane_bits, halves[:2], halves[2:4])
     copies = []
-    for t in range(2):
-        dim, stride, _ = stage_starts(stages[-1], lane_bits, half)
-
-        def store(part, start, value, t=t):
-            results[t][pl.ds(2 * start + part, dim, stride=2 * stride), :] = value
-
-        run_stage(stages[-1], weights[-1], lane_bits, done[t], store=store)
+    dim, stride, starts = stage_starts(stages[-1], lane_bits, half)
+    group = dim // 2
+
+    def put(t, upper, part, start, value):
+        at = 2 * (start + upper * group * stride) + part
+        results[t][pl.ds(at, group, stride=2 * stride), :] = value
+
+    def copy_out(t, first, count):
         size = 2 * half // PIECES
-        for piece in range(PIECES):
+        for piece in range(first, first + count):
             to = out_ref.at[pl.ds(t * 2 * half + piece * size, size)]
             copies.append(
                 pltpu.make_async_copy(results[t].at[pl.ds(piece * size, size)], to, sems.at[t * PIECES + piece])
             )
             copies[-1].start()
+
+    def both_groups(upper, start, value):
+        for part in range(2):
+            put(0, upper, part, start, value[part * group : (part + 1) * group])
+
+    apply_stage(weights[-1], starts, stage_load(stages[-1], lane_bits, done[0]), both_groups)
+    copy_out(0, 0, PIECES)
+    for upper in range(2):
+        rows_ref = weights[-1].at[pl.ds(upper * dim, dim)]
+        store = functools.partial(put, 1, upper)
+        apply_stage(rows_ref, starts, stage_load(stages[-1], lane_bits, done[1]), store)
+        copy_out(1, upper * PIECES // 2, PIECES // 2)
     for copy in copies:
         copy.wait()
 
@@ -397,15 +424,15 @@
     blocks = call(
         split_kernel,
         "split_state",
-        (shape((2 * rows // qa, lanes), F32),) * qa,
+        (shape((2 * rows // qa, lanes), F32),) * (qa - 1),
         [vmem],
         [],
         0,
         state,
     )
 
-    blocks = list(blocks)
-    blocks[1] = lax.dynamic_index_in_dim(state, partners_of(qa)[1], 0, keepdims=False)
+    first = lax.dynamic_index_in_dim(state, partners_of(qa)[1], 0, keepdims=False)
+    blocks = [blocks[0], first, *blocks[1:]]
 
     def exchange(blocks):
         came = [blocks[0]]

time: 61.5 us -> 61.1 us (level)
  starting transfers between devices: 27.7 us -> 30.3 us
  waiting for transfers between devices: 15.1 us -> 12.9 us
  Pallas kernels: 15.6 us -> 14.9 us
    ppermute x14, starting transfers between devices: 27.6 us -> 30.2 us  [exchange(): lax.ppermute(piece, 'qa', [(i, i ^ distance) for i in range(qa)])]
    ppermute x14, waiting for transfers between devices: 14.2 us -> 11.9 us  [exchange(): lax.ppermute(piece, 'qa', [(i, i ^ distance) for i in range(qa)])]
    pallas_call x7, Pallas kernels: 15.6 us -> 14.9 us  [call(): pl.pallas_call(kernel, out_shape=out_shapes, in_specs=in_specs, out_specs...]
  transfers between devices with their start and end apart: 15 -> 15, of which waited for: 8 -> 8; matrix products, arithmetic and copies ran while one was open for 0% -> 0% of each run, Pallas kernels for 15% -> 14%
where the time goes in v20:
time: 61.1 us; the launch traced here: 60.9 us
  starting transfers between devices  30.3 us (50%)
  Pallas kernels  14.9 us (24%)
  waiting for transfers between devices  12.9 us (21%)
  local copies, waits for them, and re-layouts  2.8 us (5%)
    ppermute x14, starting transfers between devices, exchange(): lax.ppermute(piece, 'qa', [(i, i ^ distance) for i in range(qa)])  30.2 us
    pallas_call x7, Pallas kernels, call(): pl.pallas_call(kernel, out_shape=out_shapes, in_specs=in_specs, out_specs...  14.9 us
    ppermute x14, waiting for transfers between devices, exchange(): lax.ppermute(piece, 'qa', [(i, i ^ distance) for i in range(qa)])  11.9 us
    unnamed x6, local copies, waits for them, and re-layouts  1.88 us
  transfers between devices with their start and end apart: 15, of which 8 were waited for; matrix products, arithmetic and copies ran while one was open for 0% of the time, Pallas kernels for 14%

profile of v20, /device:TPU:0, one launch (start us, length us, event | category | flops | bytes accessed | tf_op | source)
XLA Modules:
  0.0 60.9 jit_solution(7045813270624974262)
XLA Ops:
  0.0 0.9 %dynamic-slice_bitcast_fusion = f32[256,128]{1,0:T(8,128)S(1)} fusion(f32[8,256,128]{2,1,0:T(8,128)} %bitcast.12, s32[]{:T(128)S(6)} %select_n.4), kind=kLoop, calls=%fused_computation | loop fusion | bytes 262148 | tf_op jit(solution)/shard_map/jit(dynamic_index_in_dim)/squeeze | solution.py:434
  0.9 6.1 %collective-permute-start = (f32[256,128]{1,0:T(8,128)S(1)}, f32[256,128]{1,0:T(8,128)S(1)}, u32[]{:S(2)}, u32[]{:S(2)}) collective-permute-start(f32[256,128]{1,0:T(8,128)S(1)} %dynamic-slice_bitcast_fusion), channel_id=1, source_target_pairs={{0,14},{2,12},{4,10},{6,8},{8,6},{10,4},{12,2},{14,0},{1,15},{3,13... | collective-permute-start | bytes 393224 | tf_op jit(solution)/shard_map/ppermute | solution.py:440
  7.0 1.2 %copy-done = f32[2,131072]{1,0:T(2,128)S(1)} copy-done((f32[2,131072]{1,0:T(2,128)S(1)}, f32[2,131072]{1,0:T(2,128)}, u32[]{:S(2)}) %copy-start) | copy-done | bytes 1048600
  8.2 0.1 split_state.1
  8.3 0.3 collective-permute-start.1
  8.6 1.8 %collective-permute-start.3 = (f32[256,128]{1,0:T(8,128)S(1)}, f32[256,128]{1,0:T(8,128)S(1)}, u32[]{:S(2)}, u32[]{:S(2)}) collective-permute-start(f32[256,128]{1,0:T(8,128)S(1)} %get-tuple-element.32), channel_id=1, source_target_pairs={{0,4},{2,6},{4,0},{6,2},{8,12},{10,14},{12,8},{14,10},{1,5},{3,7},... | collective-permute-start | bytes 393224 | tf_op jit(solution)/shard_map/ppermute | solution.py:440
  10.4 3.2 %collective-permute-start.4 = (f32[256,128]{1,0:T(8,128)S(1)}, f32[256,128]{1,0:T(8,128)S(1)}, u32[]{:S(2)}, u32[]{:S(2)}) collective-permute-start(f32[256,128]{1,0:T(8,128)S(1)} %get-tuple-element.34), channel_id=1, source_target_pairs={{0,10},{2,8},{4,14},{6,12},{8,2},{10,0},{12,6},{14,4},{1,11},{3,9}... | collective-permute-start | bytes 393224 | tf_op jit(solution)/shard_map/ppermute | solution.py:440
  13.6 4.3 %collective-permute-start.5 = (f32[256,128]{1,0:T(8,128)S(1)}, f32[256,128]{1,0:T(8,128)S(1)}, u32[]{:S(2)}, u32[]{:S(2)}) collective-permute-start(f32[256,128]{1,0:T(8,128)S(1)} %get-tuple-element.35), channel_id=1, source_target_pairs={{0,8},{2,10},{4,12},{6,14},{8,0},{10,2},{12,4},{14,6},{1,9},{3,11}... | collective-permute-start | bytes 393224 | tf_op jit(solution)/shard_map/ppermute | solution.py:440
  17.9 1.5 %collective-permute-start.6 = (f32[256,128]{1,0:T(8,128)S(1)}, f32[256,128]{1,0:T(8,128)S(1)}, u32[]{:S(2)}, u32[]{:S(2)}) collective-permute-start(f32[256,128]{1,0:T(8,128)S(1)} %get-tuple-element.36), channel_id=1, source_target_pairs={{0,2},{2,0},{4,6},{6,4},{8,10},{10,8},{12,14},{14,12},{1,3},{3,1},... | collective-permute-start | bytes 393224 | tf_op jit(solution)/shard_map/ppermute | solution.py:440
  19.4 0.7 %copy-done.1 = s32[18]{0:T(128)S(1)} copy-done((s32[18]{0:T(128)S(1)}, s32[18]{0:T(128)}, u32[]{:S(2)}) %copy-start.1) | copy-done | bytes 96
  20.1 7.0 %prepare_gates.1 = (bf16[768,256]{1,0:T(8,128)(2,1)S(1)}, bf16[256,768]{1,0:T(8,128)(2,1)S(1)}, bf16[256,768]{1,0:T(8,128)(2,1)S(1)}, bf16[512,1536]{1,0:T(8,128...) custom-call(s32[18]{0:T(128)S(1)} %copy-done.1, ...), custom_call_target="tpu_custom_call" | custom-call | flops 3221225472 | bytes 4194304 | tf_op jit(solution)/shard_map/prepare_gates/pallas_call | solution.py:391
  27.1 0.4 low_gate_early.1.refs_0_
  27.5 0.0 collective-permute-done.4.refs_1_
  27.5 1.8 %collective-permute-done.5.refs_2_ = f32[256,128]{1,0:T(8,128)S(1)} collective-permute-done((f32[256,128]{1,0:T(8,128)S(1)}, f32[256,128]{1,0:T(8,128)S(1)}, u32[]{:S(2)}, u32[]{:S(2)}) %collective-permute-start.5) | collective-permute-done | bytes 131104 | tf_op jit(solution)/shard_map/ppermute | solution.py:440
  29.3 2.5 %first_section.1 = (f32[2,2,4,16,128]{4,3,2,1,0:T(8,128)S(1)}, f32[2,2,4,16,128]{4,3,2,1,0:T(8,128)S(1)}, f32[2,2,4,16,128]{4,3,2,1,0:T(8,128)S(1)}, f32[2,2,4,1...) custom-call(f32[2,1024,128]{2,1,0:T(8,128)S(1)} %low_gate_early.1.re, ...), custom_call_target="tpu_custom_call", output_to_operand_aliasing={{8}: (0, {})} | custom-call | flops 2013265920 | bytes 4194304 | tf_op jit(solution)/shard_map/first_section/pallas_call | solution.py:391
  31.8 2.5 %collective-permute-start.7 = (f32[2,2,4,16,128]{4,3,2,1,0:T(8,128)S(1)}, f32[2,2,4,16,128]{4,3,2,1,0:T(8,128)S(1)}, u32[]{:S(2)}, u32[]{:S(2)}) collective-permute-start(f32[2,2,4,16,128]{4,3,2,1,0:T(8,128)S(1)} %get-tuple-element.41), channel_id=1, source_target_pairs={{0,14},{2,12},{4,10},{6,8},{8,6},{10,4},{12,2},{14,0},{1,15},{3,13... | collective-permute-start | bytes 393224 | tf_op jit(solution)/shard_map/ppermute | solution.py:440
  34.3 1.3 %collective-permute-start.8 = (f32[2,2,4,16,128]{4,3,2,1,0:T(8,128)S(1)}, f32[2,2,4,16,128]{4,3,2,1,0:T(8,128)S(1)}, u32[]{:S(2)}, u32[]{:S(2)}) collective-permute-start(f32[2,2,4,16,128]{4,3,2,1,0:T(8,128)S(1)} %get-tuple-element.42), channel_id=1, source_target_pairs={{0,12},{2,14},{4,8},{6,10},{8,4},{10,6},{12,0},{14,2},{1,13},{3,15... | collective-permute-start | bytes 393224 | tf_op jit(solution)/shard_map/ppermute | solution.py:440
  35.6 3.0 %collective-permute-start.10 = (f32[2,2,4,16,128]{4,3,2,1,0:T(8,128)S(1)}, f32[2,2,4,16,128]{4,3,2,1,0:T(8,128)S(1)}, u32[]{:S(2)}, u32[]{:S(2)}) collective-permute-start(f32[2,2,4,16,128]{4,3,2,1,0:T(8,128)S(1)} %get-tuple-element.44), channel_id=1, source_target_pairs={{0,4},{2,6},{4,0},{6,2},{8,12},{10,14},{12,8},{14,10},{1,5},{3,7},... | collective-permute-start | bytes 393224 | tf_op jit(solution)/shard_map/ppermute | solution.py:440
  38.6 1.0 %collective-permute-start.11 = (f32[2,2,4,16,128]{4,3,2,1,0:T(8,128)S(1)}, f32[2,2,4,16,128]{4,3,2,1,0:T(8,128)S(1)}, u32[]{:S(2)}, u32[]{:S(2)}) collective-permute-start(f32[2,2,4,16,128]{4,3,2,1,0:T(8,128)S(1)} %get-tuple-element.45), channel_id=1, source_target_pairs={{0,10},{2,8},{4,14},{6,12},{8,2},{10,0},{12,6},{14,4},{1,11},{3,9}... | collective-permute-start | bytes 393224 | tf_op jit(solution)/shard_map/ppermute | solution.py:440
  39.6 1.1 %collective-permute-done.7.refs_1_ = f32[2,2,4,16,128]{4,3,2,1,0:T(8,128)S(1)} collective-permute-done((f32[2,2,4,16,128]{4,3,2,1,0:T(8,128)S(1)}, f32[2,2,4,16,128]{4,3,2,1,0:T(8,128)S(1)}, u32[]{:S(2)}, u32[]{:S(2)}) %collective-permute-start.7) | collective-permute-done | bytes 131104 | tf_op jit(solution)/shard_map/ppermute | solution.py:440
  40.7 1.8 %collective-permute-start.12 = (f32[2,2,4,16,128]{4,3,2,1,0:T(8,128)S(1)}, f32[2,2,4,16,128]{4,3,2,1,0:T(8,128)S(1)}, u32[]{:S(2)}, u32[]{:S(2)}) collective-permute-start(f32[2,2,4,16,128]{4,3,2,1,0:T(8,128)S(1)} %get-tuple-element.46), channel_id=1, source_target_pairs={{0,8},{2,10},{4,12},{6,14},{8,0},{10,2},{12,4},{14,6},{1,9},{3,11}... | collective-permute-start | bytes 393224 | tf_op jit(solution)/shard_map/ppermute | solution.py:440
  42.5 0.1 collective-permute-done.8.refs_2_
  42.6 3.4 %collective-permute-start.13 = (f32[2,2,4,16,128]{4,3,2,1,0:T(8,128)S(1)}, f32[2,2,4,16,128]{4,3,2,1,0:T(8,128)S(1)}, u32[]{:S(2)}, u32[]{:S(2)}) collective-permute-start(f32[2,2,4,16,128]{4,3,2,1,0:T(8,128)S(1)} %get-tuple-element.47), channel_id=1, source_target_pairs={{0,2},{2,0},{4,6},{6,4},{8,10},{10,8},{12,14},{14,12},{1,3},{3,1},... | collective-permute-start | bytes 393224 | tf_op jit(solution)/shard_map/ppermute | solution.py:440
  45.9 1.8 %collective-permute-done.9.refs_3_ = f32[2,2,4,16,128]{4,3,2,1,0:T(8,128)S(1)} collective-permute-done((f32[2,2,4,16,128]{4,3,2,1,0:T(8,128)S(1)}, f32[2,2,4,16,128]{4,3,2,1,0:T(8,128)S(1)}, u32[]{:S(2)}, u32[]{:S(2)}) %collective-permute-start.9) | collective-permute-done | bytes 131104 | tf_op jit(solution)/shard_map/ppermute | solution.py:440
  47.8 2.6 %collective-permute-done.10.refs_4_ = f32[2,2,4,16,128]{4,3,2,1,0:T(8,128)S(1)} collective-permute-done((f32[2,2,4,16,128]{4,3,2,1,0:T(8,128)S(1)}, f32[2,2,4,16,128]{4,3,2,1,0:T(8,128)S(1)}, u32[]{:S(2)}, u32[]{:S(2)}) %collective-permute-start.10) | collective-permute-done | bytes 131104 | tf_op jit(solution)/shard_map/ppermute | solution.py:440
  50.4 4.1 %collective-permute-done.11.refs_5_ = f32[2,2,4,16,128]{4,3,2,1,0:T(8,128)S(1)} collective-permute-done((f32[2,2,4,16,128]{4,3,2,1,0:T(8,128)S(1)}, f32[2,2,4,16,128]{4,3,2,1,0:T(8,128)S(1)}, u32[]{:S(2)}, u32[]{:S(2)}) %collective-permute-start.11) | collective-permute-done | bytes 131104 | tf_op jit(solution)/shard_map/ppermute | solution.py:440
  54.5 0.4 collective-permute-done.12.refs_6_
  54.9 1.0 %second_section_sent.1 = f32[2,512,128]{2,1,0:T(8,128)S(1)} custom-call(f32[2,2,4,16,128]{4,3,2,1,0:T(8,128)S(1)} %get-tuple-element.40.refs_0_, f32[2,2,4,16,128]{4,3,2,1,0:T(8,128)S(1)} %collective-permute-done.7.refs_1_, f32[2,2,4,16,128]{4,3,2,1,0:T(8,128)S(1)} %collective-permute-done.8.refs_2_, ...), custom_call_target="tpu_custom_call" | custom-call | flops 603979776 | bytes 4194304 | tf_op jit(solution)/shard_map/second_section_sent/pallas_call | solution.py:391
  55.9 0.1 collective-permute-start.14
  56.0 1.0 %second_section_kept.1.kept_ref = f32[2,512,128]{2,1,0:T(8,128)S(1)} custom-call(f32[2,2,4,16,128]{4,3,2,1,0:T(8,128)S(1)} %get-tuple-element.40.refs_0_, f32[2,2,4,16,128]{4,3,2,1,0:T(8,128)S(1)} %collective-permute-done.7.refs_1_, f32[2,2,4,16,128]{4,3,2,1,0:T(8,128)S(1)} %collective-permute-done.8.refs_2_, ...), custom_call_target="tpu_custom_call" | custom-call | flops 603979776 | bytes 4194304 | tf_op jit(solution)/shard_map/second_section_kept/pallas_call | solution.py:391
  56.9 0.9 %collective-permute-done.14.came_ref = f32[2,512,128]{2,1,0:T(8,128)S(1)} collective-permute-done((f32[2,512,128]{2,1,0:T(8,128)S(1)}, f32[2,512,128]{2,1,0:T(8,128)S(1)}, u32[]{:S(2)}, u32[]{:S(2)}) %collective-permute-start.14) | collective-permute-done | bytes 524320 | tf_op jit(solution)/shard_map/ppermute | solution.py:505
  57.9 3.1 %third_section.1 = f32[2048,128]{1,0:T(8,128)} custom-call(f32[2,512,128]{2,1,0:T(8,128)S(1)} %second_section_kept.1.kept_ref, f32[2,512,128]{2,1,0:T(8,128)S(1)} %collective-permute-done.14.came_ref, bf16[256,768]{1,0:T(8,128)(2,1)S(1)} %get-tuple-element.50.refs_0_, bf16[256,768]{1,0:T(8,128)(2,1)S(1)} %get-tuple-element.51.refs_1_, ...), custom_call_target="tpu_custom_call" | custom-call | flops 1610612736 | bytes 4194304 | tf_op jit(solution)/shard_map/third_section/pallas_call | solution.py:391
  (12 shorter events, 0.0 us)
Async XLA Ops:
  0.9 12.7 %collective-permute-start = (f32[256,128]{1,0:T(8,128)S(1)}, f32[256,128]{1,0:T(8,128)S(1)}, u32[]{:S(2)}, u32[]{:S(2)}) collective-permute-start(f32[256,128]{1,0:T(8,128)S(1)} %dynamic-slice_bitcast_fusion), channel_id=1, source_target_pairs={{0,14},{2,12},{4,10},{6,8},{8,6},{10,4},{12,2},{14,0},{1,15},{3,13... | collective-permute-start | bytes 393224 | tf_op jit(solution)/shard_map/ppermute | solution.py:440
  7.0 1.2 %copy-start = (f32[2,131072]{1,0:T(2,128)S(1)}, f32[2,131072]{1,0:T(2,128)}, u32[]{:S(2)}) copy-start(f32[2,131072]{1,0:T(2,128)} %param.3) | copy-start | bytes 3145732
  8.3 9.6 %collective-permute-start.1 = (f32[256,128]{1,0:T(8,128)S(1)}, f32[256,128]{1,0:T(8,128)S(1)}, u32[]{:S(2)}, u32[]{:S(2)}) collective-permute-start(f32[256,128]{1,0:T(8,128)S(1)} %get-tuple-element.30), channel_id=1, source_target_pairs={{0,12},{2,14},{4,8},{6,10},{8,4},{10,6},{12,0},{14,2},{1,13},{3,15... | collective-permute-start | bytes 393224 | tf_op jit(solution)/shard_map/ppermute | solution.py:440
  8.6 18.5 %collective-permute-start.2 = (f32[256,128]{1,0:T(8,128)S(1)}, f32[256,128]{1,0:T(8,128)S(1)}, u32[]{:S(2)}, u32[]{:S(2)}) collective-permute-start(f32[256,128]{1,0:T(8,128)S(1)} %get-tuple-element.31), channel_id=1, source_target_pairs={{0,6},{2,4},{4,2},{6,0},{8,14},{10,12},{12,10},{14,8},{1,7},{3,5},... | collective-permute-start | bytes 393224 | tf_op jit(solution)/shard_map/ppermute | solution.py:440
  8.6 18.5 %collective-permute-start.3 = (f32[256,128]{1,0:T(8,128)S(1)}, f32[256,128]{1,0:T(8,128)S(1)}, u32[]{:S(2)}, u32[]{:S(2)}) collective-permute-start(f32[256,128]{1,0:T(8,128)S(1)} %get-tuple-element.32), channel_id=1, source_target_pairs={{0,4},{2,6},{4,0},{6,2},{8,12},{10,14},{12,8},{14,10},{1,5},{3,7},... | collective-permute-start | bytes 393224 | tf_op jit(solution)/shard_map/ppermute | solution.py:440
  10.4 17.1 %collective-permute-start.4 = (f32[256,128]{1,0:T(8,128)S(1)}, f32[256,128]{1,0:T(8,128)S(1)}, u32[]{:S(2)}, u32[]{:S(2)}) collective-permute-start(f32[256,128]{1,0:T(8,128)S(1)} %get-tuple-element.34), channel_id=1, source_target_pairs={{0,10},{2,8},{4,14},{6,12},{8,2},{10,0},{12,6},{14,4},{1,11},{3,9}... | collective-permute-start | bytes 393224 | tf_op jit(solution)/shard_map/ppermute | solution.py:440
  13.6 15.7 %collective-permute-start.5 = (f32[256,128]{1,0:T(8,128)S(1)}, f32[256,128]{1,0:T(8,128)S(1)}, u32[]{:S(2)}, u32[]{:S(2)}) collective-permute-start(f32[256,128]{1,0:T(8,128)S(1)} %get-tuple-element.35), channel_id=1, source_target_pairs={{0,8},{2,10},{4,12},{6,14},{8,0},{10,2},{12,4},{14,6},{1,9},{3,11}... | collective-permute-start | bytes 393224 | tf_op jit(solution)/shard_map/ppermute | solution.py:440
  17.9 11.4 %collective-permute-start.6 = (f32[256,128]{1,0:T(8,128)S(1)}, f32[256,128]{1,0:T(8,128)S(1)}, u32[]{:S(2)}, u32[]{:S(2)}) collective-permute-start(f32[256,128]{1,0:T(8,128)S(1)} %get-tuple-element.36), channel_id=1, source_target_pairs={{0,2},{2,0},{4,6},{6,4},{8,10},{10,8},{12,14},{14,12},{1,3},{3,1},... | collective-permute-start | bytes 393224 | tf_op jit(solution)/shard_map/ppermute | solution.py:440
  19.4 0.7 %copy-start.1 = (s32[18]{0:T(128)S(1)}, s32[18]{0:T(128)}, u32[]{:S(2)}) copy-start(s32[18]{0:T(128)} %bits_ref.1) | copy-start | bytes 220
  31.8 8.9 %collective-permute-start.7 = (f32[2,2,4,16,128]{4,3,2,1,0:T(8,128)S(1)}, f32[2,2,4,16,128]{4,3,2,1,0:T(8,128)S(1)}, u32[]{:S(2)}, u32[]{:S(2)}) collective-permute-start(f32[2,2,4,16,128]{4,3,2,1,0:T(8,128)S(1)} %get-tuple-element.41), channel_id=1, source_target_pairs={{0,14},{2,12},{4,10},{6,8},{8,6},{10,4},{12,2},{14,0},{1,15},{3,13... | collective-permute-start | bytes 393224 | tf_op jit(solution)/shard_map/ppermute | solution.py:440
  34.3 8.3 %collective-permute-start.8 = (f32[2,2,4,16,128]{4,3,2,1,0:T(8,128)S(1)}, f32[2,2,4,16,128]{4,3,2,1,0:T(8,128)S(1)}, u32[]{:S(2)}, u32[]{:S(2)}) collective-permute-start(f32[2,2,4,16,128]{4,3,2,1,0:T(8,128)S(1)} %get-tuple-element.42), channel_id=1, source_target_pairs={{0,12},{2,14},{4,8},{6,10},{8,4},{10,6},{12,0},{14,2},{1,13},{3,15... | collective-permute-start | bytes 393224 | tf_op jit(solution)/shard_map/ppermute | solution.py:440
  35.6 12.2 %collective-permute-start.9 = (f32[2,2,4,16,128]{4,3,2,1,0:T(8,128)S(1)}, f32[2,2,4,16,128]{4,3,2,1,0:T(8,128)S(1)}, u32[]{:S(2)}, u32[]{:S(2)}) collective-permute-start(f32[2,2,4,16,128]{4,3,2,1,0:T(8,128)S(1)} %get-tuple-element.43), channel_id=1, source_target_pairs={{0,6},{2,4},{4,2},{6,0},{8,14},{10,12},{12,10},{14,8},{1,7},{3,5},... | collective-permute-start | bytes 393224 | tf_op jit(solution)/shard_map/ppermute | solution.py:440
  35.6 14.8 %collective-permute-start.10 = (f32[2,2,4,16,128]{4,3,2,1,0:T(8,128)S(1)}, f32[2,2,4,16,128]{4,3,2,1,0:T(8,128)S(1)}, u32[]{:S(2)}, u32[]{:S(2)}) collective-permute-start(f32[2,2,4,16,128]{4,3,2,1,0:T(8,128)S(1)} %get-tuple-element.44), channel_id=1, source_target_pairs={{0,4},{2,6},{4,0},{6,2},{8,12},{10,14},{12,8},{14,10},{1,5},{3,7},... | collective-permute-start | bytes 393224 | tf_op jit(solution)/shard_map/ppermute | solution.py:440
  38.6 15.9 %collective-permute-start.11 = (f32[2,2,4,16,128]{4,3,2,1,0:T(8,128)S(1)}, f32[2,2,4,16,128]{4,3,2,1,0:T(8,128)S(1)}, u32[]{:S(2)}, u32[]{:S(2)}) collective-permute-start(f32[2,2,4,16,128]{4,3,2,1,0:T(8,128)S(1)} %get-tuple-element.45), channel_id=1, source_target_pairs={{0,10},{2,8},{4,14},{6,12},{8,2},{10,0},{12,6},{14,4},{1,11},{3,9}... | collective-permute-start | bytes 393224 | tf_op jit(solution)/shard_map/ppermute | solution.py:440
  40.7 14.2 %collective-permute-start.12 = (f32[2,2,4,16,128]{4,3,2,1,0:T(8,128)S(1)}, f32[2,2,4,16,128]{4,3,2,1,0:T(8,128)S(1)}, u32[]{:S(2)}, u32[]{:S(2)}) collective-permute-start(f32[2,2,4,16,128]{4,3,2,1,0:T(8,128)S(1)} %get-tuple-element.46), channel_id=1, source_target_pairs={{0,8},{2,10},{4,12},{6,14},{8,0},{10,2},{12,4},{14,6},{1,9},{3,11}... | collective-permute-start | bytes 393224 | tf_op jit(solution)/shard_map/ppermute | solution.py:440
  42.6 12.3 %collective-permute-start.13 = (f32[2,2,4,16,128]{4,3,2,1,0:T(8,128)S(1)}, f32[2,2,4,16,128]{4,3,2,1,0:T(8,128)S(1)}, u32[]{:S(2)}, u32[]{:S(2)}) collective-permute-start(f32[2,2,4,16,128]{4,3,2,1,0:T(8,128)S(1)} %get-tuple-element.47), channel_id=1, source_target_pairs={{0,2},{2,0},{4,6},{6,4},{8,10},{10,8},{12,14},{14,12},{1,3},{3,1},... | collective-permute-start | bytes 393224 | tf_op jit(solution)/shard_map/ppermute | solution.py:440
  55.9 2.0 %copy-start.2 = (bf16[512,1536]{1,0:T(8,128)(2,1)S(1)}, bf16[512,1536]{1,0:T(8,128)(2,1)}, u32[]{:S(2)}) copy-start(bf16[512,1536]{1,0:T(8,128)(2,1)} %get-tuple-element.52.refs_2_) | copy-start | bytes 4718596
  55.9 2.0 %collective-permute-start.14 = (f32[2,512,128]{2,1,0:T(8,128)S(1)}, f32[2,512,128]{2,1,0:T(8,128)S(1)}, u32[]{:S(2)}, u32[]{:S(2)}) collective-permute-start(f32[2,512,128]{2,1,0:T(8,128)S(1)} %second_section_sent.1), channel_id=1, source_target_pairs={{0,1},{1,0},{2,3},{3,2},{4,5},{5,4},{6,7},{7,6},{8,9},{9,8},{10,11... | collective-permute-start | bytes 1572872 | tf_op jit(solution)/shard_map/ppermute | solution.py:505

commit v21 on v19

--- a/solution.py
+++ b/solution.py
@@ -148,7 +148,7 @@
     far, near = list(range(count - 1, half - 1, -1)), list(range(half - 1, 0, -1))
     order = [0]
     while far or near:
-        order += far[:2] + near[:2]
+        order += sorted(far[:2]) + sorted(near[:2])
         far, near = far[2:], near[2:]
     return order
 

time: 61.2 us -> 61.2 us (level)
  waiting for transfers between devices: 15.6 us -> 17.9 us
  starting transfers between devices: 28.4 us -> 26.2 us
    ppermute x14, waiting for transfers between devices: 14.8 us -> 17 us  [exchange(): lax.ppermute(piece, 'qa', [(i, i ^ distance) for i in range(qa)])]
    ppermute x14, starting transfers between devices: 28.3 us -> 26.2 us  [exchange(): lax.ppermute(piece, 'qa', [(i, i ^ distance) for i in range(qa)])]
  transfers between devices with their start and end apart: 15 -> 15, of which waited for: 9 -> 8; matrix products, arithmetic and copies ran while one was open for 0% -> 0% of each run, Pallas kernels for 12% -> 12%
where the time goes in v21:
time: 61.2 us; the launch traced here: 61 us
  starting transfers between devices  26.2 us (43%)
  waiting for transfers between devices  17.9 us (29%)
  Pallas kernels  14 us (23%)
  local copies, waits for them, and re-layouts  2.8 us (5%)
    ppermute x14, starting transfers between devices, exchange(): lax.ppermute(piece, 'qa', [(i, i ^ distance) for i in range(qa)])  26.2 us
    ppermute x14, waiting for transfers between devices, exchange(): lax.ppermute(piece, 'qa', [(i, i ^ distance) for i in range(qa)])  17 us
    pallas_call x7, Pallas kernels, call(): pl.pallas_call(kernel, out_shape=out_shapes, in_specs=in_specs, out_specs...  14 us
    unnamed x6, local copies, waits for them, and re-layouts  1.88 us
  transfers between devices with their start and end apart: 15, of which 8 were waited for; matrix products, arithmetic and copies ran while one was open for 0% of the time, Pallas kernels for 12%

profile of v21, /device:TPU:0, one launch (start us, length us, event | category | flops | bytes accessed | tf_op | source)
XLA Modules:
  0.0 61.0 jit_solution(16319355652207111344)
XLA Ops:
  0.0 0.9 %dynamic-slice_bitcast_fusion = f32[256,128]{1,0:T(8,128)S(1)} fusion(f32[8,256,128]{2,1,0:T(8,128)} %bitcast.12, s32[]{:T(128)S(6)} %select_n.4), kind=kLoop, calls=%fused_computation | loop fusion | bytes 262148 | tf_op jit(solution)/shard_map/jit(dynamic_index_in_dim)/squeeze | solution.py:354
  0.9 5.1 %collective-permute-start = (f32[256,128]{1,0:T(8,128)S(1)}, f32[256,128]{1,0:T(8,128)S(1)}, u32[]{:S(2)}, u32[]{:S(2)}) collective-permute-start(f32[256,128]{1,0:T(8,128)S(1)} %dynamic-slice_bitcast_fusion), channel_id=1, source_target_pairs={{0,12},{2,14},{4,8},{6,10},{8,4},{10,6},{12,0},{14,2},{1,13},{3,15... | collective-permute-start | bytes 393224 | tf_op jit(solution)/shard_map/ppermute | solution.py:360
  6.0 1.2 %copy-done = f32[2,131072]{1,0:T(2,128)S(1)} copy-done((f32[2,131072]{1,0:T(2,128)S(1)}, f32[2,131072]{1,0:T(2,128)}, u32[]{:S(2)}) %copy-start) | copy-done | bytes 1048600
  7.3 0.1 split_state.1
  7.3 1.2 %collective-permute-start.1 = (f32[256,128]{1,0:T(8,128)S(1)}, f32[256,128]{1,0:T(8,128)S(1)}, u32[]{:S(2)}, u32[]{:S(2)}) collective-permute-start(f32[256,128]{1,0:T(8,128)S(1)} %get-tuple-element.30), channel_id=1, source_target_pairs={{0,14},{2,12},{4,10},{6,8},{8,6},{10,4},{12,2},{14,0},{1,15},{3,13... | collective-permute-start | bytes 393224 | tf_op jit(solution)/shard_map/ppermute | solution.py:360
  8.6 0.0 collective-permute-start.2
  8.6 1.9 %collective-permute-start.3 = (f32[256,128]{1,0:T(8,128)S(1)}, f32[256,128]{1,0:T(8,128)S(1)}, u32[]{:S(2)}, u32[]{:S(2)}) collective-permute-start(f32[256,128]{1,0:T(8,128)S(1)} %get-tuple-element.32), channel_id=1, source_target_pairs={{0,6},{2,4},{4,2},{6,0},{8,14},{10,12},{12,10},{14,8},{1,7},{3,5},... | collective-permute-start | bytes 393224 | tf_op jit(solution)/shard_map/ppermute | solution.py:360
  10.4 2.3 %collective-permute-start.4 = (f32[256,128]{1,0:T(8,128)S(1)}, f32[256,128]{1,0:T(8,128)S(1)}, u32[]{:S(2)}, u32[]{:S(2)}) collective-permute-start(f32[256,128]{1,0:T(8,128)S(1)} %get-tuple-element.34), channel_id=1, source_target_pairs={{0,8},{2,10},{4,12},{6,14},{8,0},{10,2},{12,4},{14,6},{1,9},{3,11}... | collective-permute-start | bytes 393224 | tf_op jit(solution)/shard_map/ppermute | solution.py:360
  12.7 5.2 %collective-permute-start.5 = (f32[256,128]{1,0:T(8,128)S(1)}, f32[256,128]{1,0:T(8,128)S(1)}, u32[]{:S(2)}, u32[]{:S(2)}) collective-permute-start(f32[256,128]{1,0:T(8,128)S(1)} %get-tuple-element.35), channel_id=1, source_target_pairs={{0,10},{2,8},{4,14},{6,12},{8,2},{10,0},{12,6},{14,4},{1,11},{3,9}... | collective-permute-start | bytes 393224 | tf_op jit(solution)/shard_map/ppermute | solution.py:360
  18.0 0.1 collective-permute-start.6
  18.1 0.7 %copy-done.1 = s32[18]{0:T(128)S(1)} copy-done((s32[18]{0:T(128)S(1)}, s32[18]{0:T(128)}, u32[]{:S(2)}) %copy-start.1) | copy-done | bytes 96
  18.7 6.0 %prepare_gates.1 = (bf16[768,256]{1,0:T(8,128)(2,1)S(1)}, bf16[256,768]{1,0:T(8,128)(2,1)S(1)}, bf16[256,768]{1,0:T(8,128)(2,1)S(1)}, bf16[512,1536]{1,0:T(8,128...) custom-call(s32[18]{0:T(128)S(1)} %copy-done.1, ...), custom_call_target="tpu_custom_call" | custom-call | flops 3221225472 | bytes 4194304 | tf_op jit(solution)/shard_map/prepare_gates/pallas_call | solution.py:311
  24.8 0.4 low_gate_early.1.refs_0_
  25.2 1.3 %collective-permute-done.4.refs_1_ = f32[256,128]{1,0:T(8,128)S(1)} collective-permute-done((f32[256,128]{1,0:T(8,128)S(1)}, f32[256,128]{1,0:T(8,128)S(1)}, u32[]{:S(2)}, u32[]{:S(2)}) %collective-permute-start.4) | collective-permute-done | bytes 131104 | tf_op jit(solution)/shard_map/ppermute | solution.py:360
  26.5 2.8 %collective-permute-done.5.refs_2_ = f32[256,128]{1,0:T(8,128)S(1)} collective-permute-done((f32[256,128]{1,0:T(8,128)S(1)}, f32[256,128]{1,0:T(8,128)S(1)}, u32[]{:S(2)}, u32[]{:S(2)}) %collective-permute-start.5) | collective-permute-done | bytes 131104 | tf_op jit(solution)/shard_map/ppermute | solution.py:360
  29.3 2.5 %first_section.1 = (f32[2,4,2,16,128]{4,3,2,1,0:T(8,128)S(1)}, f32[2,4,2,16,128]{4,3,2,1,0:T(8,128)S(1)}, f32[2,4,2,16,128]{4,3,2,1,0:T(8,128)S(1)}, f32[2,4,2,1...) custom-call(f32[2,1024,128]{2,1,0:T(8,128)S(1)} %low_gate_early.1.re, ...), custom_call_target="tpu_custom_call", output_to_operand_aliasing={{8}: (0, {})} | custom-call | flops 2013265920 | bytes 4194304 | tf_op jit(solution)/shard_map/first_section/pallas_call | solution.py:311
  31.8 2.5 %collective-permute-start.7 = (f32[2,4,2,16,128]{4,3,2,1,0:T(8,128)S(1)}, f32[2,4,2,16,128]{4,3,2,1,0:T(8,128)S(1)}, u32[]{:S(2)}, u32[]{:S(2)}) collective-permute-start(f32[2,4,2,16,128]{4,3,2,1,0:T(8,128)S(1)} %get-tuple-element.41), channel_id=1, source_target_pairs={{0,12},{2,14},{4,8},{6,10},{8,4},{10,6},{12,0},{14,2},{1,13},{3,15... | collective-permute-start | bytes 393224 | tf_op jit(solution)/shard_map/ppermute | solution.py:360
  34.4 1.3 %collective-permute-start.8 = (f32[2,4,2,16,128]{4,3,2,1,0:T(8,128)S(1)}, f32[2,4,2,16,128]{4,3,2,1,0:T(8,128)S(1)}, u32[]{:S(2)}, u32[]{:S(2)}) collective-permute-start(f32[2,4,2,16,128]{4,3,2,1,0:T(8,128)S(1)} %get-tuple-element.42), channel_id=1, source_target_pairs={{0,14},{2,12},{4,10},{6,8},{8,6},{10,4},{12,2},{14,0},{1,15},{3,13... | collective-permute-start | bytes 393224 | tf_op jit(solution)/shard_map/ppermute | solution.py:360
  35.6 3.0 %collective-permute-start.10 = (f32[2,4,2,16,128]{4,3,2,1,0:T(8,128)S(1)}, f32[2,4,2,16,128]{4,3,2,1,0:T(8,128)S(1)}, u32[]{:S(2)}, u32[]{:S(2)}) collective-permute-start(f32[2,4,2,16,128]{4,3,2,1,0:T(8,128)S(1)} %get-tuple-element.44), channel_id=1, source_target_pairs={{0,6},{2,4},{4,2},{6,0},{8,14},{10,12},{12,10},{14,8},{1,7},{3,5},... | collective-permute-start | bytes 393224 | tf_op jit(solution)/shard_map/ppermute | solution.py:360
  38.6 1.0 %collective-permute-start.11 = (f32[2,4,2,16,128]{4,3,2,1,0:T(8,128)S(1)}, f32[2,4,2,16,128]{4,3,2,1,0:T(8,128)S(1)}, u32[]{:S(2)}, u32[]{:S(2)}) collective-permute-start(f32[2,4,2,16,128]{4,3,2,1,0:T(8,128)S(1)} %get-tuple-element.45), channel_id=1, source_target_pairs={{0,8},{2,10},{4,12},{6,14},{8,0},{10,2},{12,4},{14,6},{1,9},{3,11}... | collective-permute-start | bytes 393224 | tf_op jit(solution)/shard_map/ppermute | solution.py:360
  39.6 2.0 %collective-permute-start.12 = (f32[2,4,2,16,128]{4,3,2,1,0:T(8,128)S(1)}, f32[2,4,2,16,128]{4,3,2,1,0:T(8,128)S(1)}, u32[]{:S(2)}, u32[]{:S(2)}) collective-permute-start(f32[2,4,2,16,128]{4,3,2,1,0:T(8,128)S(1)} %get-tuple-element.46), channel_id=1, source_target_pairs={{0,10},{2,8},{4,14},{6,12},{8,2},{10,0},{12,6},{14,4},{1,11},{3,9}... | collective-permute-start | bytes 393224 | tf_op jit(solution)/shard_map/ppermute | solution.py:360
  41.6 1.9 %collective-permute-done.8.refs_2_ = f32[2,4,2,16,128]{4,3,2,1,0:T(8,128)S(1)} collective-permute-done((f32[2,4,2,16,128]{4,3,2,1,0:T(8,128)S(1)}, f32[2,4,2,16,128]{4,3,2,1,0:T(8,128)S(1)}, u32[]{:S(2)}, u32[]{:S(2)}) %collective-permute-start.8) | collective-permute-done | bytes 131104 | tf_op jit(solution)/shard_map/ppermute | solution.py:360
  43.5 0.5 collective-permute-start.13
  44.0 4.3 %collective-permute-done.9.refs_3_ = f32[2,4,2,16,128]{4,3,2,1,0:T(8,128)S(1)} collective-permute-done((f32[2,4,2,16,128]{4,3,2,1,0:T(8,128)S(1)}, f32[2,4,2,16,128]{4,3,2,1,0:T(8,128)S(1)}, u32[]{:S(2)}, u32[]{:S(2)}) %collective-permute-start.9) | collective-permute-done | bytes 131104 | tf_op jit(solution)/shard_map/ppermute | solution.py:360
  48.3 2.1 %collective-permute-done.10.refs_4_ = f32[2,4,2,16,128]{4,3,2,1,0:T(8,128)S(1)} collective-permute-done((f32[2,4,2,16,128]{4,3,2,1,0:T(8,128)S(1)}, f32[2,4,2,16,128]{4,3,2,1,0:T(8,128)S(1)}, u32[]{:S(2)}, u32[]{:S(2)}) %collective-permute-start.10) | collective-permute-done | bytes 131104 | tf_op jit(solution)/shard_map/ppermute | solution.py:360
  50.4 2.6 %collective-permute-done.11.refs_5_ = f32[2,4,2,16,128]{4,3,2,1,0:T(8,128)S(1)} collective-permute-done((f32[2,4,2,16,128]{4,3,2,1,0:T(8,128)S(1)}, f32[2,4,2,16,128]{4,3,2,1,0:T(8,128)S(1)}, u32[]{:S(2)}, u32[]{:S(2)}) %collective-permute-start.11) | collective-permute-done | bytes 131104 | tf_op jit(solution)/shard_map/ppermute | solution.py:360
  53.0 2.0 %collective-permute-done.12.refs_6_ = f32[2,4,2,16,128]{4,3,2,1,0:T(8,128)S(1)} collective-permute-done((f32[2,4,2,16,128]{4,3,2,1,0:T(8,128)S(1)}, f32[2,4,2,16,128]{4,3,2,1,0:T(8,128)S(1)}, u32[]{:S(2)}, u32[]{:S(2)}) %collective-permute-start.12) | collective-permute-done | bytes 131104 | tf_op jit(solution)/shard_map/ppermute | solution.py:360
  55.0 1.0 %second_section_sent.1 = f32[2,512,128]{2,1,0:T(8,128)S(1)} custom-call(f32[2,4,2,16,128]{4,3,2,1,0:T(8,128)S(1)} %get-tuple-element.40.refs_0_, f32[2,4,2,16,128]{4,3,2,1,0:T(8,128)S(1)} %collective-permute-done.7.refs_1_, f32[2,4,2,16,128]{4,3,2,1,0:T(8,128)S(1)} %collective-permute-done.8.refs_2_, ...), custom_call_target="tpu_custom_call" | custom-call | flops 603979776 | bytes 4194304 | tf_op jit(solution)/shard_map/second_section_sent/pallas_call | solution.py:311
  56.0 0.1 collective-permute-start.14
  56.1 1.0 %second_section_kept.1.kept_ref = f32[2,512,128]{2,1,0:T(8,128)S(1)} custom-call(f32[2,4,2,16,128]{4,3,2,1,0:T(8,128)S(1)} %get-tuple-element.40.refs_0_, f32[2,4,2,16,128]{4,3,2,1,0:T(8,128)S(1)} %collective-permute-done.7.refs_1_, f32[2,4,2,16,128]{4,3,2,1,0:T(8,128)S(1)} %collective-permute-done.8.refs_2_, ...), custom_call_target="tpu_custom_call" | custom-call | flops 603979776 | bytes 4194304 | tf_op jit(solution)/shard_map/second_section_kept/pallas_call | solution.py:311
  57.1 0.9 %collective-permute-done.14.came_ref = f32[2,512,128]{2,1,0:T(8,128)S(1)} collective-permute-done((f32[2,512,128]{2,1,0:T(8,128)S(1)}, f32[2,512,128]{2,1,0:T(8,128)S(1)}, u32[]{:S(2)}, u32[]{:S(2)}) %collective-permute-start.14) | collective-permute-done | bytes 524320 | tf_op jit(solution)/shard_map/ppermute | solution.py:425
  58.0 3.1 %third_section.1 = f32[2048,128]{1,0:T(8,128)} custom-call(f32[2,512,128]{2,1,0:T(8,128)S(1)} %second_section_kept.1.kept_ref, f32[2,512,128]{2,1,0:T(8,128)S(1)} %collective-permute-done.14.came_ref, bf16[256,768]{1,0:T(8,128)(2,1)S(1)} %get-tuple-element.50.refs_0_, bf16[256,768]{1,0:T(8,128)(2,1)S(1)} %get-tuple-element.51.refs_1_, ...), custom_call_target="tpu_custom_call" | custom-call | flops 1610612736 | bytes 4194304 | tf_op jit(solution)/shard_map/third_section/pallas_call | solution.py:311
  (12 shorter events, 0.0 us)
Async XLA Ops:
  0.9 11.8 %collective-permute-start = (f32[256,128]{1,0:T(8,128)S(1)}, f32[256,128]{1,0:T(8,128)S(1)}, u32[]{:S(2)}, u32[]{:S(2)}) collective-permute-start(f32[256,128]{1,0:T(8,128)S(1)} %dynamic-slice_bitcast_fusion), channel_id=1, source_target_pairs={{0,12},{2,14},{4,8},{6,10},{8,4},{10,6},{12,0},{14,2},{1,13},{3,15... | collective-permute-start | bytes 393224 | tf_op jit(solution)/shard_map/ppermute | solution.py:360
  6.0 1.2 %copy-start = (f32[2,131072]{1,0:T(2,128)S(1)}, f32[2,131072]{1,0:T(2,128)}, u32[]{:S(2)}) copy-start(f32[2,131072]{1,0:T(2,128)} %param.3) | copy-start | bytes 3145732
  7.3 10.7 %collective-permute-start.1 = (f32[256,128]{1,0:T(8,128)S(1)}, f32[256,128]{1,0:T(8,128)S(1)}, u32[]{:S(2)}, u32[]{:S(2)}) collective-permute-start(f32[256,128]{1,0:T(8,128)S(1)} %get-tuple-element.30), channel_id=1, source_target_pairs={{0,14},{2,12},{4,10},{6,8},{8,6},{10,4},{12,2},{14,0},{1,15},{3,13... | collective-permute-start | bytes 393224 | tf_op jit(solution)/shard_map/ppermute | solution.py:360
  8.6 16.2 %collective-permute-start.2 = (f32[256,128]{1,0:T(8,128)S(1)}, f32[256,128]{1,0:T(8,128)S(1)}, u32[]{:S(2)}, u32[]{:S(2)}) collective-permute-start(f32[256,128]{1,0:T(8,128)S(1)} %get-tuple-element.31), channel_id=1, source_target_pairs={{0,4},{2,6},{4,0},{6,2},{8,12},{10,14},{12,8},{14,10},{1,5},{3,7},... | collective-permute-start | bytes 393224 | tf_op jit(solution)/shard_map/ppermute | solution.py:360
  8.6 16.2 %collective-permute-start.3 = (f32[256,128]{1,0:T(8,128)S(1)}, f32[256,128]{1,0:T(8,128)S(1)}, u32[]{:S(2)}, u32[]{:S(2)}) collective-permute-start(f32[256,128]{1,0:T(8,128)S(1)} %get-tuple-element.32), channel_id=1, source_target_pairs={{0,6},{2,4},{4,2},{6,0},{8,14},{10,12},{12,10},{14,8},{1,7},{3,5},... | collective-permute-start | bytes 393224 | tf_op jit(solution)/shard_map/ppermute | solution.py:360
  10.4 16.0 %collective-permute-start.4 = (f32[256,128]{1,0:T(8,128)S(1)}, f32[256,128]{1,0:T(8,128)S(1)}, u32[]{:S(2)}, u32[]{:S(2)}) collective-permute-start(f32[256,128]{1,0:T(8,128)S(1)} %get-tuple-element.34), channel_id=1, source_target_pairs={{0,8},{2,10},{4,12},{6,14},{8,0},{10,2},{12,4},{14,6},{1,9},{3,11}... | collective-permute-start | bytes 393224 | tf_op jit(solution)/shard_map/ppermute | solution.py:360
  12.7 16.6 %collective-permute-start.5 = (f32[256,128]{1,0:T(8,128)S(1)}, f32[256,128]{1,0:T(8,128)S(1)}, u32[]{:S(2)}, u32[]{:S(2)}) collective-permute-start(f32[256,128]{1,0:T(8,128)S(1)} %get-tuple-element.35), channel_id=1, source_target_pairs={{0,10},{2,8},{4,14},{6,12},{8,2},{10,0},{12,6},{14,4},{1,11},{3,9}... | collective-permute-start | bytes 393224 | tf_op jit(solution)/shard_map/ppermute | solution.py:360
  18.0 11.3 %collective-permute-start.6 = (f32[256,128]{1,0:T(8,128)S(1)}, f32[256,128]{1,0:T(8,128)S(1)}, u32[]{:S(2)}, u32[]{:S(2)}) collective-permute-start(f32[256,128]{1,0:T(8,128)S(1)} %get-tuple-element.36), channel_id=1, source_target_pairs={{0,2},{2,0},{4,6},{6,4},{8,10},{10,8},{12,14},{14,12},{1,3},{3,1},... | collective-permute-start | bytes 393224 | tf_op jit(solution)/shard_map/ppermute | solution.py:360
  18.1 0.7 %copy-start.1 = (s32[18]{0:T(128)S(1)}, s32[18]{0:T(128)}, u32[]{:S(2)}) copy-start(s32[18]{0:T(128)} %bits_ref.1) | copy-start | bytes 220
  31.8 7.8 %collective-permute-start.7 = (f32[2,4,2,16,128]{4,3,2,1,0:T(8,128)S(1)}, f32[2,4,2,16,128]{4,3,2,1,0:T(8,128)S(1)}, u32[]{:S(2)}, u32[]{:S(2)}) collective-permute-start(f32[2,4,2,16,128]{4,3,2,1,0:T(8,128)S(1)} %get-tuple-element.41), channel_id=1, source_target_pairs={{0,12},{2,14},{4,8},{6,10},{8,4},{10,6},{12,0},{14,2},{1,13},{3,15... | collective-permute-start | bytes 393224 | tf_op jit(solution)/shard_map/ppermute | solution.py:360
  34.4 9.1 %collective-permute-start.8 = (f32[2,4,2,16,128]{4,3,2,1,0:T(8,128)S(1)}, f32[2,4,2,16,128]{4,3,2,1,0:T(8,128)S(1)}, u32[]{:S(2)}, u32[]{:S(2)}) collective-permute-start(f32[2,4,2,16,128]{4,3,2,1,0:T(8,128)S(1)} %get-tuple-element.42), channel_id=1, source_target_pairs={{0,14},{2,12},{4,10},{6,8},{8,6},{10,4},{12,2},{14,0},{1,15},{3,13... | collective-permute-start | bytes 393224 | tf_op jit(solution)/shard_map/ppermute | solution.py:360
  35.6 12.7 %collective-permute-start.9 = (f32[2,4,2,16,128]{4,3,2,1,0:T(8,128)S(1)}, f32[2,4,2,16,128]{4,3,2,1,0:T(8,128)S(1)}, u32[]{:S(2)}, u32[]{:S(2)}) collective-permute-start(f32[2,4,2,16,128]{4,3,2,1,0:T(8,128)S(1)} %get-tuple-element.43), channel_id=1, source_target_pairs={{0,4},{2,6},{4,0},{6,2},{8,12},{10,14},{12,8},{14,10},{1,5},{3,7},... | collective-permute-start | bytes 393224 | tf_op jit(solution)/shard_map/ppermute | solution.py:360
  35.6 14.8 %collective-permute-start.10 = (f32[2,4,2,16,128]{4,3,2,1,0:T(8,128)S(1)}, f32[2,4,2,16,128]{4,3,2,1,0:T(8,128)S(1)}, u32[]{:S(2)}, u32[]{:S(2)}) collective-permute-start(f32[2,4,2,16,128]{4,3,2,1,0:T(8,128)S(1)} %get-tuple-element.44), channel_id=1, source_target_pairs={{0,6},{2,4},{4,2},{6,0},{8,14},{10,12},{12,10},{14,8},{1,7},{3,5},... | collective-permute-start | bytes 393224 | tf_op jit(solution)/shard_map/ppermute | solution.py:360
  38.6 14.4 %collective-permute-start.11 = (f32[2,4,2,16,128]{4,3,2,1,0:T(8,128)S(1)}, f32[2,4,2,16,128]{4,3,2,1,0:T(8,128)S(1)}, u32[]{:S(2)}, u32[]{:S(2)}) collective-permute-start(f32[2,4,2,16,128]{4,3,2,1,0:T(8,128)S(1)} %get-tuple-element.45), channel_id=1, source_target_pairs={{0,8},{2,10},{4,12},{6,14},{8,0},{10,2},{12,4},{14,6},{1,9},{3,11}... | collective-permute-start | bytes 393224 | tf_op jit(solution)/shard_map/ppermute | solution.py:360
  39.6 15.3 %collective-permute-start.12 = (f32[2,4,2,16,128]{4,3,2,1,0:T(8,128)S(1)}, f32[2,4,2,16,128]{4,3,2,1,0:T(8,128)S(1)}, u32[]{:S(2)}, u32[]{:S(2)}) collective-permute-start(f32[2,4,2,16,128]{4,3,2,1,0:T(8,128)S(1)} %get-tuple-element.46), channel_id=1, source_target_pairs={{0,10},{2,8},{4,14},{6,12},{8,2},{10,0},{12,6},{14,4},{1,11},{3,9}... | collective-permute-start | bytes 393224 | tf_op jit(solution)/shard_map/ppermute | solution.py:360
  43.5 11.5 %collective-permute-start.13 = (f32[2,4,2,16,128]{4,3,2,1,0:T(8,128)S(1)}, f32[2,4,2,16,128]{4,3,2,1,0:T(8,128)S(1)}, u32[]{:S(2)}, u32[]{:S(2)}) collective-permute-start(f32[2,4,2,16,128]{4,3,2,1,0:T(8,128)S(1)} %get-tuple-element.47), channel_id=1, source_target_pairs={{0,2},{2,0},{4,6},{6,4},{8,10},{10,8},{12,14},{14,12},{1,3},{3,1},... | collective-permute-start | bytes 393224 | tf_op jit(solution)/shard_map/ppermute | solution.py:360
  56.0 2.0 %copy-start.2 = (bf16[512,1536]{1,0:T(8,128)(2,1)S(1)}, bf16[512,1536]{1,0:T(8,128)(2,1)}, u32[]{:S(2)}) copy-start(bf16[512,1536]{1,0:T(8,128)(2,1)} %get-tuple-element.52.refs_2_) | copy-start | bytes 4718596
  56.0 2.0 %collective-permute-start.14 = (f32[2,512,128]{2,1,0:T(8,128)S(1)}, f32[2,512,128]{2,1,0:T(8,128)S(1)}, u32[]{:S(2)}, u32[]{:S(2)}) collective-permute-start(f32[2,512,128]{2,1,0:T(8,128)S(1)} %second_section_sent.1), channel_id=1, source_target_pairs={{0,1},{1,0},{2,3},{3,2},{4,5},{5,4},{6,7},{7,6},{8,9},{9,8},{10,11... | collective-permute-start | bytes 1572872 | tf_op jit(solution)/shard_map/ppermute | solution.py:425

commit v22 on v19

--- a/solution.py
+++ b/solution.py
@@ -154,8 +154,11 @@
 
 
 def partners_of(count):
-    me = lax.axis_index("qa")
-    return [jnp.bitwise_xor(me, distance) for distance in distances_of(count)]
+    me, core = lax.axis_index("qa"), lax.axis_index("qb")
+    return [
+        jnp.bitwise_xor(me, jnp.bitwise_xor(distance, core) if distance > 1 else distance)
+        for distance in distances_of(count)
+    ]
 
 
 def split_kernel(x_ref, *outs):
@@ -357,7 +360,12 @@
     def exchange(blocks):
         came = [blocks[0]]
         for distance, piece in zip(distances_of(qa)[1:], blocks[1:]):
-            came.append(lax.ppermute(piece, "qa", [(i, i ^ distance) for i in range(qa)]))
+            pairs = []
+            for i in range(qa):
+                for core in range(qb):
+                    to = i ^ distance ^ (core if distance > 1 else 0)
+                    pairs.append((i * qb + core, to * qb + core))
+            came.append(lax.ppermute(piece, ("qa", "qb"), pairs))
         return came
 
     blocks = exchange(blocks)

time: 61.2 us -> 60.6 us (level)
  waiting for transfers between devices: 15.6 us -> 14 us
  starting transfers between devices: 28.4 us -> 29.4 us
    ppermute x14, waiting for transfers between devices: 14.8 us -> 13.2 us  [exchange(): came.append(lax.ppermute(piece, ('qa', 'qb'), pairs))]
    ppermute x14, starting transfers between devices: 28.3 us -> 29.3 us  [exchange(): came.append(lax.ppermute(piece, ('qa', 'qb'), pairs))]
  transfers between devices with their start and end apart: 15 -> 15, of which waited for: 9 -> 7; matrix products, arithmetic and copies ran while one was open for 0% -> 0% of each run, Pallas kernels for 12% -> 12%
where the time goes in v22:
time: 60.6 us; the launch traced here: 60.4 us
  starting transfers between devices  29.4 us (49%)
  Pallas kernels  14 us (23%)
  waiting for transfers between devices  14 us (23%)
  local copies, waits for them, and re-layouts  2.8 us (5%)
    ppermute x14, starting transfers between devices, exchange(): came.append(lax.ppermute(piece, ('qa', 'qb'), pairs))  29.3 us
    pallas_call x7, Pallas kernels, call(): pl.pallas_call(kernel, out_shape=out_shapes, in_specs=in_specs, out_specs...  14 us
    ppermute x14, waiting for transfers between devices, exchange(): came.append(lax.ppermute(piece, ('qa', 'qb'), pairs))  13.2 us
    unnamed x6, local copies, waits for them, and re-layouts  1.88 us
  transfers between devices with their start and end apart: 15, of which 7 were waited for; matrix products, arithmetic and copies ran while one was open for 0% of the time, Pallas kernels for 12%

profile of v22, /device:TPU:0, one launch (start us, length us, event | category | flops | bytes accessed | tf_op | source)
XLA Modules:
  0.0 60.4 jit_solution(877771268439187843)
XLA Ops:
  0.0 0.9 %dynamic-slice_bitcast_fusion = f32[256,128]{1,0:T(8,128)S(1)} fusion(f32[8,256,128]{2,1,0:T(8,128)} %bitcast.12, s32[]{:T(128)S(6)} %select_n.4), kind=kLoop, calls=%fused_computation | loop fusion | bytes 262148 | tf_op jit(solution)/shard_map/jit(dynamic_index_in_dim)/squeeze | solution.py:357
  0.9 6.1 %collective-permute-start = (f32[256,128]{1,0:T(8,128)S(1)}, f32[256,128]{1,0:T(8,128)S(1)}, u32[]{:S(2)}, u32[]{:S(2)}) collective-permute-start(f32[256,128]{1,0:T(8,128)S(1)} %dynamic-slice_bitcast_fusion), channel_id=1, source_target_pairs={{0,14},{1,13},{2,12},{3,15},{4,10},{5,9},{6,8},{7,11},{8,6},{9,5},... | collective-permute-start | bytes 393224 | tf_op jit(solution)/shard_map/ppermute | solution.py:368
  7.0 1.2 %copy-done = f32[2,131072]{1,0:T(2,128)S(1)} copy-done((f32[2,131072]{1,0:T(2,128)S(1)}, f32[2,131072]{1,0:T(2,128)}, u32[]{:S(2)}) %copy-start) | copy-done | bytes 1048600
  8.2 0.1 split_state.1
  8.3 0.3 collective-permute-start.1
  8.6 0.0 collective-permute-start.2
  8.6 1.8 %collective-permute-start.3 = (f32[256,128]{1,0:T(8,128)S(1)}, f32[256,128]{1,0:T(8,128)S(1)}, u32[]{:S(2)}, u32[]{:S(2)}) collective-permute-start(f32[256,128]{1,0:T(8,128)S(1)} %get-tuple-element.32), channel_id=1, source_target_pairs={{0,4},{1,7},{2,6},{3,5},{4,0},{5,3},{6,2},{7,1},{8,12},{9,15},{10,... | collective-permute-start | bytes 393224 | tf_op jit(solution)/shard_map/ppermute | solution.py:368
  10.4 3.2 %collective-permute-start.4 = (f32[256,128]{1,0:T(8,128)S(1)}, f32[256,128]{1,0:T(8,128)S(1)}, u32[]{:S(2)}, u32[]{:S(2)}) collective-permute-start(f32[256,128]{1,0:T(8,128)S(1)} %get-tuple-element.34), channel_id=1, source_target_pairs={{0,10},{1,9},{2,8},{3,11},{4,14},{5,13},{6,12},{7,15},{8,2},{9,1},... | collective-permute-start | bytes 393224 | tf_op jit(solution)/shard_map/ppermute | solution.py:368
  13.6 0.0 collective-permute-done.refs_1_
  13.6 5.1 %collective-permute-start.5 = (f32[256,128]{1,0:T(8,128)S(1)}, f32[256,128]{1,0:T(8,128)S(1)}, u32[]{:S(2)}, u32[]{:S(2)}) collective-permute-start(f32[256,128]{1,0:T(8,128)S(1)} %get-tuple-element.35), channel_id=1, source_target_pairs={{0,8},{1,11},{2,10},{3,9},{4,12},{5,15},{6,14},{7,13},{8,0},{9,3},... | collective-permute-start | bytes 393224 | tf_op jit(solution)/shard_map/ppermute | solution.py:368
  18.8 1.1 %collective-permute-start.6 = (f32[256,128]{1,0:T(8,128)S(1)}, f32[256,128]{1,0:T(8,128)S(1)}, u32[]{:S(2)}, u32[]{:S(2)}) collective-permute-start(f32[256,128]{1,0:T(8,128)S(1)} %get-tuple-element.36), channel_id=1, source_target_pairs={{0,2},{1,3},{2,0},{3,1},{4,6},{5,7},{6,4},{7,5},{8,10},{9,11},{10,... | collective-permute-start | bytes 393224 | tf_op jit(solution)/shard_map/ppermute | solution.py:368
  19.9 0.7 %copy-done.1 = s32[18]{0:T(128)S(1)} copy-done((s32[18]{0:T(128)S(1)}, s32[18]{0:T(128)}, u32[]{:S(2)}) %copy-start.1) | copy-done | bytes 96
  20.5 6.0 %prepare_gates.1 = (bf16[768,256]{1,0:T(8,128)(2,1)S(1)}, bf16[256,768]{1,0:T(8,128)(2,1)S(1)}, bf16[256,768]{1,0:T(8,128)(2,1)S(1)}, bf16[512,1536]{1,0:T(8,128...) custom-call(s32[18]{0:T(128)S(1)} %copy-done.1, ...), custom_call_target="tpu_custom_call" | custom-call | flops 3221225472 | bytes 4194304 | tf_op jit(solution)/shard_map/prepare_gates/pallas_call | solution.py:314
  26.5 0.4 low_gate_early.1.refs_0_
  27.0 1.4 %collective-permute-done.5.refs_2_ = f32[256,128]{1,0:T(8,128)S(1)} collective-permute-done((f32[256,128]{1,0:T(8,128)S(1)}, f32[256,128]{1,0:T(8,128)S(1)}, u32[]{:S(2)}, u32[]{:S(2)}) %collective-permute-start.5) | collective-permute-done | bytes 131104 | tf_op jit(solution)/shard_map/ppermute | solution.py:368
  28.3 2.5 %first_section.1 = (f32[2,4,2,16,128]{4,3,2,1,0:T(8,128)S(1)}, f32[2,4,2,16,128]{4,3,2,1,0:T(8,128)S(1)}, f32[2,4,2,16,128]{4,3,2,1,0:T(8,128)S(1)}, f32[2,4,2,1...) custom-call(f32[2,1024,128]{2,1,0:T(8,128)S(1)} %low_gate_early.1.re, ...), custom_call_target="tpu_custom_call", output_to_operand_aliasing={{8}: (0, {})} | custom-call | flops 2013265920 | bytes 4194304 | tf_op jit(solution)/shard_map/first_section/pallas_call | solution.py:314
  30.9 3.5 %collective-permute-start.7 = (f32[2,4,2,16,128]{4,3,2,1,0:T(8,128)S(1)}, f32[2,4,2,16,128]{4,3,2,1,0:T(8,128)S(1)}, u32[]{:S(2)}, u32[]{:S(2)}) collective-permute-start(f32[2,4,2,16,128]{4,3,2,1,0:T(8,128)S(1)} %get-tuple-element.41), channel_id=1, source_target_pairs={{0,14},{1,13},{2,12},{3,15},{4,10},{5,9},{6,8},{7,11},{8,6},{9,5},... | collective-permute-start | bytes 393224 | tf_op jit(solution)/shard_map/ppermute | solution.py:368
  34.4 1.4 %collective-permute-start.8 = (f32[2,4,2,16,128]{4,3,2,1,0:T(8,128)S(1)}, f32[2,4,2,16,128]{4,3,2,1,0:T(8,128)S(1)}, u32[]{:S(2)}, u32[]{:S(2)}) collective-permute-start(f32[2,4,2,16,128]{4,3,2,1,0:T(8,128)S(1)} %get-tuple-element.42), channel_id=1, source_target_pairs={{0,12},{1,15},{2,14},{3,13},{4,8},{5,11},{6,10},{7,9},{8,4},{9,7},... | collective-permute-start | bytes 393224 | tf_op jit(solution)/shard_map/ppermute | solution.py:368
  35.7 1.9 %collective-permute-start.10 = (f32[2,4,2,16,128]{4,3,2,1,0:T(8,128)S(1)}, f32[2,4,2,16,128]{4,3,2,1,0:T(8,128)S(1)}, u32[]{:S(2)}, u32[]{:S(2)}) collective-permute-start(f32[2,4,2,16,128]{4,3,2,1,0:T(8,128)S(1)} %get-tuple-element.44), channel_id=1, source_target_pairs={{0,4},{1,7},{2,6},{3,5},{4,0},{5,3},{6,2},{7,1},{8,12},{9,15},{10,... | collective-permute-start | bytes 393224 | tf_op jit(solution)/shard_map/ppermute | solution.py:368
  37.7 2.0 %collective-permute-start.11 = (f32[2,4,2,16,128]{4,3,2,1,0:T(8,128)S(1)}, f32[2,4,2,16,128]{4,3,2,1,0:T(8,128)S(1)}, u32[]{:S(2)}, u32[]{:S(2)}) collective-permute-start(f32[2,4,2,16,128]{4,3,2,1,0:T(8,128)S(1)} %get-tuple-element.45), channel_id=1, source_target_pairs={{0,10},{1,9},{2,8},{3,11},{4,14},{5,13},{6,12},{7,15},{8,2},{9,1},... | collective-permute-start | bytes 393224 | tf_op jit(solution)/shard_map/ppermute | solution.py:368
  39.6 1.9 %collective-permute-start.12 = (f32[2,4,2,16,128]{4,3,2,1,0:T(8,128)S(1)}, f32[2,4,2,16,128]{4,3,2,1,0:T(8,128)S(1)}, u32[]{:S(2)}, u32[]{:S(2)}) collective-permute-start(f32[2,4,2,16,128]{4,3,2,1,0:T(8,128)S(1)} %get-tuple-element.46), channel_id=1, source_target_pairs={{0,8},{1,11},{2,10},{3,9},{4,12},{5,15},{6,14},{7,13},{8,0},{9,3},... | collective-permute-start | bytes 393224 | tf_op jit(solution)/shard_map/ppermute | solution.py:368
  41.6 1.0 %collective-permute-done.8.refs_2_ = f32[2,4,2,16,128]{4,3,2,1,0:T(8,128)S(1)} collective-permute-done((f32[2,4,2,16,128]{4,3,2,1,0:T(8,128)S(1)}, f32[2,4,2,16,128]{4,3,2,1,0:T(8,128)S(1)}, u32[]{:S(2)}, u32[]{:S(2)}) %collective-permute-start.8) | collective-permute-done | bytes 131104 | tf_op jit(solution)/shard_map/ppermute | solution.py:368
  42.6 1.0 %collective-permute-start.13 = (f32[2,4,2,16,128]{4,3,2,1,0:T(8,128)S(1)}, f32[2,4,2,16,128]{4,3,2,1,0:T(8,128)S(1)}, u32[]{:S(2)}, u32[]{:S(2)}) collective-permute-start(f32[2,4,2,16,128]{4,3,2,1,0:T(8,128)S(1)} %get-tuple-element.47), channel_id=1, source_target_pairs={{0,2},{1,3},{2,0},{3,1},{4,6},{5,7},{6,4},{7,5},{8,10},{9,11},{10,... | collective-permute-start | bytes 393224 | tf_op jit(solution)/shard_map/ppermute | solution.py:368
  43.6 3.2 %collective-permute-done.9.refs_3_ = f32[2,4,2,16,128]{4,3,2,1,0:T(8,128)S(1)} collective-permute-done((f32[2,4,2,16,128]{4,3,2,1,0:T(8,128)S(1)}, f32[2,4,2,16,128]{4,3,2,1,0:T(8,128)S(1)}, u32[]{:S(2)}, u32[]{:S(2)}) %collective-permute-start.9) | collective-permute-done | bytes 131104 | tf_op jit(solution)/shard_map/ppermute | solution.py:368
  46.8 4.0 %collective-permute-done.10.refs_4_ = f32[2,4,2,16,128]{4,3,2,1,0:T(8,128)S(1)} collective-permute-done((f32[2,4,2,16,128]{4,3,2,1,0:T(8,128)S(1)}, f32[2,4,2,16,128]{4,3,2,1,0:T(8,128)S(1)}, u32[]{:S(2)}, u32[]{:S(2)}) %collective-permute-start.10) | collective-permute-done | bytes 131104 | tf_op jit(solution)/shard_map/ppermute | solution.py:368
  50.8 2.9 %collective-permute-done.11.refs_5_ = f32[2,4,2,16,128]{4,3,2,1,0:T(8,128)S(1)} collective-permute-done((f32[2,4,2,16,128]{4,3,2,1,0:T(8,128)S(1)}, f32[2,4,2,16,128]{4,3,2,1,0:T(8,128)S(1)}, u32[]{:S(2)}, u32[]{:S(2)}) %collective-permute-start.11) | collective-permute-done | bytes 131104 | tf_op jit(solution)/shard_map/ppermute | solution.py:368
  53.6 0.7 %collective-permute-done.12.refs_6_ = f32[2,4,2,16,128]{4,3,2,1,0:T(8,128)S(1)} collective-permute-done((f32[2,4,2,16,128]{4,3,2,1,0:T(8,128)S(1)}, f32[2,4,2,16,128]{4,3,2,1,0:T(8,128)S(1)}, u32[]{:S(2)}, u32[]{:S(2)}) %collective-permute-start.12) | collective-permute-done | bytes 131104 | tf_op jit(solution)/shard_map/ppermute | solution.py:368
  54.3 1.0 %second_section_sent.1 = f32[2,512,128]{2,1,0:T(8,128)S(1)} custom-call(f32[2,4,2,16,128]{4,3,2,1,0:T(8,128)S(1)} %get-tuple-element.40.refs_0_, f32[2,4,2,16,128]{4,3,2,1,0:T(8,128)S(1)} %collective-permute-done.7.refs_1_, f32[2,4,2,16,128]{4,3,2,1,0:T(8,128)S(1)} %collective-permute-done.8.refs_2_, ...), custom_call_target="tpu_custom_call" | custom-call | flops 603979776 | bytes 4194304 | tf_op jit(solution)/shard_map/second_section_sent/pallas_call | solution.py:314
  55.3 0.1 collective-permute-start.14
  55.4 1.0 %second_section_kept.1.kept_ref = f32[2,512,128]{2,1,0:T(8,128)S(1)} custom-call(f32[2,4,2,16,128]{4,3,2,1,0:T(8,128)S(1)} %get-tuple-element.40.refs_0_, f32[2,4,2,16,128]{4,3,2,1,0:T(8,128)S(1)} %collective-permute-done.7.refs_1_, f32[2,4,2,16,128]{4,3,2,1,0:T(8,128)S(1)} %collective-permute-done.8.refs_2_, ...), custom_call_target="tpu_custom_call" | custom-call | flops 603979776 | bytes 4194304 | tf_op jit(solution)/shard_map/second_section_kept/pallas_call | solution.py:314
  56.4 0.9 %collective-permute-done.14.came_ref = f32[2,512,128]{2,1,0:T(8,128)S(1)} collective-permute-done((f32[2,512,128]{2,1,0:T(8,128)S(1)}, f32[2,512,128]{2,1,0:T(8,128)S(1)}, u32[]{:S(2)}, u32[]{:S(2)}) %collective-permute-start.14) | collective-permute-done | bytes 524320 | tf_op jit(solution)/shard_map/ppermute | solution.py:433
  57.3 3.1 %third_section.1 = f32[2048,128]{1,0:T(8,128)} custom-call(f32[2,512,128]{2,1,0:T(8,128)S(1)} %second_section_kept.1.kept_ref, f32[2,512,128]{2,1,0:T(8,128)S(1)} %collective-permute-done.14.came_ref, bf16[256,768]{1,0:T(8,128)(2,1)S(1)} %get-tuple-element.50.refs_0_, bf16[256,768]{1,0:T(8,128)(2,1)S(1)} %get-tuple-element.51.refs_1_, ...), custom_call_target="tpu_custom_call" | custom-call | flops 1610612736 | bytes 4194304 | tf_op jit(solution)/shard_map/third_section/pallas_call | solution.py:314
  (12 shorter events, 0.0 us)
Async XLA Ops:
  0.9 12.7 %collective-permute-start = (f32[256,128]{1,0:T(8,128)S(1)}, f32[256,128]{1,0:T(8,128)S(1)}, u32[]{:S(2)}, u32[]{:S(2)}) collective-permute-start(f32[256,128]{1,0:T(8,128)S(1)} %dynamic-slice_bitcast_fusion), channel_id=1, source_target_pairs={{0,14},{1,13},{2,12},{3,15},{4,10},{5,9},{6,8},{7,11},{8,6},{9,5},... | collective-permute-start | bytes 393224 | tf_op jit(solution)/shard_map/ppermute | solution.py:368
  7.0 1.2 %copy-start = (f32[2,131072]{1,0:T(2,128)S(1)}, f32[2,131072]{1,0:T(2,128)}, u32[]{:S(2)}) copy-start(f32[2,131072]{1,0:T(2,128)} %param.3) | copy-start | bytes 3145732
  8.3 10.5 %collective-permute-start.1 = (f32[256,128]{1,0:T(8,128)S(1)}, f32[256,128]{1,0:T(8,128)S(1)}, u32[]{:S(2)}, u32[]{:S(2)}) collective-permute-start(f32[256,128]{1,0:T(8,128)S(1)} %get-tuple-element.30), channel_id=1, source_target_pairs={{0,12},{1,15},{2,14},{3,13},{4,8},{5,11},{6,10},{7,9},{8,4},{9,7},... | collective-permute-start | bytes 393224 | tf_op jit(solution)/shard_map/ppermute | solution.py:368
  8.6 17.9 %collective-permute-start.2 = (f32[256,128]{1,0:T(8,128)S(1)}, f32[256,128]{1,0:T(8,128)S(1)}, u32[]{:S(2)}, u32[]{:S(2)}) collective-permute-start(f32[256,128]{1,0:T(8,128)S(1)} %get-tuple-element.31), channel_id=1, source_target_pairs={{0,6},{1,5},{2,4},{3,7},{4,2},{5,1},{6,0},{7,3},{8,14},{9,13},{10,... | collective-permute-start | bytes 393224 | tf_op jit(solution)/shard_map/ppermute | solution.py:368
  8.6 17.9 %collective-permute-start.3 = (f32[256,128]{1,0:T(8,128)S(1)}, f32[256,128]{1,0:T(8,128)S(1)}, u32[]{:S(2)}, u32[]{:S(2)}) collective-permute-start(f32[256,128]{1,0:T(8,128)S(1)} %get-tuple-element.32), channel_id=1, source_target_pairs={{0,4},{1,7},{2,6},{3,5},{4,0},{5,3},{6,2},{7,1},{8,12},{9,15},{10,... | collective-permute-start | bytes 393224 | tf_op jit(solution)/shard_map/ppermute | solution.py:368
  10.4 16.6 %collective-permute-start.4 = (f32[256,128]{1,0:T(8,128)S(1)}, f32[256,128]{1,0:T(8,128)S(1)}, u32[]{:S(2)}, u32[]{:S(2)}) collective-permute-start(f32[256,128]{1,0:T(8,128)S(1)} %get-tuple-element.34), channel_id=1, source_target_pairs={{0,10},{1,9},{2,8},{3,11},{4,14},{5,13},{6,12},{7,15},{8,2},{9,1},... | collective-permute-start | bytes 393224 | tf_op jit(solution)/shard_map/ppermute | solution.py:368
  13.6 14.7 %collective-permute-start.5 = (f32[256,128]{1,0:T(8,128)S(1)}, f32[256,128]{1,0:T(8,128)S(1)}, u32[]{:S(2)}, u32[]{:S(2)}) collective-permute-start(f32[256,128]{1,0:T(8,128)S(1)} %get-tuple-element.35), channel_id=1, source_target_pairs={{0,8},{1,11},{2,10},{3,9},{4,12},{5,15},{6,14},{7,13},{8,0},{9,3},... | collective-permute-start | bytes 393224 | tf_op jit(solution)/shard_map/ppermute | solution.py:368
  18.8 9.6 %collective-permute-start.6 = (f32[256,128]{1,0:T(8,128)S(1)}, f32[256,128]{1,0:T(8,128)S(1)}, u32[]{:S(2)}, u32[]{:S(2)}) collective-permute-start(f32[256,128]{1,0:T(8,128)S(1)} %get-tuple-element.36), channel_id=1, source_target_pairs={{0,2},{1,3},{2,0},{3,1},{4,6},{5,7},{6,4},{7,5},{8,10},{9,11},{10,... | collective-permute-start | bytes 393224 | tf_op jit(solution)/shard_map/ppermute | solution.py:368
  19.8 0.7 %copy-start.1 = (s32[18]{0:T(128)S(1)}, s32[18]{0:T(128)}, u32[]{:S(2)}) copy-start(s32[18]{0:T(128)} %bits_ref.1) | copy-start | bytes 220
  30.9 8.8 %collective-permute-start.7 = (f32[2,4,2,16,128]{4,3,2,1,0:T(8,128)S(1)}, f32[2,4,2,16,128]{4,3,2,1,0:T(8,128)S(1)}, u32[]{:S(2)}, u32[]{:S(2)}) collective-permute-start(f32[2,4,2,16,128]{4,3,2,1,0:T(8,128)S(1)} %get-tuple-element.41), channel_id=1, source_target_pairs={{0,14},{1,13},{2,12},{3,15},{4,10},{5,9},{6,8},{7,11},{8,6},{9,5},... | collective-permute-start | bytes 393224 | tf_op jit(solution)/shard_map/ppermute | solution.py:368
  34.4 8.3 %collective-permute-start.8 = (f32[2,4,2,16,128]{4,3,2,1,0:T(8,128)S(1)}, f32[2,4,2,16,128]{4,3,2,1,0:T(8,128)S(1)}, u32[]{:S(2)}, u32[]{:S(2)}) collective-permute-start(f32[2,4,2,16,128]{4,3,2,1,0:T(8,128)S(1)} %get-tuple-element.42), channel_id=1, source_target_pairs={{0,12},{1,15},{2,14},{3,13},{4,8},{5,11},{6,10},{7,9},{8,4},{9,7},... | collective-permute-start | bytes 393224 | tf_op jit(solution)/shard_map/ppermute | solution.py:368
  35.7 11.0 %collective-permute-start.9 = (f32[2,4,2,16,128]{4,3,2,1,0:T(8,128)S(1)}, f32[2,4,2,16,128]{4,3,2,1,0:T(8,128)S(1)}, u32[]{:S(2)}, u32[]{:S(2)}) collective-permute-start(f32[2,4,2,16,128]{4,3,2,1,0:T(8,128)S(1)} %get-tuple-element.43), channel_id=1, source_target_pairs={{0,6},{1,5},{2,4},{3,7},{4,2},{5,1},{6,0},{7,3},{8,14},{9,13},{10,... | collective-permute-start | bytes 393224 | tf_op jit(solution)/shard_map/ppermute | solution.py:368
  35.7 15.0 %collective-permute-start.10 = (f32[2,4,2,16,128]{4,3,2,1,0:T(8,128)S(1)}, f32[2,4,2,16,128]{4,3,2,1,0:T(8,128)S(1)}, u32[]{:S(2)}, u32[]{:S(2)}) collective-permute-start(f32[2,4,2,16,128]{4,3,2,1,0:T(8,128)S(1)} %get-tuple-element.44), channel_id=1, source_target_pairs={{0,4},{1,7},{2,6},{3,5},{4,0},{5,3},{6,2},{7,1},{8,12},{9,15},{10,... | collective-permute-start | bytes 393224 | tf_op jit(solution)/shard_map/ppermute | solution.py:368
  37.7 16.0 %collective-permute-start.11 = (f32[2,4,2,16,128]{4,3,2,1,0:T(8,128)S(1)}, f32[2,4,2,16,128]{4,3,2,1,0:T(8,128)S(1)}, u32[]{:S(2)}, u32[]{:S(2)}) collective-permute-start(f32[2,4,2,16,128]{4,3,2,1,0:T(8,128)S(1)} %get-tuple-element.45), channel_id=1, source_target_pairs={{0,10},{1,9},{2,8},{3,11},{4,14},{5,13},{6,12},{7,15},{8,2},{9,1},... | collective-permute-start | bytes 393224 | tf_op jit(solution)/shard_map/ppermute | solution.py:368
  39.6 14.7 %collective-permute-start.12 = (f32[2,4,2,16,128]{4,3,2,1,0:T(8,128)S(1)}, f32[2,4,2,16,128]{4,3,2,1,0:T(8,128)S(1)}, u32[]{:S(2)}, u32[]{:S(2)}) collective-permute-start(f32[2,4,2,16,128]{4,3,2,1,0:T(8,128)S(1)} %get-tuple-element.46), channel_id=1, source_target_pairs={{0,8},{1,11},{2,10},{3,9},{4,12},{5,15},{6,14},{7,13},{8,0},{9,3},... | collective-permute-start | bytes 393224 | tf_op jit(solution)/shard_map/ppermute | solution.py:368
  42.6 11.7 %collective-permute-start.13 = (f32[2,4,2,16,128]{4,3,2,1,0:T(8,128)S(1)}, f32[2,4,2,16,128]{4,3,2,1,0:T(8,128)S(1)}, u32[]{:S(2)}, u32[]{:S(2)}) collective-permute-start(f32[2,4,2,16,128]{4,3,2,1,0:T(8,128)S(1)} %get-tuple-element.47), channel_id=1, source_target_pairs={{0,2},{1,3},{2,0},{3,1},{4,6},{5,7},{6,4},{7,5},{8,10},{9,11},{10,... | collective-permute-start | bytes 393224 | tf_op jit(solution)/shard_map/ppermute | solution.py:368
  55.3 2.0 %copy-start.2 = (bf16[512,1536]{1,0:T(8,128)(2,1)S(1)}, bf16[512,1536]{1,0:T(8,128)(2,1)}, u32[]{:S(2)}) copy-start(bf16[512,1536]{1,0:T(8,128)(2,1)} %get-tuple-element.52.refs_2_) | copy-start | bytes 4718596
  55.3 2.0 %collective-permute-start.14 = (f32[2,512,128]{2,1,0:T(8,128)S(1)}, f32[2,512,128]{2,1,0:T(8,128)S(1)}, u32[]{:S(2)}, u32[]{:S(2)}) collective-permute-start(f32[2,512,128]{2,1,0:T(8,128)S(1)} %second_section_sent.1), channel_id=1, source_target_pairs={{0,1},{1,0},{2,3},{3,2},{4,5},{5,4},{6,7},{7,6},{8,9},{9,8},{10,11... | collective-permute-start | bytes 1572872 | tf_op jit(solution)/shard_map/ppermute | solution.py:433

commit v23 on v22

--- a/solution.py
+++ b/solution.py
@@ -148,7 +148,7 @@
     far, near = list(range(count - 1, half - 1, -1)), list(range(half - 1, 0, -1))
     order = [0]
     while far or near:
-        order += far[:2] + near[:2]
+        order += sorted(far[:2]) + sorted(near[:2])
         far, near = far[2:], near[2:]
     return order
 

time: 60.6 us -> 63.2 us (1.043)
  waiting for transfers between devices: 14 us -> 16.8 us
    ppermute x14, waiting for transfers between devices: 13.2 us -> 15.9 us  [exchange(): came.append(lax.ppermute(piece, ('qa', 'qb'), pairs))]
  transfers between devices with their start and end apart: 15 -> 15, of which waited for: 7 -> 8; matrix products, arithmetic and copies ran while one was open for 0% -> 0% of each run, Pallas kernels for 12% -> 12%
where the time goes in v23:
time: 63.2 us; the launch traced here: 63 us
  starting transfers between devices  29.2 us (46%)
  waiting for transfers between devices  16.8 us (27%)
  Pallas kernels  14.1 us (22%)
  local copies, waits for them, and re-layouts  2.8 us (4%)
    ppermute x14, starting transfers between devices, exchange(): came.append(lax.ppermute(piece, ('qa', 'qb'), pairs))  29.2 us
    ppermute x14, waiting for transfers between devices, exchange(): came.append(lax.ppermute(piece, ('qa', 'qb'), pairs))  15.9 us
    pallas_call x7, Pallas kernels, call(): pl.pallas_call(kernel, out_shape=out_shapes, in_specs=in_specs, out_specs...  14.1 us
    unnamed x6, local copies, waits for them, and re-layouts  1.88 us
  transfers between devices with their start and end apart: 15, of which 8 were waited for; matrix products, arithmetic and copies ran while one was open for 0% of the time, Pallas kernels for 12%

profile of v23, /device:TPU:0, one launch (start us, length us, event | category | flops | bytes accessed | tf_op | source)
XLA Modules:
  0.0 63.0 jit_solution(10187400281271001379)
XLA Ops:
  0.0 0.9 %dynamic-slice_bitcast_fusion = f32[256,128]{1,0:T(8,128)S(1)} fusion(f32[8,256,128]{2,1,0:T(8,128)} %bitcast.12, s32[]{:T(128)S(6)} %select_n.4), kind=kLoop, calls=%fused_computation | loop fusion | bytes 262148 | tf_op jit(solution)/shard_map/jit(dynamic_index_in_dim)/squeeze | solution.py:357
  0.9 5.1 %collective-permute-start = (f32[256,128]{1,0:T(8,128)S(1)}, f32[256,128]{1,0:T(8,128)S(1)}, u32[]{:S(2)}, u32[]{:S(2)}) collective-permute-start(f32[256,128]{1,0:T(8,128)S(1)} %dynamic-slice_bitcast_fusion), channel_id=1, source_target_pairs={{0,12},{1,15},{2,14},{3,13},{4,8},{5,11},{6,10},{7,9},{8,4},{9,7},... | collective-permute-start | bytes 393224 | tf_op jit(solution)/shard_map/ppermute | solution.py:368
  6.0 1.2 %copy-done = f32[2,131072]{1,0:T(2,128)S(1)} copy-done((f32[2,131072]{1,0:T(2,128)S(1)}, f32[2,131072]{1,0:T(2,128)}, u32[]{:S(2)}) %copy-start) | copy-done | bytes 1048600
  7.3 0.1 split_state.1
  7.3 1.2 %collective-permute-start.1 = (f32[256,128]{1,0:T(8,128)S(1)}, f32[256,128]{1,0:T(8,128)S(1)}, u32[]{:S(2)}, u32[]{:S(2)}) collective-permute-start(f32[256,128]{1,0:T(8,128)S(1)} %get-tuple-element.30), channel_id=1, source_target_pairs={{0,14},{1,13},{2,12},{3,15},{4,10},{5,9},{6,8},{7,11},{8,6},{9,5},... | collective-permute-start | bytes 393224 | tf_op jit(solution)/shard_map/ppermute | solution.py:368
  8.6 0.0 collective-permute-start.2
  8.6 1.9 %collective-permute-start.3 = (f32[256,128]{1,0:T(8,128)S(1)}, f32[256,128]{1,0:T(8,128)S(1)}, u32[]{:S(2)}, u32[]{:S(2)}) collective-permute-start(f32[256,128]{1,0:T(8,128)S(1)} %get-tuple-element.32), channel_id=1, source_target_pairs={{0,6},{1,5},{2,4},{3,7},{4,2},{5,1},{6,0},{7,3},{8,14},{9,13},{10,... | collective-permute-start | bytes 393224 | tf_op jit(solution)/shard_map/ppermute | solution.py:368
  10.4 2.3 %collective-permute-start.4 = (f32[256,128]{1,0:T(8,128)S(1)}, f32[256,128]{1,0:T(8,128)S(1)}, u32[]{:S(2)}, u32[]{:S(2)}) collective-permute-start(f32[256,128]{1,0:T(8,128)S(1)} %get-tuple-element.34), channel_id=1, source_target_pairs={{0,8},{1,11},{2,10},{3,9},{4,12},{5,15},{6,14},{7,13},{8,0},{9,3},... | collective-permute-start | bytes 393224 | tf_op jit(solution)/shard_map/ppermute | solution.py:368
  12.7 5.2 %collective-permute-start.5 = (f32[256,128]{1,0:T(8,128)S(1)}, f32[256,128]{1,0:T(8,128)S(1)}, u32[]{:S(2)}, u32[]{:S(2)}) collective-permute-start(f32[256,128]{1,0:T(8,128)S(1)} %get-tuple-element.35), channel_id=1, source_target_pairs={{0,10},{1,9},{2,8},{3,11},{4,14},{5,13},{6,12},{7,15},{8,2},{9,1},... | collective-permute-start | bytes 393224 | tf_op jit(solution)/shard_map/ppermute | solution.py:368
  18.0 0.5 collective-permute-start.6
  18.5 0.7 %copy-done.1 = s32[18]{0:T(128)S(1)} copy-done((s32[18]{0:T(128)S(1)}, s32[18]{0:T(128)}, u32[]{:S(2)}) %copy-start.1) | copy-done | bytes 96
  19.1 6.0 %prepare_gates.1 = (bf16[768,256]{1,0:T(8,128)(2,1)S(1)}, bf16[256,768]{1,0:T(8,128)(2,1)S(1)}, bf16[256,768]{1,0:T(8,128)(2,1)S(1)}, bf16[512,1536]{1,0:T(8,128...) custom-call(s32[18]{0:T(128)S(1)} %copy-done.1, ...), custom_call_target="tpu_custom_call" | custom-call | flops 3221225472 | bytes 4194304 | tf_op jit(solution)/shard_map/prepare_gates/pallas_call | solution.py:314
  25.2 0.4 low_gate_early.1.refs_0_
  25.6 1.1 %collective-permute-done.4.refs_1_ = f32[256,128]{1,0:T(8,128)S(1)} collective-permute-done((f32[256,128]{1,0:T(8,128)S(1)}, f32[256,128]{1,0:T(8,128)S(1)}, u32[]{:S(2)}, u32[]{:S(2)}) %collective-permute-start.4) | collective-permute-done | bytes 131104 | tf_op jit(solution)/shard_map/ppermute | solution.py:368
  26.7 2.5 %collective-permute-done.5.refs_2_ = f32[256,128]{1,0:T(8,128)S(1)} collective-permute-done((f32[256,128]{1,0:T(8,128)S(1)}, f32[256,128]{1,0:T(8,128)S(1)}, u32[]{:S(2)}, u32[]{:S(2)}) %collective-permute-start.5) | collective-permute-done | bytes 131104 | tf_op jit(solution)/shard_map/ppermute | solution.py:368
  29.2 2.5 %first_section.1 = (f32[2,4,2,16,128]{4,3,2,1,0:T(8,128)S(1)}, f32[2,4,2,16,128]{4,3,2,1,0:T(8,128)S(1)}, f32[2,4,2,16,128]{4,3,2,1,0:T(8,128)S(1)}, f32[2,4,2,1...) custom-call(f32[2,1024,128]{2,1,0:T(8,128)S(1)} %low_gate_early.1.re, ...), custom_call_target="tpu_custom_call", output_to_operand_aliasing={{8}: (0, {})} | custom-call | flops 2013265920 | bytes 4194304 | tf_op jit(solution)/shard_map/first_section/pallas_call | solution.py:314
  31.7 2.5 %collective-permute-start.7 = (f32[2,4,2,16,128]{4,3,2,1,0:T(8,128)S(1)}, f32[2,4,2,16,128]{4,3,2,1,0:T(8,128)S(1)}, u32[]{:S(2)}, u32[]{:S(2)}) collective-permute-start(f32[2,4,2,16,128]{4,3,2,1,0:T(8,128)S(1)} %get-tuple-element.41), channel_id=1, source_target_pairs={{0,12},{1,15},{2,14},{3,13},{4,8},{5,11},{6,10},{7,9},{8,4},{9,7},... | collective-permute-start | bytes 393224 | tf_op jit(solution)/shard_map/ppermute | solution.py:368
  34.3 2.3 %collective-permute-start.8 = (f32[2,4,2,16,128]{4,3,2,1,0:T(8,128)S(1)}, f32[2,4,2,16,128]{4,3,2,1,0:T(8,128)S(1)}, u32[]{:S(2)}, u32[]{:S(2)}) collective-permute-start(f32[2,4,2,16,128]{4,3,2,1,0:T(8,128)S(1)} %get-tuple-element.42), channel_id=1, source_target_pairs={{0,14},{1,13},{2,12},{3,15},{4,10},{5,9},{6,8},{7,11},{8,6},{9,5},... | collective-permute-start | bytes 393224 | tf_op jit(solution)/shard_map/ppermute | solution.py:368
  36.6 1.9 %collective-permute-start.10 = (f32[2,4,2,16,128]{4,3,2,1,0:T(8,128)S(1)}, f32[2,4,2,16,128]{4,3,2,1,0:T(8,128)S(1)}, u32[]{:S(2)}, u32[]{:S(2)}) collective-permute-start(f32[2,4,2,16,128]{4,3,2,1,0:T(8,128)S(1)} %get-tuple-element.44), channel_id=1, source_target_pairs={{0,6},{1,5},{2,4},{3,7},{4,2},{5,1},{6,0},{7,3},{8,14},{9,13},{10,... | collective-permute-start | bytes 393224 | tf_op jit(solution)/shard_map/ppermute | solution.py:368
  38.6 1.1 %collective-permute-start.11 = (f32[2,4,2,16,128]{4,3,2,1,0:T(8,128)S(1)}, f32[2,4,2,16,128]{4,3,2,1,0:T(8,128)S(1)}, u32[]{:S(2)}, u32[]{:S(2)}) collective-permute-start(f32[2,4,2,16,128]{4,3,2,1,0:T(8,128)S(1)} %get-tuple-element.45), channel_id=1, source_target_pairs={{0,8},{1,11},{2,10},{3,9},{4,12},{5,15},{6,14},{7,13},{8,0},{9,3},... | collective-permute-start | bytes 393224 | tf_op jit(solution)/shard_map/ppermute | solution.py:368
  39.7 0.3 collective-permute-done.7.refs_1_
  40.0 3.8 %collective-permute-start.12 = (f32[2,4,2,16,128]{4,3,2,1,0:T(8,128)S(1)}, f32[2,4,2,16,128]{4,3,2,1,0:T(8,128)S(1)}, u32[]{:S(2)}, u32[]{:S(2)}) collective-permute-start(f32[2,4,2,16,128]{4,3,2,1,0:T(8,128)S(1)} %get-tuple-element.46), channel_id=1, source_target_pairs={{0,10},{1,9},{2,8},{3,11},{4,14},{5,13},{6,12},{7,15},{8,2},{9,1},... | collective-permute-start | bytes 393224 | tf_op jit(solution)/shard_map/ppermute | solution.py:368
  43.8 1.2 %collective-permute-start.13 = (f32[2,4,2,16,128]{4,3,2,1,0:T(8,128)S(1)}, f32[2,4,2,16,128]{4,3,2,1,0:T(8,128)S(1)}, u32[]{:S(2)}, u32[]{:S(2)}) collective-permute-start(f32[2,4,2,16,128]{4,3,2,1,0:T(8,128)S(1)} %get-tuple-element.47), channel_id=1, source_target_pairs={{0,2},{1,3},{2,0},{3,1},{4,6},{5,7},{6,4},{7,5},{8,10},{9,11},{10,... | collective-permute-start | bytes 393224 | tf_op jit(solution)/shard_map/ppermute | solution.py:368
  45.0 1.4 %collective-permute-done.9.refs_3_ = f32[2,4,2,16,128]{4,3,2,1,0:T(8,128)S(1)} collective-permute-done((f32[2,4,2,16,128]{4,3,2,1,0:T(8,128)S(1)}, f32[2,4,2,16,128]{4,3,2,1,0:T(8,128)S(1)}, u32[]{:S(2)}, u32[]{:S(2)}) %collective-permute-start.9) | collective-permute-done | bytes 131104 | tf_op jit(solution)/shard_map/ppermute | solution.py:368
  46.4 4.9 %collective-permute-done.10.refs_4_ = f32[2,4,2,16,128]{4,3,2,1,0:T(8,128)S(1)} collective-permute-done((f32[2,4,2,16,128]{4,3,2,1,0:T(8,128)S(1)}, f32[2,4,2,16,128]{4,3,2,1,0:T(8,128)S(1)}, u32[]{:S(2)}, u32[]{:S(2)}) %collective-permute-start.10) | collective-permute-done | bytes 131104 | tf_op jit(solution)/shard_map/ppermute | solution.py:368
  51.3 2.1 %collective-permute-done.11.refs_5_ = f32[2,4,2,16,128]{4,3,2,1,0:T(8,128)S(1)} collective-permute-done((f32[2,4,2,16,128]{4,3,2,1,0:T(8,128)S(1)}, f32[2,4,2,16,128]{4,3,2,1,0:T(8,128)S(1)}, u32[]{:S(2)}, u32[]{:S(2)}) %collective-permute-start.11) | collective-permute-done | bytes 131104 | tf_op jit(solution)/shard_map/ppermute | solution.py:368
  53.5 3.5 %collective-permute-done.12.refs_6_ = f32[2,4,2,16,128]{4,3,2,1,0:T(8,128)S(1)} collective-permute-done((f32[2,4,2,16,128]{4,3,2,1,0:T(8,128)S(1)}, f32[2,4,2,16,128]{4,3,2,1,0:T(8,128)S(1)}, u32[]{:S(2)}, u32[]{:S(2)}) %collective-permute-start.12) | collective-permute-done | bytes 131104 | tf_op jit(solution)/shard_map/ppermute | solution.py:368
  57.0 1.0 %second_section_sent.1 = f32[2,512,128]{2,1,0:T(8,128)S(1)} custom-call(f32[2,4,2,16,128]{4,3,2,1,0:T(8,128)S(1)} %get-tuple-element.40.refs_0_, f32[2,4,2,16,128]{4,3,2,1,0:T(8,128)S(1)} %collective-permute-done.7.refs_1_, f32[2,4,2,16,128]{4,3,2,1,0:T(8,128)S(1)} %collective-permute-done.8.refs_2_, ...), custom_call_target="tpu_custom_call" | custom-call | flops 603979776 | bytes 4194304 | tf_op jit(solution)/shard_map/second_section_sent/pallas_call | solution.py:314
  58.0 0.1 collective-permute-start.14
  58.0 1.0 %second_section_kept.1.kept_ref = f32[2,512,128]{2,1,0:T(8,128)S(1)} custom-call(f32[2,4,2,16,128]{4,3,2,1,0:T(8,128)S(1)} %get-tuple-element.40.refs_0_, f32[2,4,2,16,128]{4,3,2,1,0:T(8,128)S(1)} %collective-permute-done.7.refs_1_, f32[2,4,2,16,128]{4,3,2,1,0:T(8,128)S(1)} %collective-permute-done.8.refs_2_, ...), custom_call_target="tpu_custom_call" | custom-call | flops 603979776 | bytes 4194304 | tf_op jit(solution)/shard_map/second_section_kept/pallas_call | solution.py:314
  59.0 0.9 %collective-permute-done.14.came_ref = f32[2,512,128]{2,1,0:T(8,128)S(1)} collective-permute-done((f32[2,512,128]{2,1,0:T(8,128)S(1)}, f32[2,512,128]{2,1,0:T(8,128)S(1)}, u32[]{:S(2)}, u32[]{:S(2)}) %collective-permute-start.14) | collective-permute-done | bytes 524320 | tf_op jit(solution)/shard_map/ppermute | solution.py:433
  59.9 3.1 %third_section.1 = f32[2048,128]{1,0:T(8,128)} custom-call(f32[2,512,128]{2,1,0:T(8,128)S(1)} %second_section_kept.1.kept_ref, f32[2,512,128]{2,1,0:T(8,128)S(1)} %collective-permute-done.14.came_ref, bf16[256,768]{1,0:T(8,128)(2,1)S(1)} %get-tuple-element.50.refs_0_, bf16[256,768]{1,0:T(8,128)(2,1)S(1)} %get-tuple-element.51.refs_1_, ...), custom_call_target="tpu_custom_call" | custom-call | flops 1610612736 | bytes 4194304 | tf_op jit(solution)/shard_map/third_section/pallas_call | solution.py:314
  (12 shorter events, 0.0 us)
Async XLA Ops:
  0.9 11.8 %collective-permute-start = (f32[256,128]{1,0:T(8,128)S(1)}, f32[256,128]{1,0:T(8,128)S(1)}, u32[]{:S(2)}, u32[]{:S(2)}) collective-permute-start(f32[256,128]{1,0:T(8,128)S(1)} %dynamic-slice_bitcast_fusion), channel_id=1, source_target_pairs={{0,12},{1,15},{2,14},{3,13},{4,8},{5,11},{6,10},{7,9},{8,4},{9,7},... | collective-permute-start | bytes 393224 | tf_op jit(solution)/shard_map/ppermute | solution.py:368
  6.0 1.2 %copy-start = (f32[2,131072]{1,0:T(2,128)S(1)}, f32[2,131072]{1,0:T(2,128)}, u32[]{:S(2)}) copy-start(f32[2,131072]{1,0:T(2,128)} %param.3) | copy-start | bytes 3145732
  7.3 10.7 %collective-permute-start.1 = (f32[256,128]{1,0:T(8,128)S(1)}, f32[256,128]{1,0:T(8,128)S(1)}, u32[]{:S(2)}, u32[]{:S(2)}) collective-permute-start(f32[256,128]{1,0:T(8,128)S(1)} %get-tuple-element.30), channel_id=1, source_target_pairs={{0,14},{1,13},{2,12},{3,15},{4,10},{5,9},{6,8},{7,11},{8,6},{9,5},... | collective-permute-start | bytes 393224 | tf_op jit(solution)/shard_map/ppermute | solution.py:368
  8.6 16.6 %collective-permute-start.2 = (f32[256,128]{1,0:T(8,128)S(1)}, f32[256,128]{1,0:T(8,128)S(1)}, u32[]{:S(2)}, u32[]{:S(2)}) collective-permute-start(f32[256,128]{1,0:T(8,128)S(1)} %get-tuple-element.31), channel_id=1, source_target_pairs={{0,4},{1,7},{2,6},{3,5},{4,0},{5,3},{6,2},{7,1},{8,12},{9,15},{10,... | collective-permute-start | bytes 393224 | tf_op jit(solution)/shard_map/ppermute | solution.py:368
  8.6 16.6 %collective-permute-start.3 = (f32[256,128]{1,0:T(8,128)S(1)}, f32[256,128]{1,0:T(8,128)S(1)}, u32[]{:S(2)}, u32[]{:S(2)}) collective-permute-start(f32[256,128]{1,0:T(8,128)S(1)} %get-tuple-element.32), channel_id=1, source_target_pairs={{0,6},{1,5},{2,4},{3,7},{4,2},{5,1},{6,0},{7,3},{8,14},{9,13},{10,... | collective-permute-start | bytes 393224 | tf_op jit(solution)/shard_map/ppermute | solution.py:368
  10.4 16.3 %collective-permute-start.4 = (f32[256,128]{1,0:T(8,128)S(1)}, f32[256,128]{1,0:T(8,128)S(1)}, u32[]{:S(2)}, u32[]{:S(2)}) collective-permute-start(f32[256,128]{1,0:T(8,128)S(1)} %get-tuple-element.34), channel_id=1, source_target_pairs={{0,8},{1,11},{2,10},{3,9},{4,12},{5,15},{6,14},{7,13},{8,0},{9,3},... | collective-permute-start | bytes 393224 | tf_op jit(solution)/shard_map/ppermute | solution.py:368
  12.7 16.5 %collective-permute-start.5 = (f32[256,128]{1,0:T(8,128)S(1)}, f32[256,128]{1,0:T(8,128)S(1)}, u32[]{:S(2)}, u32[]{:S(2)}) collective-permute-start(f32[256,128]{1,0:T(8,128)S(1)} %get-tuple-element.35), channel_id=1, source_target_pairs={{0,10},{1,9},{2,8},{3,11},{4,14},{5,13},{6,12},{7,15},{8,2},{9,1},... | collective-permute-start | bytes 393224 | tf_op jit(solution)/shard_map/ppermute | solution.py:368
  18.0 11.3 %collective-permute-start.6 = (f32[256,128]{1,0:T(8,128)S(1)}, f32[256,128]{1,0:T(8,128)S(1)}, u32[]{:S(2)}, u32[]{:S(2)}) collective-permute-start(f32[256,128]{1,0:T(8,128)S(1)} %get-tuple-element.36), channel_id=1, source_target_pairs={{0,2},{1,3},{2,0},{3,1},{4,6},{5,7},{6,4},{7,5},{8,10},{9,11},{10,... | collective-permute-start | bytes 393224 | tf_op jit(solution)/shard_map/ppermute | solution.py:368
  18.5 0.7 %copy-start.1 = (s32[18]{0:T(128)S(1)}, s32[18]{0:T(128)}, u32[]{:S(2)}) copy-start(s32[18]{0:T(128)} %bits_ref.1) | copy-start | bytes 220
  31.7 8.3 %collective-permute-start.7 = (f32[2,4,2,16,128]{4,3,2,1,0:T(8,128)S(1)}, f32[2,4,2,16,128]{4,3,2,1,0:T(8,128)S(1)}, u32[]{:S(2)}, u32[]{:S(2)}) collective-permute-start(f32[2,4,2,16,128]{4,3,2,1,0:T(8,128)S(1)} %get-tuple-element.41), channel_id=1, source_target_pairs={{0,12},{1,15},{2,14},{3,13},{4,8},{5,11},{6,10},{7,9},{8,4},{9,7},... | collective-permute-start | bytes 393224 | tf_op jit(solution)/shard_map/ppermute | solution.py:368
  34.3 9.5 %collective-permute-start.8 = (f32[2,4,2,16,128]{4,3,2,1,0:T(8,128)S(1)}, f32[2,4,2,16,128]{4,3,2,1,0:T(8,128)S(1)}, u32[]{:S(2)}, u32[]{:S(2)}) collective-permute-start(f32[2,4,2,16,128]{4,3,2,1,0:T(8,128)S(1)} %get-tuple-element.42), channel_id=1, source_target_pairs={{0,14},{1,13},{2,12},{3,15},{4,10},{5,9},{6,8},{7,11},{8,6},{9,5},... | collective-permute-start | bytes 393224 | tf_op jit(solution)/shard_map/ppermute | solution.py:368
  36.6 9.8 %collective-permute-start.9 = (f32[2,4,2,16,128]{4,3,2,1,0:T(8,128)S(1)}, f32[2,4,2,16,128]{4,3,2,1,0:T(8,128)S(1)}, u32[]{:S(2)}, u32[]{:S(2)}) collective-permute-start(f32[2,4,2,16,128]{4,3,2,1,0:T(8,128)S(1)} %get-tuple-element.43), channel_id=1, source_target_pairs={{0,4},{1,7},{2,6},{3,5},{4,0},{5,3},{6,2},{7,1},{8,12},{9,15},{10,... | collective-permute-start | bytes 393224 | tf_op jit(solution)/shard_map/ppermute | solution.py:368
  36.6 14.7 %collective-permute-start.10 = (f32[2,4,2,16,128]{4,3,2,1,0:T(8,128)S(1)}, f32[2,4,2,16,128]{4,3,2,1,0:T(8,128)S(1)}, u32[]{:S(2)}, u32[]{:S(2)}) collective-permute-start(f32[2,4,2,16,128]{4,3,2,1,0:T(8,128)S(1)} %get-tuple-element.44), channel_id=1, source_target_pairs={{0,6},{1,5},{2,4},{3,7},{4,2},{5,1},{6,0},{7,3},{8,14},{9,13},{10,... | collective-permute-start | bytes 393224 | tf_op jit(solution)/shard_map/ppermute | solution.py:368
  38.6 14.9 %collective-permute-start.11 = (f32[2,4,2,16,128]{4,3,2,1,0:T(8,128)S(1)}, f32[2,4,2,16,128]{4,3,2,1,0:T(8,128)S(1)}, u32[]{:S(2)}, u32[]{:S(2)}) collective-permute-start(f32[2,4,2,16,128]{4,3,2,1,0:T(8,128)S(1)} %get-tuple-element.45), channel_id=1, source_target_pairs={{0,8},{1,11},{2,10},{3,9},{4,12},{5,15},{6,14},{7,13},{8,0},{9,3},... | collective-permute-start | bytes 393224 | tf_op jit(solution)/shard_map/ppermute | solution.py:368
  40.0 16.9 %collective-permute-start.12 = (f32[2,4,2,16,128]{4,3,2,1,0:T(8,128)S(1)}, f32[2,4,2,16,128]{4,3,2,1,0:T(8,128)S(1)}, u32[]{:S(2)}, u32[]{:S(2)}) collective-permute-start(f32[2,4,2,16,128]{4,3,2,1,0:T(8,128)S(1)} %get-tuple-element.46), channel_id=1, source_target_pairs={{0,10},{1,9},{2,8},{3,11},{4,14},{5,13},{6,12},{7,15},{8,2},{9,1},... | collective-permute-start | bytes 393224 | tf_op jit(solution)/shard_map/ppermute | solution.py:368
  43.8 13.1 %collective-permute-start.13 = (f32[2,4,2,16,128]{4,3,2,1,0:T(8,128)S(1)}, f32[2,4,2,16,128]{4,3,2,1,0:T(8,128)S(1)}, u32[]{:S(2)}, u32[]{:S(2)}) collective-permute-start(f32[2,4,2,16,128]{4,3,2,1,0:T(8,128)S(1)} %get-tuple-element.47), channel_id=1, source_target_pairs={{0,2},{1,3},{2,0},{3,1},{4,6},{5,7},{6,4},{7,5},{8,10},{9,11},{10,... | collective-permute-start | bytes 393224 | tf_op jit(solution)/shard_map/ppermute | solution.py:368
  58.0 2.0 %copy-start.2 = (bf16[512,1536]{1,0:T(8,128)(2,1)S(1)}, bf16[512,1536]{1,0:T(8,128)(2,1)}, u32[]{:S(2)}) copy-start(bf16[512,1536]{1,0:T(8,128)(2,1)} %get-tuple-element.52.refs_2_) | copy-start | bytes 4718596
  58.0 2.0 %collective-permute-start.14 = (f32[2,512,128]{2,1,0:T(8,128)S(1)}, f32[2,512,128]{2,1,0:T(8,128)S(1)}, u32[]{:S(2)}, u32[]{:S(2)}) collective-permute-start(f32[2,512,128]{2,1,0:T(8,128)S(1)} %second_section_sent.1), channel_id=1, source_target_pairs={{0,1},{1,0},{2,3},{3,2},{4,5},{5,4},{6,7},{7,6},{8,9},{9,8},{10,11... | collective-permute-start | bytes 1572872 | tf_op jit(solution)/shard_map/ppermute | solution.py:433
